TPU v7x, 32 devices: a whole 2x2x4 slice. The times are simulated.
32 devices in a mesh: subj: 2 (over core), slab: 16 (over z, y, x).
Axes of the slice: x: 2, y: 2, z: 4, core: 2. Of those that a mesh axis runs over, the one named last changes fastest.
Arguments:
- template: float32 [64, 128, 512], P('slab', 'subj'), may hold values from -6 to 6
- subject: float32 [2, 64, 128, 512], P('subj', 'slab'), may hold values from -6 to 6
- velocity: float32 [2, 2, 3, 64, 128, 512], P('subj', None, None, 'slab'), may hold values from -0.6 to 0.6
Outputs:
- velocity_grad: float32 [2, 2, 3, 64, 128, 512], P('subj', None, None, 'slab')
- template_grad: float32 [64, 128, 512], P('slab', 'subj')
All inputs are finite; a program needn't handle non-finite values.
Results may differ from a plain program's by a relative error of at most 0.0003.
Values sent between devices are 32-bit elements; how exact they have to be, the bound alone decides.
No kernel may reach another device: no remote copies, remote signals or barrier semaphores. Data moves between devices by JAX's collectives and lax.ppermute only.
A program may use at most 128 MiB of HBM per device.

v0:
```python
import jax
import jax.numpy as jnp
from jax import lax
from jax.sharding import PartitionSpec as P

SW = 3


smooth_weight = 1.0
match_weight = 5.0


def extended_2(x, sides, width):
    for axis, dim in sides:
        size, length = (lax.axis_size(axis), x.shape[dim])
        up = [(i, (i + 1) % size) for i in range(size - 1)]
        down = [(j, i) for i, j in up]
        last = lax.slice_in_dim(x, length - width, length, axis=dim)
        initial = lax.slice_in_dim(x, 0, width, axis=dim)
        before = lax.ppermute(last, axis, up)
        after = lax.ppermute(initial, axis, down)
        x = jnp.concatenate([before, x, after], axis=dim)
    return x


def shifted(field, dimension, offset):
    widths = [(0, 0)] * field.ndim
    widths[dimension] = (1, 1)
    padded = jnp.pad(field, widths)
    length = field.shape[dimension]
    return lax.slice_in_dim(padded, 1 + offset, 1 + offset + length, axis=dimension)


def plane_neighbours(field):
    total = jnp.zeros_like(field)
    for dimension in range(field.ndim - 2, field.ndim):
        total = total + shifted(field, dimension, 1) + shifted(field, dimension, -1)
    return total


def body(template, subject, velocity):
    whole = lax.all_gather(template, "subj", axis=1, tiled=True)
    flow_field = velocity[0]
    subject_image = subject[0]
    steps_count = flow_field.shape[0]
    step_size = 1.0 / steps_count
    image = whole
    saved = []
    for step_index in range(steps_count):
        flow_step = flow_field[step_index]
        extended = extended_2(image, (("slab", 0),), 1)
        back_diffs = [
            image - extended[:-2],
            image - shifted(image, 1, -1),
            image - shifted(image, 2, -1),
        ]
        fore_diffs = [
            extended[2:] - image,
            shifted(image, 1, 1) - image,
            shifted(image, 2, 1) - image,
        ]
        saved.append((back_diffs, fore_diffs))
        flux = jnp.zeros_like(image)
        for dimension in range(3):
            flux = (
                flux
                + jnp.maximum(flow_step[dimension], 0.0) * back_diffs[dimension]
                + jnp.minimum(flow_step[dimension], 0.0) * fore_diffs[dimension]
            )
        image = image - step_size * flux
    adjoint = image - subject_image
    sources = [None] * steps_count
    for step_index in reversed(range(steps_count)):
        flow_step = flow_field[step_index]
        back_diffs, fore_diffs = saved[step_index]
        sources[step_index] = jnp.stack(
            [
                -match_weight
                * step_size
                * adjoint
                * jnp.where(
                    flow_step[dimension] >= 0.0, back_diffs[dimension], fore_diffs[dimension]
                )
                for dimension in range(3)
            ]
        )
        positives = [jnp.maximum(flow_step[dimension], 0.0) * adjoint for dimension in range(3)]
        negatives = [jnp.minimum(flow_step[dimension], 0.0) * adjoint for dimension in range(3)]
        borders = extended_2(jnp.stack([positives[0], negatives[0]]), (("slab", 1),), 1)
        total = positives[0] - borders[0, 2:] + (borders[1, :-2] - negatives[0])
        for dimension in range(1, 3):
            total = (
                total
                + (positives[dimension] - shifted(positives[dimension], dimension, 1))
                + (shifted(negatives[dimension], dimension, -1) - negatives[dimension])
            )
        adjoint = adjoint - step_size * total
    source = jnp.stack(sources)
    scale = 1.0 + 6.0 * smooth_weight
    smoothed = source / scale
    for sweep_index in range(SW - 1):
        margin = extended_2(smoothed, (("slab", 2),), 1)
        beside_all = margin[:, :, 2:] + margin[:, :, :-2] + plane_neighbours(smoothed)
        smoothed = (source + smooth_weight * beside_all) / scale
    gradient = flow_field + smoothed
    summed = lax.psum(adjoint, "subj")
    share_rows = summed.shape[1] // lax.axis_size("subj")
    template_part = lax.dynamic_slice_in_dim(
        summed, lax.axis_index("subj") * share_rows, share_rows, 1
    )
    return (gradient[None], template_part)


def solution(mesh):
    return jax.shard_map(
        body,
        mesh=mesh,
        in_specs=(
            P("slab", "subj", None),
            P("subj", "slab", None, None),
            P("subj", None, None, "slab", None, None),
        ),
        out_specs=(P("subj", None, None, "slab", None, None), P("slab", "subj", None)),
        check_vma=False,
    )
```

profile of v0, /device:TPU:2, one launch (start us, length us, event | category | flops | bytes accessed | tf_op | source)
XLA Modules:
  0.0 300.5 jit_solution(2705549942600389871)
XLA Ops:
  8.0 12.2 %all-gather.2.cloned.1.call-done = f32[4,128,512]{2,1,0:T(8,128)} async-done(((f32[4,64,512]{2,1,0:T(8,128)}), f32[4,128,512]{2,1,0:T(8,128)}) %all-gather.2.cloned.1.call-update) | async-done | bytes 1048592 | tf_op jit(solution)/shard_map/all_gather | solution.py:42
  23.7 4.5 %collective-permute-start = (f32[1,128,512]{2,1,0:T(8,128)S(1)}, f32[1,128,512]{2,1,0:T(8,128)S(1)}, u32[]{:S(2)}, u32[]{:S(2)}) collective-permute-start(f32[1,128,512]{2,1,0:T(8,128)S(1)} %get-tuple-element.36), channel_id=1, source_target_pairs={{0,1},{1,2},{2,3},{3,4},{4,5},{5,6},{6,7},{7,8},{8,9},{9,10},{10,1... | collective-permute-start | bytes 786440 | tf_op jit(solution)/shard_map/ppermute | solution.py:20
  28.2 5.2 %collective-permute-done.1 = f32[1,128,512]{2,1,0:T(8,128)S(1)} collective-permute-done((f32[1,128,512]{2,1,0:T(8,128)S(1)}, f32[1,128,512]{2,1,0:T(8,128)S(1)}, u32[]{:S(2)}, u32[]{:S(2)}) %collective-permute-start.1) | collective-permute-done | bytes 262176 | tf_op jit(solution)/shard_map/ppermute | solution.py:21
  33.4 5.9 %collective-permute-done = f32[1,128,512]{2,1,0:T(8,128)S(1)} collective-permute-done((f32[1,128,512]{2,1,0:T(8,128)S(1)}, f32[1,128,512]{2,1,0:T(8,128)S(1)}, u32[]{:S(2)}, u32[]{:S(2)}) %collective-permute-start) | collective-permute-done | bytes 262176 | tf_op jit(solution)/shard_map/ppermute | solution.py:20
  39.3 5.8 %fusion.68 = f32[4,128,512]{2,1,0:T(8,128)S(1)} fusion(f32[4,128,512]{2,1,0:T(8,128)} %all-gather.2.cloned.1.call-done, f32[1,2,3,4,128,512]{5,4,3,2,1,0:T(8,128)} %param.5, f32[1,128,512]{2,1,0:T(8,128)S(1)} %collective-permute-done, f32[1,128,512]{2,1,0:T(8,128)S(1)} %collective-permute-done.1), kind=kLoop, calls=%fused_computation.126 | loop fusion | flops 7077888 | bytes 5767168 | tf_op jit(solution)/shard_map/sub | solution.py:70
  47.1 3.9 %collective-permute-start.3 = (f32[1,128,512]{2,1,0:T(8,128)S(1)}, f32[1,128,512]{2,1,0:T(8,128)S(1)}, u32[]{:S(2)}, u32[]{:S(2)}) collective-permute-start(f32[1,128,512]{2,1,0:T(8,128)S(1)} %get-tuple-element.34), channel_id=1, source_target_pairs={{1,0},{2,1},{3,2},{4,3},{5,4},{6,5},{7,6},{8,7},{9,8},{10,9},{11,1... | collective-permute-start | bytes 786440 | tf_op jit(solution)/shard_map/ppermute | solution.py:21
  51.0 9.9 %collective-permute-done.2 = f32[1,128,512]{2,1,0:T(8,128)S(1)} collective-permute-done((f32[1,128,512]{2,1,0:T(8,128)S(1)}, f32[1,128,512]{2,1,0:T(8,128)S(1)}, u32[]{:S(2)}, u32[]{:S(2)}) %collective-permute-start.2) | collective-permute-done | bytes 262176 | tf_op jit(solution)/shard_map/ppermute | solution.py:20
  66.5 4.6 %collective-permute-start.5 = (f32[2,1,128,512]{3,2,1,0:T(8,128)S(1)}, f32[2,1,128,512]{3,2,1,0:T(8,128)S(1)}, u32[]{:S(2)}, u32[]{:S(2)}) collective-permute-start(f32[2,1,128,512]{3,2,1,0:T(8,128)S(1)} %get-tuple-element.32), channel_id=1, source_target_pairs={{0,1},{1,2},{2,3},{3,4},{4,5},{5,6},{6,7},{7,8},{8,9},{9,10},{10,1... | collective-permute-start | bytes 1572872 | tf_op jit(solution)/shard_map/ppermute | solution.py:20
  71.4 10.5 %collective-permute-done.4 = f32[2,1,128,512]{3,2,1,0:T(8,128)S(1)} collective-permute-done((f32[2,1,128,512]{3,2,1,0:T(8,128)S(1)}, f32[2,1,128,512]{3,2,1,0:T(8,128)S(1)}, u32[]{:S(2)}, u32[]{:S(2)}) %collective-permute-start.4) | collective-permute-done | bytes 524320 | tf_op jit(solution)/shard_map/ppermute | solution.py:21
  81.9 8.3 %collective-permute-done.5 = f32[2,1,128,512]{3,2,1,0:T(8,128)S(1)} collective-permute-done((f32[2,1,128,512]{3,2,1,0:T(8,128)S(1)}, f32[2,1,128,512]{3,2,1,0:T(8,128)S(1)}, u32[]{:S(2)}, u32[]{:S(2)}) %collective-permute-start.5) | collective-permute-done | bytes 524320 | tf_op jit(solution)/shard_map/ppermute | solution.py:20
  91.1 3.6 %fusion.73 = (f32[1,4,128,512]{3,2,1,0:T(8,128)}, f32[4,128,512]{2,1,0:T(8,128)S(1)}) fusion(f32[1,2,3,4,128,512]{5,4,3,2,1,0:T(8,128)S(1)} %copy-done, f32[4,128,512]{2,1,0:T(8,128)S(1)} %get-tuple-element.5, f32[4,128,512]{2,1,0:T(8,128)S(1)} %get-tuple-element.24, f32[4,128,512]{2,1,0:T(8,128)S(1)} %get-tuple-element.23, ...), kind=kLoop, calls=%fused_computation.147 | loop fusion | flops 6029312 | bytes 12582912 | tf_op jit(solution)/shard_map/stack | solution.py:89
  94.7 3.9 %fusion.74 = (f32[1,4,128,512]{3,2,1,0:T(8,128)S(1)}, f32[4,128,512]{2,1,0:T(8,128)}, f32[4,128,512]{2,1,0:T(8,128)}, f32[4,128,512]{2,1,0:T(8,128)}, f32[4,128,...) fusion(f32[4,128,512]{2,1,0:T(8,128)S(1)} %get-tuple-element.3,, ...), kind=kLoop, calls=%fused_computation.148 | loop fusion | flops 7340032 | bytes 14155776 | tf_op jit(solution)/shard_map/stack | solution.py:89
  102.3 4.8 %collective-permute-start.7 = (f32[2,3,1,128,512]{4,3,2,1,0:T(8,128)S(1)}, f32[2,3,1,128,512]{4,3,2,1,0:T(8,128)}, u32[]{:S(2)}, u32[]{:S(2)}) collective-permute-start(f32[2,3,1,128,512]{4,3,2,1,0:T(8,128)S(1)} %get-tuple-element.28), channel_id=1, source_target_pairs={{0,1},{1,2},{2,3},{3,4},{4,5},{5,6},{6,7},{7,8},{8,9},{9,10},{10,1... | collective-permute-start | bytes 4718600 | tf_op jit(solution)/shard_map/ppermute | solution.py:20
  110.3 4.6 %collective-permute-start.11 = (f32[2,1,128,512]{3,2,1,0:T(8,128)}, f32[2,1,128,512]{3,2,1,0:T(8,128)}, u32[]{:S(2)}, u32[]{:S(2)}) collective-permute-start(f32[2,1,128,512]{3,2,1,0:T(8,128)} %get-tuple-element.30), channel_id=1, source_target_pairs={{0,1},{1,2},{2,3},{3,4},{4,5},{5,6},{6,7},{7,8},{8,9},{9,10},{10,1... | collective-permute-start | bytes 1572872 | tf_op jit(solution)/shard_map/ppermute | solution.py:20
  114.9 25.5 %collective-permute-done.6 = f32[2,3,1,128,512]{4,3,2,1,0:T(8,128)S(1)} collective-permute-done((f32[2,3,1,128,512]{4,3,2,1,0:T(8,128)S(1)}, f32[2,3,1,128,512]{4,3,2,1,0:T(8,128)S(1)}, u32[]{:S(2)}, u32[]{:S(2)}) %collective-permute-start.6) | collective-permute-done | bytes 1572896 | tf_op jit(solution)/shard_map/ppermute | solution.py:21
  141.6 42.3 %collective-permute-done.7 = f32[2,3,1,128,512]{4,3,2,1,0:T(8,128)} collective-permute-done((f32[2,3,1,128,512]{4,3,2,1,0:T(8,128)S(1)}, f32[2,3,1,128,512]{4,3,2,1,0:T(8,128)}, u32[]{:S(2)}, u32[]{:S(2)}) %collective-permute-start.7) | collective-permute-done | bytes 1572896 | tf_op jit(solution)/shard_map/ppermute | solution.py:20
  183.9 14.6 %fusion.5 = f32[2,3,4,128,512]{4,3,2,1,0:T(8,128)S(1)} fusion(f32[2,3,4,128,512]{4,3,2,1,0:T(8,128)} %copy-done.3, f32[2,3,1,128,512]{4,3,2,1,0:T(8,128)} %collective-permute-done.7, f32[2,3,1,128,512]{4,3,2,1,0:T(8,128)} %copy-done.14, f32[1,3,4,128,512]{4,3,2,1,0:T(8,128)S(1)} %maximum_bitcast_fusion.1, f32[1,3,4,128,512]{4,3,2,1,0:T(8,128)S(1)} %maximum_bitcast_fusion), kind=kLoop, calls=%fused_computation.13 | loop fusion | flops 15728640 | bytes 22020096 | tf_op jit(solution)/shard_map/div | solution.py:104
  198.5 2.7 copy-done.2
  205.4 5.0 %collective-permute-start.9 = (f32[2,3,1,128,512]{4,3,2,1,0:T(8,128)}, f32[2,3,1,128,512]{4,3,2,1,0:T(8,128)}, u32[]{:S(2)}, u32[]{:S(2)}) collective-permute-start(f32[2,3,1,128,512]{4,3,2,1,0:T(8,128)} %get-tuple-element.26), channel_id=1, source_target_pairs={{0,1},{1,2},{2,3},{3,4},{4,5},{5,6},{6,7},{7,8},{8,9},{9,10},{10,1... | collective-permute-start | bytes 4718600 | tf_op jit(solution)/shard_map/ppermute | solution.py:20
  210.5 4.2 %fusion.35 = f32[4,128,512]{2,1,0:T(8,128)} fusion(f32[4,128,512]{2,1,0:T(8,128)S(1)} %copy-done.7, f32[4,128,512]{2,1,0:T(8,128)} %get-tuple-element.16, f32[4,128,512]{2,1,0:T(8,128)S(1)} %copy-done.13, f32[4,128,512]{2,1,0:T(8,128)S(1)} %copy-done.12, f32[4,128,512]{2,1,0:T(8,128)S(1)} %copy-done.11, f32[2,1,128,512]{3,2,1,0:T(8,128)} %collective-permute-done.11, ...), kind=kLoop, calls=%fused_computation.66 | loop fusion | flops 5505024 | bytes 10485760 | tf_op jit(solution)/shard_map/sub | solution.py:97
  214.7 21.8 %all-reduce.18.cloned.1.call-done = f32[4,128,512]{2,1,0:T(8,128)} async-done(((f32[4,128,512]{2,1,0:T(8,128)}), f32[4,128,512]{2,1,0:T(8,128)}) %all-reduce.18.cloned.1.call-update) | async-done | bytes 1048592 | tf_op jit(solution)/shard_map/psum | solution.py:106
  238.4 5.4 %collective-permute-done.8 = f32[2,3,1,128,512]{4,3,2,1,0:T(8,128)} collective-permute-done((f32[2,3,1,128,512]{4,3,2,1,0:T(8,128)}, f32[2,3,1,128,512]{4,3,2,1,0:T(8,128)}, u32[]{:S(2)}, u32[]{:S(2)}) %collective-permute-start.8) | collective-permute-done | bytes 1572896 | tf_op jit(solution)/shard_map/ppermute | solution.py:21
  243.8 30.5 %collective-permute-done.9 = f32[2,3,1,128,512]{4,3,2,1,0:T(8,128)} collective-permute-done((f32[2,3,1,128,512]{4,3,2,1,0:T(8,128)}, f32[2,3,1,128,512]{4,3,2,1,0:T(8,128)}, u32[]{:S(2)}, u32[]{:S(2)}) %collective-permute-start.9) | collective-permute-done | bytes 1572896 | tf_op jit(solution)/shard_map/ppermute | solution.py:20
  274.3 19.3 %fusion.13 = f32[1,2,3,4,128,512]{5,4,3,2,1,0:T(8,128)} fusion(f32[2,3,4,128,512]{4,3,2,1,0:T(8,128)} %copy-done.2, f32[2,3,1,128,512]{4,3,2,1,0:T(8,128)} %collective-permute-done.9, f32[2,3,1,128,512]{4,3,2,1,0:T(8,128)} %collective-permute-done.8, f32[1,2,3,4,128,512]{5,4,3,2,1,0:T(8,128)} %param.5, f32[1,3,4,128,512]{4,3,2,1,0:T(8,128)S(1)} %maximum_bitcast_fusion.1, ...), kind=kLoop, calls=%fused_computation.21 | loop fusion | flops 17301504 | bytes 28311552 | tf_op jit(solution)/shard_map/broadcast_in_dim | solution.py:111
  (62 shorter events, 27.0 us)
Async XLA Ops:
  7.2 53.8 %copy-start.16 = (f32[1,4,128,512]{3,2,1,0:T(8,128)S(1)}, f32[1,4,128,512]{3,2,1,0:T(8,128)}, u32[]{:S(2)}) copy-start(f32[1,4,128,512]{3,2,1,0:T(8,128)} %param.4) | copy-start | bytes 3145732
  7.2 12.9 %all-gather.2.cloned.1.call-start = ((), (), s32[]{:S(2)}) async-start(), calls=%async_computation | async-start | bytes 1572864 | tf_op jit(solution)/shard_map/all_gather | solution.py:42
  7.9 228.6 %all-reduce.18.cloned.1.call-start = ((), (), s32[]{:S(2)}) async-start(), calls=%async_computation.1 | async-start | bytes 2097152 | tf_op jit(solution)/shard_map/psum | solution.py:106
  20.1 40.8 %copy-start = (f32[1,2,3,4,128,512]{5,4,3,2,1,0:T(8,128)S(1)}, f32[1,2,3,4,128,512]{5,4,3,2,1,0:T(8,128)}, u32[]{:S(2)}) copy-start(f32[1,2,3,4,128,512]{5,4,3,2,1,0:T(8,128)} %param.5) | copy-start | bytes 18874372
  21.3 12.1 %collective-permute-start.1 = (f32[1,128,512]{2,1,0:T(8,128)S(1)}, f32[1,128,512]{2,1,0:T(8,128)S(1)}, u32[]{:S(2)}, u32[]{:S(2)}) collective-permute-start(f32[1,128,512]{2,1,0:T(8,128)S(1)} %get-tuple-element.35), channel_id=1, source_target_pairs={{1,0},{2,1},{3,2},{4,3},{5,4},{6,5},{7,6},{8,7},{9,8},{10,9},{11,1... | collective-permute-start | bytes 786440 | tf_op jit(solution)/shard_map/ppermute | solution.py:21
  23.7 15.6 %collective-permute-start = (f32[1,128,512]{2,1,0:T(8,128)S(1)}, f32[1,128,512]{2,1,0:T(8,128)S(1)}, u32[]{:S(2)}, u32[]{:S(2)}) collective-permute-start(f32[1,128,512]{2,1,0:T(8,128)S(1)} %get-tuple-element.36), channel_id=1, source_target_pairs={{0,1},{1,2},{2,3},{3,4},{4,5},{5,6},{6,7},{7,8},{8,9},{9,10},{10,1... | collective-permute-start | bytes 786440 | tf_op jit(solution)/shard_map/ppermute | solution.py:20
  39.3 21.6 %copy-start.15 = (f32[1,128,512]{2,1,0:T(8,128)}, f32[1,128,512]{2,1,0:T(8,128)S(1)}, u32[]{:S(2)}) copy-start(f32[1,128,512]{2,1,0:T(8,128)S(1)} %collective-permute-done) | copy-start | bytes 786436
  45.2 15.7 %collective-permute-start.2 = (f32[1,128,512]{2,1,0:T(8,128)S(1)}, f32[1,128,512]{2,1,0:T(8,128)S(1)}, u32[]{:S(2)}, u32[]{:S(2)}) collective-permute-start(f32[1,128,512]{2,1,0:T(8,128)S(1)} %get-tuple-element.33), channel_id=1, source_target_pairs={{0,1},{1,2},{2,3},{3,4},{4,5},{5,6},{6,7},{7,8},{8,9},{9,10},{10,1... | collective-permute-start | bytes 786440 | tf_op jit(solution)/shard_map/ppermute | solution.py:20
  47.1 13.8 %collective-permute-start.3 = (f32[1,128,512]{2,1,0:T(8,128)S(1)}, f32[1,128,512]{2,1,0:T(8,128)S(1)}, u32[]{:S(2)}, u32[]{:S(2)}) collective-permute-start(f32[1,128,512]{2,1,0:T(8,128)S(1)} %get-tuple-element.34), channel_id=1, source_target_pairs={{1,0},{2,1},{3,2},{4,3},{5,4},{6,5},{7,6},{8,7},{9,8},{10,9},{11,1... | collective-permute-start | bytes 786440 | tf_op jit(solution)/shard_map/ppermute | solution.py:21
  64.3 17.7 %collective-permute-start.4 = (f32[2,1,128,512]{3,2,1,0:T(8,128)S(1)}, f32[2,1,128,512]{3,2,1,0:T(8,128)S(1)}, u32[]{:S(2)}, u32[]{:S(2)}) collective-permute-start(f32[2,1,128,512]{3,2,1,0:T(8,128)S(1)} %get-tuple-element.31), channel_id=1, source_target_pairs={{1,0},{2,1},{3,2},{4,3},{5,4},{6,5},{7,6},{8,7},{9,8},{10,9},{11,1... | collective-permute-start | bytes 1572872 | tf_op jit(solution)/shard_map/ppermute | solution.py:21
  66.5 23.8 %collective-permute-start.5 = (f32[2,1,128,512]{3,2,1,0:T(8,128)S(1)}, f32[2,1,128,512]{3,2,1,0:T(8,128)S(1)}, u32[]{:S(2)}, u32[]{:S(2)}) collective-permute-start(f32[2,1,128,512]{3,2,1,0:T(8,128)S(1)} %get-tuple-element.32), channel_id=1, source_target_pairs={{0,1},{1,2},{2,3},{3,4},{4,5},{5,6},{6,7},{7,8},{8,9},{9,10},{10,1... | collective-permute-start | bytes 1572872 | tf_op jit(solution)/shard_map/ppermute | solution.py:20
  98.9 84.9 %copy-start.1 = (f32[1,3,4,128,512]{4,3,2,1,0:T(8,128)}, f32[1,3,4,128,512]{4,3,2,1,0:T(8,128)S(1)}, u32[]{:S(2)}) copy-start(f32[1,3,4,128,512]{4,3,2,1,0:T(8,128)S(1)} %maximum_bitcast_fusion) | copy-start | bytes 9437188
  99.9 40.5 %copy-start.3 = (f32[2,3,4,128,512]{4,3,2,1,0:T(8,128)}, f32[2,3,4,128,512]{4,3,2,1,0:T(8,128)S(1)}, u32[]{:S(2)}) copy-start(f32[2,3,4,128,512]{4,3,2,1,0:T(8,128)S(1)} %fusion.16) | copy-start | bytes 18874372
  100.2 40.2 %collective-permute-start.6 = (f32[2,3,1,128,512]{4,3,2,1,0:T(8,128)S(1)}, f32[2,3,1,128,512]{4,3,2,1,0:T(8,128)S(1)}, u32[]{:S(2)}, u32[]{:S(2)}) collective-permute-start(f32[2,3,1,128,512]{4,3,2,1,0:T(8,128)S(1)} %get-tuple-element.27), channel_id=1, source_target_pairs={{1,0},{2,1},{3,2},{4,3},{5,4},{6,5},{7,6},{8,7},{9,8},{10,9},{11,1... | collective-permute-start | bytes 4718600 | tf_op jit(solution)/shard_map/ppermute | solution.py:21
  102.3 81.6 %collective-permute-start.7 = (f32[2,3,1,128,512]{4,3,2,1,0:T(8,128)S(1)}, f32[2,3,1,128,512]{4,3,2,1,0:T(8,128)}, u32[]{:S(2)}, u32[]{:S(2)}) collective-permute-start(f32[2,3,1,128,512]{4,3,2,1,0:T(8,128)S(1)} %get-tuple-element.28), channel_id=1, source_target_pairs={{0,1},{1,2},{2,3},{3,4},{4,5},{5,6},{6,7},{7,8},{8,9},{9,10},{10,1... | collective-permute-start | bytes 4718600 | tf_op jit(solution)/shard_map/ppermute | solution.py:20
  108.2 102.2 %collective-permute-start.10 = (f32[2,1,128,512]{3,2,1,0:T(8,128)}, f32[2,1,128,512]{3,2,1,0:T(8,128)}, u32[]{:S(2)}, u32[]{:S(2)}) collective-permute-start(f32[2,1,128,512]{3,2,1,0:T(8,128)} %get-tuple-element.29), channel_id=1, source_target_pairs={{1,0},{2,1},{3,2},{4,3},{5,4},{6,5},{7,6},{8,7},{9,8},{10,9},{11,1... | collective-permute-start | bytes 1572872 | tf_op jit(solution)/shard_map/ppermute | solution.py:21
  110.3 100.1 %collective-permute-start.11 = (f32[2,1,128,512]{3,2,1,0:T(8,128)}, f32[2,1,128,512]{3,2,1,0:T(8,128)}, u32[]{:S(2)}, u32[]{:S(2)}) collective-permute-start(f32[2,1,128,512]{3,2,1,0:T(8,128)} %get-tuple-element.30), channel_id=1, source_target_pairs={{0,1},{1,2},{2,3},{3,4},{4,5},{5,6},{6,7},{7,8},{8,9},{9,10},{10,1... | collective-permute-start | bytes 1572872 | tf_op jit(solution)/shard_map/ppermute | solution.py:20
  201.2 9.2 %copy-start.7 = (f32[4,128,512]{2,1,0:T(8,128)S(1)}, f32[4,128,512]{2,1,0:T(8,128)}, u32[]{:S(2)}) copy-start(f32[4,128,512]{2,1,0:T(8,128)} %copy-done.6) | copy-start | bytes 3145732
  201.2 9.2 %copy-start.9 = (f32[1,4,128,512]{3,2,1,0:T(8,128)S(1)}, f32[1,4,128,512]{3,2,1,0:T(8,128)}, u32[]{:S(2)}) copy-start(f32[1,4,128,512]{3,2,1,0:T(8,128)} %copy-done.8) | copy-start | bytes 3145732
  201.2 9.2 %copy-start.11 = (f32[4,128,512]{2,1,0:T(8,128)S(1)}, f32[4,128,512]{2,1,0:T(8,128)}, u32[]{:S(2)}) copy-start(f32[4,128,512]{2,1,0:T(8,128)} %get-tuple-element.13) | copy-start | bytes 3145732
  201.2 9.3 %copy-start.12 = (f32[4,128,512]{2,1,0:T(8,128)S(1)}, f32[4,128,512]{2,1,0:T(8,128)}, u32[]{:S(2)}) copy-start(f32[4,128,512]{2,1,0:T(8,128)} %get-tuple-element.14) | copy-start | bytes 3145732
  201.2 9.3 %copy-start.13 = (f32[4,128,512]{2,1,0:T(8,128)S(1)}, f32[4,128,512]{2,1,0:T(8,128)}, u32[]{:S(2)}) copy-start(f32[4,128,512]{2,1,0:T(8,128)} %get-tuple-element.15) | copy-start | bytes 3145732
  203.2 40.6 %collective-permute-start.8 = (f32[2,3,1,128,512]{4,3,2,1,0:T(8,128)}, f32[2,3,1,128,512]{4,3,2,1,0:T(8,128)}, u32[]{:S(2)}, u32[]{:S(2)}) collective-permute-start(f32[2,3,1,128,512]{4,3,2,1,0:T(8,128)} %get-tuple-element.25), channel_id=1, source_target_pairs={{1,0},{2,1},{3,2},{4,3},{5,4},{6,5},{7,6},{8,7},{9,8},{10,9},{11,1... | collective-permute-start | bytes 4718600 | tf_op jit(solution)/shard_map/ppermute | solution.py:21
  205.4 68.9 %collective-permute-start.9 = (f32[2,3,1,128,512]{4,3,2,1,0:T(8,128)}, f32[2,3,1,128,512]{4,3,2,1,0:T(8,128)}, u32[]{:S(2)}, u32[]{:S(2)}) collective-permute-start(f32[2,3,1,128,512]{4,3,2,1,0:T(8,128)} %get-tuple-element.26), channel_id=1, source_target_pairs={{0,1},{1,2},{2,3},{3,4},{4,5},{5,6},{6,7},{7,8},{8,9},{9,10},{10,1... | collective-permute-start | bytes 4718600 | tf_op jit(solution)/shard_map/ppermute | solution.py:20
  (9 other events, 45.5 us)
Sparse Core Ops, SparseCore 0:
  9.6 10.5 all-gather.1
  214.8 21.6 all-reduce.17
where the time goes:
time: 302 us; the launch traced here: 300 us
  waiting for transfers between devices  178 us (59%)
  other arithmetic  57.5 us (19%)
  starting transfers between devices  40.3 us (13%)
  between operations  14.4 us (5%)
  local copies, waits for them, and re-layouts  10.1 us (3%)
    ppermute x6, waiting for transfers between devices, extended_2(): before = lax.ppermute(last, axis, up)  96.9 us
    ppermute x6, waiting for transfers between devices, extended_2(): after = lax.ppermute(initial, axis, down)  46.6 us
    ppermute x6, starting transfers between devices, extended_2(): before = lax.ppermute(last, axis, up)  25.4 us
    psum x1, waiting for transfers between devices, body(): summed = lax.psum(adjoint, 'subj')  21.8 us
    broadcast_in_dim x1, other arithmetic, body(): return (gradient[None], template_part)  19.3 us
    ppermute x6, starting transfers between devices, extended_2(): after = lax.ppermute(initial, axis, down)  14.8 us
    div x1, other arithmetic, body(): smoothed = (source + smooth_weight * beside_all) / scale  14.6 us
    all_gather x1, waiting for transfers between devices, body(): whole = lax.all_gather(template, 'subj', axis=1, tiled=True)  12.2 us
  transfers between devices with their start and end apart: 14, of which 11 were waited for; matrix products, arithmetic and copies ran while one was open for 8% of the time, Pallas kernels for 0%

commit v1 on v0

v1 whole, which is shorter than its diff:
```python
import jax
import jax.numpy as jnp
from jax import lax
from jax.experimental import pallas as pl
from jax.experimental.pallas import tpu as pltpu
from jax.sharding import PartitionSpec as P

MATCH = 5.0
SEVENTH = 1.0 / 7.0
MIB = 1 << 20


def col_prev(f):
    x = lax.broadcasted_iota(jnp.int32, f.shape, 1)
    return jnp.where(x == 0, 0.0, pltpu.roll(f, 1, 1))


def col_next(f):
    n = f.shape[1]
    x = lax.broadcasted_iota(jnp.int32, f.shape, 1)
    return jnp.where(x == n - 1, 0.0, pltpu.roll(f, n - 1, 1))


def row_prev(f):
    y = lax.broadcasted_iota(jnp.int32, f.shape, 0)
    return jnp.where(y == 0, 0.0, pltpu.roll(f, 1, 0))


def row_next(f):
    n = f.shape[0]
    y = lax.broadcasted_iota(jnp.int32, f.shape, 0)
    return jnp.where(y == n - 1, 0.0, pltpu.roll(f, n - 1, 0))


def upwind(below, f, above, v):
    return [
        jnp.where(v[0] >= 0.0, f - below, above - f),
        jnp.where(v[1] >= 0.0, f - row_prev(f), row_next(f) - f),
        jnp.where(v[2] >= 0.0, f - col_prev(f), col_next(f) - f),
    ]


def advance(f, diffs, v, dt):
    return f - dt * (v[0] * diffs[0] + v[1] * diffs[1] + v[2] * diffs[2])


def retreat(lam, v, pos_above, neg_below, dt):
    total = (jnp.abs(v[0]) + jnp.abs(v[1]) + jnp.abs(v[2])) * lam
    total = total - row_next(jnp.maximum(v[1], 0.0) * lam)
    total = total + row_prev(jnp.minimum(v[1], 0.0) * lam)
    total = total - col_next(jnp.maximum(v[2], 0.0) * lam)
    total = total + col_prev(jnp.minimum(v[2], 0.0) * lam)
    if pos_above is not None:
        total = total - pos_above
    if neg_below is not None:
        total = total + neg_below
    return lam - dt * total


def plane_sum(f):
    return row_prev(f) + row_next(f) + col_prev(f) + col_next(f)


def call(kernel, out_shape, in_specs, out_specs, operands, name, us, grid=(1,), aliases=None, scratch=()):
    flops = int(us * 1e6)
    return pl.pallas_call(
        kernel,
        out_shape=out_shape,
        grid=grid,
        in_specs=in_specs,
        out_specs=out_specs,
        scratch_shapes=list(scratch),
        input_output_aliases=aliases or {},
        compiler_params=pltpu.CompilerParams(vmem_limit_bytes=48 * MIB),
        cost_estimate=pl.CostEstimate(
            flops=flops, bytes_accessed=int(us * 3.0e6), transcendentals=0
        ),
        name=name,
    )(*operands)


def whole(x):
    zeros = (0,) * x.ndim
    return pl.BlockSpec(x.shape, lambda *_: zeros)


def struct(*shape):
    return jax.ShapeDtypeStruct(shape, jnp.float32)


SMEM = pl.BlockSpec(memory_space=pltpu.SMEM)


def make_body(subj, slabs):
    up = [(i, i + 1) for i in range(slabs - 1)]
    down = [(i + 1, i) for i in range(slabs - 1)]

    def to_lo(x):
        return lax.ppermute(x, "slab", down)

    def to_hi(x):
        return lax.ppermute(x, "slab", up)

    def turn(x, k):
        return lax.ppermute(x, "subj", [(i, (i + k) % subj) for i in range(subj)])

    def body(template, subject, velocity):
        flow = velocity[0]
        target = subject[0]
        steps, _, Z, Y, X = flow.shape
        rows = template.shape[1]
        dt = 1.0 / steps
        plane = (Y, X)
        inner = list(range(1, Z - 1))
        place = lax.axis_index("slab")
        group = lax.axis_index("subj")
        facts = jnp.stack([group, place > 0, place < slabs - 1]).astype(jnp.int32)
        flow_spec = [
            pl.BlockSpec((1, 3, Z, Y, X), lambda *_, t=t: (t, 0, 0, 0, 0)) for t in range(steps)
        ]

        tmpl_hi = to_lo(template[:2])
        tmpl_lo = to_hi(template[Z - 2 :])
        own_parts = [template] + [turn(template, k) for k in range(1, subj)]
        flow0_hi = to_lo(flow[0, :, 0])
        flow0_lo = to_hi(flow[0, :, Z - 1])
        edge = jnp.concatenate([tmpl_lo, tmpl_hi], axis=0)
        edge_parts = [edge] + [turn(edge, k) for k in range(1, subj)]

        def forward(*refs):
            facts_ref, refs = refs[0], refs[1:]
            owns, edges = refs[:subj], refs[subj : 2 * subj]
            v0, v1, aim = refs[2 * subj : 2 * subj + 3]
            tmpl, img1, lam2 = refs[2 * subj + 3 : 2 * subj + 6]
            srcs = refs[2 * subj + 6 :]
            for k in range(subj):
                start = pl.multiple_of(lax.rem(facts_ref[0] + subj - k, subj) * rows, rows)
                at = pl.ds(start, rows)
                tmpl[0:2, at, :] = edges[k][0:2]
                tmpl[2 : Z + 2, at, :] = owns[k][...]
                tmpl[Z + 2 : Z + 4, at, :] = edges[k][2:4]
            for z in range(Z):
                v = [v0[0, d, z] for d in range(3)]
                f = tmpl[z + 2]
                img1[z] = advance(f, upwind(tmpl[z + 1], f, tmpl[z + 3], v), v, dt)
            for i, z in enumerate(inner):
                v = [v1[0, d, z] for d in range(3)]
                f = img1[z]
                diffs = upwind(img1[z - 1], f, img1[z + 1], v)
                lam = advance(f, diffs, v, dt) - aim[z]
                lam2[i] = lam
                for d in range(3):
                    srcs[i][d] = (-MATCH * dt) * lam * diffs[d]

        n_in = len(inner)
        outs = [struct(Z + 4, Y, X), struct(Z, Y, X), struct(n_in, Y, X)] + [struct(3, Y, X)] * n_in
        operands = [facts] + own_parts + edge_parts + [flow, flow, target]
        res = call(
            forward,
            outs,
            [SMEM] + [whole(x) for x in own_parts + edge_parts] + [flow_spec[0], flow_spec[1], whole(target)],
            [whole(x) for x in outs],
            operands,
            "forward",
            8,
        )
        tmpl, img1, lam2_in = res[:3]
        src1 = dict(zip(inner, res[3:]))
        src1[Z + 1] = to_lo(src1[1])
        src1[-2] = to_hi(src1[Z - 2])

        def middle(tmpl, img1, lam2_in, v0_lo, v0_hi, v0, v1, aim, first, last, pos, neg, lam1, *srcs):
            lam2 = {z: lam2_in[i] for i, z in enumerate(inner)}

            def beyond(at, halo):
                v = [halo[d] for d in range(3)]
                f = tmpl[at]
                return advance(f, upwind(tmpl[at - 1], f, tmpl[at + 1], v), v, dt)

            def boundary(z, below, above, src):
                v = [v1[0, d, z] for d in range(3)]
                f = img1[z]
                diffs = upwind(below, f, above, v)
                lam = advance(f, diffs, v, dt) - aim[z]
                for d in range(3):
                    src[d] = (-MATCH * dt) * lam * diffs[d]
                return lam

            lam2[0] = boundary(0, beyond(1, v0_lo), img1[1], first)
            pos[...] = jnp.maximum(v1[0, 0, 0], 0.0) * lam2[0]
            lam2[Z - 1] = boundary(Z - 1, img1[Z - 2], beyond(Z + 2, v0_hi), last)
            neg[...] = jnp.minimum(v1[0, 0, Z - 1], 0.0) * lam2[Z - 1]
            for z in range(Z):
                v = [v1[0, d, z] for d in range(3)]
                above = jnp.maximum(v1[0, 0, z + 1], 0.0) * lam2[z + 1] if z < Z - 1 else None
                below = jnp.minimum(v1[0, 0, z - 1], 0.0) * lam2[z - 1] if z > 0 else None
                lam1[z] = retreat(lam2[z], v, above, below, dt)
            for i, z in enumerate(inner):
                v = [v0[0, d, z] for d in range(3)]
                diffs = upwind(tmpl[z + 1], tmpl[z + 2], tmpl[z + 3], v)
                lam = lam1[z]
                for d in range(3):
                    srcs[i][d] = (-MATCH * dt) * lam * diffs[d]

        outs = [struct(3, Y, X), struct(3, Y, X), struct(Y, X), struct(Y, X), struct(Z, Y, X)]
        outs = outs + [struct(3, Y, X)] * n_in
        operands = [tmpl, img1, lam2_in, flow0_lo, flow0_hi, flow, flow, target]
        res = call(
            middle,
            outs,
            [whole(x) for x in operands[:5]] + [flow_spec[0], flow_spec[1], whole(target)],
            [whole(x) for x in outs],
            operands,
            "middle",
            8,
        )
        src1[0], src1[Z - 1], pos1, neg1, lam1_part = res[:5]
        src0 = dict(zip(inner, res[5:]))
        pos1_hi = to_lo(pos1)
        neg1_lo = to_hi(neg1)
        src1[Z] = to_lo(src1[0])
        src1[-1] = to_hi(src1[Z - 1])

        lam1_first = lam1_part[0] - dt * neg1_lo
        lam1_last = lam1_part[Z - 1] + dt * pos1_hi
        lam1_hi = to_lo(lam1_first)
        lam1_lo = to_hi(lam1_last)
        held_1, held_2, _, _ = lax.optimization_barrier(
            (src0[1], src0[Z - 2], lam1_first, lam1_last)
        )
        src0[Z + 1] = to_lo(held_1)
        src0[-2] = to_hi(held_2)

        def sweeps(facts_ref, s, v, out, u2):
            for z in range(-1, Z + 1):
                beside = plane_sum(s[z][0])
                if z - 1 in s:
                    beside = beside + s[z - 1][0]
                if z + 1 in s:
                    beside = beside + s[z + 1][0]
                u = (s[z][0] + beside * SEVENTH) * SEVENTH
                if z == -1:
                    u = jnp.where(facts_ref[1] > 0, u, 0.0)
                if z == Z:
                    u = jnp.where(facts_ref[2] > 0, u, 0.0)
                u2[z + 1] = u
            for z in range(Z):
                u = u2[z + 1]
                beside = plane_sum(u) + u2[z] + u2[z + 2]
                out[0, 0, z] = v[0, 0, z] + (s[z][0] + beside) * SEVENTH

        part = pl.BlockSpec((1, Y, X), lambda d: (d, 0, 0))
        flow_part = [
            pl.BlockSpec((1, 1, Z, Y, X), lambda d, t=t: (t, d, 0, 0, 0)) for t in range(steps)
        ]
        scratch = [pltpu.VMEM((Z + 2, Y, X), jnp.float32)]
        order = list(range(-2, Z + 2))

        def smooth_1(facts_ref, *refs):
            s = dict(zip(order, refs[: len(order)]))
            sweeps(facts_ref, s, *refs[len(order) :])

        gradient = call(
            smooth_1,
            struct(*flow.shape),
            [SMEM] + [part] * len(order) + [flow_part[1]],
            flow_part[1],
            [facts] + [src1[z] for z in order] + [flow],
            "smooth_1",
            10,
            grid=(3,),
            scratch=scratch,
        )

        def last(facts_ref, tmpl, part1, first1, last1, lam1_lo, lam1_hi, v0_lo, v0_hi, v0, lam0, *srcs):
            lam = {z: part1[z] for z in inner}
            lam[0], lam[Z - 1] = first1[...], last1[...]
            lam[-1], lam[Z] = lam1_lo[...], lam1_hi[...]

            def flow_at(z):
                ref = v0_lo if z < 0 else v0_hi
                return [ref[d] if z in (-1, Z) else v0[0, d, z] for d in range(3)]

            for src, z in zip(srcs, (-1, 0, Z - 1, Z)):
                diffs = upwind(tmpl[z + 1], tmpl[z + 2], tmpl[z + 3], flow_at(z))
                for d in range(3):
                    src[d] = (-MATCH * dt) * lam[z] * diffs[d]
            for z in range(Z):
                above = jnp.maximum(flow_at(z + 1)[0], 0.0) * lam[z + 1]
                below = jnp.minimum(flow_at(z - 1)[0], 0.0) * lam[z - 1]
                lam0[z] = retreat(lam[z], flow_at(z), above, below, dt)

        outs = [struct(Z, Y, X)] + [struct(3, Y, X)] * 4
        operands = [facts, tmpl, lam1_part, lam1_first, lam1_last, lam1_lo, lam1_hi, flow0_lo, flow0_hi, flow]
        res = call(
            last,
            outs,
            [SMEM] + [whole(x) for x in operands[1:9]] + [flow_spec[0]],
            [whole(x) for x in outs],
            operands,
            "last",
            8,
        )
        lam0 = res[0]
        src0[-1], src0[0], src0[Z - 1], src0[Z] = res[1:]

        def share(k):
            start = lax.rem(group + k, subj) * rows
            return lax.dynamic_slice_in_dim(lam0, start, rows, axis=1)

        template_grad = share(0)
        for k in range(1, subj):
            template_grad = template_grad + turn(share(k), k)

        near = list(range(-1, Z + 1))

        def smooth_0(facts_ref, *refs):
            s = dict(zip(near, refs[: len(near)]))
            _, v, out, u2 = refs[len(near) :]
            sweeps(facts_ref, s, v, out, u2)

        gradient = call(
            smooth_0,
            struct(*flow.shape),
            [SMEM] + [part] * len(near) + [pl.BlockSpec(memory_space=pl.ANY), flow_part[0]],
            flow_part[0],
            [facts] + [src0[z] for z in near] + [gradient, flow],
            "smooth_0",
            10,
            grid=(3,),
            aliases={len(near) + 1: 0},
            scratch=scratch,
        )

        def add_far(src, grad, out):
            out[0, 0, 0] = grad[0, 0, 0] + src[0] * SEVENTH**3

        for src, z in ((src0[Z + 1], Z - 1), (src0[-2], 0)):
            block = pl.BlockSpec((1, 1, 1, Y, X), lambda d, z=z: (0, d, z, 0, 0))
            gradient = call(
                add_far,
                struct(*flow.shape),
                [part, block],
                block,
                [src, gradient],
                "add_far",
                1,
                grid=(3,),
                aliases={1: 0},
            )
        return gradient[None], template_grad

    return body


def solution(mesh):
    sizes = dict(mesh.shape)
    return jax.shard_map(
        make_body(sizes["subj"], sizes["slab"]),
        mesh=mesh,
        in_specs=(
            P("slab", "subj", None),
            P("subj", "slab", None, None),
            P("subj", None, None, "slab", None, None),
        ),
        out_specs=(P("subj", None, None, "slab", None, None), P("slab", "subj", None)),
        check_vma=False,
    )
```

time: 302 us -> 203 us (0.67)
  waiting for transfers between devices: 178 us -> 98.8 us
  other arithmetic: 57.5 us -> 2.08 us
  Pallas kernels: 0 us -> 44 us
  between operations: 14.4 us -> 0.9 us
  starting transfers between devices: 40.3 us -> 43.6 us
    ppermute x12 -> x17, waiting for transfers between devices: 144 us -> 98.8 us  [the longest x7 97 us: to_hi(): return lax.ppermute(x, 'slab', up)]
    pallas_call x0 -> x7, Pallas kernels: none -> 44 us  [call(): pl.pallas_call(kernel, out_shape=out_shape, grid=grid, in_specs=in_specs,...]
    psum x1 -> x0, waiting for transfers between devices: 21.8 us -> none  [body(): summed = lax.psum(adjoint, 'subj')]
    broadcast_in_dim x1 -> x0, other arithmetic: 19.3 us -> none  [body(): return (gradient[None], template_part)]
    div x2 -> x0, other arithmetic: 15.6 us -> none  [the longest x1 14.6 us: body(): smoothed = (source + smooth_weight * beside_all) / scale]
    all_gather x1 -> x0, waiting for transfers between devices: 12.2 us -> none  [body(): whole = lax.all_gather(template, 'subj', axis=1, tiled=True)]
    another operation x6 -> x1, other arithmetic: 11.4 us -> 0.08 us  [body(): facts = jnp.stack([group, place > 0, place < slabs - 1]).astype(jnp.int32)]
    sub x2 -> x0, other arithmetic: 10 us -> none  [the longest x1 5.83 us: body(): image = image - step_size * flux]
  transfers between devices with their start and end apart: 14 -> 17, of which waited for: 11 -> 5; matrix products, arithmetic and copies ran while one was open for 8% -> 3% of each run, Pallas kernels for 0% -> 17%
where the time goes in v1:
time: 203 us; the launch traced here: 201 us
  waiting for transfers between devices  98.8 us (49%)
  Pallas kernels  44 us (22%)
  starting transfers between devices  43.6 us (21%)
  local copies, waits for them, and re-layouts  11.3 us (6%)
  other arithmetic  2.08 us (1%)
    ppermute x7, waiting for transfers between devices, to_hi(): return lax.ppermute(x, 'slab', up)  97 us
    pallas_call x7, Pallas kernels, call(): pl.pallas_call(kernel, out_shape=out_shape, grid=grid, in_specs=in_specs,...  44 us
    ppermute x7, starting transfers between devices, to_hi(): return lax.ppermute(x, 'slab', up)  24.1 us
    ppermute x7, starting transfers between devices, to_lo(): return lax.ppermute(x, 'slab', down)  19.4 us
    unnamed x23, local copies, waits for them, and re-layouts  5.61 us
  transfers between devices with their start and end apart: 17, of which 5 were waited for; matrix products, arithmetic and copies ran while one was open for 3% of the time, Pallas kernels for 17%

profile of v1, /device:TPU:2, one launch (start us, length us, event | category | flops | bytes accessed | tf_op | source)
XLA Modules:
  0.0 200.8 jit_solution(3936221154088930854)
XLA Ops:
  1.7 1.9 collective-permute-start.2
  3.6 4.8 %collective-permute-start.1 = (f32[2,64,512]{2,1,0:T(8,128)S(1)}, f32[2,64,512]{2,1,0:T(8,128)S(1)}, u32[]{:S(2)}, u32[]{:S(2)}) collective-permute-start(f32[2,64,512]{2,1,0:T(8,128)S(1)} %get-tuple-element.45), channel_id=1, source_target_pairs={{0,1},{1,2},{2,3},{3,4},{4,5},{5,6},{6,7},{7,8},{8,9},{9,10},{10,1... | collective-permute-start | bytes 786440 | tf_op jit(solution)/shard_map/ppermute | solution.py:102
  8.5 2.7 %slice_bitcast_fusion = (f32[3,128,512]{2,1,0:T(8,128)}, f32[3,128,512]{2,1,0:T(8,128)}) fusion(f32[2,3,4,128,512]{4,3,2,1,0:T(8,128)} %bitcast.14), kind=kLoop, calls=%fused_computation | loop fusion | bytes 3145728 | tf_op jit(solution)/shard_map/squeeze | solution.py:125
  13.1 4.8 %collective-permute-start.4 = (f32[3,128,512]{2,1,0:T(8,128)}, f32[3,128,512]{2,1,0:T(8,128)S(1)}, u32[]{:S(2)}, u32[]{:S(2)}) collective-permute-start(f32[3,128,512]{2,1,0:T(8,128)} %get-tuple-element.41), channel_id=1, source_target_pairs={{0,1},{1,2},{2,3},{3,4},{4,5},{5,6},{6,7},{7,8},{8,9},{9,10},{10,1... | collective-permute-start | bytes 2359304 | tf_op jit(solution)/shard_map/ppermute | solution.py:102
  18.0 18.0 %collective-permute-done.1 = f32[2,64,512]{2,1,0:T(8,128)S(1)} collective-permute-done((f32[2,64,512]{2,1,0:T(8,128)S(1)}, f32[2,64,512]{2,1,0:T(8,128)S(1)}, u32[]{:S(2)}, u32[]{:S(2)}) %collective-permute-start.1) | collective-permute-done | bytes 262176 | tf_op jit(solution)/shard_map/ppermute | solution.py:102
  39.1 6.7 %forward.1 = (f32[8,128,512]{2,1,0:T(8,128)}, f32[4,128,512]{2,1,0:T(8,128)S(1)}, f32[2,128,512]{2,1,0:T(8,128)S(1)}, f32[3,128,512]{2,1,0:T(8,128)}, f32[3,128,512]{2,1,0:T(8,128)}) custom-call(s32[3]{0:T(128)S(1)} %pad_add_fusion.refs_0_.facts_ref, f32[4,64,512]{2,1,0:T(8,128)S(1)} %copy-done, f32[4,64,512]{2,1,0:T(8,128)S(1)} %collective-permute-done.refs_2_, ...), custom_call_target="tpu_custom_call" | custom-call | flops 8000000 | bytes 24000000 | tf_op jit(solution)/shard_map/forward/pallas_call | solution.py:66
  46.8 6.1 %collective-permute-done.4.v0_lo = f32[3,128,512]{2,1,0:T(8,128)S(1)} collective-permute-done((f32[3,128,512]{2,1,0:T(8,128)}, f32[3,128,512]{2,1,0:T(8,128)S(1)}, u32[]{:S(2)}, u32[]{:S(2)}) %collective-permute-start.4) | collective-permute-done | bytes 786464 | tf_op jit(solution)/shard_map/ppermute | solution.py:102
  52.8 7.8 %middle.1 = (f32[3,128,512]{2,1,0:T(8,128)}, f32[3,128,512]{2,1,0:T(8,128)}, f32[128,512]{1,0:T(8,128)S(1)}, f32[128,512]{1,0:T(8,128)S(1)}, f32[4,128,512]{2,1,...) custom-call(f32[8,128,512]{2,1,0:T(8,128)} %get-tuple-element.21.tmpl, f32[4,128,512]{2,1,0:T(8,128)} %copy-done.1, ...), custom_call_target="tpu_custom_call" | custom-call | flops 8000000 | bytes 24000000 | tf_op jit(solution)/shard_map/middle/pallas_call | solution.py:66
  62.6 3.9 %collective-permute-start.7 = (f32[128,512]{1,0:T(8,128)S(1)}, f32[128,512]{1,0:T(8,128)S(1)}, u32[]{:S(2)}, u32[]{:S(2)}) collective-permute-start(f32[128,512]{1,0:T(8,128)S(1)} %get-tuple-element.28), channel_id=1, source_target_pairs={{1,0},{2,1},{3,2},{4,3},{5,4},{6,5},{7,6},{8,7},{9,8},{10,9},{11,1... | collective-permute-start | bytes 786440 | tf_op jit(solution)/shard_map/ppermute | solution.py:99
  66.5 2.8 %collective-permute-start.12 = (f32[3,128,512]{2,1,0:T(8,128)}, f32[3,128,512]{2,1,0:T(8,128)}, u32[]{:S(2)}, u32[]{:S(2)}) collective-permute-start(f32[3,128,512]{2,1,0:T(8,128)} %get-tuple-element.35.refs_4_), channel_id=1, source_target_pairs={{0,1},{1,2},{2,3},{3,4},{4,5},{5,6},{6,7},{7,8},{8,9},{9,10},{10,1... | collective-permute-start | bytes 2359304 | tf_op jit(solution)/shard_map/ppermute | solution.py:102
  69.3 3.9 %collective-permute-start.15 = (f32[3,128,512]{2,1,0:T(8,128)}, f32[3,128,512]{2,1,0:T(8,128)}, u32[]{:S(2)}, u32[]{:S(2)}) collective-permute-start(f32[3,128,512]{2,1,0:T(8,128)} %get-tuple-element.38.refs_3_), channel_id=1, source_target_pairs={{1,0},{2,1},{3,2},{4,3},{5,4},{6,5},{7,6},{8,7},{9,8},{10,9},{11,1... | collective-permute-start | bytes 2359304 | tf_op jit(solution)/shard_map/ppermute | solution.py:99
  73.2 23.7 %collective-permute-done.6 = f32[128,512]{1,0:T(8,128)S(1)} collective-permute-done((f32[128,512]{1,0:T(8,128)S(1)}, f32[128,512]{1,0:T(8,128)S(1)}, u32[]{:S(2)}, u32[]{:S(2)}) %collective-permute-start.6) | collective-permute-done | bytes 262176 | tf_op jit(solution)/shard_map/ppermute | solution.py:102
  98.1 1.9 collective-permute-start.10
  100.0 3.9 %collective-permute-start.11 = (f32[128,512]{1,0:T(8,128)S(1)}, f32[128,512]{1,0:T(8,128)S(1)}, u32[]{:S(2)}, u32[]{:S(2)}) collective-permute-start(f32[128,512]{1,0:T(8,128)S(1)} %get-tuple-element.43.first1), channel_id=1, source_target_pairs={{1,0},{2,1},{3,2},{4,3},{5,4},{6,5},{7,6},{8,7},{9,8},{10,9},{11,1... | collective-permute-start | bytes 786440 | tf_op jit(solution)/shard_map/ppermute | solution.py:99
  104.0 2.8 %collective-permute-start.13 = (f32[3,128,512]{2,1,0:T(8,128)}, f32[3,128,512]{2,1,0:T(8,128)}, u32[]{:S(2)}, u32[]{:S(2)}) collective-permute-start(f32[3,128,512]{2,1,0:T(8,128)} %get-tuple-element.36.refs_5_), channel_id=1, source_target_pairs={{0,1},{1,2},{2,3},{3,4},{4,5},{5,6},{6,7},{7,8},{8,9},{9,10},{10,1... | collective-permute-start | bytes 2359304 | tf_op jit(solution)/shard_map/ppermute | solution.py:102
  106.8 49.2 %collective-permute-done.10.lam1_lo = f32[128,512]{1,0:T(8,128)S(1)} collective-permute-done((f32[128,512]{1,0:T(8,128)S(1)}, f32[128,512]{1,0:T(8,128)S(1)}, u32[]{:S(2)}, u32[]{:S(2)}) %collective-permute-start.10) | collective-permute-done | bytes 262176 | tf_op jit(solution)/shard_map/ppermute | solution.py:102
  156.0 1.9 collective-permute-start.14
  157.9 1.9 collective-permute-start.9
  159.8 6.2 %last.1 = (f32[4,128,512]{2,1,0:T(8,128)}, f32[3,128,512]{2,1,0:T(8,128)S(1)}, f32[3,128,512]{2,1,0:T(8,128)S(1)}, f32[3,128,512]{2,1,0:T(8,128)S(1)}, f32[3,128,512]{2,1,0:T(8,128)S(1)}) custom-call(s32[3]{0:T(128)S(1)} %pad_add_fusion.refs_0_.facts_ref, f32[8,128,512]{2,1,0:T(8,128)} %get-tuple-element.21.tmpl, f32[4,128,512]{2,1,0:T(8,128)} %get-tuple-element.26.part1, ...), custom_call_target="tpu_custom_call" | custom-call | flops 8000000 | bytes 24000000 | tf_op jit(solution)/shard_map/last/pallas_call | solution.py:66
  169.6 5.0 %collective-permute-start.8 = (f32[3,128,512]{2,1,0:T(8,128)S(1)}, f32[3,128,512]{2,1,0:T(8,128)S(1)}, u32[]{:S(2)}, u32[]{:S(2)}) collective-permute-start(f32[3,128,512]{2,1,0:T(8,128)S(1)} %get-tuple-element.29.refs_3_), channel_id=1, source_target_pairs={{0,1},{1,2},{2,3},{3,4},{4,5},{5,6},{6,7},{7,8},{8,9},{9,10},{10,1... | collective-permute-start | bytes 2359304 | tf_op jit(solution)/shard_map/ppermute | solution.py:102
  176.6 8.9 %smooth_1.1.refs_6_ = f32[2,3,4,128,512]{4,3,2,1,0:T(8,128)} custom-call(s32[3]{0:T(128)S(1)} %pad_add_fusion.refs_0_.facts_ref, f32[3,128,512]{2,1,0:T(8,128)} %collective-permute-done.12.refs_0_, f32[3,128,512]{2,1,0:T(8,128)} %collective-permute-done.13.refs_1_, f32[3,128,512]{2,1,0:T(8,128)} %get-tuple-element.37.refs_2_, ...), custom_call_target="tpu_custom_call" | custom-call | flops 10000000 | bytes 30000000 | tf_op jit(solution)/shard_map/smooth_1/pallas_call | solution.py:66
  185.5 8.4 %smooth_0.1.grad = f32[2,3,4,128,512]{4,3,2,1,0:T(8,128)} custom-call(s32[3]{0:T(128)S(1)} %pad_add_fusion.refs_0_.facts_ref, f32[3,128,512]{2,1,0:T(8,128)S(1)} %copy-done.3, f32[3,128,512]{2,1,0:T(8,128)S(1)} %copy-done.5, f32[3,128,512]{2,1,0:T(8,128)} %get-tuple-element.30.refs_2_, ...), custom_call_target="tpu_custom_call", output_to_operand_aliasing={{}: (7, {})} | custom-call | flops 10000000 | bytes 30000000 | tf_op jit(solution)/shard_map/smooth_0/pallas_call | solution.py:66
  193.9 3.1 %add_far.2.grad = f32[2,3,4,128,512]{4,3,2,1,0:T(8,128)} custom-call(f32[3,128,512]{2,1,0:T(8,128)} %collective-permute-done.9.src, f32[2,3,4,128,512]{4,3,2,1,0:T(8,128)} %smooth_0.1.grad), custom_call_target="tpu_custom_call", output_to_operand_aliasing={{}: (1, {})} | custom-call | flops 1000000 | bytes 3000000 | tf_op jit(solution)/shard_map/add_far/pallas_call | solution.py:66
  198.0 2.9 %add_far.3 = f32[2,3,4,128,512]{4,3,2,1,0:T(8,128)} custom-call(f32[3,128,512]{2,1,0:T(8,128)S(1)} %collective-permute-done.8.src, f32[2,3,4,128,512]{4,3,2,1,0:T(8,128)} %add_far.2.grad), custom_call_target="tpu_custom_call", output_to_operand_aliasing={{}: (1, {})} | custom-call | flops 1000000 | bytes 3000000 | tf_op jit(solution)/shard_map/add_far/pallas_call | solution.py:66
  (47 shorter events, 16.5 us)
Async XLA Ops:
  1.7 34.4 %collective-permute-start.2 = (f32[2,64,512]{2,1,0:T(8,128)S(1)}, f32[2,64,512]{2,1,0:T(8,128)S(1)}, u32[]{:S(2)}, u32[]{:S(2)}) collective-permute-start(f32[2,64,512]{2,1,0:T(8,128)S(1)} %get-tuple-element.44), channel_id=1, source_target_pairs={{1,0},{2,1},{3,2},{4,3},{5,4},{6,5},{7,6},{8,7},{9,8},{10,9},{11,1... | collective-permute-start | bytes 786440 | tf_op jit(solution)/shard_map/ppermute | solution.py:99
  3.6 32.4 %collective-permute-start.1 = (f32[2,64,512]{2,1,0:T(8,128)S(1)}, f32[2,64,512]{2,1,0:T(8,128)S(1)}, u32[]{:S(2)}, u32[]{:S(2)}) collective-permute-start(f32[2,64,512]{2,1,0:T(8,128)S(1)} %get-tuple-element.45), channel_id=1, source_target_pairs={{0,1},{1,2},{2,3},{3,4},{4,5},{5,6},{6,7},{7,8},{8,9},{9,10},{10,1... | collective-permute-start | bytes 786440 | tf_op jit(solution)/shard_map/ppermute | solution.py:102
  11.2 35.6 %collective-permute-start.5 = (f32[3,128,512]{2,1,0:T(8,128)}, f32[3,128,512]{2,1,0:T(8,128)S(1)}, u32[]{:S(2)}, u32[]{:S(2)}) collective-permute-start(f32[3,128,512]{2,1,0:T(8,128)} %get-tuple-element.40), channel_id=1, source_target_pairs={{1,0},{2,1},{3,2},{4,3},{5,4},{6,5},{7,6},{8,7},{9,8},{10,9},{11,1... | collective-permute-start | bytes 2359304 | tf_op jit(solution)/shard_map/ppermute | solution.py:99
  13.1 39.7 %collective-permute-start.4 = (f32[3,128,512]{2,1,0:T(8,128)}, f32[3,128,512]{2,1,0:T(8,128)S(1)}, u32[]{:S(2)}, u32[]{:S(2)}) collective-permute-start(f32[3,128,512]{2,1,0:T(8,128)} %get-tuple-element.41), channel_id=1, source_target_pairs={{0,1},{1,2},{2,3},{3,4},{4,5},{5,6},{6,7},{7,8},{8,9},{9,10},{10,1... | collective-permute-start | bytes 2359304 | tf_op jit(solution)/shard_map/ppermute | solution.py:102
  17.9 18.3 %collective-permute-start = (f32[4,64,512]{2,1,0:T(8,128)}, f32[4,64,512]{2,1,0:T(8,128)S(1)}, u32[]{:S(2)}, u32[]{:S(2)}) collective-permute-start(f32[4,64,512]{2,1,0:T(8,128)} %refs_1_.1), channel_id=1, source_target_pairs={{0,16},{16,0},{1,17},{17,1},{2,18},{18,2},{3,19},{19,3},{4,20},{20... | collective-permute-start | bytes 1572872 | tf_op jit(solution)/shard_map/ppermute | solution.py:105
  36.1 2.0 collective-permute-start.3
  38.1 1.0 copy-start
  45.8 1.0 copy-start.1
  60.6 36.3 %collective-permute-start.6 = (f32[128,512]{1,0:T(8,128)S(1)}, f32[128,512]{1,0:T(8,128)S(1)}, u32[]{:S(2)}, u32[]{:S(2)}) collective-permute-start(f32[128,512]{1,0:T(8,128)S(1)} %get-tuple-element.27), channel_id=1, source_target_pairs={{0,1},{1,2},{2,3},{3,4},{4,5},{5,6},{6,7},{7,8},{8,9},{9,10},{10,1... | collective-permute-start | bytes 786440 | tf_op jit(solution)/shard_map/ppermute | solution.py:102
  62.6 34.4 %collective-permute-start.7 = (f32[128,512]{1,0:T(8,128)S(1)}, f32[128,512]{1,0:T(8,128)S(1)}, u32[]{:S(2)}, u32[]{:S(2)}) collective-permute-start(f32[128,512]{1,0:T(8,128)S(1)} %get-tuple-element.28), channel_id=1, source_target_pairs={{1,0},{2,1},{3,2},{4,3},{5,4},{6,5},{7,6},{8,7},{9,8},{10,9},{11,1... | collective-permute-start | bytes 786440 | tf_op jit(solution)/shard_map/ppermute | solution.py:99
  66.5 103.1 %collective-permute-start.12 = (f32[3,128,512]{2,1,0:T(8,128)}, f32[3,128,512]{2,1,0:T(8,128)}, u32[]{:S(2)}, u32[]{:S(2)}) collective-permute-start(f32[3,128,512]{2,1,0:T(8,128)} %get-tuple-element.35.refs_4_), channel_id=1, source_target_pairs={{0,1},{1,2},{2,3},{3,4},{4,5},{5,6},{6,7},{7,8},{8,9},{9,10},{10,1... | collective-permute-start | bytes 2359304 | tf_op jit(solution)/shard_map/ppermute | solution.py:102
  69.3 107.2 %collective-permute-start.15 = (f32[3,128,512]{2,1,0:T(8,128)}, f32[3,128,512]{2,1,0:T(8,128)}, u32[]{:S(2)}, u32[]{:S(2)}) collective-permute-start(f32[3,128,512]{2,1,0:T(8,128)} %get-tuple-element.38.refs_3_), channel_id=1, source_target_pairs={{1,0},{2,1},{3,2},{4,3},{5,4},{6,5},{7,6},{8,7},{9,8},{10,9},{11,1... | collective-permute-start | bytes 2359304 | tf_op jit(solution)/shard_map/ppermute | solution.py:99
  98.1 57.9 %collective-permute-start.10 = (f32[128,512]{1,0:T(8,128)S(1)}, f32[128,512]{1,0:T(8,128)S(1)}, u32[]{:S(2)}, u32[]{:S(2)}) collective-permute-start(f32[128,512]{1,0:T(8,128)S(1)} %get-tuple-element.42.last1), channel_id=1, source_target_pairs={{0,1},{1,2},{2,3},{3,4},{4,5},{5,6},{6,7},{7,8},{8,9},{9,10},{10,1... | collective-permute-start | bytes 786440 | tf_op jit(solution)/shard_map/ppermute | solution.py:102
  100.0 57.9 %collective-permute-start.11 = (f32[128,512]{1,0:T(8,128)S(1)}, f32[128,512]{1,0:T(8,128)S(1)}, u32[]{:S(2)}, u32[]{:S(2)}) collective-permute-start(f32[128,512]{1,0:T(8,128)S(1)} %get-tuple-element.43.first1), channel_id=1, source_target_pairs={{1,0},{2,1},{3,2},{4,3},{5,4},{6,5},{7,6},{8,7},{9,8},{10,9},{11,1... | collective-permute-start | bytes 786440 | tf_op jit(solution)/shard_map/ppermute | solution.py:99
  104.0 72.6 %collective-permute-start.13 = (f32[3,128,512]{2,1,0:T(8,128)}, f32[3,128,512]{2,1,0:T(8,128)}, u32[]{:S(2)}, u32[]{:S(2)}) collective-permute-start(f32[3,128,512]{2,1,0:T(8,128)} %get-tuple-element.36.refs_5_), channel_id=1, source_target_pairs={{0,1},{1,2},{2,3},{3,4},{4,5},{5,6},{6,7},{7,8},{8,9},{9,10},{10,1... | collective-permute-start | bytes 2359304 | tf_op jit(solution)/shard_map/ppermute | solution.py:102
  156.0 20.6 %collective-permute-start.14 = (f32[3,128,512]{2,1,0:T(8,128)}, f32[3,128,512]{2,1,0:T(8,128)}, u32[]{:S(2)}, u32[]{:S(2)}) collective-permute-start(f32[3,128,512]{2,1,0:T(8,128)} %get-tuple-element.37.refs_2_), channel_id=1, source_target_pairs={{1,0},{2,1},{3,2},{4,3},{5,4},{6,5},{7,6},{8,7},{9,8},{10,9},{11,1... | collective-permute-start | bytes 2359304 | tf_op jit(solution)/shard_map/ppermute | solution.py:99
  157.9 36.0 %collective-permute-start.9 = (f32[3,128,512]{2,1,0:T(8,128)}, f32[3,128,512]{2,1,0:T(8,128)}, u32[]{:S(2)}, u32[]{:S(2)}) collective-permute-start(f32[3,128,512]{2,1,0:T(8,128)} %get-tuple-element.30.refs_2_), channel_id=1, source_target_pairs={{1,0},{2,1},{3,2},{4,3},{5,4},{6,5},{7,6},{8,7},{9,8},{10,9},{11,1... | collective-permute-start | bytes 2359304 | tf_op jit(solution)/shard_map/ppermute | solution.py:99
  169.6 28.3 %collective-permute-start.8 = (f32[3,128,512]{2,1,0:T(8,128)S(1)}, f32[3,128,512]{2,1,0:T(8,128)S(1)}, u32[]{:S(2)}, u32[]{:S(2)}) collective-permute-start(f32[3,128,512]{2,1,0:T(8,128)S(1)} %get-tuple-element.29.refs_3_), channel_id=1, source_target_pairs={{0,1},{1,2},{2,3},{3,4},{4,5},{5,6},{6,7},{7,8},{8,9},{9,10},{10,1... | collective-permute-start | bytes 2359304 | tf_op jit(solution)/shard_map/ppermute | solution.py:102
  176.5 20.6 %collective-permute-start.16 = (f32[4,64,512]{2,1,0:T(8,128)}, f32[4,64,512]{2,1,0:T(8,128)S(1)}, u32[]{:S(2)}, u32[]{:S(2)}) collective-permute-start(f32[4,64,512]{2,1,0:T(8,128)} %constant_dynamic-slice_fusion), channel_id=1, source_target_pairs={{0,16},{16,0},{1,17},{17,1},{2,18},{18,2},{3,19},{19,3},{4,20},{20... | collective-permute-start | bytes 1572872 | tf_op jit(solution)/shard_map/ppermute | solution.py:105
  176.5 9.0 %copy-start.3 = (f32[3,128,512]{2,1,0:T(8,128)S(1)}, f32[3,128,512]{2,1,0:T(8,128)}, u32[]{:S(2)}) copy-start(f32[3,128,512]{2,1,0:T(8,128)} %copy-done.2) | copy-start | bytes 2359300
  176.5 9.0 %copy-start.5 = (f32[3,128,512]{2,1,0:T(8,128)S(1)}, f32[3,128,512]{2,1,0:T(8,128)}, u32[]{:S(2)}) copy-start(f32[3,128,512]{2,1,0:T(8,128)} %copy-done.4) | copy-start | bytes 2359300
  176.5 9.0 %copy-start.7 = (f32[3,128,512]{2,1,0:T(8,128)S(1)}, f32[3,128,512]{2,1,0:T(8,128)}, u32[]{:S(2)}) copy-start(f32[3,128,512]{2,1,0:T(8,128)} %copy-done.6) | copy-start | bytes 2359300
  176.5 9.0 %copy-start.9 = (f32[3,128,512]{2,1,0:T(8,128)S(1)}, f32[3,128,512]{2,1,0:T(8,128)}, u32[]{:S(2)}) copy-start(f32[3,128,512]{2,1,0:T(8,128)} %copy-done.8) | copy-start | bytes 2359300
  193.9 3.2 %copy-start.10 = (f32[4,128,512]{2,1,0:T(8,128)S(1)}, f32[4,128,512]{2,1,0:T(8,128)}, u32[]{:S(2)}) copy-start(f32[4,128,512]{2,1,0:T(8,128)} %get-tuple-element.39) | copy-start | bytes 3145732
  (4 other events, 3.6 us)

commit v2 on v1

--- a/solution.py
+++ b/solution.py
@@ -61,8 +61,7 @@
     return row_prev(f) + row_next(f) + col_prev(f) + col_next(f)
 
 
-def call(kernel, out_shape, in_specs, out_specs, operands, name, us, grid=(1,), aliases=None, scratch=()):
-    flops = int(us * 1e6)
+def call(kernel, out_shape, in_specs, out_specs, operands, name, weight=0, grid=(1,), aliases=None, scratch=()):
     return pl.pallas_call(
         kernel,
         out_shape=out_shape,
@@ -73,7 +72,7 @@
         input_output_aliases=aliases or {},
         compiler_params=pltpu.CompilerParams(vmem_limit_bytes=48 * MIB),
         cost_estimate=pl.CostEstimate(
-            flops=flops, bytes_accessed=int(us * 3.0e6), transcendentals=0
+            flops=1024, bytes_accessed=1024 + weight * 3000000, transcendentals=0
         ),
         name=name,
     )(*operands)
@@ -119,11 +118,15 @@
             pl.BlockSpec((1, 3, Z, Y, X), lambda *_, t=t: (t, 0, 0, 0, 0)) for t in range(steps)
         ]
 
+        tmpl_lo = to_hi(template[Z - 2 :])
         tmpl_hi = to_lo(template[:2])
-        tmpl_lo = to_hi(template[Z - 2 :])
+        flow0_first, flow0_last = flow[0, :, 0], flow[0, :, Z - 1]
+        flow0_hi = to_lo(flow0_first)
+        flow0_lo = to_hi(flow0_last)
         own_parts = [template] + [turn(template, k) for k in range(1, subj)]
-        flow0_hi = to_lo(flow[0, :, 0])
-        flow0_lo = to_hi(flow[0, :, Z - 1])
+        tmpl_lo, tmpl_hi, _, _ = lax.optimization_barrier(
+            (tmpl_lo, tmpl_hi, flow0_first, flow0_last)
+        )
         edge = jnp.concatenate([tmpl_lo, tmpl_hi], axis=0)
         edge_parts = [edge] + [turn(edge, k) for k in range(1, subj)]
 
@@ -162,16 +165,13 @@
             [whole(x) for x in outs],
             operands,
             "forward",
-            8,
         )
         tmpl, img1, lam2_in = res[:3]
         src1 = dict(zip(inner, res[3:]))
         src1[Z + 1] = to_lo(src1[1])
         src1[-2] = to_hi(src1[Z - 2])
 
-        def middle(tmpl, img1, lam2_in, v0_lo, v0_hi, v0, v1, aim, first, last, pos, neg, lam1, *srcs):
-            lam2 = {z: lam2_in[i] for i, z in enumerate(inner)}
-
+        def middle(tmpl, img1, v0_lo, v0_hi, v1, aim, first, last, pos, neg, lam2):
             def beyond(at, halo):
                 v = [halo[d] for d in range(3)]
                 f = tmpl[at]
@@ -186,10 +186,27 @@
                     src[d] = (-MATCH * dt) * lam * diffs[d]
                 return lam
 
-            lam2[0] = boundary(0, beyond(1, v0_lo), img1[1], first)
-            pos[...] = jnp.maximum(v1[0, 0, 0], 0.0) * lam2[0]
-            lam2[Z - 1] = boundary(Z - 1, img1[Z - 2], beyond(Z + 2, v0_hi), last)
-            neg[...] = jnp.minimum(v1[0, 0, Z - 1], 0.0) * lam2[Z - 1]
+            lam = boundary(0, beyond(1, v0_lo), img1[1], first)
+            lam2[0] = lam
+            pos[...] = jnp.maximum(v1[0, 0, 0], 0.0) * lam
+            lam = boundary(Z - 1, img1[Z - 2], beyond(Z + 2, v0_hi), last)
+            lam2[1] = lam
+            neg[...] = jnp.minimum(v1[0, 0, Z - 1], 0.0) * lam
+
+        outs = [struct(3, Y, X), struct(3, Y, X), struct(Y, X), struct(Y, X), struct(2, Y, X)]
+        operands = [tmpl, img1, flow0_lo, flow0_hi, flow, target]
+        src1[0], src1[Z - 1], pos1, neg1, lam2_out = call(
+            middle,
+            outs,
+            [whole(x) for x in operands[:4]] + [flow_spec[1], whole(target)],
+            [whole(x) for x in outs],
+            operands,
+            "middle",
+        )
+
+        def back(tmpl, lam2_in, lam2_out, v0, v1, lam1, *srcs):
+            lam2 = {z: lam2_in[i] for i, z in enumerate(inner)}
+            lam2[0], lam2[Z - 1] = lam2_out[0], lam2_out[1]
             for z in range(Z):
                 v = [v1[0, d, z] for d in range(3)]
                 above = jnp.maximum(v1[0, 0, z + 1], 0.0) * lam2[z + 1] if z < Z - 1 else None
@@ -202,34 +219,35 @@
                 for d in range(3):
                     srcs[i][d] = (-MATCH * dt) * lam * diffs[d]
 
-        outs = [struct(3, Y, X), struct(3, Y, X), struct(Y, X), struct(Y, X), struct(Z, Y, X)]
-        outs = outs + [struct(3, Y, X)] * n_in
-        operands = [tmpl, img1, lam2_in, flow0_lo, flow0_hi, flow, flow, target]
+        outs = [struct(Z, Y, X)] + [struct(3, Y, X)] * n_in
+        operands = [tmpl, lam2_in, lam2_out, flow, flow]
         res = call(
-            middle,
+            back,
             outs,
-            [whole(x) for x in operands[:5]] + [flow_spec[0], flow_spec[1], whole(target)],
+            [whole(x) for x in operands[:3]] + [flow_spec[0], flow_spec[1]],
             [whole(x) for x in outs],
             operands,
-            "middle",
-            8,
-        )
-        src1[0], src1[Z - 1], pos1, neg1, lam1_part = res[:5]
-        src0 = dict(zip(inner, res[5:]))
+            "back",
+        )
+        lam1_part = res[0]
+        src0 = dict(zip(inner, res[1:]))
+        neg1_lo = to_hi(neg1)
         pos1_hi = to_lo(pos1)
-        neg1_lo = to_hi(neg1)
-        src1[Z] = to_lo(src1[0])
-        src1[-1] = to_hi(src1[Z - 1])
-
+        first, last, src1[Z + 1], lam1_part = lax.optimization_barrier(
+            (src1[0], src1[Z - 1], src1[Z + 1], lam1_part)
+        )
+        src1[Z] = to_lo(first)
+        src1[-1] = to_hi(last)
+
+        neg1_lo, pos1_hi, src1[-2] = lax.optimization_barrier((neg1_lo, pos1_hi, src1[-2]))
         lam1_first = lam1_part[0] - dt * neg1_lo
         lam1_last = lam1_part[Z - 1] + dt * pos1_hi
+        lam1_lo = to_hi(lam1_last)
         lam1_hi = to_lo(lam1_first)
-        lam1_lo = to_hi(lam1_last)
-        held_1, held_2, _, _ = lax.optimization_barrier(
-            (src0[1], src0[Z - 2], lam1_first, lam1_last)
-        )
-        src0[Z + 1] = to_lo(held_1)
-        src0[-2] = to_hi(held_2)
+        held, _, _ = lax.optimization_barrier((src0[1], lam1_first, lam1_last))
+        src0[Z + 1] = to_lo(held)
+        held, src1[Z] = lax.optimization_barrier((src0[Z - 2], src1[Z]))
+        src0[-2] = to_hi(held)
 
         def sweeps(facts_ref, s, v, out, u2):
             for z in range(-1, Z + 1):
@@ -267,7 +285,7 @@
             flow_part[1],
             [facts] + [src1[z] for z in order] + [flow],
             "smooth_1",
-            10,
+            weight=30,
             grid=(3,),
             scratch=scratch,
         )
@@ -299,7 +317,7 @@
             [whole(x) for x in outs],
             operands,
             "last",
-            8,
+            weight=20,
         )
         lam0 = res[0]
         src0[-1], src0[0], src0[Z - 1], src0[Z] = res[1:]
@@ -326,7 +344,7 @@
             flow_part[0],
             [facts] + [src0[z] for z in near] + [gradient, flow],
             "smooth_0",
-            10,
+            weight=30,
             grid=(3,),
             aliases={len(near) + 1: 0},
             scratch=scratch,
@@ -344,7 +362,6 @@
                 block,
                 [src, gradient],
                 "add_far",
-                1,
                 grid=(3,),
                 aliases={1: 0},
             )

time: 203 us -> 202 us (level)
  the two profiles are of different devices: /device:TPU:2 before, /device:TPU:18 now
where the time goes in v2:
time: 202 us; the launch traced here: 201 us
  waiting for transfers between devices  94.8 us (47%)
  starting transfers between devices  47.3 us (23%)
  Pallas kernels  46 us (23%)
  local copies, waits for them, and re-layouts  10.8 us (5%)
    ppermute x7, waiting for transfers between devices, to_hi(): return lax.ppermute(x, 'slab', up)  73.5 us
    pallas_call x8, Pallas kernels, call(): pl.pallas_call(kernel, out_shape=out_shape, grid=grid, in_specs=in_specs,...  46 us
    ppermute x7, starting transfers between devices, to_lo(): return lax.ppermute(x, 'slab', down)  24.9 us
    ppermute x7, starting transfers between devices, to_hi(): return lax.ppermute(x, 'slab', up)  22.2 us
    ppermute x7, waiting for transfers between devices, to_lo(): return lax.ppermute(x, 'slab', down)  21.3 us
    unnamed x39, local copies, waits for them, and re-layouts  5.88 us
  transfers between devices with their start and end apart: 17, of which 7 were waited for; matrix products, arithmetic and copies ran while one was open for 3% of the time, Pallas kernels for 21%

profile of v2, /device:TPU:18, one launch (start us, length us, event | category | flops | bytes accessed | tf_op | source)
XLA Modules:
  0.0 200.9 jit_solution(14159472602517565023)
XLA Ops:
  1.8 3.4 %collective-permute-start.1 = (f32[2,64,512]{2,1,0:T(8,128)S(1)}, f32[2,64,512]{2,1,0:T(8,128)S(1)}, u32[]{:S(2)}, u32[]{:S(2)}) collective-permute-start(f32[2,64,512]{2,1,0:T(8,128)S(1)} %get-tuple-element.67), channel_id=1, source_target_pairs={{0,1},{1,2},{2,3},{3,4},{4,5},{5,6},{6,7},{7,8},{8,9},{9,10},{10,1... | collective-permute-start | bytes 786440 | tf_op jit(solution)/shard_map/ppermute | solution.py:101
  7.6 2.8 %slice_bitcast_fusion = (f32[3,128,512]{2,1,0:T(8,128)}, f32[3,128,512]{2,1,0:T(8,128)}) fusion(f32[2,3,4,128,512]{4,3,2,1,0:T(8,128)} %bitcast.14), kind=kLoop, calls=%fused_computation | loop fusion | bytes 3145728 | tf_op jit(solution)/shard_map/squeeze | solution.py:123
  10.4 7.6 %collective-permute-done.1 = f32[2,64,512]{2,1,0:T(8,128)S(1)} collective-permute-done((f32[2,64,512]{2,1,0:T(8,128)S(1)}, f32[2,64,512]{2,1,0:T(8,128)S(1)}, u32[]{:S(2)}, u32[]{:S(2)}) %collective-permute-start.1) | collective-permute-done | bytes 262176 | tf_op jit(solution)/shard_map/ppermute | solution.py:101
  19.1 3.3 %collective-permute-start.4 = (f32[3,128,512]{2,1,0:T(8,128)}, f32[3,128,512]{2,1,0:T(8,128)S(1)}, u32[]{:S(2)}, u32[]{:S(2)}) collective-permute-start(f32[3,128,512]{2,1,0:T(8,128)} %get-tuple-element.62), channel_id=1, source_target_pairs={{0,1},{1,2},{2,3},{3,4},{4,5},{5,6},{6,7},{7,8},{8,9},{9,10},{10,1... | collective-permute-start | bytes 2359304 | tf_op jit(solution)/shard_map/ppermute | solution.py:101
  22.4 2.5 %collective-permute-start.5 = (f32[3,128,512]{2,1,0:T(8,128)}, f32[3,128,512]{2,1,0:T(8,128)}, u32[]{:S(2)}, u32[]{:S(2)}) collective-permute-start(f32[3,128,512]{2,1,0:T(8,128)} %get-tuple-element.63), channel_id=1, source_target_pairs={{1,0},{2,1},{3,2},{4,3},{5,4},{6,5},{7,6},{8,7},{9,8},{10,9},{11,1... | collective-permute-start | bytes 2359304 | tf_op jit(solution)/shard_map/ppermute | solution.py:98
  26.1 5.8 %forward.1 = (f32[8,128,512]{2,1,0:T(8,128)}, f32[4,128,512]{2,1,0:T(8,128)S(1)}, f32[2,128,512]{2,1,0:T(8,128)S(1)}, f32[3,128,512]{2,1,0:T(8,128)S(1)}, f32[3,128,512]{2,1,0:T(8,128)S(1)}) custom-call(s32[3]{0:T(128)S(1)} %pad_add_fusion.refs_0_.facts_ref, f32[4,64,512]{2,1,0:T(8,128)S(1)} %copy-done.2, f32[4,64,512]{2,1,0:T(8,128)S(1)} %collective-permute-done.refs_2_, ...), custom_call_target="tpu_custom_call" | custom-call | flops 1024 | bytes 1024 | tf_op jit(solution)/shard_map/forward/pallas_call | solution.py:65
  31.9 4.5 %collective-permute-start.6 = (f32[3,128,512]{2,1,0:T(8,128)S(1)}, f32[3,128,512]{2,1,0:T(8,128)S(1)}, u32[]{:S(2)}, u32[]{:S(2)}) collective-permute-start(f32[3,128,512]{2,1,0:T(8,128)S(1)} %get-tuple-element.41.refs_3_), channel_id=1, source_target_pairs={{1,0},{2,1},{3,2},{4,3},{5,4},{6,5},{7,6},{8,7},{9,8},{10,9},{11,1... | collective-permute-start | bytes 2359304 | tf_op jit(solution)/shard_map/ppermute | solution.py:98
  36.4 2.5 %collective-permute-start.11 = (f32[3,128,512]{2,1,0:T(8,128)S(1)}, f32[3,128,512]{2,1,0:T(8,128)S(1)}, u32[]{:S(2)}, u32[]{:S(2)}) collective-permute-start(f32[3,128,512]{2,1,0:T(8,128)S(1)} %get-tuple-element.49.refs_4_), channel_id=1, source_target_pairs={{0,1},{1,2},{2,3},{3,4},{4,5},{5,6},{6,7},{7,8},{8,9},{9,10},{10,1... | collective-permute-start | bytes 2359304 | tf_op jit(solution)/shard_map/ppermute | solution.py:101
  38.9 36.3 %collective-permute-done.4.v0_lo = f32[3,128,512]{2,1,0:T(8,128)S(1)} collective-permute-done((f32[3,128,512]{2,1,0:T(8,128)}, f32[3,128,512]{2,1,0:T(8,128)S(1)}, u32[]{:S(2)}, u32[]{:S(2)}) %collective-permute-start.4) | collective-permute-done | bytes 786464 | tf_op jit(solution)/shard_map/ppermute | solution.py:101
  75.2 5.2 %middle.1 = (f32[3,128,512]{2,1,0:T(8,128)}, f32[3,128,512]{2,1,0:T(8,128)}, f32[128,512]{1,0:T(8,128)S(1)}, f32[128,512]{1,0:T(8,128)S(1)}, f32[2,128,512]{2,1,0:T(8,128)S(1)}) custom-call(f32[8,128,512]{2,1,0:T(8,128)} %get-tuple-element.34.tmpl, f32[4,128,512]{2,1,0:T(8,128)S(1)} %get-tuple-element.36.img1, ...), custom_call_target="tpu_custom_call" | custom-call | flops 1024 | bytes 1024 | tf_op jit(solution)/shard_map/middle/pallas_call | solution.py:65
  80.5 5.6 %back.1 = (f32[4,128,512]{2,1,0:T(8,128)S(1)}, f32[3,128,512]{2,1,0:T(8,128)}, f32[3,128,512]{2,1,0:T(8,128)}) custom-call(f32[8,128,512]{2,1,0:T(8,128)S(1)} %copy-done, f32[2,128,512]{2,1,0:T(8,128)S(1)} %get-tuple-element.35.lam2_in, f32[2,128,512]{2,1,0:T(8,128)S(1)} %get-tuple-element.37.lam2_out, f32[2,3,4,128,512]{4,3,2,1,0:T(8,128)} %bitcast.18, ...), custom_call_target="tpu_custom_call" | custom-call | flops 1024 | bytes 1024 | tf_op jit(solution)/shard_map/back/pallas_call | solution.py:65
  88.0 9.3 %collective-permute-start.10 = (f32[128,512]{1,0:T(8,128)S(1)}, f32[128,512]{1,0:T(8,128)S(1)}, u32[]{:S(2)}, u32[]{:S(2)}) collective-permute-start(f32[128,512]{1,0:T(8,128)S(1)} %get-tuple-element.48), channel_id=1, source_target_pairs={{1,0},{2,1},{3,2},{4,3},{5,4},{6,5},{7,6},{8,7},{9,8},{10,9},{11,1... | collective-permute-start | bytes 786440 | tf_op jit(solution)/shard_map/ppermute | solution.py:98
  99.8 20.3 %collective-permute-done.10 = f32[128,512]{1,0:T(8,128)S(1)} collective-permute-done((f32[128,512]{1,0:T(8,128)S(1)}, f32[128,512]{1,0:T(8,128)S(1)}, u32[]{:S(2)}, u32[]{:S(2)}) %collective-permute-start.10) | collective-permute-done | bytes 262176 | tf_op jit(solution)/shard_map/ppermute | solution.py:98
  120.1 5.2 %collective-permute-done.9 = f32[128,512]{1,0:T(8,128)S(1)} collective-permute-done((f32[128,512]{1,0:T(8,128)S(1)}, f32[128,512]{1,0:T(8,128)S(1)}, u32[]{:S(2)}, u32[]{:S(2)}) %collective-permute-start.9) | collective-permute-done | bytes 262176 | tf_op jit(solution)/shard_map/ppermute | solution.py:101
  125.4 3.5 %collective-permute-start.13 = (f32[128,512]{1,0:T(8,128)S(1)}, f32[128,512]{1,0:T(8,128)S(1)}, u32[]{:S(2)}, u32[]{:S(2)}) collective-permute-start(f32[128,512]{1,0:T(8,128)S(1)} %get-tuple-element.64.last1), channel_id=1, source_target_pairs={{0,1},{1,2},{2,3},{3,4},{4,5},{5,6},{6,7},{7,8},{8,9},{9,10},{10,1... | collective-permute-start | bytes 786440 | tf_op jit(solution)/shard_map/ppermute | solution.py:101
  131.3 4.4 %collective-permute-start.15 = (f32[3,128,512]{2,1,0:T(8,128)}, f32[3,128,512]{2,1,0:T(8,128)}, u32[]{:S(2)}, u32[]{:S(2)}) collective-permute-start(f32[3,128,512]{2,1,0:T(8,128)} %get-tuple-element.58.refs_5_), channel_id=1, source_target_pairs={{0,1},{1,2},{2,3},{3,4},{4,5},{5,6},{6,7},{7,8},{8,9},{9,10},{10,1... | collective-permute-start | bytes 2359304 | tf_op jit(solution)/shard_map/ppermute | solution.py:101
  137.6 21.3 %collective-permute-done.13.lam1_lo = f32[128,512]{1,0:T(8,128)S(1)} collective-permute-done((f32[128,512]{1,0:T(8,128)S(1)}, f32[128,512]{1,0:T(8,128)S(1)}, u32[]{:S(2)}, u32[]{:S(2)}) %collective-permute-start.13) | collective-permute-done | bytes 262176 | tf_op jit(solution)/shard_map/ppermute | solution.py:101
  158.9 6.5 %last.1 = (f32[4,128,512]{2,1,0:T(8,128)}, f32[3,128,512]{2,1,0:T(8,128)S(1)}, f32[3,128,512]{2,1,0:T(8,128)S(1)}, f32[3,128,512]{2,1,0:T(8,128)S(1)}, f32[3,128,512]{2,1,0:T(8,128)S(1)}) custom-call(s32[3]{0:T(128)S(1)} %pad_add_fusion.refs_0_.facts_ref, f32[8,128,512]{2,1,0:T(8,128)} %get-tuple-element.34.tmpl, f32[4,128,512]{2,1,0:T(8,128)} %copy-done.1, ...), custom_call_target="tpu_custom_call" | custom-call | flops 1024 | bytes 60001024 | tf_op jit(solution)/shard_map/last/pallas_call | solution.py:65
  169.0 2.6 %collective-permute-start.8 = (f32[3,128,512]{2,1,0:T(8,128)}, f32[3,128,512]{2,1,0:T(8,128)S(1)}, u32[]{:S(2)}, u32[]{:S(2)}) collective-permute-start(f32[3,128,512]{2,1,0:T(8,128)} %get-tuple-element.44.refs_3_), channel_id=1, source_target_pairs={{0,1},{1,2},{2,3},{3,4},{4,5},{5,6},{6,7},{7,8},{8,9},{9,10},{10,1... | collective-permute-start | bytes 2359304 | tf_op jit(solution)/shard_map/ppermute | solution.py:101
  172.8 3.1 %collective-permute-done.15.refs_1_ = f32[3,128,512]{2,1,0:T(8,128)} collective-permute-done((f32[3,128,512]{2,1,0:T(8,128)}, f32[3,128,512]{2,1,0:T(8,128)}, u32[]{:S(2)}, u32[]{:S(2)}) %collective-permute-start.15) | collective-permute-done | bytes 786464 | tf_op jit(solution)/shard_map/ppermute | solution.py:101
  177.0 8.5 %smooth_1.1.refs_6_ = f32[2,3,4,128,512]{4,3,2,1,0:T(8,128)} custom-call(s32[3]{0:T(128)S(1)} %pad_add_fusion.refs_0_.facts_ref, f32[3,128,512]{2,1,0:T(8,128)S(1)} %copy-done.8, f32[3,128,512]{2,1,0:T(8,128)} %collective-permute-done.15.refs_1_, f32[3,128,512]{2,1,0:T(8,128)} %get-tuple-element.43.refs_2_, f32[3,128,512]{2,1,0:T(8,128)S(1)} %copy-done.4, ...), custom_call_target="tpu_custom_call" | custom-call | flops 1024 | bytes 90001024 | tf_op jit(solution)/shard_map/smooth_1/pallas_call | solution.py:65
  185.5 8.4 %smooth_0.1.grad = f32[2,3,4,128,512]{4,3,2,1,0:T(8,128)} custom-call(s32[3]{0:T(128)S(1)} %pad_add_fusion.refs_0_.facts_ref, f32[3,128,512]{2,1,0:T(8,128)S(1)} %copy-done.10, f32[3,128,512]{2,1,0:T(8,128)S(1)} %copy-done.12, f32[3,128,512]{2,1,0:T(8,128)} %get-tuple-element.52.refs_2_, ...), custom_call_target="tpu_custom_call", output_to_operand_aliasing={{}: (7, {})} | custom-call | flops 1024 | bytes 90001024 | tf_op jit(solution)/shard_map/smooth_0/pallas_call | solution.py:65
  194.0 3.1 %add_far.2.grad = f32[2,3,4,128,512]{4,3,2,1,0:T(8,128)} custom-call(f32[3,128,512]{2,1,0:T(8,128)} %collective-permute-done.12.src, f32[2,3,4,128,512]{4,3,2,1,0:T(8,128)} %smooth_0.1.grad), custom_call_target="tpu_custom_call", output_to_operand_aliasing={{}: (1, {})} | custom-call | flops 1024 | bytes 1024 | tf_op jit(solution)/shard_map/add_far/pallas_call | solution.py:65
  198.0 2.9 %add_far.3 = f32[2,3,4,128,512]{4,3,2,1,0:T(8,128)} custom-call(f32[3,128,512]{2,1,0:T(8,128)S(1)} %collective-permute-done.8.src, f32[2,3,4,128,512]{4,3,2,1,0:T(8,128)} %add_far.2.grad), custom_call_target="tpu_custom_call", output_to_operand_aliasing={{}: (1, {})} | custom-call | flops 1024 | bytes 1024 | tf_op jit(solution)/shard_map/add_far/pallas_call | solution.py:65
  (64 shorter events, 21.4 us)
Async XLA Ops:
  0.6 24.4 %collective-permute-start = (f32[4,64,512]{2,1,0:T(8,128)}, f32[4,64,512]{2,1,0:T(8,128)S(1)}, u32[]{:S(2)}, u32[]{:S(2)}) collective-permute-start(f32[4,64,512]{2,1,0:T(8,128)} %refs_1_.1), channel_id=1, source_target_pairs={{0,16},{16,0},{1,17},{17,1},{2,18},{18,2},{3,19},{19,3},{4,20},{20... | collective-permute-start | bytes 1572872 | tf_op jit(solution)/shard_map/ppermute | solution.py:104
  1.8 16.2 %collective-permute-start.1 = (f32[2,64,512]{2,1,0:T(8,128)S(1)}, f32[2,64,512]{2,1,0:T(8,128)S(1)}, u32[]{:S(2)}, u32[]{:S(2)}) collective-permute-start(f32[2,64,512]{2,1,0:T(8,128)S(1)} %get-tuple-element.67), channel_id=1, source_target_pairs={{0,1},{1,2},{2,3},{3,4},{4,5},{5,6},{6,7},{7,8},{8,9},{9,10},{10,1... | collective-permute-start | bytes 786440 | tf_op jit(solution)/shard_map/ppermute | solution.py:101
  5.2 13.8 %collective-permute-start.2 = (f32[2,64,512]{2,1,0:T(8,128)S(1)}, f32[2,64,512]{2,1,0:T(8,128)S(1)}, u32[]{:S(2)}, u32[]{:S(2)}) collective-permute-start(f32[2,64,512]{2,1,0:T(8,128)S(1)} %get-tuple-element.66), channel_id=1, source_target_pairs={{1,0},{2,1},{3,2},{4,3},{5,4},{6,5},{7,6},{8,7},{9,8},{10,9},{11,1... | collective-permute-start | bytes 786440 | tf_op jit(solution)/shard_map/ppermute | solution.py:98
  19.0 6.0 %collective-permute-start.3 = (f32[4,64,512]{2,1,0:T(8,128)S(1)}, f32[4,64,512]{2,1,0:T(8,128)S(1)}, u32[]{:S(2)}, u32[]{:S(2)}) collective-permute-start(f32[4,64,512]{2,1,0:T(8,128)S(1)} %constant_dynamic-update-slice_fusion.refs_3_), channel_id=1, source_target_pairs={{0,16},{16,0},{1,17},{17,1},{2,18},{18,2},{3,19},{19,3},{4,20},{20... | collective-permute-start | bytes 1572872 | tf_op jit(solution)/shard_map/ppermute | solution.py:104
  19.1 56.1 %collective-permute-start.4 = (f32[3,128,512]{2,1,0:T(8,128)}, f32[3,128,512]{2,1,0:T(8,128)S(1)}, u32[]{:S(2)}, u32[]{:S(2)}) collective-permute-start(f32[3,128,512]{2,1,0:T(8,128)} %get-tuple-element.62), channel_id=1, source_target_pairs={{0,1},{1,2},{2,3},{3,4},{4,5},{5,6},{6,7},{7,8},{8,9},{9,10},{10,1... | collective-permute-start | bytes 2359304 | tf_op jit(solution)/shard_map/ppermute | solution.py:101
  22.4 52.8 %collective-permute-start.5 = (f32[3,128,512]{2,1,0:T(8,128)}, f32[3,128,512]{2,1,0:T(8,128)}, u32[]{:S(2)}, u32[]{:S(2)}) collective-permute-start(f32[3,128,512]{2,1,0:T(8,128)} %get-tuple-element.63), channel_id=1, source_target_pairs={{1,0},{2,1},{3,2},{4,3},{5,4},{6,5},{7,6},{8,7},{9,8},{10,9},{11,1... | collective-permute-start | bytes 2359304 | tf_op jit(solution)/shard_map/ppermute | solution.py:98
  31.9 54.2 %copy-start.3 = (f32[3,128,512]{2,1,0:T(8,128)}, f32[3,128,512]{2,1,0:T(8,128)S(1)}, u32[]{:S(2)}) copy-start(f32[3,128,512]{2,1,0:T(8,128)S(1)} %get-tuple-element.41.refs_3_) | copy-start | bytes 2359300
  31.9 54.2 %copy-start.5 = (f32[3,128,512]{2,1,0:T(8,128)}, f32[3,128,512]{2,1,0:T(8,128)S(1)}, u32[]{:S(2)}) copy-start(f32[3,128,512]{2,1,0:T(8,128)S(1)} %get-tuple-element.49.refs_4_) | copy-start | bytes 2359300
  31.9 48.6 %copy-start = (f32[8,128,512]{2,1,0:T(8,128)S(1)}, f32[8,128,512]{2,1,0:T(8,128)}, u32[]{:S(2)}) copy-start(f32[8,128,512]{2,1,0:T(8,128)} %get-tuple-element.34.tmpl) | copy-start | bytes 6291460
  31.9 54.2 %collective-permute-start.6 = (f32[3,128,512]{2,1,0:T(8,128)S(1)}, f32[3,128,512]{2,1,0:T(8,128)S(1)}, u32[]{:S(2)}, u32[]{:S(2)}) collective-permute-start(f32[3,128,512]{2,1,0:T(8,128)S(1)} %get-tuple-element.41.refs_3_), channel_id=1, source_target_pairs={{1,0},{2,1},{3,2},{4,3},{5,4},{6,5},{7,6},{8,7},{9,8},{10,9},{11,1... | collective-permute-start | bytes 2359304 | tf_op jit(solution)/shard_map/ppermute | solution.py:98
  36.4 88.9 %collective-permute-start.11 = (f32[3,128,512]{2,1,0:T(8,128)S(1)}, f32[3,128,512]{2,1,0:T(8,128)S(1)}, u32[]{:S(2)}, u32[]{:S(2)}) collective-permute-start(f32[3,128,512]{2,1,0:T(8,128)S(1)} %get-tuple-element.49.refs_4_), channel_id=1, source_target_pairs={{0,1},{1,2},{2,3},{3,4},{4,5},{5,6},{6,7},{7,8},{8,9},{9,10},{10,1... | collective-permute-start | bytes 2359304 | tf_op jit(solution)/shard_map/ppermute | solution.py:101
  86.0 39.2 %copy-start.1 = (f32[4,128,512]{2,1,0:T(8,128)}, f32[4,128,512]{2,1,0:T(8,128)S(1)}, u32[]{:S(2)}) copy-start(f32[4,128,512]{2,1,0:T(8,128)S(1)} %get-tuple-element.46.part1) | copy-start | bytes 3145732
  86.1 42.8 %copy-start.18 = (f32[3,128,512]{2,1,0:T(8,128)}, f32[3,128,512]{2,1,0:T(8,128)S(1)}, u32[]{:S(2)}) copy-start(f32[3,128,512]{2,1,0:T(8,128)S(1)} %collective-permute-done.6.refs_7_) | copy-start | bytes 2359300
  86.1 83.0 %collective-permute-start.7 = (f32[3,128,512]{2,1,0:T(8,128)}, f32[3,128,512]{2,1,0:T(8,128)}, u32[]{:S(2)}, u32[]{:S(2)}) collective-permute-start(f32[3,128,512]{2,1,0:T(8,128)} %get-tuple-element.43.refs_2_), channel_id=1, source_target_pairs={{1,0},{2,1},{3,2},{4,3},{5,4},{6,5},{7,6},{8,7},{9,8},{10,9},{11,1... | collective-permute-start | bytes 2359304 | tf_op jit(solution)/shard_map/ppermute | solution.py:98
  88.0 32.1 %collective-permute-start.10 = (f32[128,512]{1,0:T(8,128)S(1)}, f32[128,512]{1,0:T(8,128)S(1)}, u32[]{:S(2)}, u32[]{:S(2)}) collective-permute-start(f32[128,512]{1,0:T(8,128)S(1)} %get-tuple-element.48), channel_id=1, source_target_pairs={{1,0},{2,1},{3,2},{4,3},{5,4},{6,5},{7,6},{8,7},{9,8},{10,9},{11,1... | collective-permute-start | bytes 786440 | tf_op jit(solution)/shard_map/ppermute | solution.py:98
  97.3 28.0 %collective-permute-start.9 = (f32[128,512]{1,0:T(8,128)S(1)}, f32[128,512]{1,0:T(8,128)S(1)}, u32[]{:S(2)}, u32[]{:S(2)}) collective-permute-start(f32[128,512]{1,0:T(8,128)S(1)} %get-tuple-element.47), channel_id=1, source_target_pairs={{0,1},{1,2},{2,3},{3,4},{4,5},{5,6},{6,7},{7,8},{8,9},{9,10},{10,1... | collective-permute-start | bytes 786440 | tf_op jit(solution)/shard_map/ppermute | solution.py:101
  125.4 33.5 %collective-permute-start.13 = (f32[128,512]{1,0:T(8,128)S(1)}, f32[128,512]{1,0:T(8,128)S(1)}, u32[]{:S(2)}, u32[]{:S(2)}) collective-permute-start(f32[128,512]{1,0:T(8,128)S(1)} %get-tuple-element.64.last1), channel_id=1, source_target_pairs={{0,1},{1,2},{2,3},{3,4},{4,5},{5,6},{6,7},{7,8},{8,9},{9,10},{10,1... | collective-permute-start | bytes 786440 | tf_op jit(solution)/shard_map/ppermute | solution.py:101
  128.9 30.0 %collective-permute-start.14 = (f32[128,512]{1,0:T(8,128)S(1)}, f32[128,512]{1,0:T(8,128)S(1)}, u32[]{:S(2)}, u32[]{:S(2)}) collective-permute-start(f32[128,512]{1,0:T(8,128)S(1)} %get-tuple-element.65.first1), channel_id=1, source_target_pairs={{1,0},{2,1},{3,2},{4,3},{5,4},{6,5},{7,6},{8,7},{9,8},{10,9},{11,1... | collective-permute-start | bytes 786440 | tf_op jit(solution)/shard_map/ppermute | solution.py:98
  131.3 44.6 %collective-permute-start.15 = (f32[3,128,512]{2,1,0:T(8,128)}, f32[3,128,512]{2,1,0:T(8,128)}, u32[]{:S(2)}, u32[]{:S(2)}) collective-permute-start(f32[3,128,512]{2,1,0:T(8,128)} %get-tuple-element.58.refs_5_), channel_id=1, source_target_pairs={{0,1},{1,2},{2,3},{3,4},{4,5},{5,6},{6,7},{7,8},{8,9},{9,10},{10,1... | collective-permute-start | bytes 2359304 | tf_op jit(solution)/shard_map/ppermute | solution.py:101
  135.7 58.3 %collective-permute-start.12 = (f32[3,128,512]{2,1,0:T(8,128)}, f32[3,128,512]{2,1,0:T(8,128)}, u32[]{:S(2)}, u32[]{:S(2)}) collective-permute-start(f32[3,128,512]{2,1,0:T(8,128)} %get-tuple-element.52.refs_2_), channel_id=1, source_target_pairs={{1,0},{2,1},{3,2},{4,3},{5,4},{6,5},{7,6},{8,7},{9,8},{10,9},{11,1... | collective-permute-start | bytes 2359304 | tf_op jit(solution)/shard_map/ppermute | solution.py:98
  137.6 38.3 %copy-start.4 = (f32[3,128,512]{2,1,0:T(8,128)S(1)}, f32[3,128,512]{2,1,0:T(8,128)}, u32[]{:S(2)}) copy-start(f32[3,128,512]{2,1,0:T(8,128)} %copy-done.3) | copy-start | bytes 2359300
  137.6 38.3 %copy-start.6 = (f32[3,128,512]{2,1,0:T(8,128)S(1)}, f32[3,128,512]{2,1,0:T(8,128)}, u32[]{:S(2)}) copy-start(f32[3,128,512]{2,1,0:T(8,128)} %copy-done.5) | copy-start | bytes 2359300
  169.0 29.0 %collective-permute-start.8 = (f32[3,128,512]{2,1,0:T(8,128)}, f32[3,128,512]{2,1,0:T(8,128)S(1)}, u32[]{:S(2)}, u32[]{:S(2)}) collective-permute-start(f32[3,128,512]{2,1,0:T(8,128)} %get-tuple-element.44.refs_3_), channel_id=1, source_target_pairs={{0,1},{1,2},{2,3},{3,4},{4,5},{5,6},{6,7},{7,8},{8,9},{9,10},{10,1... | collective-permute-start | bytes 2359304 | tf_op jit(solution)/shard_map/ppermute | solution.py:101
  172.7 24.4 %collective-permute-start.16 = (f32[4,64,512]{2,1,0:T(8,128)S(1)}, f32[4,64,512]{2,1,0:T(8,128)S(1)}, u32[]{:S(2)}, u32[]{:S(2)}) collective-permute-start(f32[4,64,512]{2,1,0:T(8,128)S(1)} %constant_dynamic-slice_fusion), channel_id=1, source_target_pairs={{0,16},{16,0},{1,17},{17,1},{2,18},{18,2},{3,19},{19,3},{4,20},{20... | collective-permute-start | bytes 1572872 | tf_op jit(solution)/shard_map/ppermute | solution.py:104
  (12 other events, 46.6 us)

commit v3 on v2

v3 whole, which is shorter than its diff:
```python
import jax
import jax.numpy as jnp
from jax import lax
from jax.experimental import pallas as pl
from jax.experimental.pallas import tpu as pltpu
from jax.sharding import PartitionSpec as P

MATCH = 5.0
SEVENTH = 1.0 / 7.0
MIB = 1 << 20
FORWARD, MIDDLE, BACK, LAST, SMOOTH = 0, 0, 0, 100, 150


def col_prev(f):
    x = lax.broadcasted_iota(jnp.int32, f.shape, 1)
    return jnp.where(x == 0, 0.0, pltpu.roll(f, 1, 1))


def col_next(f):
    n = f.shape[1]
    x = lax.broadcasted_iota(jnp.int32, f.shape, 1)
    return jnp.where(x == n - 1, 0.0, pltpu.roll(f, n - 1, 1))


def row_prev(f):
    y = lax.broadcasted_iota(jnp.int32, f.shape, 0)
    return jnp.where(y == 0, 0.0, pltpu.roll(f, 1, 0))


def row_next(f):
    n = f.shape[0]
    y = lax.broadcasted_iota(jnp.int32, f.shape, 0)
    return jnp.where(y == n - 1, 0.0, pltpu.roll(f, n - 1, 0))


def upwind(below, f, above, v):
    return [
        jnp.where(v[0] >= 0.0, f - below, above - f),
        jnp.where(v[1] >= 0.0, f - row_prev(f), row_next(f) - f),
        jnp.where(v[2] >= 0.0, f - col_prev(f), col_next(f) - f),
    ]


def advance(f, diffs, v, dt):
    return f - dt * (v[0] * diffs[0] + v[1] * diffs[1] + v[2] * diffs[2])


def retreat(lam, v, pos_above, neg_below, dt):
    total = (jnp.abs(v[0]) + jnp.abs(v[1]) + jnp.abs(v[2])) * lam
    total = total - row_next(jnp.maximum(v[1], 0.0) * lam)
    total = total + row_prev(jnp.minimum(v[1], 0.0) * lam)
    total = total - col_next(jnp.maximum(v[2], 0.0) * lam)
    total = total + col_prev(jnp.minimum(v[2], 0.0) * lam)
    if pos_above is not None:
        total = total - pos_above
    if neg_below is not None:
        total = total + neg_below
    return lam - dt * total


def plane_sum(f):
    return row_prev(f) + row_next(f) + col_prev(f) + col_next(f)


def call(kernel, out_shape, in_specs, out_specs, operands, name, weight=0, grid=(1,), aliases=None, scratch=(), prefetch=0):
    return pl.pallas_call(
        kernel,
        out_shape=out_shape,
        grid_spec=pltpu.PrefetchScalarGridSpec(
            num_scalar_prefetch=prefetch,
            grid=grid,
            in_specs=in_specs,
            out_specs=out_specs,
            scratch_shapes=list(scratch),
        ),
        input_output_aliases=aliases or {},
        compiler_params=pltpu.CompilerParams(vmem_limit_bytes=48 * MIB),
        cost_estimate=pl.CostEstimate(
            flops=1024 + weight * 10000000, bytes_accessed=1024, transcendentals=0
        ),
        name=name,
    )(*operands)


def whole(x):
    zeros = (0,) * x.ndim
    return pl.BlockSpec(x.shape, lambda *_: zeros)


def struct(*shape):
    return jax.ShapeDtypeStruct(shape, jnp.float32)


SMEM = pl.BlockSpec(memory_space=pltpu.SMEM)
SIDES = (0, 1)


def make_body(subj, slabs):
    pairs = []
    for first in SIDES:
        lower = [(i, i + 1) for i in range(first, slabs - 1, 2)]
        pairs.append(lower + [(j, i) for i, j in lower])

    def swap(x, side):
        return lax.ppermute(x, "slab", pairs[side])

    def turn(x, k):
        return lax.ppermute(x, "subj", [(i, (i + k) % subj) for i in range(subj)])

    def after(x, *others):
        return lax.optimization_barrier((x, *others))

    def body(template, subject, velocity):
        flow = velocity[0]
        target = subject[0]
        steps, _, Z, Y, X = flow.shape
        assert Z == 4 and steps == 2
        rows = template.shape[1]
        dt = 1.0 / steps
        place = lax.axis_index("slab")
        group = lax.axis_index("subj")
        even = 1 - place % 2
        facts = jnp.stack([group, place > 0, place < slabs - 1, even]).astype(jnp.int32)
        ups = (even, 1 - even)
        flow_spec = [
            pl.BlockSpec((1, 3, Z, Y, X), lambda *_, t=t: (t, 0, 0, 0, 0)) for t in range(steps)
        ]

        def up_at(facts_ref, i):
            return facts_ref[3] if i == 0 else 1 - facts_ref[3]

        tmpl_far = [
            swap(lax.dynamic_slice_in_dim(template, up * (Z - 2), 2, 0), i)
            for i, up in enumerate(ups)
        ]
        flow0_edge = [
            lax.dynamic_slice_in_dim(flow[0], up * (Z - 1), 1, 1)[:, 0] for up in ups
        ]
        flow0_far = [swap(flow0_edge[i], i) for i in SIDES]
        own_parts = [template] + [turn(template, k) for k in range(1, subj)]
        tmpl_far[0], tmpl_far[1], _, _ = after(*tmpl_far, *flow0_edge)
        edge = jnp.concatenate(tmpl_far, axis=0)
        edge_parts = [edge] + [turn(edge, k) for k in range(1, subj)]

        def forward(*refs):
            facts_ref, refs = refs[0], refs[1:]
            owns, edges = refs[:subj], refs[subj : 2 * subj]
            v0, v1, aim = refs[2 * subj : 2 * subj + 3]
            tmpl, img1, lam2, *srcs = refs[2 * subj + 3 :]
            for k in range(subj):
                start = pl.multiple_of(lax.rem(facts_ref[0] + subj - k, subj) * rows, rows)
                at = pl.ds(start, rows)
                tmpl[2 : Z + 2, at, :] = owns[k][...]
                for i in SIDES:
                    up = up_at(facts_ref, i)
                    for j in range(2):
                        tmpl[up * (Z + 2) + j, at, :] = edges[k][2 * i + j]
            for z in range(Z):
                v = [v0[0, d, z] for d in range(3)]
                f = tmpl[z + 2]
                img1[z] = advance(f, upwind(tmpl[z + 1], f, tmpl[z + 3], v), v, dt)
            for i in SIDES:
                z = 1 + up_at(facts_ref, i) * (Z - 3)
                v = [v1[0, d, z] for d in range(3)]
                f = img1[z]
                diffs = upwind(img1[z - 1], f, img1[z + 1], v)
                lam = advance(f, diffs, v, dt) - aim[z]
                lam2[i] = lam
                for d in range(3):
                    srcs[i][d] = (-MATCH * dt) * lam * diffs[d]

        outs = [struct(Z + 4, Y, X), struct(Z, Y, X), struct(2, Y, X)] + [struct(3, Y, X)] * 2
        operands = [facts] + own_parts + edge_parts + [flow, flow, target]
        tmpl, img1, lam2_in, *inner1 = call(
            forward,
            outs,
            [SMEM]
            + [whole(x) for x in own_parts + edge_parts]
            + [flow_spec[0], flow_spec[1], whole(target)],
            [whole(x) for x in outs],
            operands,
            "forward",
            weight=FORWARD,
        )
        far1 = [swap(inner1[0], 0), None]

        def middle(facts_ref, tmpl, img1, halo0, halo1, v1, aim, src0, src1, flux0, flux1, lam2, v0_far):
            for i, halo, src, flux in ((0, halo0, src0, flux0), (1, halo1, src1, flux1)):
                up = up_at(facts_ref, i)
                at = 1 + up * (Z + 1)
                v = [halo[d] for d in range(3)]
                for d in range(3):
                    v0_far[up, d] = v[d]
                f = tmpl[at]
                outside = advance(f, upwind(tmpl[at - 1], f, tmpl[at + 1], v), v, dt)
                z = up * (Z - 1)
                inside = img1[z + 1 - 2 * up]
                below = jnp.where(up == 1, inside, outside)
                above = jnp.where(up == 1, outside, inside)
                v = [v1[0, d, z] for d in range(3)]
                f = img1[z]
                diffs = upwind(below, f, above, v)
                lam = advance(f, diffs, v, dt) - aim[z]
                for d in range(3):
                    src[d] = (-MATCH * dt) * lam * diffs[d]
                lam2[i] = lam
                flux[...] = jnp.where(up == 1, jnp.minimum(v[0], 0.0), jnp.maximum(v[0], 0.0)) * lam

        outs = [struct(3, Y, X)] * 2 + [struct(Y, X)] * 2 + [struct(2, Y, X), struct(2, 3, Y, X)]
        operands = [facts, tmpl, img1, *flow0_far, flow, target]
        *outer1, flux_0, flux_1, lam2_out, v0_far = call(
            middle,
            outs,
            [SMEM] + [whole(x) for x in operands[1:5]] + [flow_spec[1], whole(target)],
            [whole(x) for x in outs],
            operands,
            "middle",
            weight=MIDDLE,
        )
        flux_far = [swap(flux_0, 0), swap(flux_1, 1)]

        def back(facts_ref, tmpl, lam2_in, lam2_out, v0, v1, lam1, part0, part1, src0, src1, lam2):
            for i in SIDES:
                up = up_at(facts_ref, i)
                lam2[1 + up * (Z - 3)] = lam2_in[i]
                lam2[up * (Z - 1)] = lam2_out[i]
            for z in range(Z):
                v = [v1[0, d, z] for d in range(3)]
                above = jnp.maximum(v1[0, 0, z + 1], 0.0) * lam2[z + 1] if z < Z - 1 else None
                below = jnp.minimum(v1[0, 0, z - 1], 0.0) * lam2[z - 1] if z > 0 else None
                lam1[z] = retreat(lam2[z], v, above, below, dt)
            for i, part, src in ((0, part0, src0), (1, part1, src1)):
                up = up_at(facts_ref, i)
                part[...] = lam1[up * (Z - 1)]
                z = 1 + up * (Z - 3)
                v = [v0[0, d, z] for d in range(3)]
                diffs = upwind(tmpl[z + 1], tmpl[z + 2], tmpl[z + 3], v)
                lam = lam1[z]
                for d in range(3):
                    src[d] = (-MATCH * dt) * lam * diffs[d]

        outs = [struct(Z, Y, X)] + [struct(Y, X)] * 2 + [struct(3, Y, X)] * 2
        operands = [facts, tmpl, lam2_in, lam2_out, flow, flow]
        lam1_part, part_0, part_1, *inner0 = call(
            back,
            outs,
            [SMEM] + [whole(x) for x in operands[1:4]] + [flow_spec[0], flow_spec[1]],
            [whole(x) for x in outs],
            operands,
            "back",
            weight=BACK,
            scratch=[pltpu.VMEM((Z, Y, X), jnp.float32)],
        )

        near1 = [swap(outer1[0], 0), None]

        *flux_far, far1[0] = after(*flux_far, far1[0])
        toward = (2 * even - 1).astype(jnp.float32) * dt
        lam1_edge = [part_0 + toward * flux_far[0], part_1 - toward * flux_far[1]]
        lam1_far = [swap(lam1_edge[i], i) for i in SIDES]

        held = after(inner0[0], *lam1_edge)[0]
        far0 = [swap(held, 0), None]
        far1[1] = swap(after(inner1[1], *lam1_edge)[0], 1)
        held, near1[0] = after(outer1[1], near1[0])
        near1[1] = swap(held, 1)
        held, far0[0] = after(inner0[1], far0[0])
        far0[1] = swap(held, 1)

        def sweeps(facts_ref, s, v, out, u2):
            for z in range(-1, Z + 1):
                beside = plane_sum(s[z])
                if z - 1 in s:
                    beside = beside + s[z - 1]
                if z + 1 in s:
                    beside = beside + s[z + 1]
                u = (s[z] + beside * SEVENTH) * SEVENTH
                if z == -1:
                    u = jnp.where(facts_ref[1] > 0, u, 0.0)
                if z == Z:
                    u = jnp.where(facts_ref[2] > 0, u, 0.0)
                u2[z + 1] = u
            for z in range(Z):
                u = u2[z + 1]
                beside = plane_sum(u) + u2[z] + u2[z + 2]
                out[0, 0, z] = v[0, 0, z] + (s[z] + beside) * SEVENTH

        class Planes:
            def __init__(self, ref, low, high):
                self.ref, self.low, self.high = ref, low, high

            def __contains__(self, z):
                return self.low <= z <= self.high

            def __getitem__(self, z):
                return self.ref[z - self.low]

        part = pl.BlockSpec((1, Y, X), lambda d: (d, 0, 0))
        flow_part = [
            pl.BlockSpec((1, 1, Z, Y, X), lambda d, t=t: (t, d, 0, 0, 0)) for t in range(steps)
        ]
        u2_scratch = pltpu.VMEM((Z + 2, Y, X), jnp.float32)

        def smooth_1(facts_ref, in0, in1, out0, out1, near0, near1, far0, far1, v, out, u2, s):
            for i, inner, outer, near, far in ((0, in0, out0, near0, far0), (1, in1, out1, near1, far1)):
                up = up_at(facts_ref, i)
                s[3 + up * (Z - 3)] = inner[0]
                s[2 + up * (Z - 1)] = outer[0]
                s[1 + up * (Z + 1)] = near[0]
                s[up * (Z + 3)] = far[0]
            sweeps(facts_ref, Planes(s, -2, Z + 1), v, out, u2)

        gradient = call(
            smooth_1,
            struct(*flow.shape),
            [SMEM] + [part] * 8 + [flow_part[1]],
            flow_part[1],
            [facts, *inner1, *outer1, *near1, *far1, flow],
            "smooth_1",
            weight=SMOOTH,
            grid=(3,),
            scratch=[u2_scratch, pltpu.VMEM((Z + 4, Y, X), jnp.float32)],
        )

        def last(facts_ref, tmpl, part, edge0, edge1, beyond0, beyond1, v0_far, v0, lam0, src, lam):
            for z in range(1, Z - 1):
                lam[z + 1] = part[z]
            for i, edge, beyond in ((0, edge0, beyond0), (1, edge1, beyond1)):
                up = up_at(facts_ref, i)
                lam[1 + up * (Z - 1)] = edge[...]
                lam[up * (Z + 1)] = beyond[...]

            def flow_at(z, d):
                return v0[0, d, z] if 0 <= z < Z else v0_far[0 if z < 0 else 1, d]

            for j, z in enumerate((-1, 0, Z - 1, Z)):
                v = [flow_at(z, d) for d in range(3)]
                diffs = upwind(tmpl[z + 1], tmpl[z + 2], tmpl[z + 3], v)
                for d in range(3):
                    src[j, d] = (-MATCH * dt) * lam[z + 1] * diffs[d]
            for z in range(Z):
                above = jnp.maximum(flow_at(z + 1, 0), 0.0) * lam[z + 2]
                below = jnp.minimum(flow_at(z - 1, 0), 0.0) * lam[z]
                v = [flow_at(z, d) for d in range(3)]
                lam0[z] = retreat(lam[z + 1], v, above, below, dt)

        outs = [struct(Z, Y, X), struct(4, 3, Y, X)]
        operands = [facts, tmpl, lam1_part, *lam1_edge, *lam1_far, v0_far, flow]
        lam0, rest0 = call(
            last,
            outs,
            [SMEM] + [whole(x) for x in operands[1:8]] + [flow_spec[0]],
            [whole(x) for x in outs],
            operands,
            "last",
            weight=LAST,
            scratch=[pltpu.VMEM((Z + 2, Y, X), jnp.float32)],
        )

        def share(k):
            start = lax.rem(group + k, subj) * rows
            return lax.dynamic_slice_in_dim(lam0, start, rows, axis=1)

        template_grad = share(0)
        for k in range(1, subj):
            template_grad = template_grad + turn(share(k), k)

        def smooth_0(facts_ref, in0, in1, rest, _, v, out, u2, s):
            for i, inner in ((0, in0), (1, in1)):
                s[2 + up_at(facts_ref, i) * (Z - 3)] = inner[0]
            for j, z in enumerate((-1, 0, Z - 1, Z)):
                s[z + 1] = rest[j, 0]
            sweeps(facts_ref, Planes(s, -1, Z), v, out, u2)

        gradient = call(
            smooth_0,
            struct(*flow.shape),
            [SMEM, part, part]
            + [pl.BlockSpec((4, 1, Y, X), lambda d: (0, d, 0, 0))]
            + [pl.BlockSpec(memory_space=pl.ANY), flow_part[0]],
            flow_part[0],
            [facts, *inner0, rest0, gradient, flow],
            "smooth_0",
            weight=SMOOTH,
            grid=(3,),
            aliases={4: 0},
            scratch=[u2_scratch, pltpu.VMEM((Z + 2, Y, X), jnp.float32)],
        )

        def add_far(facts_ref, src, grad, out):
            for d in range(3):
                out[0, d, 0] = grad[0, d, 0] + src[d] * SEVENTH**3

        for i in SIDES:

            def boundary(_, facts_ref, i=i):
                return (0, 0, up_at(facts_ref, i) * (Z - 1), 0, 0)

            block = pl.BlockSpec((1, 3, 1, Y, X), boundary)
            gradient = call(
                add_far,
                struct(*flow.shape),
                [pl.BlockSpec((3, Y, X), lambda *_: (0, 0, 0)), block],
                block,
                [facts, far0[i], gradient],
                "add_far",
                aliases={2: 0},
                prefetch=1,
            )
        return gradient[None], template_grad

    return body


def solution(mesh):
    sizes = dict(mesh.shape)
    return jax.shard_map(
        make_body(sizes["subj"], sizes["slab"]),
        mesh=mesh,
        in_specs=(
            P("slab", "subj", None),
            P("subj", "slab", None, None),
            P("subj", None, None, "slab", None, None),
        ),
        out_specs=(P("subj", None, None, "slab", None, None), P("slab", "subj", None)),
        check_vma=False,
    )
```

time: 202 us -> 200 us (0.990)
  the two profiles are of different devices: /device:TPU:18 before, /device:TPU:2 now
where the time goes in v3:
time: 200 us; the launch traced here: 197 us
  waiting for transfers between devices  98.6 us (49%)
  Pallas kernels  46.4 us (23%)
  starting transfers between devices  26 us (13%)
  local copies, waits for them, and re-layouts  21.5 us (11%)
  other arithmetic  4.04 us (2%)
    ppermute x14, waiting for transfers between devices, swap(): return lax.ppermute(x, 'slab', pairs[side])  98.6 us
    pallas_call x8, Pallas kernels, call(): pl.pallas_call(kernel, out_shape=out_shape, grid_spec=pltpu.PrefetchScala...  46.4 us
    ppermute x14, starting transfers between devices, swap(): return lax.ppermute(x, 'slab', pairs[side])  25.8 us
    unnamed x37, local copies, waits for them, and re-layouts  13.7 us
  transfers between devices with their start and end apart: 17, of which 6 were waited for; matrix products, arithmetic and copies ran while one was open for 5% of the time, Pallas kernels for 22%

profile of v3, /device:TPU:2, one launch (start us, length us, event | category | flops | bytes accessed | tf_op | source)
XLA Modules:
  0.0 197.5 jit_solution(6942781149665391909)
XLA Ops:
  1.9 4.9 %collective-permute-start.2 = (f32[2,64,512]{2,1,0:T(8,128)S(1)}, f32[2,64,512]{2,1,0:T(8,128)S(1)}, u32[]{:S(2)}, u32[]{:S(2)}) collective-permute-start(f32[2,64,512]{2,1,0:T(8,128)S(1)} %get-tuple-element.62), channel_id=1, source_target_pairs={{1,2},{3,4},{5,6},{7,8},{9,10},{11,12},{13,14},{2,1},{4,3},{6,5},{... | collective-permute-start | bytes 786440 | tf_op jit(solution)/shard_map/ppermute | solution.py:105
  6.8 3.9 %slice.5 = f32[1,1,3,4,128,512]{5,4,3,2,1,0:T(8,128)} slice(f32[1,2,3,4,128,512]{5,4,3,2,1,0:T(8,128)} %param.5), slice={[0:1], [0:1], [0:3], [0:4], [0:128], [0:512]} | slice | bytes 6291456 | tf_op jit(solution)/shard_map/slice | solution.py:137
  10.7 2.8 %dynamic-slice_bitcast_fusion = (f32[3,128,512]{2,1,0:T(8,128)}, f32[3,128,512]{2,1,0:T(8,128)}) fusion(f32[1,1,3,4,128,512]{5,4,3,2,1,0:T(8,128)} %slice.5, s32[]{:T(128)S(6)} %select_n.29, s32[]{:T(128)S(6)} %select_n.28), kind=kLoop, calls=%fused_computation | loop fusion | bytes 3145736 | tf_op jit(solution)/shard_map/squeeze | solution.py:137
  13.5 2.0 %collective-permute-done.1 = f32[2,64,512]{2,1,0:T(8,128)S(1)} collective-permute-done((f32[2,64,512]{2,1,0:T(8,128)S(1)}, f32[2,64,512]{2,1,0:T(8,128)S(1)}, u32[]{:S(2)}, u32[]{:S(2)}) %collective-permute-start.1) | collective-permute-done | bytes 262176 | tf_op jit(solution)/shard_map/ppermute | solution.py:105
  16.7 2.3 %collective-permute-start.5 = (f32[3,128,512]{2,1,0:T(8,128)}, f32[3,128,512]{2,1,0:T(8,128)}, u32[]{:S(2)}, u32[]{:S(2)}) collective-permute-start(f32[3,128,512]{2,1,0:T(8,128)} %get-tuple-element.60), channel_id=1, source_target_pairs={{1,2},{3,4},{5,6},{7,8},{9,10},{11,12},{13,14},{2,1},{4,3},{6,5},{... | collective-permute-start | bytes 2359304 | tf_op jit(solution)/shard_map/ppermute | solution.py:105
  22.8 6.0 %forward.1 = (f32[8,128,512]{2,1,0:T(8,128)}, f32[4,128,512]{2,1,0:T(8,128)S(1)}, f32[2,128,512]{2,1,0:T(8,128)S(1)}, f32[3,128,512]{2,1,0:T(8,128)S(1)}, f32[3,128,512]{2,1,0:T(8,128)S(1)}) custom-call(s32[4]{0:T(128)S(1)} %pad_add_fusion.refs_0_.facts_ref, f32[4,64,512]{2,1,0:T(8,128)S(1)} %copy-done.1, f32[4,64,512]{2,1,0:T(8,128)S(1)} %copy-done.11, ...), custom_call_target="tpu_custom_call" | custom-call | flops 1024 | bytes 1024 | tf_op jit(solution)/shard_map/forward/pallas_call | solution.py:66
  31.7 22.5 %collective-permute-done.4.halo0 = f32[3,128,512]{2,1,0:T(8,128)} collective-permute-done((f32[3,128,512]{2,1,0:T(8,128)}, f32[3,128,512]{2,1,0:T(8,128)}, u32[]{:S(2)}, u32[]{:S(2)}) %collective-permute-start.4) | collective-permute-done | bytes 786464 | tf_op jit(solution)/shard_map/ppermute | solution.py:105
  54.2 5.6 %middle.1 = (f32[3,128,512]{2,1,0:T(8,128)}, f32[3,128,512]{2,1,0:T(8,128)S(1)}, f32[128,512]{1,0:T(8,128)}, f32[128,512]{1,0:T(8,128)}, f32[2,128,512]{2,1,0:T(8,128)S(1)}, /*index=5*/f32[2,3,128,512]{3,2,1,0:T(8,128)}) custom-call(s32[4]{0:T(128)S(1)} %pad_add_fusion.refs_0_.facts_ref, f32[8,128,512]{2,1,0:T(8,128)} %get-tuple-element.33.tmpl, ...), custom_call_target="tpu_custom_call" | custom-call | flops 1024 | bytes 1024 | tf_op jit(solution)/shard_map/middle/pallas_call | solution.py:66
  61.6 2.9 %collective-permute-start.7 = (f32[128,512]{1,0:T(8,128)}, f32[128,512]{1,0:T(8,128)}, u32[]{:S(2)}, u32[]{:S(2)}) collective-permute-start(f32[128,512]{1,0:T(8,128)} %get-tuple-element.41), channel_id=1, source_target_pairs={{1,2},{3,4},{5,6},{7,8},{9,10},{11,12},{13,14},{2,1},{4,3},{6,5},{... | collective-permute-start | bytes 786440 | tf_op jit(solution)/shard_map/ppermute | solution.py:105
  67.1 6.5 %back.1 = (f32[4,128,512]{2,1,0:T(8,128)S(1)}, f32[128,512]{1,0:T(8,128)S(1)}, f32[128,512]{1,0:T(8,128)S(1)}, f32[3,128,512]{2,1,0:T(8,128)}, f32[3,128,512]{2,1,0:T(8,128)}) custom-call(s32[4]{0:T(128)S(1)} %pad_add_fusion.refs_0_.facts_ref, f32[8,128,512]{2,1,0:T(8,128)} %get-tuple-element.33.tmpl, f32[2,128,512]{2,1,0:T(8,128)S(1)} %copy-done.13, ...), custom_call_target="tpu_custom_call" | custom-call | flops 1024 | bytes 1024 | tf_op jit(solution)/shard_map/back/pallas_call | solution.py:66
  73.5 8.7 %collective-permute-done.6 = f32[128,512]{1,0:T(8,128)} collective-permute-done((f32[128,512]{1,0:T(8,128)}, f32[128,512]{1,0:T(8,128)}, u32[]{:S(2)}, u32[]{:S(2)}) %collective-permute-start.6) | collective-permute-done | bytes 262176 | tf_op jit(solution)/shard_map/ppermute | solution.py:105
  84.4 2.9 %collective-permute-start.12 = (f32[128,512]{1,0:T(8,128)S(1)}, f32[128,512]{1,0:T(8,128)S(1)}, u32[]{:S(2)}, u32[]{:S(2)}) collective-permute-start(f32[128,512]{1,0:T(8,128)S(1)} %multiply_subtract_fusion.edge1), channel_id=1, source_target_pairs={{1,2},{3,4},{5,6},{7,8},{9,10},{11,12},{13,14},{2,1},{4,3},{6,5},{... | collective-permute-start | bytes 786440 | tf_op jit(solution)/shard_map/ppermute | solution.py:105
  87.3 6.8 %collective-permute-start.15 = (f32[3,128,512]{2,1,0:T(8,128)}, f32[3,128,512]{2,1,0:T(8,128)}, u32[]{:S(2)}, u32[]{:S(2)}) collective-permute-start(f32[3,128,512]{2,1,0:T(8,128)} %copy-done.6), channel_id=1, source_target_pairs={{1,2},{3,4},{5,6},{7,8},{9,10},{11,12},{13,14},{2,1},{4,3},{6,5},{... | collective-permute-start | bytes 2359304 | tf_op jit(solution)/shard_map/ppermute | solution.py:105
  94.2 27.4 %collective-permute-done.13.near0 = f32[3,128,512]{2,1,0:T(8,128)} collective-permute-done((f32[3,128,512]{2,1,0:T(8,128)}, f32[3,128,512]{2,1,0:T(8,128)}, u32[]{:S(2)}, u32[]{:S(2)}) %collective-permute-start.13) | collective-permute-done | bytes 786464 | tf_op jit(solution)/shard_map/ppermute | solution.py:105
  121.6 1.9 collective-permute-start.14
  123.5 36.9 %collective-permute-done.11.beyond0 = f32[128,512]{1,0:T(8,128)} collective-permute-done((f32[128,512]{1,0:T(8,128)S(1)}, f32[128,512]{1,0:T(8,128)}, u32[]{:S(2)}, u32[]{:S(2)}) %collective-permute-start.11) | collective-permute-done | bytes 262176 | tf_op jit(solution)/shard_map/ppermute | solution.py:105
  160.5 5.6 %last.1 = (f32[4,128,512]{2,1,0:T(8,128)S(1)}, f32[4,3,128,512]{3,2,1,0:T(8,128)}) custom-call(s32[4]{0:T(128)S(1)} %pad_add_fusion.refs_0_.facts_ref, f32[8,128,512]{2,1,0:T(8,128)} %get-tuple-element.33.tmpl, f32[4,128,512]{2,1,0:T(8,128)S(1)} %get-tuple-element.49.part, f32[128,512]{1,0:T(8,128)S(1)} %multiply_add_fusion.edge0, ...), custom_call_target="tpu_custom_call" | custom-call | flops 1000001024 | bytes 1024 | tf_op jit(solution)/shard_map/last/pallas_call | solution.py:66
  167.1 2.1 %collective-permute-start.10 = (f32[3,128,512]{2,1,0:T(8,128)}, f32[3,128,512]{2,1,0:T(8,128)S(1)}, u32[]{:S(2)}, u32[]{:S(2)}) collective-permute-start(f32[3,128,512]{2,1,0:T(8,128)} %get-tuple-element.47.in1), channel_id=1, source_target_pairs={{1,2},{3,4},{5,6},{7,8},{9,10},{11,12},{13,14},{2,1},{4,3},{6,5},{... | collective-permute-start | bytes 2359304 | tf_op jit(solution)/shard_map/ppermute | solution.py:105
  169.3 2.0 dynamic-slice_add_fusion
  171.2 1.3 copy-done.5
  174.8 8.8 %smooth_1.1._ = f32[2,3,4,128,512]{4,3,2,1,0:T(8,128)} custom-call(s32[4]{0:T(128)S(1)} %pad_add_fusion.refs_0_.facts_ref, f32[3,128,512]{2,1,0:T(8,128)S(1)} %copy-done.5, f32[3,128,512]{2,1,0:T(8,128)S(1)} %copy-done.7, f32[3,128,512]{2,1,0:T(8,128)} %get-tuple-element.53.out0, f32[3,128,512]{2,1,0:T(8,128)S(1)} %copy-done.9, ...), custom_call_target="tpu_custom_call" | custom-call | flops 1500001024 | bytes 1024 | tf_op jit(solution)/shard_map/smooth_1/pallas_call | solution.py:66
  183.6 8.3 %smooth_0.1.grad = f32[2,3,4,128,512]{4,3,2,1,0:T(8,128)} custom-call(s32[4]{0:T(128)S(1)} %pad_add_fusion.refs_0_.facts_ref, f32[3,128,512]{2,1,0:T(8,128)} %get-tuple-element.46.in0, f32[3,128,512]{2,1,0:T(8,128)} %get-tuple-element.47.in1, f32[4,3,128,512]{3,2,1,0:T(8,128)S(1)} %copy-done, ...), custom_call_target="tpu_custom_call", output_to_operand_aliasing={{}: (4, {})} | custom-call | flops 1500001024 | bytes 1024 | tf_op jit(solution)/shard_map/smooth_0/pallas_call | solution.py:66
  191.9 2.9 %add_far.2.grad = f32[2,3,4,128,512]{4,3,2,1,0:T(8,128)} custom-call(s32[4]{0:T(128)S(1)} %pad_add_fusion.refs_0_.facts_ref, f32[3,128,512]{2,1,0:T(8,128)} %collective-permute-done.9.src, f32[2,3,4,128,512]{4,3,2,1,0:T(8,128)} %smooth_0.1.grad), custom_call_target="tpu_custom_call", output_to_operand_aliasing={{}: (2, {})} | custom-call | flops 1024 | bytes 1024 | tf_op jit(solution)/shard_map/add_far/pallas_call | solution.py:66
  194.8 2.7 %add_far.3 = f32[2,3,4,128,512]{4,3,2,1,0:T(8,128)} custom-call(s32[4]{0:T(128)S(1)} %pad_add_fusion.refs_0_.facts_ref, f32[3,128,512]{2,1,0:T(8,128)S(1)} %collective-permute-done.10.src, f32[2,3,4,128,512]{4,3,2,1,0:T(8,128)} %add_far.2.grad), custom_call_target="tpu_custom_call", output_to_operand_aliasing={{}: (2, {})} | custom-call | flops 1024 | bytes 1024 | tf_op jit(solution)/shard_map/add_far/pallas_call | solution.py:66
  (64 shorter events, 18.9 us)
Async XLA Ops:
  0.6 20.1 %copy-start.1 = (f32[4,64,512]{2,1,0:T(8,128)S(1)}, f32[4,64,512]{2,1,0:T(8,128)}, u32[]{:S(2)}) copy-start(f32[4,64,512]{2,1,0:T(8,128)} %refs_1_.1) | copy-start | bytes 1572868
  1.8 13.7 %collective-permute-start.1 = (f32[2,64,512]{2,1,0:T(8,128)S(1)}, f32[2,64,512]{2,1,0:T(8,128)S(1)}, u32[]{:S(2)}, u32[]{:S(2)}) collective-permute-start(f32[2,64,512]{2,1,0:T(8,128)S(1)} %get-tuple-element.63), channel_id=1, source_target_pairs={{0,1},{2,3},{4,5},{6,7},{8,9},{10,11},{12,13},{14,15},{1,0},{3,2},... | collective-permute-start | bytes 786440 | tf_op jit(solution)/shard_map/ppermute | solution.py:105
  1.9 14.6 %collective-permute-start.2 = (f32[2,64,512]{2,1,0:T(8,128)S(1)}, f32[2,64,512]{2,1,0:T(8,128)S(1)}, u32[]{:S(2)}, u32[]{:S(2)}) collective-permute-start(f32[2,64,512]{2,1,0:T(8,128)S(1)} %get-tuple-element.62), channel_id=1, source_target_pairs={{1,2},{3,4},{5,6},{7,8},{9,10},{11,12},{13,14},{2,1},{4,3},{6,5},{... | collective-permute-start | bytes 786440 | tf_op jit(solution)/shard_map/ppermute | solution.py:105
  6.7 12.4 %collective-permute-start = (f32[4,64,512]{2,1,0:T(8,128)}, f32[4,64,512]{2,1,0:T(8,128)S(1)}, u32[]{:S(2)}, u32[]{:S(2)}) collective-permute-start(f32[4,64,512]{2,1,0:T(8,128)} %refs_1_.1), channel_id=1, source_target_pairs={{0,16},{16,0},{1,17},{17,1},{2,18},{18,2},{3,19},{19,3},{4,20},{20... | collective-permute-start | bytes 1572872 | tf_op jit(solution)/shard_map/ppermute | solution.py:108
  16.5 3.4 %collective-permute-start.3 = (f32[4,64,512]{2,1,0:T(8,128)S(1)}, f32[4,64,512]{2,1,0:T(8,128)S(1)}, u32[]{:S(2)}, u32[]{:S(2)}) collective-permute-start(f32[4,64,512]{2,1,0:T(8,128)S(1)} %constant_dynamic-update-slice_fusion.refs_3_), channel_id=1, source_target_pairs={{0,16},{16,0},{1,17},{17,1},{2,18},{18,2},{3,19},{19,3},{4,20},{20... | collective-permute-start | bytes 1572872 | tf_op jit(solution)/shard_map/ppermute | solution.py:108
  16.6 37.6 %collective-permute-start.4 = (f32[3,128,512]{2,1,0:T(8,128)}, f32[3,128,512]{2,1,0:T(8,128)}, u32[]{:S(2)}, u32[]{:S(2)}) collective-permute-start(f32[3,128,512]{2,1,0:T(8,128)} %get-tuple-element.61), channel_id=1, source_target_pairs={{0,1},{2,3},{4,5},{6,7},{8,9},{10,11},{12,13},{14,15},{1,0},{3,2},... | collective-permute-start | bytes 2359304 | tf_op jit(solution)/shard_map/ppermute | solution.py:105
  16.7 37.5 %collective-permute-start.5 = (f32[3,128,512]{2,1,0:T(8,128)}, f32[3,128,512]{2,1,0:T(8,128)}, u32[]{:S(2)}, u32[]{:S(2)}) collective-permute-start(f32[3,128,512]{2,1,0:T(8,128)} %get-tuple-element.60), channel_id=1, source_target_pairs={{1,2},{3,4},{5,6},{7,8},{9,10},{11,12},{13,14},{2,1},{4,3},{6,5},{... | collective-permute-start | bytes 2359304 | tf_op jit(solution)/shard_map/ppermute | solution.py:105
  30.5 43.0 %copy-start.4 = (f32[3,128,512]{2,1,0:T(8,128)}, f32[3,128,512]{2,1,0:T(8,128)S(1)}, u32[]{:S(2)}) copy-start(f32[3,128,512]{2,1,0:T(8,128)S(1)} %get-tuple-element.42.in0) | copy-start | bytes 2359300
  30.5 51.8 %collective-permute-start.8 = (f32[3,128,512]{2,1,0:T(8,128)S(1)}, f32[3,128,512]{2,1,0:T(8,128)}, u32[]{:S(2)}, u32[]{:S(2)}) collective-permute-start(f32[3,128,512]{2,1,0:T(8,128)S(1)} %get-tuple-element.42.in0), channel_id=1, source_target_pairs={{0,1},{2,3},{4,5},{6,7},{8,9},{10,11},{12,13},{14,15},{1,0},{3,2},... | collective-permute-start | bytes 2359304 | tf_op jit(solution)/shard_map/ppermute | solution.py:105
  61.6 20.7 %collective-permute-start.6 = (f32[128,512]{1,0:T(8,128)}, f32[128,512]{1,0:T(8,128)}, u32[]{:S(2)}, u32[]{:S(2)}) collective-permute-start(f32[128,512]{1,0:T(8,128)} %get-tuple-element.40), channel_id=1, source_target_pairs={{0,1},{2,3},{4,5},{6,7},{8,9},{10,11},{12,13},{14,15},{1,0},{3,2},... | collective-permute-start | bytes 786440 | tf_op jit(solution)/shard_map/ppermute | solution.py:105
  61.6 20.7 %collective-permute-start.7 = (f32[128,512]{1,0:T(8,128)}, f32[128,512]{1,0:T(8,128)}, u32[]{:S(2)}, u32[]{:S(2)}) collective-permute-start(f32[128,512]{1,0:T(8,128)} %get-tuple-element.41), channel_id=1, source_target_pairs={{1,2},{3,4},{5,6},{7,8},{9,10},{11,12},{13,14},{2,1},{4,3},{6,5},{... | collective-permute-start | bytes 786440 | tf_op jit(solution)/shard_map/ppermute | solution.py:105
  64.5 57.1 %collective-permute-start.13 = (f32[3,128,512]{2,1,0:T(8,128)}, f32[3,128,512]{2,1,0:T(8,128)}, u32[]{:S(2)}, u32[]{:S(2)}) collective-permute-start(f32[3,128,512]{2,1,0:T(8,128)} %get-tuple-element.53.out0), channel_id=1, source_target_pairs={{0,1},{2,3},{4,5},{6,7},{8,9},{10,11},{12,13},{14,15},{1,0},{3,2},... | collective-permute-start | bytes 2359304 | tf_op jit(solution)/shard_map/ppermute | solution.py:105
  67.1 93.4 %copy-start.2 = (f32[2,3,128,512]{3,2,1,0:T(8,128)S(1)}, f32[2,3,128,512]{3,2,1,0:T(8,128)}, u32[]{:S(2)}) copy-start(f32[2,3,128,512]{3,2,1,0:T(8,128)} %get-tuple-element.50.v0_far) | copy-start | bytes 4718596
  84.3 82.8 %collective-permute-start.9 = (f32[3,128,512]{2,1,0:T(8,128)}, f32[3,128,512]{2,1,0:T(8,128)}, u32[]{:S(2)}, u32[]{:S(2)}) collective-permute-start(f32[3,128,512]{2,1,0:T(8,128)} %get-tuple-element.46.in0), channel_id=1, source_target_pairs={{0,1},{2,3},{4,5},{6,7},{8,9},{10,11},{12,13},{14,15},{1,0},{3,2},... | collective-permute-start | bytes 2359304 | tf_op jit(solution)/shard_map/ppermute | solution.py:105
  84.4 39.1 %collective-permute-start.12 = (f32[128,512]{1,0:T(8,128)S(1)}, f32[128,512]{1,0:T(8,128)S(1)}, u32[]{:S(2)}, u32[]{:S(2)}) collective-permute-start(f32[128,512]{1,0:T(8,128)S(1)} %multiply_subtract_fusion.edge1), channel_id=1, source_target_pairs={{1,2},{3,4},{5,6},{7,8},{9,10},{11,12},{13,14},{2,1},{4,3},{6,5},{... | collective-permute-start | bytes 786440 | tf_op jit(solution)/shard_map/ppermute | solution.py:105
  87.3 73.2 %collective-permute-start.11 = (f32[128,512]{1,0:T(8,128)S(1)}, f32[128,512]{1,0:T(8,128)}, u32[]{:S(2)}, u32[]{:S(2)}) collective-permute-start(f32[128,512]{1,0:T(8,128)S(1)} %multiply_add_fusion.edge0), channel_id=1, source_target_pairs={{0,1},{2,3},{4,5},{6,7},{8,9},{10,11},{12,13},{14,15},{1,0},{3,2},... | collective-permute-start | bytes 786440 | tf_op jit(solution)/shard_map/ppermute | solution.py:105
  87.3 83.9 %collective-permute-start.15 = (f32[3,128,512]{2,1,0:T(8,128)}, f32[3,128,512]{2,1,0:T(8,128)}, u32[]{:S(2)}, u32[]{:S(2)}) collective-permute-start(f32[3,128,512]{2,1,0:T(8,128)} %copy-done.6), channel_id=1, source_target_pairs={{1,2},{3,4},{5,6},{7,8},{9,10},{11,12},{13,14},{2,1},{4,3},{6,5},{... | collective-permute-start | bytes 2359304 | tf_op jit(solution)/shard_map/ppermute | solution.py:105
  121.6 49.6 %collective-permute-start.14 = (f32[3,128,512]{2,1,0:T(8,128)}, f32[3,128,512]{2,1,0:T(8,128)}, u32[]{:S(2)}, u32[]{:S(2)}) collective-permute-start(f32[3,128,512]{2,1,0:T(8,128)} %copy-done.8), channel_id=1, source_target_pairs={{1,2},{3,4},{5,6},{7,8},{9,10},{11,12},{13,14},{2,1},{4,3},{6,5},{... | collective-permute-start | bytes 2359304 | tf_op jit(solution)/shard_map/ppermute | solution.py:105
  167.0 2.2 %collective-permute-start.16 = (f32[4,64,512]{2,1,0:T(8,128)S(1)}, f32[4,64,512]{2,1,0:T(8,128)S(1)}, u32[]{:S(2)}, u32[]{:S(2)}) collective-permute-start(f32[4,64,512]{2,1,0:T(8,128)S(1)} %constant_dynamic-slice_fusion), channel_id=1, source_target_pairs={{0,16},{16,0},{1,17},{17,1},{2,18},{18,2},{3,19},{19,3},{4,20},{20... | collective-permute-start | bytes 1572872 | tf_op jit(solution)/shard_map/ppermute | solution.py:108
  167.1 27.6 %collective-permute-start.10 = (f32[3,128,512]{2,1,0:T(8,128)}, f32[3,128,512]{2,1,0:T(8,128)S(1)}, u32[]{:S(2)}, u32[]{:S(2)}) collective-permute-start(f32[3,128,512]{2,1,0:T(8,128)} %get-tuple-element.47.in1), channel_id=1, source_target_pairs={{1,2},{3,4},{5,6},{7,8},{9,10},{11,12},{13,14},{2,1},{4,3},{6,5},{... | collective-permute-start | bytes 2359304 | tf_op jit(solution)/shard_map/ppermute | solution.py:105
  171.2 12.4 %copy-start = (f32[4,3,128,512]{3,2,1,0:T(8,128)S(1)}, f32[4,3,128,512]{3,2,1,0:T(8,128)}, u32[]{:S(2)}) copy-start(f32[4,3,128,512]{3,2,1,0:T(8,128)} %get-tuple-element.51.rest) | copy-start | bytes 9437188
  171.2 1.3 copy-start.5
  172.5 1.1 copy-start.7
  173.6 1.1 copy-start.9
  (11 other events, 10.2 us)

commit v4 on v3

--- a/solution.py
+++ b/solution.py
@@ -259,12 +259,11 @@
         lam1_edge = [part_0 + toward * flux_far[0], part_1 - toward * flux_far[1]]
         lam1_far = [swap(lam1_edge[i], i) for i in SIDES]
 
-        held = after(inner0[0], *lam1_edge)[0]
-        far0 = [swap(held, 0), None]
-        far1[1] = swap(after(inner1[1], *lam1_edge)[0], 1)
-        held, near1[0] = after(outer1[1], near1[0])
-        near1[1] = swap(held, 1)
-        held, far0[0] = after(inner0[1], far0[0])
+        far0 = [swap(after(inner0[0], *lam1_edge)[0], 0), None]
+        held1, held2, near1[0], *lam1_far = after(inner1[1], outer1[1], near1[0], *lam1_far)
+        far1[1] = swap(held1, 1)
+        near1[1] = swap(held2, 1)
+        held, far0[0] = after(inner0[1], far0[0], *lam1_far)[:2]
         far0[1] = swap(held, 1)
 
         def sweeps(facts_ref, s, v, out, u2):
@@ -301,27 +300,6 @@
         ]
         u2_scratch = pltpu.VMEM((Z + 2, Y, X), jnp.float32)
 
-        def smooth_1(facts_ref, in0, in1, out0, out1, near0, near1, far0, far1, v, out, u2, s):
-            for i, inner, outer, near, far in ((0, in0, out0, near0, far0), (1, in1, out1, near1, far1)):
-                up = up_at(facts_ref, i)
-                s[3 + up * (Z - 3)] = inner[0]
-                s[2 + up * (Z - 1)] = outer[0]
-                s[1 + up * (Z + 1)] = near[0]
-                s[up * (Z + 3)] = far[0]
-            sweeps(facts_ref, Planes(s, -2, Z + 1), v, out, u2)
-
-        gradient = call(
-            smooth_1,
-            struct(*flow.shape),
-            [SMEM] + [part] * 8 + [flow_part[1]],
-            flow_part[1],
-            [facts, *inner1, *outer1, *near1, *far1, flow],
-            "smooth_1",
-            weight=SMOOTH,
-            grid=(3,),
-            scratch=[u2_scratch, pltpu.VMEM((Z + 4, Y, X), jnp.float32)],
-        )
-
         def last(facts_ref, tmpl, part, edge0, edge1, beyond0, beyond1, v0_far, v0, lam0, src, lam):
             for z in range(1, Z - 1):
                 lam[z + 1] = part[z]
@@ -365,7 +343,7 @@
         for k in range(1, subj):
             template_grad = template_grad + turn(share(k), k)
 
-        def smooth_0(facts_ref, in0, in1, rest, _, v, out, u2, s):
+        def smooth_0(facts_ref, in0, in1, rest, v, out, u2, s):
             for i, inner in ((0, in0), (1, in1)):
                 s[2 + up_at(facts_ref, i) * (Z - 3)] = inner[0]
             for j, z in enumerate((-1, 0, Z - 1, Z)):
@@ -377,14 +355,35 @@
             struct(*flow.shape),
             [SMEM, part, part]
             + [pl.BlockSpec((4, 1, Y, X), lambda d: (0, d, 0, 0))]
-            + [pl.BlockSpec(memory_space=pl.ANY), flow_part[0]],
+            + [flow_part[0]],
             flow_part[0],
-            [facts, *inner0, rest0, gradient, flow],
+            [facts, *inner0, rest0, flow],
             "smooth_0",
             weight=SMOOTH,
             grid=(3,),
-            aliases={4: 0},
             scratch=[u2_scratch, pltpu.VMEM((Z + 2, Y, X), jnp.float32)],
+        )
+
+        def smooth_1(facts_ref, in0, in1, out0, out1, near0, near1, far0, far1, _, v, out, u2, s):
+            for i, inner, outer, near, far in ((0, in0, out0, near0, far0), (1, in1, out1, near1, far1)):
+                up = up_at(facts_ref, i)
+                s[3 + up * (Z - 3)] = inner[0]
+                s[2 + up * (Z - 1)] = outer[0]
+                s[1 + up * (Z + 1)] = near[0]
+                s[up * (Z + 3)] = far[0]
+            sweeps(facts_ref, Planes(s, -2, Z + 1), v, out, u2)
+
+        gradient = call(
+            smooth_1,
+            struct(*flow.shape),
+            [SMEM] + [part] * 8 + [pl.BlockSpec(memory_space=pl.ANY), flow_part[1]],
+            flow_part[1],
+            [facts, *inner1, *outer1, *near1, *far1, gradient, flow],
+            "smooth_1",
+            weight=SMOOTH,
+            grid=(3,),
+            aliases={9: 0},
+            scratch=[u2_scratch, pltpu.VMEM((Z + 4, Y, X), jnp.float32)],
         )
 
         def add_far(facts_ref, src, grad, out):

time: 200 us -> 191 us (0.955)
  waiting for transfers between devices: 98.6 us -> 94.7 us
    ppermute x14, waiting for transfers between devices: 98.6 us -> 94.7 us  [swap(): return lax.ppermute(x, 'slab', pairs[side])]
    unnamed x37 -> x39, local copies, waits for them, and re-layouts: 13.7 us -> 12 us
  transfers between devices with their start and end apart: 17 -> 17, of which waited for: 6 -> 11; matrix products, arithmetic and copies ran while one was open for 5% -> 5% of each run, Pallas kernels for 22% -> 23%
where the time goes in v4:
time: 191 us; the launch traced here: 189 us
  waiting for transfers between devices  94.7 us (50%)
  Pallas kernels  46.7 us (24%)
  starting transfers between devices  24.4 us (13%)
  local copies, waits for them, and re-layouts  19.8 us (10%)
  other arithmetic  2.97 us (2%)
    ppermute x14, waiting for transfers between devices, swap(): return lax.ppermute(x, 'slab', pairs[side])  94.7 us
    pallas_call x8, Pallas kernels, call(): pl.pallas_call(kernel, out_shape=out_shape, grid_spec=pltpu.PrefetchScala...  46.7 us
    ppermute x14, starting transfers between devices, swap(): return lax.ppermute(x, 'slab', pairs[side])  24.1 us
    unnamed x39, local copies, waits for them, and re-layouts  12 us
    slice x1, local copies, waits for them, and re-layouts, body(): flow[0]  3.87 us
  transfers between devices with their start and end apart: 17, of which 11 were waited for; matrix products, arithmetic and copies ran while one was open for 5% of the time, Pallas kernels for 23%

profile of v4, /device:TPU:2, one launch (start us, length us, event | category | flops | bytes accessed | tf_op | source)
XLA Modules:
  0.0 189.5 jit_solution(3940018915441639300)
XLA Ops:
  1.8 3.4 %collective-permute-start.2 = (f32[2,64,512]{2,1,0:T(8,128)S(1)}, f32[2,64,512]{2,1,0:T(8,128)S(1)}, u32[]{:S(2)}, u32[]{:S(2)}) collective-permute-start(f32[2,64,512]{2,1,0:T(8,128)S(1)} %get-tuple-element.66), channel_id=1, source_target_pairs={{1,2},{3,4},{5,6},{7,8},{9,10},{11,12},{13,14},{2,1},{4,3},{6,5},{... | collective-permute-start | bytes 786440 | tf_op jit(solution)/shard_map/ppermute | solution.py:105
  5.4 3.9 %slice.5 = f32[1,1,3,4,128,512]{5,4,3,2,1,0:T(8,128)} slice(f32[1,2,3,4,128,512]{5,4,3,2,1,0:T(8,128)} %param.5), slice={[0:1], [0:1], [0:3], [0:4], [0:128], [0:512]} | slice | bytes 6291456 | tf_op jit(solution)/shard_map/slice | solution.py:137
  9.2 2.7 %dynamic-slice_bitcast_fusion = (f32[3,128,512]{2,1,0:T(8,128)}, f32[3,128,512]{2,1,0:T(8,128)}) fusion(f32[1,1,3,4,128,512]{5,4,3,2,1,0:T(8,128)} %slice.5, s32[]{:T(128)S(6)} %select_n.29, s32[]{:T(128)S(6)} %select_n.28), kind=kLoop, calls=%fused_computation | loop fusion | bytes 3145736 | tf_op jit(solution)/shard_map/squeeze | solution.py:137
  13.8 4.9 %collective-permute-done.1 = f32[2,64,512]{2,1,0:T(8,128)S(1)} collective-permute-done((f32[2,64,512]{2,1,0:T(8,128)S(1)}, f32[2,64,512]{2,1,0:T(8,128)S(1)}, u32[]{:S(2)}, u32[]{:S(2)}) %collective-permute-start.1) | collective-permute-done | bytes 262176 | tf_op jit(solution)/shard_map/ppermute | solution.py:105
  24.6 6.1 %forward.1 = (f32[8,128,512]{2,1,0:T(8,128)}, f32[4,128,512]{2,1,0:T(8,128)S(1)}, f32[2,128,512]{2,1,0:T(8,128)S(1)}, f32[3,128,512]{2,1,0:T(8,128)S(1)}, f32[3,128,512]{2,1,0:T(8,128)S(1)}) custom-call(s32[4]{0:T(128)S(1)} %pad_add_fusion.refs_0_.facts_ref, f32[4,64,512]{2,1,0:T(8,128)S(1)} %copy-done.1, f32[4,64,512]{2,1,0:T(8,128)S(1)} %copy-done.12, ...), custom_call_target="tpu_custom_call" | custom-call | flops 1024 | bytes 1024 | tf_op jit(solution)/shard_map/forward/pallas_call | solution.py:66
  34.3 7.9 %collective-permute-done.5.halo1 = f32[3,128,512]{2,1,0:T(8,128)} collective-permute-done((f32[3,128,512]{2,1,0:T(8,128)}, f32[3,128,512]{2,1,0:T(8,128)}, u32[]{:S(2)}, u32[]{:S(2)}) %collective-permute-start.5) | collective-permute-done | bytes 786464 | tf_op jit(solution)/shard_map/ppermute | solution.py:105
  42.2 16.0 %collective-permute-done.4.halo0 = f32[3,128,512]{2,1,0:T(8,128)} collective-permute-done((f32[3,128,512]{2,1,0:T(8,128)}, f32[3,128,512]{2,1,0:T(8,128)}, u32[]{:S(2)}, u32[]{:S(2)}) %collective-permute-start.4) | collective-permute-done | bytes 786464 | tf_op jit(solution)/shard_map/ppermute | solution.py:105
  58.3 5.7 %middle.1 = (f32[3,128,512]{2,1,0:T(8,128)}, f32[3,128,512]{2,1,0:T(8,128)S(1)}, f32[128,512]{1,0:T(8,128)}, f32[128,512]{1,0:T(8,128)}, f32[2,128,512]{2,1,0:T(8,128)S(1)}, /*index=5*/f32[2,3,128,512]{3,2,1,0:T(8,128)}) custom-call(s32[4]{0:T(128)S(1)} %pad_add_fusion.refs_0_.facts_ref, f32[8,128,512]{2,1,0:T(8,128)} %get-tuple-element.35.tmpl, ...), custom_call_target="tpu_custom_call" | custom-call | flops 1024 | bytes 1024 | tf_op jit(solution)/shard_map/middle/pallas_call | solution.py:66
  65.6 4.7 %collective-permute-start.7 = (f32[128,512]{1,0:T(8,128)}, f32[128,512]{1,0:T(8,128)}, u32[]{:S(2)}, u32[]{:S(2)}) collective-permute-start(f32[128,512]{1,0:T(8,128)} %get-tuple-element.43), channel_id=1, source_target_pairs={{1,2},{3,4},{5,6},{7,8},{9,10},{11,12},{13,14},{2,1},{4,3},{6,5},{... | collective-permute-start | bytes 786440 | tf_op jit(solution)/shard_map/ppermute | solution.py:105
  72.5 6.5 %back.1 = (f32[4,128,512]{2,1,0:T(8,128)S(1)}, f32[128,512]{1,0:T(8,128)S(1)}, f32[128,512]{1,0:T(8,128)S(1)}, f32[3,128,512]{2,1,0:T(8,128)}, f32[3,128,512]{2,1,0:T(8,128)}) custom-call(s32[4]{0:T(128)S(1)} %pad_add_fusion.refs_0_.facts_ref, f32[8,128,512]{2,1,0:T(8,128)} %get-tuple-element.35.tmpl, f32[2,128,512]{2,1,0:T(8,128)S(1)} %copy-done.14, ...), custom_call_target="tpu_custom_call" | custom-call | flops 1024 | bytes 1024 | tf_op jit(solution)/shard_map/back/pallas_call | solution.py:66
  79.1 7.3 %collective-permute-done.6 = f32[128,512]{1,0:T(8,128)} collective-permute-done((f32[128,512]{1,0:T(8,128)}, f32[128,512]{1,0:T(8,128)}, u32[]{:S(2)}, u32[]{:S(2)}) %collective-permute-start.6) | collective-permute-done | bytes 262176 | tf_op jit(solution)/shard_map/ppermute | solution.py:105
  92.0 16.8 %collective-permute-done.10.near0 = f32[3,128,512]{2,1,0:T(8,128)} collective-permute-done((f32[3,128,512]{2,1,0:T(8,128)}, f32[3,128,512]{2,1,0:T(8,128)}, u32[]{:S(2)}, u32[]{:S(2)}) %collective-permute-start.10) | collective-permute-done | bytes 786464 | tf_op jit(solution)/shard_map/ppermute | solution.py:105
  108.8 17.6 %collective-permute-done.12.beyond1 = f32[128,512]{1,0:T(8,128)S(1)} collective-permute-done((f32[128,512]{1,0:T(8,128)S(1)}, f32[128,512]{1,0:T(8,128)S(1)}, u32[]{:S(2)}, u32[]{:S(2)}) %collective-permute-start.12) | collective-permute-done | bytes 262176 | tf_op jit(solution)/shard_map/ppermute | solution.py:105
  126.4 4.5 %collective-permute-done.11.beyond0 = f32[128,512]{1,0:T(8,128)} collective-permute-done((f32[128,512]{1,0:T(8,128)S(1)}, f32[128,512]{1,0:T(8,128)}, u32[]{:S(2)}, u32[]{:S(2)}) %collective-permute-start.11) | collective-permute-done | bytes 262176 | tf_op jit(solution)/shard_map/ppermute | solution.py:105
  130.9 2.1 %collective-permute-start.14 = (f32[3,128,512]{2,1,0:T(8,128)}, f32[3,128,512]{2,1,0:T(8,128)}, u32[]{:S(2)}, u32[]{:S(2)}) collective-permute-start(f32[3,128,512]{2,1,0:T(8,128)} %copy-done.9), channel_id=1, source_target_pairs={{1,2},{3,4},{5,6},{7,8},{9,10},{11,12},{13,14},{2,1},{4,3},{6,5},{... | collective-permute-start | bytes 2359304 | tf_op jit(solution)/shard_map/ppermute | solution.py:105
  133.0 4.6 %collective-permute-start.15 = (f32[3,128,512]{2,1,0:T(8,128)}, f32[3,128,512]{2,1,0:T(8,128)}, u32[]{:S(2)}, u32[]{:S(2)}) collective-permute-start(f32[3,128,512]{2,1,0:T(8,128)} %copy-done.7), channel_id=1, source_target_pairs={{1,2},{3,4},{5,6},{7,8},{9,10},{11,12},{13,14},{2,1},{4,3},{6,5},{... | collective-permute-start | bytes 2359304 | tf_op jit(solution)/shard_map/ppermute | solution.py:105
  137.7 5.6 %last.1 = (f32[4,128,512]{2,1,0:T(8,128)S(1)}, f32[4,3,128,512]{3,2,1,0:T(8,128)}) custom-call(s32[4]{0:T(128)S(1)} %pad_add_fusion.refs_0_.facts_ref, f32[8,128,512]{2,1,0:T(8,128)} %get-tuple-element.35.tmpl, f32[4,128,512]{2,1,0:T(8,128)S(1)} %get-tuple-element.60.part, f32[128,512]{1,0:T(8,128)S(1)} %multiply_add_fusion.edge0, ...), custom_call_target="tpu_custom_call" | custom-call | flops 1000001024 | bytes 1024 | tf_op jit(solution)/shard_map/last/pallas_call | solution.py:66
  144.4 2.3 %collective-permute-start.13 = (f32[3,128,512]{2,1,0:T(8,128)}, f32[3,128,512]{2,1,0:T(8,128)S(1)}, u32[]{:S(2)}, u32[]{:S(2)}) collective-permute-start(f32[3,128,512]{2,1,0:T(8,128)} %get-tuple-element.54.in1), channel_id=1, source_target_pairs={{1,2},{3,4},{5,6},{7,8},{9,10},{11,12},{13,14},{2,1},{4,3},{6,5},{... | collective-permute-start | bytes 2359304 | tf_op jit(solution)/shard_map/ppermute | solution.py:105
  148.6 8.4 %smooth_0.1._ = f32[2,3,4,128,512]{4,3,2,1,0:T(8,128)} custom-call(s32[4]{0:T(128)S(1)} %pad_add_fusion.refs_0_.facts_ref, f32[3,128,512]{2,1,0:T(8,128)} %get-tuple-element.48.in0, f32[3,128,512]{2,1,0:T(8,128)} %get-tuple-element.54.in1, f32[4,3,128,512]{3,2,1,0:T(8,128)S(1)} %copy-done, f32[2,3,4,128,512]{4,3,2,1,0:T(8,128)} %bitcast.17), custom_call_target="tpu_custom_call" | custom-call | flops 1500001024 | bytes 1024 | tf_op jit(solution)/shard_map/smooth_0/pallas_call | solution.py:66
  157.9 13.4 %collective-permute-done.15.far1 = f32[3,128,512]{2,1,0:T(8,128)} collective-permute-done((f32[3,128,512]{2,1,0:T(8,128)}, f32[3,128,512]{2,1,0:T(8,128)}, u32[]{:S(2)}, u32[]{:S(2)}) %collective-permute-start.15) | collective-permute-done | bytes 786464 | tf_op jit(solution)/shard_map/ppermute | solution.py:105
  171.3 8.8 %smooth_1.1.grad = f32[2,3,4,128,512]{4,3,2,1,0:T(8,128)} custom-call(s32[4]{0:T(128)S(1)} %pad_add_fusion.refs_0_.facts_ref, f32[3,128,512]{2,1,0:T(8,128)S(1)} %copy-done.6, f32[3,128,512]{2,1,0:T(8,128)S(1)} %copy-done.8, f32[3,128,512]{2,1,0:T(8,128)} %get-tuple-element.51.out0, f32[3,128,512]{2,1,0:T(8,128)S(1)} %copy-done.10, ...), custom_call_target="tpu_custom_call", output_to_operand_aliasing={{}: (9, {})} | custom-call | flops 1500001024 | bytes 1024 | tf_op jit(solution)/shard_map/smooth_1/pallas_call | solution.py:66
  180.1 2.9 %add_far.2.grad = f32[2,3,4,128,512]{4,3,2,1,0:T(8,128)} custom-call(s32[4]{0:T(128)S(1)} %pad_add_fusion.refs_0_.facts_ref, f32[3,128,512]{2,1,0:T(8,128)} %collective-permute-done.9.src, f32[2,3,4,128,512]{4,3,2,1,0:T(8,128)} %smooth_1.1.grad), custom_call_target="tpu_custom_call", output_to_operand_aliasing={{}: (2, {})} | custom-call | flops 1024 | bytes 1024 | tf_op jit(solution)/shard_map/add_far/pallas_call | solution.py:66
  183.0 3.7 %collective-permute-done.13.src = f32[3,128,512]{2,1,0:T(8,128)S(1)} collective-permute-done((f32[3,128,512]{2,1,0:T(8,128)}, f32[3,128,512]{2,1,0:T(8,128)S(1)}, u32[]{:S(2)}, u32[]{:S(2)}) %collective-permute-start.13) | collective-permute-done | bytes 786464 | tf_op jit(solution)/shard_map/ppermute | solution.py:105
  186.8 2.7 %add_far.3 = f32[2,3,4,128,512]{4,3,2,1,0:T(8,128)} custom-call(s32[4]{0:T(128)S(1)} %pad_add_fusion.refs_0_.facts_ref, f32[3,128,512]{2,1,0:T(8,128)S(1)} %collective-permute-done.13.src, f32[2,3,4,128,512]{4,3,2,1,0:T(8,128)} %add_far.2.grad), custom_call_target="tpu_custom_call", output_to_operand_aliasing={{}: (2, {})} | custom-call | flops 1024 | bytes 1024 | tf_op jit(solution)/shard_map/add_far/pallas_call | solution.py:66
  (66 shorter events, 26.0 us)
Async XLA Ops:
  0.6 21.8 %copy-start.1 = (f32[4,64,512]{2,1,0:T(8,128)S(1)}, f32[4,64,512]{2,1,0:T(8,128)}, u32[]{:S(2)}) copy-start(f32[4,64,512]{2,1,0:T(8,128)} %refs_1_.1) | copy-start | bytes 1572868
  1.8 12.0 %collective-permute-start.2 = (f32[2,64,512]{2,1,0:T(8,128)S(1)}, f32[2,64,512]{2,1,0:T(8,128)S(1)}, u32[]{:S(2)}, u32[]{:S(2)}) collective-permute-start(f32[2,64,512]{2,1,0:T(8,128)S(1)} %get-tuple-element.66), channel_id=1, source_target_pairs={{1,2},{3,4},{5,6},{7,8},{9,10},{11,12},{13,14},{2,1},{4,3},{6,5},{... | collective-permute-start | bytes 786440 | tf_op jit(solution)/shard_map/ppermute | solution.py:105
  5.2 13.4 %collective-permute-start.1 = (f32[2,64,512]{2,1,0:T(8,128)S(1)}, f32[2,64,512]{2,1,0:T(8,128)S(1)}, u32[]{:S(2)}, u32[]{:S(2)}) collective-permute-start(f32[2,64,512]{2,1,0:T(8,128)S(1)} %get-tuple-element.67), channel_id=1, source_target_pairs={{0,1},{2,3},{4,5},{6,7},{8,9},{10,11},{12,13},{14,15},{1,0},{3,2},... | collective-permute-start | bytes 786440 | tf_op jit(solution)/shard_map/ppermute | solution.py:105
  5.3 15.6 %collective-permute-start = (f32[4,64,512]{2,1,0:T(8,128)}, f32[4,64,512]{2,1,0:T(8,128)S(1)}, u32[]{:S(2)}, u32[]{:S(2)}) collective-permute-start(f32[4,64,512]{2,1,0:T(8,128)} %refs_1_.1), channel_id=1, source_target_pairs={{0,16},{16,0},{1,17},{17,1},{2,18},{18,2},{3,19},{19,3},{4,20},{20... | collective-permute-start | bytes 1572872 | tf_op jit(solution)/shard_map/ppermute | solution.py:108
  18.7 3.0 %collective-permute-start.3 = (f32[4,64,512]{2,1,0:T(8,128)S(1)}, f32[4,64,512]{2,1,0:T(8,128)S(1)}, u32[]{:S(2)}, u32[]{:S(2)}) collective-permute-start(f32[4,64,512]{2,1,0:T(8,128)S(1)} %constant_dynamic-update-slice_fusion.refs_3_), channel_id=1, source_target_pairs={{0,16},{16,0},{1,17},{17,1},{2,18},{18,2},{3,19},{19,3},{4,20},{20... | collective-permute-start | bytes 1572872 | tf_op jit(solution)/shard_map/ppermute | solution.py:108
  18.8 23.4 %collective-permute-start.5 = (f32[3,128,512]{2,1,0:T(8,128)}, f32[3,128,512]{2,1,0:T(8,128)}, u32[]{:S(2)}, u32[]{:S(2)}) collective-permute-start(f32[3,128,512]{2,1,0:T(8,128)} %get-tuple-element.64), channel_id=1, source_target_pairs={{1,2},{3,4},{5,6},{7,8},{9,10},{11,12},{13,14},{2,1},{4,3},{6,5},{... | collective-permute-start | bytes 2359304 | tf_op jit(solution)/shard_map/ppermute | solution.py:105
  20.7 37.6 %collective-permute-start.4 = (f32[3,128,512]{2,1,0:T(8,128)}, f32[3,128,512]{2,1,0:T(8,128)}, u32[]{:S(2)}, u32[]{:S(2)}) collective-permute-start(f32[3,128,512]{2,1,0:T(8,128)} %get-tuple-element.65), channel_id=1, source_target_pairs={{0,1},{2,3},{4,5},{6,7},{8,9},{10,11},{12,13},{14,15},{1,0},{3,2},... | collective-permute-start | bytes 2359304 | tf_op jit(solution)/shard_map/ppermute | solution.py:105
  32.3 46.7 %copy-start.5 = (f32[3,128,512]{2,1,0:T(8,128)}, f32[3,128,512]{2,1,0:T(8,128)S(1)}, u32[]{:S(2)}) copy-start(f32[3,128,512]{2,1,0:T(8,128)S(1)} %get-tuple-element.44.in0) | copy-start | bytes 2359300
  32.3 54.9 %collective-permute-start.8 = (f32[3,128,512]{2,1,0:T(8,128)S(1)}, f32[3,128,512]{2,1,0:T(8,128)}, u32[]{:S(2)}, u32[]{:S(2)}) collective-permute-start(f32[3,128,512]{2,1,0:T(8,128)S(1)} %get-tuple-element.44.in0), channel_id=1, source_target_pairs={{0,1},{2,3},{4,5},{6,7},{8,9},{10,11},{12,13},{14,15},{1,0},{3,2},... | collective-permute-start | bytes 2359304 | tf_op jit(solution)/shard_map/ppermute | solution.py:105
  65.6 20.7 %collective-permute-start.6 = (f32[128,512]{1,0:T(8,128)}, f32[128,512]{1,0:T(8,128)}, u32[]{:S(2)}, u32[]{:S(2)}) collective-permute-start(f32[128,512]{1,0:T(8,128)} %get-tuple-element.42), channel_id=1, source_target_pairs={{0,1},{2,3},{4,5},{6,7},{8,9},{10,11},{12,13},{14,15},{1,0},{3,2},... | collective-permute-start | bytes 786440 | tf_op jit(solution)/shard_map/ppermute | solution.py:105
  65.6 21.5 %collective-permute-start.7 = (f32[128,512]{1,0:T(8,128)}, f32[128,512]{1,0:T(8,128)}, u32[]{:S(2)}, u32[]{:S(2)}) collective-permute-start(f32[128,512]{1,0:T(8,128)} %get-tuple-element.43), channel_id=1, source_target_pairs={{1,2},{3,4},{5,6},{7,8},{9,10},{11,12},{13,14},{2,1},{4,3},{6,5},{... | collective-permute-start | bytes 786440 | tf_op jit(solution)/shard_map/ppermute | solution.py:105
  70.4 38.5 %collective-permute-start.10 = (f32[3,128,512]{2,1,0:T(8,128)}, f32[3,128,512]{2,1,0:T(8,128)}, u32[]{:S(2)}, u32[]{:S(2)}) collective-permute-start(f32[3,128,512]{2,1,0:T(8,128)} %get-tuple-element.51.out0), channel_id=1, source_target_pairs={{0,1},{2,3},{4,5},{6,7},{8,9},{10,11},{12,13},{14,15},{1,0},{3,2},... | collective-permute-start | bytes 2359304 | tf_op jit(solution)/shard_map/ppermute | solution.py:105
  72.5 65.1 %copy-start.2 = (f32[2,3,128,512]{3,2,1,0:T(8,128)S(1)}, f32[2,3,128,512]{3,2,1,0:T(8,128)}, u32[]{:S(2)}) copy-start(f32[2,3,128,512]{3,2,1,0:T(8,128)} %get-tuple-element.61.v0_far) | copy-start | bytes 4718596
  89.2 55.2 %collective-permute-start.9 = (f32[3,128,512]{2,1,0:T(8,128)}, f32[3,128,512]{2,1,0:T(8,128)}, u32[]{:S(2)}, u32[]{:S(2)}) collective-permute-start(f32[3,128,512]{2,1,0:T(8,128)} %get-tuple-element.48.in0), channel_id=1, source_target_pairs={{0,1},{2,3},{4,5},{6,7},{8,9},{10,11},{12,13},{14,15},{1,0},{3,2},... | collective-permute-start | bytes 2359304 | tf_op jit(solution)/shard_map/ppermute | solution.py:105
  89.3 37.1 %collective-permute-start.12 = (f32[128,512]{1,0:T(8,128)S(1)}, f32[128,512]{1,0:T(8,128)S(1)}, u32[]{:S(2)}, u32[]{:S(2)}) collective-permute-start(f32[128,512]{1,0:T(8,128)S(1)} %multiply_subtract_fusion.edge1), channel_id=1, source_target_pairs={{1,2},{3,4},{5,6},{7,8},{9,10},{11,12},{13,14},{2,1},{4,3},{6,5},{... | collective-permute-start | bytes 786440 | tf_op jit(solution)/shard_map/ppermute | solution.py:105
  91.3 39.6 %collective-permute-start.11 = (f32[128,512]{1,0:T(8,128)S(1)}, f32[128,512]{1,0:T(8,128)}, u32[]{:S(2)}, u32[]{:S(2)}) collective-permute-start(f32[128,512]{1,0:T(8,128)S(1)} %multiply_add_fusion.edge0), channel_id=1, source_target_pairs={{0,1},{2,3},{4,5},{6,7},{8,9},{10,11},{12,13},{14,15},{1,0},{3,2},... | collective-permute-start | bytes 786440 | tf_op jit(solution)/shard_map/ppermute | solution.py:105
  130.9 27.0 %collective-permute-start.14 = (f32[3,128,512]{2,1,0:T(8,128)}, f32[3,128,512]{2,1,0:T(8,128)}, u32[]{:S(2)}, u32[]{:S(2)}) collective-permute-start(f32[3,128,512]{2,1,0:T(8,128)} %copy-done.9), channel_id=1, source_target_pairs={{1,2},{3,4},{5,6},{7,8},{9,10},{11,12},{13,14},{2,1},{4,3},{6,5},{... | collective-permute-start | bytes 2359304 | tf_op jit(solution)/shard_map/ppermute | solution.py:105
  133.0 38.3 %collective-permute-start.15 = (f32[3,128,512]{2,1,0:T(8,128)}, f32[3,128,512]{2,1,0:T(8,128)}, u32[]{:S(2)}, u32[]{:S(2)}) collective-permute-start(f32[3,128,512]{2,1,0:T(8,128)} %copy-done.7), channel_id=1, source_target_pairs={{1,2},{3,4},{5,6},{7,8},{9,10},{11,12},{13,14},{2,1},{4,3},{6,5},{... | collective-permute-start | bytes 2359304 | tf_op jit(solution)/shard_map/ppermute | solution.py:105
  144.3 12.8 %collective-permute-start.16 = (f32[4,64,512]{2,1,0:T(8,128)S(1)}, f32[4,64,512]{2,1,0:T(8,128)S(1)}, u32[]{:S(2)}, u32[]{:S(2)}) collective-permute-start(f32[4,64,512]{2,1,0:T(8,128)S(1)} %constant_dynamic-slice_fusion), channel_id=1, source_target_pairs={{0,16},{16,0},{1,17},{17,1},{2,18},{18,2},{3,19},{19,3},{4,20},{20... | collective-permute-start | bytes 1572872 | tf_op jit(solution)/shard_map/ppermute | solution.py:108
  144.4 42.4 %collective-permute-start.13 = (f32[3,128,512]{2,1,0:T(8,128)}, f32[3,128,512]{2,1,0:T(8,128)S(1)}, u32[]{:S(2)}, u32[]{:S(2)}) collective-permute-start(f32[3,128,512]{2,1,0:T(8,128)} %get-tuple-element.54.in1), channel_id=1, source_target_pairs={{1,2},{3,4},{5,6},{7,8},{9,10},{11,12},{13,14},{2,1},{4,3},{6,5},{... | collective-permute-start | bytes 2359304 | tf_op jit(solution)/shard_map/ppermute | solution.py:105
  148.6 8.4 %copy-start.4 = (f32[4,128,512]{2,1,0:T(8,128)S(1)}, f32[4,128,512]{2,1,0:T(8,128)}, u32[]{:S(2)}) copy-start(f32[4,128,512]{2,1,0:T(8,128)} %copy-done.3) | copy-start | bytes 3145732
  148.6 22.7 %copy-start.6 = (f32[3,128,512]{2,1,0:T(8,128)S(1)}, f32[3,128,512]{2,1,0:T(8,128)}, u32[]{:S(2)}) copy-start(f32[3,128,512]{2,1,0:T(8,128)} %copy-done.5) | copy-start | bytes 2359300
  148.6 22.7 %copy-start.8 = (f32[3,128,512]{2,1,0:T(8,128)S(1)}, f32[3,128,512]{2,1,0:T(8,128)}, u32[]{:S(2)}) copy-start(f32[3,128,512]{2,1,0:T(8,128)} %copy-done.7) | copy-start | bytes 2359300
  148.6 22.7 %copy-start.10 = (f32[3,128,512]{2,1,0:T(8,128)S(1)}, f32[3,128,512]{2,1,0:T(8,128)}, u32[]{:S(2)}) copy-start(f32[3,128,512]{2,1,0:T(8,128)} %copy-done.9) | copy-start | bytes 2359300
  (12 other events, 12.0 us)

commit v5 on v4

--- a/solution.py
+++ b/solution.py
@@ -8,7 +8,7 @@
 MATCH = 5.0
 SEVENTH = 1.0 / 7.0
 MIB = 1 << 20
-FORWARD, MIDDLE, BACK, LAST, SMOOTH = 0, 0, 0, 100, 150
+FORWARD, MIDDLE, BACK, SOURCES, LAST, SMOOTH = 0, 0, 1000, 0, 2000, 150
 
 
 def col_prev(f):
@@ -219,7 +219,7 @@
         )
         flux_far = [swap(flux_0, 0), swap(flux_1, 1)]
 
-        def back(facts_ref, tmpl, lam2_in, lam2_out, v0, v1, lam1, part0, part1, src0, src1, lam2):
+        def back(facts_ref, lam2_in, lam2_out, v1, lam1, part0, part1, lam2):
             for i in SIDES:
                 up = up_at(facts_ref, i)
                 lam2[1 + up * (Z - 3)] = lam2_in[i]
@@ -229,22 +229,15 @@
                 above = jnp.maximum(v1[0, 0, z + 1], 0.0) * lam2[z + 1] if z < Z - 1 else None
                 below = jnp.minimum(v1[0, 0, z - 1], 0.0) * lam2[z - 1] if z > 0 else None
                 lam1[z] = retreat(lam2[z], v, above, below, dt)
-            for i, part, src in ((0, part0, src0), (1, part1, src1)):
-                up = up_at(facts_ref, i)
-                part[...] = lam1[up * (Z - 1)]
-                z = 1 + up * (Z - 3)
-                v = [v0[0, d, z] for d in range(3)]
-                diffs = upwind(tmpl[z + 1], tmpl[z + 2], tmpl[z + 3], v)
-                lam = lam1[z]
-                for d in range(3):
-                    src[d] = (-MATCH * dt) * lam * diffs[d]
-
-        outs = [struct(Z, Y, X)] + [struct(Y, X)] * 2 + [struct(3, Y, X)] * 2
-        operands = [facts, tmpl, lam2_in, lam2_out, flow, flow]
-        lam1_part, part_0, part_1, *inner0 = call(
+            for i, part in ((0, part0), (1, part1)):
+                part[...] = lam1[up_at(facts_ref, i) * (Z - 1)]
+
+        outs = [struct(Z, Y, X)] + [struct(Y, X)] * 2
+        operands = [facts, lam2_in, lam2_out, flow]
+        lam1_part, part_0, part_1 = call(
             back,
             outs,
-            [SMEM] + [whole(x) for x in operands[1:4]] + [flow_spec[0], flow_spec[1]],
+            [SMEM] + [whole(x) for x in operands[1:3]] + [flow_spec[1]],
             [whole(x) for x in outs],
             operands,
             "back",
@@ -259,7 +252,31 @@
         lam1_edge = [part_0 + toward * flux_far[0], part_1 - toward * flux_far[1]]
         lam1_far = [swap(lam1_edge[i], i) for i in SIDES]
 
-        far0 = [swap(after(inner0[0], *lam1_edge)[0], 0), None]
+        def sources(facts_ref, tmpl, part, edge0, edge1, v0, lam1, src0, src1, out0, out1):
+            for i, edge, inner, outer in ((0, edge0, src0, out0), (1, edge1, src1, out1)):
+                up = up_at(facts_ref, i)
+                for z, src in ((1 + up * (Z - 3), inner), (up * (Z - 1), outer)):
+                    lam = part[z] if src is inner else edge[...]
+                    lam1[z] = lam
+                    v = [v0[0, d, z] for d in range(3)]
+                    diffs = upwind(tmpl[z + 1], tmpl[z + 2], tmpl[z + 3], v)
+                    for d in range(3):
+                        src[d] = (-MATCH * dt) * lam * diffs[d]
+
+        outs = [struct(Z, Y, X)] + [struct(3, Y, X)] * 4
+        operands = [facts, tmpl, lam1_part, *lam1_edge, flow]
+        lam1, *inner_outer = call(
+            sources,
+            outs,
+            [SMEM] + [whole(x) for x in operands[1:5]] + [flow_spec[0]],
+            [whole(x) for x in outs],
+            operands,
+            "sources",
+            weight=SOURCES,
+        )
+        inner0, outer0 = inner_outer[:2], inner_outer[2:]
+
+        far0 = [swap(inner0[0], 0), None]
         held1, held2, near1[0], *lam1_far = after(inner1[1], outer1[1], near1[0], *lam1_far)
         far1[1] = swap(held1, 1)
         near1[1] = swap(held2, 1)
@@ -300,18 +317,16 @@
         ]
         u2_scratch = pltpu.VMEM((Z + 2, Y, X), jnp.float32)
 
-        def last(facts_ref, tmpl, part, edge0, edge1, beyond0, beyond1, v0_far, v0, lam0, src, lam):
-            for z in range(1, Z - 1):
-                lam[z + 1] = part[z]
-            for i, edge, beyond in ((0, edge0, beyond0), (1, edge1, beyond1)):
-                up = up_at(facts_ref, i)
-                lam[1 + up * (Z - 1)] = edge[...]
-                lam[up * (Z + 1)] = beyond[...]
+        def last(facts_ref, tmpl, lam1, beyond0, beyond1, v0_far, v0, lam0, src, lam):
+            for z in range(Z):
+                lam[z + 1] = lam1[z]
+            for i, beyond in ((0, beyond0), (1, beyond1)):
+                lam[up_at(facts_ref, i) * (Z + 1)] = beyond[...]
 
             def flow_at(z, d):
                 return v0[0, d, z] if 0 <= z < Z else v0_far[0 if z < 0 else 1, d]
 
-            for j, z in enumerate((-1, 0, Z - 1, Z)):
+            for j, z in enumerate((-1, Z)):
                 v = [flow_at(z, d) for d in range(3)]
                 diffs = upwind(tmpl[z + 1], tmpl[z + 2], tmpl[z + 3], v)
                 for d in range(3):
@@ -322,12 +337,12 @@
                 v = [flow_at(z, d) for d in range(3)]
                 lam0[z] = retreat(lam[z + 1], v, above, below, dt)
 
-        outs = [struct(Z, Y, X), struct(4, 3, Y, X)]
-        operands = [facts, tmpl, lam1_part, *lam1_edge, *lam1_far, v0_far, flow]
-        lam0, rest0 = call(
+        outs = [struct(Z, Y, X), struct(2, 3, Y, X)]
+        operands = [facts, tmpl, lam1, *lam1_far, v0_far, flow]
+        lam0, near0 = call(
             last,
             outs,
-            [SMEM] + [whole(x) for x in operands[1:8]] + [flow_spec[0]],
+            [SMEM] + [whole(x) for x in operands[1:6]] + [flow_spec[0]],
             [whole(x) for x in outs],
             operands,
             "last",
@@ -343,21 +358,22 @@
         for k in range(1, subj):
             template_grad = template_grad + turn(share(k), k)
 
-        def smooth_0(facts_ref, in0, in1, rest, v, out, u2, s):
-            for i, inner in ((0, in0), (1, in1)):
-                s[2 + up_at(facts_ref, i) * (Z - 3)] = inner[0]
-            for j, z in enumerate((-1, 0, Z - 1, Z)):
-                s[z + 1] = rest[j, 0]
+        def smooth_0(facts_ref, in0, in1, out0, out1, near, v, out, u2, s):
+            for i, inner, outer in ((0, in0, out0), (1, in1, out1)):
+                up = up_at(facts_ref, i)
+                s[2 + up * (Z - 3)] = inner[0]
+                s[1 + up * (Z - 1)] = outer[0]
+            s[0] = near[0, 0]
+            s[Z + 1] = near[1, 0]
             sweeps(facts_ref, Planes(s, -1, Z), v, out, u2)
 
         gradient = call(
             smooth_0,
             struct(*flow.shape),
-            [SMEM, part, part]
-            + [pl.BlockSpec((4, 1, Y, X), lambda d: (0, d, 0, 0))]
-            + [flow_part[0]],
+            [SMEM] + [part] * 4
+            + [pl.BlockSpec((2, 1, Y, X), lambda d: (0, d, 0, 0)), flow_part[0]],
             flow_part[0],
-            [facts, *inner0, rest0, flow],
+            [facts, *inner0, *outer0, near0, flow],
             "smooth_0",
             weight=SMOOTH,
             grid=(3,),

time: 191 us -> 192 us (level)
    ppermute x14, waiting for transfers between devices: 94.7 us -> 92.1 us  [swap(): return lax.ppermute(x, 'slab', pairs[side])]
    unnamed x39 -> x41, local copies, waits for them, and re-layouts: 12 us -> 12.6 us
    pallas_call x8 -> x9, Pallas kernels: 46.7 us -> 46.4 us  [call(): pl.pallas_call(kernel, out_shape=out_shape, grid_spec=pltpu.PrefetchScala...]
  transfers between devices with their start and end apart: 17 -> 17, of which waited for: 11 -> 8; matrix products, arithmetic and copies ran while one was open for 5% -> 5% of each run, Pallas kernels for 23% -> 23%
where the time goes in v5:
time: 192 us; the launch traced here: 190 us
  waiting for transfers between devices  93.9 us (49%)
  Pallas kernels  46.4 us (24%)
  starting transfers between devices  25.8 us (13%)
  local copies, waits for them, and re-layouts  21.1 us (11%)
  other arithmetic  2.07 us (1%)
    ppermute x14, waiting for transfers between devices, swap(): return lax.ppermute(x, 'slab', pairs[side])  92.1 us
    pallas_call x9, Pallas kernels, call(): pl.pallas_call(kernel, out_shape=out_shape, grid_spec=pltpu.PrefetchScala...  46.4 us
    ppermute x14, starting transfers between devices, swap(): return lax.ppermute(x, 'slab', pairs[side])  25.7 us
    unnamed x41, local copies, waits for them, and re-layouts  12.6 us
    slice x1, local copies, waits for them, and re-layouts, body(): flow[0]  3.87 us
  transfers between devices with their start and end apart: 17, of which 8 were waited for; matrix products, arithmetic and copies ran while one was open for 5% of the time, Pallas kernels for 23%

profile of v5, /device:TPU:2, one launch (start us, length us, event | category | flops | bytes accessed | tf_op | source)
XLA Modules:
  0.0 190.3 jit_solution(3418165709729318925)
XLA Ops:
  1.8 3.4 %collective-permute-start.2 = (f32[2,64,512]{2,1,0:T(8,128)S(1)}, f32[2,64,512]{2,1,0:T(8,128)S(1)}, u32[]{:S(2)}, u32[]{:S(2)}) collective-permute-start(f32[2,64,512]{2,1,0:T(8,128)S(1)} %get-tuple-element.70), channel_id=1, source_target_pairs={{1,2},{3,4},{5,6},{7,8},{9,10},{11,12},{13,14},{2,1},{4,3},{6,5},{... | collective-permute-start | bytes 786440 | tf_op jit(solution)/shard_map/ppermute | solution.py:105
  5.3 3.9 %slice.5 = f32[1,1,3,4,128,512]{5,4,3,2,1,0:T(8,128)} slice(f32[1,2,3,4,128,512]{5,4,3,2,1,0:T(8,128)} %param.5), slice={[0:1], [0:1], [0:3], [0:4], [0:128], [0:512]} | slice | bytes 6291456 | tf_op jit(solution)/shard_map/slice | solution.py:137
  9.2 2.7 %dynamic-slice_bitcast_fusion = (f32[3,128,512]{2,1,0:T(8,128)}, f32[3,128,512]{2,1,0:T(8,128)}) fusion(f32[1,1,3,4,128,512]{5,4,3,2,1,0:T(8,128)} %slice.5, s32[]{:T(128)S(6)} %select_n.29, s32[]{:T(128)S(6)} %select_n.28), kind=kLoop, calls=%fused_computation | loop fusion | bytes 3145736 | tf_op jit(solution)/shard_map/squeeze | solution.py:137
  11.9 4.8 %collective-permute-start.5 = (f32[3,128,512]{2,1,0:T(8,128)}, f32[3,128,512]{2,1,0:T(8,128)S(1)}, u32[]{:S(2)}, u32[]{:S(2)}) collective-permute-start(f32[3,128,512]{2,1,0:T(8,128)} %get-tuple-element.68), channel_id=1, source_target_pairs={{1,2},{3,4},{5,6},{7,8},{9,10},{11,12},{13,14},{2,1},{4,3},{6,5},{... | collective-permute-start | bytes 2359304 | tf_op jit(solution)/shard_map/ppermute | solution.py:105
  16.9 18.9 %collective-permute-done.1 = f32[2,64,512]{2,1,0:T(8,128)S(1)} collective-permute-done((f32[2,64,512]{2,1,0:T(8,128)S(1)}, f32[2,64,512]{2,1,0:T(8,128)S(1)}, u32[]{:S(2)}, u32[]{:S(2)}) %collective-permute-start.1) | collective-permute-done | bytes 262176 | tf_op jit(solution)/shard_map/ppermute | solution.py:105
  39.7 5.8 %forward.1 = (f32[8,128,512]{2,1,0:T(8,128)}, f32[4,128,512]{2,1,0:T(8,128)S(1)}, f32[2,128,512]{2,1,0:T(8,128)S(1)}, f32[3,128,512]{2,1,0:T(8,128)S(1)}, f32[3,128,512]{2,1,0:T(8,128)}) custom-call(s32[4]{0:T(128)S(1)} %pad_add_fusion.refs_0_.facts_ref, f32[4,64,512]{2,1,0:T(8,128)S(1)} %copy-done, f32[4,64,512]{2,1,0:T(8,128)S(1)} %collective-permute-done.refs_2_, ...), custom_call_target="tpu_custom_call" | custom-call | flops 1024 | bytes 1024 | tf_op jit(solution)/shard_map/forward/pallas_call | solution.py:66
  46.4 6.3 %collective-permute-done.4.halo0 = f32[3,128,512]{2,1,0:T(8,128)} collective-permute-done((f32[3,128,512]{2,1,0:T(8,128)}, f32[3,128,512]{2,1,0:T(8,128)}, u32[]{:S(2)}, u32[]{:S(2)}) %collective-permute-start.4) | collective-permute-done | bytes 786464 | tf_op jit(solution)/shard_map/ppermute | solution.py:105
  53.9 5.3 %middle.1 = (f32[3,128,512]{2,1,0:T(8,128)S(1)}, f32[3,128,512]{2,1,0:T(8,128)}, f32[128,512]{1,0:T(8,128)S(1)}, f32[128,512]{1,0:T(8,128)S(1)}, f32[2,128,512]{2,1,0:T(8,128)S(1)}, /*index=5*/f32[2,3,128,512]{3,2,1,0:T(8,128)}) custom-call(s32[4]{0:T(128)S(1)} %pad_add_fusion.refs_0_.facts_ref, f32[8,128,512]{2,1,0:T(8,128)} %get-tuple-element.37.tmpl, ...), custom_call_target="tpu_custom_call" | custom-call | flops 1024 | bytes 1024 | tf_op jit(solution)/shard_map/middle/pallas_call | solution.py:66
  60.8 2.8 %collective-permute-start.7 = (f32[128,512]{1,0:T(8,128)S(1)}, f32[128,512]{1,0:T(8,128)S(1)}, u32[]{:S(2)}, u32[]{:S(2)}) collective-permute-start(f32[128,512]{1,0:T(8,128)S(1)} %get-tuple-element.44), channel_id=1, source_target_pairs={{1,2},{3,4},{5,6},{7,8},{9,10},{11,12},{13,14},{2,1},{4,3},{6,5},{... | collective-permute-start | bytes 786440 | tf_op jit(solution)/shard_map/ppermute | solution.py:105
  63.7 3.3 %back.1 = (f32[4,128,512]{2,1,0:T(8,128)S(1)}, f32[128,512]{1,0:T(8,128)S(1)}, f32[128,512]{1,0:T(8,128)S(1)}) custom-call(s32[4]{0:T(128)S(1)} %pad_add_fusion.refs_0_.facts_ref, f32[2,128,512]{2,1,0:T(8,128)S(1)} %get-tuple-element.38.lam2_in, f32[2,128,512]{2,1,0:T(8,128)S(1)} %get-tuple-element.40.lam2_out, f32[2,3,4,128,512]{4,3,2,1,0:T(8,128)} %bitcast.14), custom_call_target="tpu_custom_call" | custom-call | flops 10000001024 | bytes 1024 | tf_op jit(solution)/shard_map/back/pallas_call | solution.py:66
  67.0 13.8 %collective-permute-done.6 = f32[128,512]{1,0:T(8,128)S(1)} collective-permute-done((f32[128,512]{1,0:T(8,128)S(1)}, f32[128,512]{1,0:T(8,128)S(1)}, u32[]{:S(2)}, u32[]{:S(2)}) %collective-permute-start.6) | collective-permute-done | bytes 262176 | tf_op jit(solution)/shard_map/ppermute | solution.py:105
  82.2 4.0 %collective-permute-start.12 = (f32[128,512]{1,0:T(8,128)S(1)}, f32[128,512]{1,0:T(8,128)}, u32[]{:S(2)}, u32[]{:S(2)}) collective-permute-start(f32[128,512]{1,0:T(8,128)S(1)} %multiply_subtract_fusion.edge1), channel_id=1, source_target_pairs={{1,2},{3,4},{5,6},{7,8},{9,10},{11,12},{13,14},{2,1},{4,3},{6,5},{... | collective-permute-start | bytes 786440 | tf_op jit(solution)/shard_map/ppermute | solution.py:105
  86.3 4.4 %sources.1 = (f32[4,128,512]{2,1,0:T(8,128)S(1)}, f32[3,128,512]{2,1,0:T(8,128)S(1)}, f32[3,128,512]{2,1,0:T(8,128)}, f32[3,128,512]{2,1,0:T(8,128)S(1)}, f32[3,128,512]{2,1,0:T(8,128)S(1)}) custom-call(s32[4]{0:T(128)S(1)} %pad_add_fusion.refs_0_.facts_ref, f32[8,128,512]{2,1,0:T(8,128)} %get-tuple-element.37.tmpl, ...), custom_call_target="tpu_custom_call" | custom-call | flops 1024 | bytes 1024 | tf_op jit(solution)/shard_map/sources/pallas_call | solution.py:66
  92.5 10.9 %collective-permute-done.10.near0 = f32[3,128,512]{2,1,0:T(8,128)} collective-permute-done((f32[3,128,512]{2,1,0:T(8,128)S(1)}, f32[3,128,512]{2,1,0:T(8,128)}, u32[]{:S(2)}, u32[]{:S(2)}) %collective-permute-start.10) | collective-permute-done | bytes 786464 | tf_op jit(solution)/shard_map/ppermute | solution.py:105
  103.3 5.5 %collective-permute-done.11.beyond0 = f32[128,512]{1,0:T(8,128)S(1)} collective-permute-done((f32[128,512]{1,0:T(8,128)S(1)}, f32[128,512]{1,0:T(8,128)S(1)}, u32[]{:S(2)}, u32[]{:S(2)}) %collective-permute-start.11) | collective-permute-done | bytes 262176 | tf_op jit(solution)/shard_map/ppermute | solution.py:105
  109.6 3.8 %collective-permute-start.14 = (f32[3,128,512]{2,1,0:T(8,128)}, f32[3,128,512]{2,1,0:T(8,128)}, u32[]{:S(2)}, u32[]{:S(2)}) collective-permute-start(f32[3,128,512]{2,1,0:T(8,128)} %get-tuple-element.59.out1), channel_id=1, source_target_pairs={{1,2},{3,4},{5,6},{7,8},{9,10},{11,12},{13,14},{2,1},{4,3},{6,5},{... | collective-permute-start | bytes 2359304 | tf_op jit(solution)/shard_map/ppermute | solution.py:105
  113.4 3.0 %collective-permute-start.15 = (f32[3,128,512]{2,1,0:T(8,128)}, f32[3,128,512]{2,1,0:T(8,128)}, u32[]{:S(2)}, u32[]{:S(2)}) collective-permute-start(f32[3,128,512]{2,1,0:T(8,128)} %get-tuple-element.61.in1), channel_id=1, source_target_pairs={{1,2},{3,4},{5,6},{7,8},{9,10},{11,12},{13,14},{2,1},{4,3},{6,5},{... | collective-permute-start | bytes 2359304 | tf_op jit(solution)/shard_map/ppermute | solution.py:105
  117.3 4.7 %last.1 = (f32[4,128,512]{2,1,0:T(8,128)S(1)}, f32[2,3,128,512]{3,2,1,0:T(8,128)S(1)}) custom-call(s32[4]{0:T(128)S(1)} %pad_add_fusion.refs_0_.facts_ref, f32[8,128,512]{2,1,0:T(8,128)} %get-tuple-element.37.tmpl, f32[4,128,512]{2,1,0:T(8,128)S(1)} %get-tuple-element.64.lam1, f32[128,512]{1,0:T(8,128)S(1)} %copy-done.19, ...), custom_call_target="tpu_custom_call" | custom-call | flops 20000002048 | bytes 1024 | tf_op jit(solution)/shard_map/last/pallas_call | solution.py:66
  122.8 36.3 %collective-permute-done.9.src = f32[3,128,512]{2,1,0:T(8,128)S(1)} collective-permute-done((f32[3,128,512]{2,1,0:T(8,128)S(1)}, f32[3,128,512]{2,1,0:T(8,128)S(1)}, u32[]{:S(2)}, u32[]{:S(2)}) %collective-permute-start.9) | collective-permute-done | bytes 786464 | tf_op jit(solution)/shard_map/ppermute | solution.py:105
  160.0 2.1 %collective-permute-start.13 = (f32[3,128,512]{2,1,0:T(8,128)}, f32[3,128,512]{2,1,0:T(8,128)}, u32[]{:S(2)}, u32[]{:S(2)}) collective-permute-start(f32[3,128,512]{2,1,0:T(8,128)} %get-tuple-element.56.in1), channel_id=1, source_target_pairs={{1,2},{3,4},{5,6},{7,8},{9,10},{11,12},{13,14},{2,1},{4,3},{6,5},{... | collective-permute-start | bytes 2359304 | tf_op jit(solution)/shard_map/ppermute | solution.py:105
  165.5 8.4 %smooth_0.1._ = f32[2,3,4,128,512]{4,3,2,1,0:T(8,128)} custom-call(s32[4]{0:T(128)S(1)} %pad_add_fusion.refs_0_.facts_ref, f32[3,128,512]{2,1,0:T(8,128)S(1)} %copy-done.6, f32[3,128,512]{2,1,0:T(8,128)} %get-tuple-element.56.in1, f32[3,128,512]{2,1,0:T(8,128)S(1)} %copy-done.8, f32[3,128,512]{2,1,0:T(8,128)S(1)} %copy-done.10, ...), custom_call_target="tpu_custom_call" | custom-call | flops 1500001024 | bytes 1024 | tf_op jit(solution)/shard_map/smooth_0/pallas_call | solution.py:66
  175.9 8.9 %smooth_1.1.grad = f32[2,3,4,128,512]{4,3,2,1,0:T(8,128)} custom-call(s32[4]{0:T(128)S(1)} %pad_add_fusion.refs_0_.facts_ref, f32[3,128,512]{2,1,0:T(8,128)S(1)} %get-tuple-element.45.in0, f32[3,128,512]{2,1,0:T(8,128)} %get-tuple-element.61.in1, f32[3,128,512]{2,1,0:T(8,128)S(1)} %copy-done.4, ...), custom_call_target="tpu_custom_call", output_to_operand_aliasing={{}: (9, {})} | custom-call | flops 1500001024 | bytes 1024 | tf_op jit(solution)/shard_map/smooth_1/pallas_call | solution.py:66
  184.7 2.7 %add_far.2.grad = f32[2,3,4,128,512]{4,3,2,1,0:T(8,128)} custom-call(s32[4]{0:T(128)S(1)} %pad_add_fusion.refs_0_.facts_ref, f32[3,128,512]{2,1,0:T(8,128)S(1)} %copy-done.14, f32[2,3,4,128,512]{4,3,2,1,0:T(8,128)} %smooth_1.1.grad), custom_call_target="tpu_custom_call", output_to_operand_aliasing={{}: (2, {})} | custom-call | flops 1024 | bytes 1024 | tf_op jit(solution)/shard_map/add_far/pallas_call | solution.py:66
  187.4 2.9 %add_far.3 = f32[2,3,4,128,512]{4,3,2,1,0:T(8,128)} custom-call(s32[4]{0:T(128)S(1)} %pad_add_fusion.refs_0_.facts_ref, f32[3,128,512]{2,1,0:T(8,128)} %collective-permute-done.13.src, f32[2,3,4,128,512]{4,3,2,1,0:T(8,128)} %add_far.2.grad), custom_call_target="tpu_custom_call", output_to_operand_aliasing={{}: (2, {})} | custom-call | flops 1024 | bytes 1024 | tf_op jit(solution)/shard_map/add_far/pallas_call | solution.py:66
  (69 shorter events, 20.9 us)
Async XLA Ops:
  0.6 16.2 %copy-start = (f32[4,64,512]{2,1,0:T(8,128)S(1)}, f32[4,64,512]{2,1,0:T(8,128)}, u32[]{:S(2)}) copy-start(f32[4,64,512]{2,1,0:T(8,128)} %refs_1_.1) | copy-start | bytes 1572868
  1.8 15.1 %collective-permute-start.2 = (f32[2,64,512]{2,1,0:T(8,128)S(1)}, f32[2,64,512]{2,1,0:T(8,128)S(1)}, u32[]{:S(2)}, u32[]{:S(2)}) collective-permute-start(f32[2,64,512]{2,1,0:T(8,128)S(1)} %get-tuple-element.70), channel_id=1, source_target_pairs={{1,2},{3,4},{5,6},{7,8},{9,10},{11,12},{13,14},{2,1},{4,3},{6,5},{... | collective-permute-start | bytes 786440 | tf_op jit(solution)/shard_map/ppermute | solution.py:105
  5.2 30.6 %collective-permute-start.1 = (f32[2,64,512]{2,1,0:T(8,128)S(1)}, f32[2,64,512]{2,1,0:T(8,128)S(1)}, u32[]{:S(2)}, u32[]{:S(2)}) collective-permute-start(f32[2,64,512]{2,1,0:T(8,128)S(1)} %get-tuple-element.71), channel_id=1, source_target_pairs={{0,1},{2,3},{4,5},{6,7},{8,9},{10,11},{12,13},{14,15},{1,0},{3,2},... | collective-permute-start | bytes 786440 | tf_op jit(solution)/shard_map/ppermute | solution.py:105
  11.9 33.7 %collective-permute-start.5 = (f32[3,128,512]{2,1,0:T(8,128)}, f32[3,128,512]{2,1,0:T(8,128)S(1)}, u32[]{:S(2)}, u32[]{:S(2)}) collective-permute-start(f32[3,128,512]{2,1,0:T(8,128)} %get-tuple-element.68), channel_id=1, source_target_pairs={{1,2},{3,4},{5,6},{7,8},{9,10},{11,12},{13,14},{2,1},{4,3},{6,5},{... | collective-permute-start | bytes 2359304 | tf_op jit(solution)/shard_map/ppermute | solution.py:105
  16.7 36.0 %collective-permute-start.4 = (f32[3,128,512]{2,1,0:T(8,128)}, f32[3,128,512]{2,1,0:T(8,128)}, u32[]{:S(2)}, u32[]{:S(2)}) collective-permute-start(f32[3,128,512]{2,1,0:T(8,128)} %get-tuple-element.69), channel_id=1, source_target_pairs={{0,1},{2,3},{4,5},{6,7},{8,9},{10,11},{12,13},{14,15},{1,0},{3,2},... | collective-permute-start | bytes 2359304 | tf_op jit(solution)/shard_map/ppermute | solution.py:105
  16.8 19.2 %collective-permute-start = (f32[4,64,512]{2,1,0:T(8,128)S(1)}, f32[4,64,512]{2,1,0:T(8,128)S(1)}, u32[]{:S(2)}, u32[]{:S(2)}) collective-permute-start(f32[4,64,512]{2,1,0:T(8,128)S(1)} %copy-done), channel_id=1, source_target_pairs={{0,16},{16,0},{1,17},{17,1},{2,18},{18,2},{3,19},{19,3},{4,20},{20... | collective-permute-start | bytes 1572872 | tf_op jit(solution)/shard_map/ppermute | solution.py:108
  35.9 2.0 %collective-permute-start.3 = (f32[4,64,512]{2,1,0:T(8,128)S(1)}, f32[4,64,512]{2,1,0:T(8,128)S(1)}, u32[]{:S(2)}, u32[]{:S(2)}) collective-permute-start(f32[4,64,512]{2,1,0:T(8,128)S(1)} %constant_dynamic-update-slice_fusion.refs_3_), channel_id=1, source_target_pairs={{0,16},{16,0},{1,17},{17,1},{2,18},{18,2},{3,19},{19,3},{4,20},{20... | collective-permute-start | bytes 1572872 | tf_op jit(solution)/shard_map/ppermute | solution.py:108
  45.5 35.6 %collective-permute-start.8 = (f32[3,128,512]{2,1,0:T(8,128)S(1)}, f32[3,128,512]{2,1,0:T(8,128)S(1)}, u32[]{:S(2)}, u32[]{:S(2)}) collective-permute-start(f32[3,128,512]{2,1,0:T(8,128)S(1)} %get-tuple-element.45.in0), channel_id=1, source_target_pairs={{0,1},{2,3},{4,5},{6,7},{8,9},{10,11},{12,13},{14,15},{1,0},{3,2},... | collective-permute-start | bytes 2359304 | tf_op jit(solution)/shard_map/ppermute | solution.py:105
  59.3 7.7 %copy-start.3 = (f32[3,128,512]{2,1,0:T(8,128)}, f32[3,128,512]{2,1,0:T(8,128)S(1)}, u32[]{:S(2)}) copy-start(f32[3,128,512]{2,1,0:T(8,128)S(1)} %get-tuple-element.53.out0) | copy-start | bytes 2359300
  59.3 21.5 %collective-permute-start.6 = (f32[128,512]{1,0:T(8,128)S(1)}, f32[128,512]{1,0:T(8,128)S(1)}, u32[]{:S(2)}, u32[]{:S(2)}) collective-permute-start(f32[128,512]{1,0:T(8,128)S(1)} %get-tuple-element.43), channel_id=1, source_target_pairs={{0,1},{2,3},{4,5},{6,7},{8,9},{10,11},{12,13},{14,15},{1,0},{3,2},... | collective-permute-start | bytes 786440 | tf_op jit(solution)/shard_map/ppermute | solution.py:105
  60.8 20.3 %collective-permute-start.7 = (f32[128,512]{1,0:T(8,128)S(1)}, f32[128,512]{1,0:T(8,128)S(1)}, u32[]{:S(2)}, u32[]{:S(2)}) collective-permute-start(f32[128,512]{1,0:T(8,128)S(1)} %get-tuple-element.44), channel_id=1, source_target_pairs={{1,2},{3,4},{5,6},{7,8},{9,10},{11,12},{13,14},{2,1},{4,3},{6,5},{... | collective-permute-start | bytes 786440 | tf_op jit(solution)/shard_map/ppermute | solution.py:105
  63.6 39.7 %collective-permute-start.10 = (f32[3,128,512]{2,1,0:T(8,128)S(1)}, f32[3,128,512]{2,1,0:T(8,128)}, u32[]{:S(2)}, u32[]{:S(2)}) collective-permute-start(f32[3,128,512]{2,1,0:T(8,128)S(1)} %get-tuple-element.53.out0), channel_id=1, source_target_pairs={{0,1},{2,3},{4,5},{6,7},{8,9},{10,11},{12,13},{14,15},{1,0},{3,2},... | collective-permute-start | bytes 2359304 | tf_op jit(solution)/shard_map/ppermute | solution.py:105
  82.1 26.7 %collective-permute-start.11 = (f32[128,512]{1,0:T(8,128)S(1)}, f32[128,512]{1,0:T(8,128)S(1)}, u32[]{:S(2)}, u32[]{:S(2)}) collective-permute-start(f32[128,512]{1,0:T(8,128)S(1)} %multiply_add_fusion.edge0), channel_id=1, source_target_pairs={{0,1},{2,3},{4,5},{6,7},{8,9},{10,11},{12,13},{14,15},{1,0},{3,2},... | collective-permute-start | bytes 786440 | tf_op jit(solution)/shard_map/ppermute | solution.py:105
  82.2 27.3 %collective-permute-start.12 = (f32[128,512]{1,0:T(8,128)S(1)}, f32[128,512]{1,0:T(8,128)}, u32[]{:S(2)}, u32[]{:S(2)}) collective-permute-start(f32[128,512]{1,0:T(8,128)S(1)} %multiply_subtract_fusion.edge1), channel_id=1, source_target_pairs={{1,2},{3,4},{5,6},{7,8},{9,10},{11,12},{13,14},{2,1},{4,3},{6,5},{... | collective-permute-start | bytes 786440 | tf_op jit(solution)/shard_map/ppermute | solution.py:105
  86.2 30.1 %copy-start.17 = (f32[2,3,128,512]{3,2,1,0:T(8,128)S(1)}, f32[2,3,128,512]{3,2,1,0:T(8,128)}, u32[]{:S(2)}) copy-start(f32[2,3,128,512]{3,2,1,0:T(8,128)} %get-tuple-element.65.v0_far) | copy-start | bytes 4718596
  92.5 29.5 %copy-start.5 = (f32[3,128,512]{2,1,0:T(8,128)}, f32[3,128,512]{2,1,0:T(8,128)S(1)}, u32[]{:S(2)}) copy-start(f32[3,128,512]{2,1,0:T(8,128)S(1)} %get-tuple-element.50.in0) | copy-start | bytes 2359300
  92.5 66.6 %collective-permute-start.9 = (f32[3,128,512]{2,1,0:T(8,128)S(1)}, f32[3,128,512]{2,1,0:T(8,128)S(1)}, u32[]{:S(2)}, u32[]{:S(2)}) collective-permute-start(f32[3,128,512]{2,1,0:T(8,128)S(1)} %get-tuple-element.50.in0), channel_id=1, source_target_pairs={{0,1},{2,3},{4,5},{6,7},{8,9},{10,11},{12,13},{14,15},{1,0},{3,2},... | collective-permute-start | bytes 2359304 | tf_op jit(solution)/shard_map/ppermute | solution.py:105
  109.6 66.3 %collective-permute-start.14 = (f32[3,128,512]{2,1,0:T(8,128)}, f32[3,128,512]{2,1,0:T(8,128)}, u32[]{:S(2)}, u32[]{:S(2)}) collective-permute-start(f32[3,128,512]{2,1,0:T(8,128)} %get-tuple-element.59.out1), channel_id=1, source_target_pairs={{1,2},{3,4},{5,6},{7,8},{9,10},{11,12},{13,14},{2,1},{4,3},{6,5},{... | collective-permute-start | bytes 2359304 | tf_op jit(solution)/shard_map/ppermute | solution.py:105
  113.4 62.5 %collective-permute-start.15 = (f32[3,128,512]{2,1,0:T(8,128)}, f32[3,128,512]{2,1,0:T(8,128)}, u32[]{:S(2)}, u32[]{:S(2)}) collective-permute-start(f32[3,128,512]{2,1,0:T(8,128)} %get-tuple-element.61.in1), channel_id=1, source_target_pairs={{1,2},{3,4},{5,6},{7,8},{9,10},{11,12},{13,14},{2,1},{4,3},{6,5},{... | collective-permute-start | bytes 2359304 | tf_op jit(solution)/shard_map/ppermute | solution.py:105
  122.8 51.1 %collective-permute-start.16 = (f32[4,64,512]{2,1,0:T(8,128)}, f32[4,64,512]{2,1,0:T(8,128)}, u32[]{:S(2)}, u32[]{:S(2)}) collective-permute-start(f32[4,64,512]{2,1,0:T(8,128)} %constant_dynamic-slice_fusion), channel_id=1, source_target_pairs={{0,16},{16,0},{1,17},{17,1},{2,18},{18,2},{3,19},{19,3},{4,20},{20... | collective-permute-start | bytes 1572872 | tf_op jit(solution)/shard_map/ppermute | solution.py:108
  160.0 27.4 %collective-permute-start.13 = (f32[3,128,512]{2,1,0:T(8,128)}, f32[3,128,512]{2,1,0:T(8,128)}, u32[]{:S(2)}, u32[]{:S(2)}) collective-permute-start(f32[3,128,512]{2,1,0:T(8,128)} %get-tuple-element.56.in1), channel_id=1, source_target_pairs={{1,2},{3,4},{5,6},{7,8},{9,10},{11,12},{13,14},{2,1},{4,3},{6,5},{... | collective-permute-start | bytes 2359304 | tf_op jit(solution)/shard_map/ppermute | solution.py:105
  165.5 10.4 %copy-start.2 = (f32[3,128,512]{2,1,0:T(8,128)S(1)}, f32[3,128,512]{2,1,0:T(8,128)}, u32[]{:S(2)}) copy-start(f32[3,128,512]{2,1,0:T(8,128)} %copy-done.1) | copy-start | bytes 2359300
  165.5 10.4 %copy-start.4 = (f32[3,128,512]{2,1,0:T(8,128)S(1)}, f32[3,128,512]{2,1,0:T(8,128)}, u32[]{:S(2)}) copy-start(f32[3,128,512]{2,1,0:T(8,128)} %copy-done.3) | copy-start | bytes 2359300
  175.8 8.9 %copy-start.14 = (f32[3,128,512]{2,1,0:T(8,128)S(1)}, f32[3,128,512]{2,1,0:T(8,128)}, u32[]{:S(2)}) copy-start(f32[3,128,512]{2,1,0:T(8,128)} %copy-done.13) | copy-start | bytes 2359300
  (13 other events, 12.5 us)

commit v6 on v5

--- a/solution.py
+++ b/solution.py
@@ -8,7 +8,7 @@
 MATCH = 5.0
 SEVENTH = 1.0 / 7.0
 MIB = 1 << 20
-FORWARD, MIDDLE, BACK, SOURCES, LAST, SMOOTH = 0, 0, 1000, 0, 2000, 150
+FORWARD, MIDDLE, BACK, SOURCES, LAST, SMOOTH = 0, 0, 1000, 0, 2000, 1000
 
 
 def col_prev(f):
@@ -277,11 +277,8 @@
         inner0, outer0 = inner_outer[:2], inner_outer[2:]
 
         far0 = [swap(inner0[0], 0), None]
-        held1, held2, near1[0], *lam1_far = after(inner1[1], outer1[1], near1[0], *lam1_far)
-        far1[1] = swap(held1, 1)
-        near1[1] = swap(held2, 1)
-        held, far0[0] = after(inner0[1], far0[0], *lam1_far)[:2]
-        far0[1] = swap(held, 1)
+        held, near1[0], *lam1_far = after((inner1[1], outer1[1]), near1[0], *lam1_far)
+        far1[1], near1[1] = [swap(x, 1) for x in held]
 
         def sweeps(facts_ref, s, v, out, u2):
             for z in range(-1, Z + 1):
@@ -350,6 +347,9 @@
             scratch=[pltpu.VMEM((Z + 2, Y, X), jnp.float32)],
         )
 
+        held, lam0 = after(inner0[1], lam0)
+        far0[1] = swap(held, 1)
+
         def share(k):
             start = lax.rem(group + k, subj) * rows
             return lax.dynamic_slice_in_dim(lam0, start, rows, axis=1)
@@ -402,26 +402,30 @@
             scratch=[u2_scratch, pltpu.VMEM((Z + 4, Y, X), jnp.float32)],
         )
 
-        def add_far(facts_ref, src, grad, out):
-            for d in range(3):
-                out[0, d, 0] = grad[0, d, 0] + src[d] * SEVENTH**3
-
-        for i in SIDES:
-
-            def boundary(_, facts_ref, i=i):
-                return (0, 0, up_at(facts_ref, i) * (Z - 1), 0, 0)
-
-            block = pl.BlockSpec((1, 3, 1, Y, X), boundary)
-            gradient = call(
-                add_far,
-                struct(*flow.shape),
-                [pl.BlockSpec((3, Y, X), lambda *_: (0, 0, 0)), block],
-                block,
-                [facts, far0[i], gradient],
-                "add_far",
-                aliases={2: 0},
-                prefetch=1,
-            )
+        def add_far(facts_ref, far_0, far_1, grad, out):
+            def add(far):
+                for d in range(3):
+                    out[0, d, 0] = grad[0, d, 0] + far[d] * SEVENTH**3
+
+            pl.when(pl.program_id(0) == 0)(lambda: add(far_0))
+            pl.when(pl.program_id(0) == 1)(lambda: add(far_1))
+
+        def boundary(i, facts_ref):
+            up = jnp.where(i == 0, facts_ref[3], 1 - facts_ref[3])
+            return (0, 0, up * (Z - 1), 0, 0)
+
+        block = pl.BlockSpec((1, 3, 1, Y, X), boundary)
+        gradient = call(
+            add_far,
+            struct(*flow.shape),
+            [whole(x) for x in far0] + [block],
+            block,
+            [facts, *far0, gradient],
+            "add_far",
+            grid=(2,),
+            aliases={3: 0},
+            prefetch=1,
+        )
         return gradient[None], template_grad
 
     return body

time: 192 us -> 180 us (0.938)
  local copies, waits for them, and re-layouts: 21.1 us -> 11.3 us
  Pallas kernels: 46.4 us -> 43.2 us
  starting transfers between devices: 25.8 us -> 28.4 us
    unnamed x41 -> x23, local copies, waits for them, and re-layouts: 12.6 us -> 3.51 us
    pallas_call x9 -> x8, Pallas kernels: 46.4 us -> 43.2 us  [call(): pl.pallas_call(kernel, out_shape=out_shape, grid_spec=pltpu.PrefetchScala...]
    ppermute x14, starting transfers between devices: 25.7 us -> 28.1 us  [swap(): return lax.ppermute(x, 'slab', pairs[side])]
  transfers between devices with their start and end apart: 17 -> 17, of which waited for: 8 -> 11; matrix products, arithmetic and copies ran while one was open for 5% -> 5% of each run, Pallas kernels for 23% -> 22%
where the time goes in v6:
time: 180 us; the launch traced here: 179 us
  waiting for transfers between devices  94 us (52%)
  Pallas kernels  43.2 us (24%)
  starting transfers between devices  28.4 us (16%)
  local copies, waits for them, and re-layouts  11.3 us (6%)
    ppermute x14, waiting for transfers between devices, swap(): return lax.ppermute(x, 'slab', pairs[side])  92 us
    pallas_call x8, Pallas kernels, call(): pl.pallas_call(kernel, out_shape=out_shape, grid_spec=pltpu.PrefetchScala...  43.2 us
    ppermute x14, starting transfers between devices, swap(): return lax.ppermute(x, 'slab', pairs[side])  28.1 us
    slice x1, local copies, waits for them, and re-layouts, body(): flow[0]  3.87 us
  transfers between devices with their start and end apart: 17, of which 11 were waited for; matrix products, arithmetic and copies ran while one was open for 5% of the time, Pallas kernels for 22%

profile of v6, /device:TPU:2, one launch (start us, length us, event | category | flops | bytes accessed | tf_op | source)
XLA Modules:
  0.0 178.9 jit_solution(8045259381014504449)
XLA Ops:
  1.7 3.4 %collective-permute-start.2 = (f32[2,64,512]{2,1,0:T(8,128)S(1)}, f32[2,64,512]{2,1,0:T(8,128)S(1)}, u32[]{:S(2)}, u32[]{:S(2)}) collective-permute-start(f32[2,64,512]{2,1,0:T(8,128)S(1)} %get-tuple-element.70), channel_id=1, source_target_pairs={{1,2},{3,4},{5,6},{7,8},{9,10},{11,12},{13,14},{2,1},{4,3},{6,5},{... | collective-permute-start | bytes 786440 | tf_op jit(solution)/shard_map/ppermute | solution.py:105
  5.2 3.9 %slice.5 = f32[1,1,3,4,128,512]{5,4,3,2,1,0:T(8,128)} slice(f32[1,2,3,4,128,512]{5,4,3,2,1,0:T(8,128)} %param.5), slice={[0:1], [0:1], [0:3], [0:4], [0:128], [0:512]} | slice | bytes 6291456 | tf_op jit(solution)/shard_map/slice | solution.py:137
  9.1 2.8 %dynamic-slice_bitcast_fusion = (f32[3,128,512]{2,1,0:T(8,128)}, f32[3,128,512]{2,1,0:T(8,128)}) fusion(f32[1,1,3,4,128,512]{5,4,3,2,1,0:T(8,128)} %slice.5, s32[]{:T(128)S(6)} %select_n.29, s32[]{:T(128)S(6)} %select_n.28), kind=kLoop, calls=%fused_computation | loop fusion | bytes 3145736 | tf_op jit(solution)/shard_map/squeeze | solution.py:137
  11.9 4.8 %collective-permute-start.5 = (f32[3,128,512]{2,1,0:T(8,128)}, f32[3,128,512]{2,1,0:T(8,128)S(1)}, u32[]{:S(2)}, u32[]{:S(2)}) collective-permute-start(f32[3,128,512]{2,1,0:T(8,128)} %get-tuple-element.68), channel_id=1, source_target_pairs={{1,2},{3,4},{5,6},{7,8},{9,10},{11,12},{13,14},{2,1},{4,3},{6,5},{... | collective-permute-start | bytes 2359304 | tf_op jit(solution)/shard_map/ppermute | solution.py:105
  16.9 18.9 %collective-permute-done.1 = f32[2,64,512]{2,1,0:T(8,128)} collective-permute-done((f32[2,64,512]{2,1,0:T(8,128)S(1)}, f32[2,64,512]{2,1,0:T(8,128)}, u32[]{:S(2)}, u32[]{:S(2)}) %collective-permute-start.1) | collective-permute-done | bytes 262176 | tf_op jit(solution)/shard_map/ppermute | solution.py:105
  38.9 6.2 %forward.1 = (f32[8,128,512]{2,1,0:T(8,128)}, f32[4,128,512]{2,1,0:T(8,128)S(1)}, f32[2,128,512]{2,1,0:T(8,128)S(1)}, f32[3,128,512]{2,1,0:T(8,128)S(1)}, f32[3,128,512]{2,1,0:T(8,128)S(1)}) custom-call(s32[4]{0:T(128)S(1)} %pad_add_fusion.refs_0_.facts_ref, f32[4,64,512]{2,1,0:T(8,128)S(1)} %copy-done, f32[4,64,512]{2,1,0:T(8,128)S(1)} %collective-permute-done.refs_2_, ...), custom_call_target="tpu_custom_call" | custom-call | flops 1024 | bytes 1024 | tf_op jit(solution)/shard_map/forward/pallas_call | solution.py:66
  46.0 6.6 %collective-permute-done.4.halo0 = f32[3,128,512]{2,1,0:T(8,128)S(1)} collective-permute-done((f32[3,128,512]{2,1,0:T(8,128)}, f32[3,128,512]{2,1,0:T(8,128)S(1)}, u32[]{:S(2)}, u32[]{:S(2)}) %collective-permute-start.4) | collective-permute-done | bytes 786464 | tf_op jit(solution)/shard_map/ppermute | solution.py:105
  52.5 5.1 %middle.1 = (f32[3,128,512]{2,1,0:T(8,128)}, f32[3,128,512]{2,1,0:T(8,128)S(1)}, f32[128,512]{1,0:T(8,128)S(1)}, f32[128,512]{1,0:T(8,128)S(1)}, f32[2,128,512]{2,1,0:T(8,128)S(1)}, /*index=5*/f32[2,3,128,512]{3,2,1,0:T(8,128)}) custom-call(s32[4]{0:T(128)S(1)} %pad_add_fusion.refs_0_.facts_ref, f32[8,128,512]{2,1,0:T(8,128)} %get-tuple-element.37.tmpl, ...), custom_call_target="tpu_custom_call" | custom-call | flops 1024 | bytes 1024 | tf_op jit(solution)/shard_map/middle/pallas_call | solution.py:66
  62.0 3.3 %back.1 = (f32[4,128,512]{2,1,0:T(8,128)S(1)}, f32[128,512]{1,0:T(8,128)S(1)}, f32[128,512]{1,0:T(8,128)S(1)}) custom-call(s32[4]{0:T(128)S(1)} %pad_add_fusion.refs_0_.facts_ref, f32[2,128,512]{2,1,0:T(8,128)S(1)} %get-tuple-element.38.lam2_in, f32[2,128,512]{2,1,0:T(8,128)S(1)} %get-tuple-element.40.lam2_out, f32[2,3,4,128,512]{4,3,2,1,0:T(8,128)} %bitcast.14), custom_call_target="tpu_custom_call" | custom-call | flops 10000001024 | bytes 1024 | tf_op jit(solution)/shard_map/back/pallas_call | solution.py:66
  65.4 15.3 %collective-permute-done.6 = f32[128,512]{1,0:T(8,128)S(1)} collective-permute-done((f32[128,512]{1,0:T(8,128)S(1)}, f32[128,512]{1,0:T(8,128)S(1)}, u32[]{:S(2)}, u32[]{:S(2)}) %collective-permute-start.6) | collective-permute-done | bytes 262176 | tf_op jit(solution)/shard_map/ppermute | solution.py:105
  81.9 4.2 %collective-permute-start.12 = (f32[128,512]{1,0:T(8,128)S(1)}, f32[128,512]{1,0:T(8,128)}, u32[]{:S(2)}, u32[]{:S(2)}) collective-permute-start(f32[128,512]{1,0:T(8,128)S(1)} %multiply_subtract_fusion.edge1), channel_id=1, source_target_pairs={{1,2},{3,4},{5,6},{7,8},{9,10},{11,12},{13,14},{2,1},{4,3},{6,5},{... | collective-permute-start | bytes 786440 | tf_op jit(solution)/shard_map/ppermute | solution.py:105
  86.1 3.9 %sources.1 = (f32[4,128,512]{2,1,0:T(8,128)S(1)}, f32[3,128,512]{2,1,0:T(8,128)S(1)}, f32[3,128,512]{2,1,0:T(8,128)S(1)}, f32[3,128,512]{2,1,0:T(8,128)S(1)}, f32[3,128,512]{2,1,0:T(8,128)S(1)}) custom-call(s32[4]{0:T(128)S(1)} %pad_add_fusion.refs_0_.facts_ref, f32[8,128,512]{2,1,0:T(8,128)} %get-tuple-element.37.tmpl, ...), custom_call_target="tpu_custom_call" | custom-call | flops 1024 | bytes 1024 | tf_op jit(solution)/shard_map/sources/pallas_call | solution.py:66
  90.1 13.1 %collective-permute-done.10.near0 = f32[3,128,512]{2,1,0:T(8,128)} collective-permute-done((f32[3,128,512]{2,1,0:T(8,128)}, f32[3,128,512]{2,1,0:T(8,128)}, u32[]{:S(2)}, u32[]{:S(2)}) %collective-permute-start.10) | collective-permute-done | bytes 786464 | tf_op jit(solution)/shard_map/ppermute | solution.py:105
  103.2 5.5 %collective-permute-done.11.beyond0 = f32[128,512]{1,0:T(8,128)S(1)} collective-permute-done((f32[128,512]{1,0:T(8,128)S(1)}, f32[128,512]{1,0:T(8,128)S(1)}, u32[]{:S(2)}, u32[]{:S(2)}) %collective-permute-start.11) | collective-permute-done | bytes 262176 | tf_op jit(solution)/shard_map/ppermute | solution.py:105
  109.2 4.2 %collective-permute-start.14 = (f32[3,128,512]{2,1,0:T(8,128)S(1)}, f32[3,128,512]{2,1,0:T(8,128)S(1)}, u32[]{:S(2)}, u32[]{:S(2)}) collective-permute-start(f32[3,128,512]{2,1,0:T(8,128)S(1)} %copy-done.9), channel_id=1, source_target_pairs={{1,2},{3,4},{5,6},{7,8},{9,10},{11,12},{13,14},{2,1},{4,3},{6,5},{... | collective-permute-start | bytes 2359304 | tf_op jit(solution)/shard_map/ppermute | solution.py:105
  113.4 2.6 %collective-permute-start.15 = (f32[3,128,512]{2,1,0:T(8,128)S(1)}, f32[3,128,512]{2,1,0:T(8,128)S(1)}, u32[]{:S(2)}, u32[]{:S(2)}) collective-permute-start(f32[3,128,512]{2,1,0:T(8,128)S(1)} %copy-done.5), channel_id=1, source_target_pairs={{1,2},{3,4},{5,6},{7,8},{9,10},{11,12},{13,14},{2,1},{4,3},{6,5},{... | collective-permute-start | bytes 2359304 | tf_op jit(solution)/shard_map/ppermute | solution.py:105
  116.0 4.8 %last.1 = (f32[4,128,512]{2,1,0:T(8,128)S(1)}, f32[2,3,128,512]{3,2,1,0:T(8,128)S(1)}) custom-call(s32[4]{0:T(128)S(1)} %pad_add_fusion.refs_0_.facts_ref, f32[8,128,512]{2,1,0:T(8,128)} %get-tuple-element.37.tmpl, f32[4,128,512]{2,1,0:T(8,128)S(1)} %get-tuple-element.51.lam1, f32[128,512]{1,0:T(8,128)S(1)} %collective-permute-done.11.beyond0, ...), custom_call_target="tpu_custom_call" | custom-call | flops 20000002048 | bytes 1024 | tf_op jit(solution)/shard_map/last/pallas_call | solution.py:66
  120.9 4.3 %collective-permute-start.13 = (f32[3,128,512]{2,1,0:T(8,128)S(1)}, f32[3,128,512]{2,1,0:T(8,128)S(1)}, u32[]{:S(2)}, u32[]{:S(2)}) collective-permute-start(f32[3,128,512]{2,1,0:T(8,128)S(1)} %get-tuple-element.59.in1), channel_id=1, source_target_pairs={{1,2},{3,4},{5,6},{7,8},{9,10},{11,12},{13,14},{2,1},{4,3},{6,5},{... | collective-permute-start | bytes 2359304 | tf_op jit(solution)/shard_map/ppermute | solution.py:105
  125.3 8.4 %smooth_0.1._ = f32[2,3,4,128,512]{4,3,2,1,0:T(8,128)} custom-call(s32[4]{0:T(128)S(1)} %pad_add_fusion.refs_0_.facts_ref, f32[3,128,512]{2,1,0:T(8,128)S(1)} %get-tuple-element.49.in0, f32[3,128,512]{2,1,0:T(8,128)S(1)} %get-tuple-element.59.in1, f32[3,128,512]{2,1,0:T(8,128)S(1)} %get-tuple-element.64.out0, f32[3,128,512]{2,1,0:T(8,128)S(1)} %get-tuple-element.65.out1, ...), custom_call_target="tpu_custom_call" | custom-call | flops 10000001024 | bytes 1024 | tf_op jit(solution)/shard_map/smooth_0/pallas_call | solution.py:66
  134.5 8.3 %collective-permute-done.14.near1 = f32[3,128,512]{2,1,0:T(8,128)S(1)} collective-permute-done((f32[3,128,512]{2,1,0:T(8,128)S(1)}, f32[3,128,512]{2,1,0:T(8,128)S(1)}, u32[]{:S(2)}, u32[]{:S(2)}) %collective-permute-start.14) | collective-permute-done | bytes 786464 | tf_op jit(solution)/shard_map/ppermute | solution.py:105
  142.8 16.9 %collective-permute-done.15.far1 = f32[3,128,512]{2,1,0:T(8,128)S(1)} collective-permute-done((f32[3,128,512]{2,1,0:T(8,128)S(1)}, f32[3,128,512]{2,1,0:T(8,128)S(1)}, u32[]{:S(2)}, u32[]{:S(2)}) %collective-permute-start.15) | collective-permute-done | bytes 786464 | tf_op jit(solution)/shard_map/ppermute | solution.py:105
  160.5 8.6 %smooth_1.1.grad = f32[2,3,4,128,512]{4,3,2,1,0:T(8,128)} custom-call(s32[4]{0:T(128)S(1)} %pad_add_fusion.refs_0_.facts_ref, f32[3,128,512]{2,1,0:T(8,128)S(1)} %copy-done.3, f32[3,128,512]{2,1,0:T(8,128)S(1)} %copy-done.5, f32[3,128,512]{2,1,0:T(8,128)} %get-tuple-element.54.out0, f32[3,128,512]{2,1,0:T(8,128)S(1)} %copy-done.9, ...), custom_call_target="tpu_custom_call", output_to_operand_aliasing={{}: (9, {})} | custom-call | flops 10000001024 | bytes 1024 | tf_op jit(solution)/shard_map/smooth_1/pallas_call | solution.py:66
  169.2 6.7 %collective-permute-done.9.far_0 = f32[3,128,512]{2,1,0:T(8,128)S(1)} collective-permute-done((f32[3,128,512]{2,1,0:T(8,128)S(1)}, f32[3,128,512]{2,1,0:T(8,128)S(1)}, u32[]{:S(2)}, u32[]{:S(2)}) %collective-permute-start.9) | collective-permute-done | bytes 786464 | tf_op jit(solution)/shard_map/ppermute | solution.py:105
  175.9 3.0 %add_far.1 = f32[2,3,4,128,512]{4,3,2,1,0:T(8,128)} custom-call(s32[4]{0:T(128)S(1)} %pad_add_fusion.refs_0_.facts_ref, f32[3,128,512]{2,1,0:T(8,128)S(1)} %collective-permute-done.9.far_0, f32[3,128,512]{2,1,0:T(8,128)S(1)} %collective-permute-done.13.far_1, f32[2,3,4,128,512]{4,3,2,1,0:T(8,128)} %smooth_1.1.grad), custom_call_target="tpu_custom_call", output_to_operand_aliasing={{}: (3, {})} | custom-call | flops 1024 | bytes 1024 | tf_op jit(solution)/shard_map/add_far/pallas_call | solution.py:66
  (50 shorter events, 13.4 us)
Async XLA Ops:
  1.7 15.2 %collective-permute-start.2 = (f32[2,64,512]{2,1,0:T(8,128)S(1)}, f32[2,64,512]{2,1,0:T(8,128)S(1)}, u32[]{:S(2)}, u32[]{:S(2)}) collective-permute-start(f32[2,64,512]{2,1,0:T(8,128)S(1)} %get-tuple-element.70), channel_id=1, source_target_pairs={{1,2},{3,4},{5,6},{7,8},{9,10},{11,12},{13,14},{2,1},{4,3},{6,5},{... | collective-permute-start | bytes 786440 | tf_op jit(solution)/shard_map/ppermute | solution.py:105
  5.1 30.7 %collective-permute-start.1 = (f32[2,64,512]{2,1,0:T(8,128)S(1)}, f32[2,64,512]{2,1,0:T(8,128)}, u32[]{:S(2)}, u32[]{:S(2)}) collective-permute-start(f32[2,64,512]{2,1,0:T(8,128)S(1)} %get-tuple-element.71), channel_id=1, source_target_pairs={{0,1},{2,3},{4,5},{6,7},{8,9},{10,11},{12,13},{14,15},{1,0},{3,2},... | collective-permute-start | bytes 786440 | tf_op jit(solution)/shard_map/ppermute | solution.py:105
  9.1 7.7 %copy-start = (f32[4,64,512]{2,1,0:T(8,128)S(1)}, f32[4,64,512]{2,1,0:T(8,128)}, u32[]{:S(2)}) copy-start(f32[4,64,512]{2,1,0:T(8,128)} %refs_1_.1) | copy-start | bytes 1572868
  11.9 34.1 %collective-permute-start.5 = (f32[3,128,512]{2,1,0:T(8,128)}, f32[3,128,512]{2,1,0:T(8,128)S(1)}, u32[]{:S(2)}, u32[]{:S(2)}) collective-permute-start(f32[3,128,512]{2,1,0:T(8,128)} %get-tuple-element.68), channel_id=1, source_target_pairs={{1,2},{3,4},{5,6},{7,8},{9,10},{11,12},{13,14},{2,1},{4,3},{6,5},{... | collective-permute-start | bytes 2359304 | tf_op jit(solution)/shard_map/ppermute | solution.py:105
  16.8 35.8 %collective-permute-start.4 = (f32[3,128,512]{2,1,0:T(8,128)}, f32[3,128,512]{2,1,0:T(8,128)S(1)}, u32[]{:S(2)}, u32[]{:S(2)}) collective-permute-start(f32[3,128,512]{2,1,0:T(8,128)} %get-tuple-element.69), channel_id=1, source_target_pairs={{0,1},{2,3},{4,5},{6,7},{8,9},{10,11},{12,13},{14,15},{1,0},{3,2},... | collective-permute-start | bytes 2359304 | tf_op jit(solution)/shard_map/ppermute | solution.py:105
  16.9 20.1 %collective-permute-start = (f32[4,64,512]{2,1,0:T(8,128)S(1)}, f32[4,64,512]{2,1,0:T(8,128)S(1)}, u32[]{:S(2)}, u32[]{:S(2)}) collective-permute-start(f32[4,64,512]{2,1,0:T(8,128)S(1)} %copy-done), channel_id=1, source_target_pairs={{0,16},{16,0},{1,17},{17,1},{2,18},{18,2},{3,19},{19,3},{4,20},{20... | collective-permute-start | bytes 1572872 | tf_op jit(solution)/shard_map/ppermute | solution.py:108
  36.8 2.1 %collective-permute-start.3 = (f32[4,64,512]{2,1,0:T(8,128)S(1)}, f32[4,64,512]{2,1,0:T(8,128)}, u32[]{:S(2)}, u32[]{:S(2)}) collective-permute-start(f32[4,64,512]{2,1,0:T(8,128)S(1)} %constant_dynamic-update-slice_fusion.refs_3_), channel_id=1, source_target_pairs={{0,16},{16,0},{1,17},{17,1},{2,18},{18,2},{3,19},{19,3},{4,20},{20... | collective-permute-start | bytes 1572872 | tf_op jit(solution)/shard_map/ppermute | solution.py:108
  46.0 11.7 %copy-start.2 = (f32[3,128,512]{2,1,0:T(8,128)}, f32[3,128,512]{2,1,0:T(8,128)S(1)}, u32[]{:S(2)}) copy-start(f32[3,128,512]{2,1,0:T(8,128)S(1)} %get-tuple-element.45.in0) | copy-start | bytes 2359300
  46.0 35.0 %collective-permute-start.8 = (f32[3,128,512]{2,1,0:T(8,128)S(1)}, f32[3,128,512]{2,1,0:T(8,128)S(1)}, u32[]{:S(2)}, u32[]{:S(2)}) collective-permute-start(f32[3,128,512]{2,1,0:T(8,128)S(1)} %get-tuple-element.45.in0), channel_id=1, source_target_pairs={{0,1},{2,3},{4,5},{6,7},{8,9},{10,11},{12,13},{14,15},{1,0},{3,2},... | collective-permute-start | bytes 2359304 | tf_op jit(solution)/shard_map/ppermute | solution.py:105
  57.6 23.0 %collective-permute-start.6 = (f32[128,512]{1,0:T(8,128)S(1)}, f32[128,512]{1,0:T(8,128)S(1)}, u32[]{:S(2)}, u32[]{:S(2)}) collective-permute-start(f32[128,512]{1,0:T(8,128)S(1)} %get-tuple-element.43), channel_id=1, source_target_pairs={{0,1},{2,3},{4,5},{6,7},{8,9},{10,11},{12,13},{14,15},{1,0},{3,2},... | collective-permute-start | bytes 786440 | tf_op jit(solution)/shard_map/ppermute | solution.py:105
  59.4 21.6 %collective-permute-start.7 = (f32[128,512]{1,0:T(8,128)S(1)}, f32[128,512]{1,0:T(8,128)S(1)}, u32[]{:S(2)}, u32[]{:S(2)}) collective-permute-start(f32[128,512]{1,0:T(8,128)S(1)} %get-tuple-element.44), channel_id=1, source_target_pairs={{1,2},{3,4},{5,6},{7,8},{9,10},{11,12},{13,14},{2,1},{4,3},{6,5},{... | collective-permute-start | bytes 786440 | tf_op jit(solution)/shard_map/ppermute | solution.py:105
  62.0 41.2 %collective-permute-start.10 = (f32[3,128,512]{2,1,0:T(8,128)}, f32[3,128,512]{2,1,0:T(8,128)}, u32[]{:S(2)}, u32[]{:S(2)}) collective-permute-start(f32[3,128,512]{2,1,0:T(8,128)} %get-tuple-element.54.out0), channel_id=1, source_target_pairs={{0,1},{2,3},{4,5},{6,7},{8,9},{10,11},{12,13},{14,15},{1,0},{3,2},... | collective-permute-start | bytes 2359304 | tf_op jit(solution)/shard_map/ppermute | solution.py:105
  81.1 27.7 %collective-permute-start.11 = (f32[128,512]{1,0:T(8,128)S(1)}, f32[128,512]{1,0:T(8,128)S(1)}, u32[]{:S(2)}, u32[]{:S(2)}) collective-permute-start(f32[128,512]{1,0:T(8,128)S(1)} %multiply_add_fusion.edge0), channel_id=1, source_target_pairs={{0,1},{2,3},{4,5},{6,7},{8,9},{10,11},{12,13},{14,15},{1,0},{3,2},... | collective-permute-start | bytes 786440 | tf_op jit(solution)/shard_map/ppermute | solution.py:105
  81.9 27.3 %collective-permute-start.12 = (f32[128,512]{1,0:T(8,128)S(1)}, f32[128,512]{1,0:T(8,128)}, u32[]{:S(2)}, u32[]{:S(2)}) collective-permute-start(f32[128,512]{1,0:T(8,128)S(1)} %multiply_subtract_fusion.edge1), channel_id=1, source_target_pairs={{1,2},{3,4},{5,6},{7,8},{9,10},{11,12},{13,14},{2,1},{4,3},{6,5},{... | collective-permute-start | bytes 786440 | tf_op jit(solution)/shard_map/ppermute | solution.py:105
  86.1 23.1 %copy-start.9 = (f32[3,128,512]{2,1,0:T(8,128)S(1)}, f32[3,128,512]{2,1,0:T(8,128)}, u32[]{:S(2)}) copy-start(f32[3,128,512]{2,1,0:T(8,128)} %copy-done.8) | copy-start | bytes 2359300
  86.1 27.3 %copy-start.5 = (f32[3,128,512]{2,1,0:T(8,128)S(1)}, f32[3,128,512]{2,1,0:T(8,128)}, u32[]{:S(2)}) copy-start(f32[3,128,512]{2,1,0:T(8,128)} %copy-done.4) | copy-start | bytes 2359300
  86.1 29.8 %copy-start.1 = (f32[2,3,128,512]{3,2,1,0:T(8,128)S(1)}, f32[2,3,128,512]{3,2,1,0:T(8,128)}, u32[]{:S(2)}) copy-start(f32[2,3,128,512]{3,2,1,0:T(8,128)} %get-tuple-element.57.v0_far) | copy-start | bytes 4718596
  90.0 85.9 %collective-permute-start.9 = (f32[3,128,512]{2,1,0:T(8,128)S(1)}, f32[3,128,512]{2,1,0:T(8,128)S(1)}, u32[]{:S(2)}, u32[]{:S(2)}) collective-permute-start(f32[3,128,512]{2,1,0:T(8,128)S(1)} %get-tuple-element.49.in0), channel_id=1, source_target_pairs={{0,1},{2,3},{4,5},{6,7},{8,9},{10,11},{12,13},{14,15},{1,0},{3,2},... | collective-permute-start | bytes 2359304 | tf_op jit(solution)/shard_map/ppermute | solution.py:105
  109.2 33.6 %collective-permute-start.14 = (f32[3,128,512]{2,1,0:T(8,128)S(1)}, f32[3,128,512]{2,1,0:T(8,128)S(1)}, u32[]{:S(2)}, u32[]{:S(2)}) collective-permute-start(f32[3,128,512]{2,1,0:T(8,128)S(1)} %copy-done.9), channel_id=1, source_target_pairs={{1,2},{3,4},{5,6},{7,8},{9,10},{11,12},{13,14},{2,1},{4,3},{6,5},{... | collective-permute-start | bytes 2359304 | tf_op jit(solution)/shard_map/ppermute | solution.py:105
  113.4 46.3 %collective-permute-start.15 = (f32[3,128,512]{2,1,0:T(8,128)S(1)}, f32[3,128,512]{2,1,0:T(8,128)S(1)}, u32[]{:S(2)}, u32[]{:S(2)}) collective-permute-start(f32[3,128,512]{2,1,0:T(8,128)S(1)} %copy-done.5), channel_id=1, source_target_pairs={{1,2},{3,4},{5,6},{7,8},{9,10},{11,12},{13,14},{2,1},{4,3},{6,5},{... | collective-permute-start | bytes 2359304 | tf_op jit(solution)/shard_map/ppermute | solution.py:105
  120.8 12.8 %collective-permute-start.16 = (f32[4,64,512]{2,1,0:T(8,128)S(1)}, f32[4,64,512]{2,1,0:T(8,128)S(1)}, u32[]{:S(2)}, u32[]{:S(2)}) collective-permute-start(f32[4,64,512]{2,1,0:T(8,128)S(1)} %constant_dynamic-slice_fusion), channel_id=1, source_target_pairs={{0,16},{16,0},{1,17},{17,1},{2,18},{18,2},{3,19},{19,3},{4,20},{20... | collective-permute-start | bytes 1572872 | tf_op jit(solution)/shard_map/ppermute | solution.py:108
  120.9 55.0 %collective-permute-start.13 = (f32[3,128,512]{2,1,0:T(8,128)S(1)}, f32[3,128,512]{2,1,0:T(8,128)S(1)}, u32[]{:S(2)}, u32[]{:S(2)}) collective-permute-start(f32[3,128,512]{2,1,0:T(8,128)S(1)} %get-tuple-element.59.in1), channel_id=1, source_target_pairs={{1,2},{3,4},{5,6},{7,8},{9,10},{11,12},{13,14},{2,1},{4,3},{6,5},{... | collective-permute-start | bytes 2359304 | tf_op jit(solution)/shard_map/ppermute | solution.py:105
  125.3 35.3 %copy-start.3 = (f32[3,128,512]{2,1,0:T(8,128)S(1)}, f32[3,128,512]{2,1,0:T(8,128)}, u32[]{:S(2)}) copy-start(f32[3,128,512]{2,1,0:T(8,128)} %copy-done.2) | copy-start | bytes 2359300
  125.3 35.3 %copy-start.7 = (f32[3,128,512]{2,1,0:T(8,128)S(1)}, f32[3,128,512]{2,1,0:T(8,128)}, u32[]{:S(2)}) copy-start(f32[3,128,512]{2,1,0:T(8,128)} %copy-done.6) | copy-start | bytes 2359300
  (4 other events, 10.4 us)

commit v7 on v6

--- a/solution.py
+++ b/solution.py
@@ -134,7 +134,8 @@
             for i, up in enumerate(ups)
         ]
         flow0_edge = [
-            lax.dynamic_slice_in_dim(flow[0], up * (Z - 1), 1, 1)[:, 0] for up in ups
+            lax.dynamic_slice(velocity, (0, 0, 0, up * (Z - 1), 0, 0), (1, 1, 3, 1, Y, X))[0, 0, :, 0]
+            for up in ups
         ]
         flow0_far = [swap(flow0_edge[i], i) for i in SIDES]
         own_parts = [template] + [turn(template, k) for k in range(1, subj)]
@@ -358,7 +359,7 @@
         for k in range(1, subj):
             template_grad = template_grad + turn(share(k), k)
 
-        def smooth_0(facts_ref, in0, in1, out0, out1, near, v, out, u2, s):
+        def smooth_0(facts_ref, in0, in1, out0, out1, near, v, out, rim, u2, s):
             for i, inner, outer in ((0, in0, out0), (1, in1, out1)):
                 up = up_at(facts_ref, i)
                 s[2 + up * (Z - 3)] = inner[0]
@@ -366,13 +367,15 @@
             s[0] = near[0, 0]
             s[Z + 1] = near[1, 0]
             sweeps(facts_ref, Planes(s, -1, Z), v, out, u2)
-
-        gradient = call(
+            for i in SIDES:
+                rim[i, 0] = out[0, 0, up_at(facts_ref, i) * (Z - 1)]
+
+        both = pl.BlockSpec((2, 1, Y, X), lambda d: (0, d, 0, 0))
+        gradient, rim = call(
             smooth_0,
-            struct(*flow.shape),
-            [SMEM] + [part] * 4
-            + [pl.BlockSpec((2, 1, Y, X), lambda d: (0, d, 0, 0)), flow_part[0]],
-            flow_part[0],
+            [struct(*flow.shape), struct(2, 3, Y, X)],
+            [SMEM] + [part] * 4 + [both, flow_part[0]],
+            [flow_part[0], both],
             [facts, *inner0, *outer0, near0, flow],
             "smooth_0",
             weight=SMOOTH,
@@ -402,28 +405,27 @@
             scratch=[u2_scratch, pltpu.VMEM((Z + 4, Y, X), jnp.float32)],
         )
 
-        def add_far(facts_ref, far_0, far_1, grad, out):
-            def add(far):
+        def add_far(facts_ref, far_0, far_1, rim, _, out):
+            def add(i, far):
                 for d in range(3):
-                    out[0, d, 0] = grad[0, d, 0] + far[d] * SEVENTH**3
-
-            pl.when(pl.program_id(0) == 0)(lambda: add(far_0))
-            pl.when(pl.program_id(0) == 1)(lambda: add(far_1))
+                    out[0, d, 0] = rim[i, d] + far[d] * SEVENTH**3
+
+            pl.when(pl.program_id(0) == 0)(lambda: add(0, far_0))
+            pl.when(pl.program_id(0) == 1)(lambda: add(1, far_1))
 
         def boundary(i, facts_ref):
             up = jnp.where(i == 0, facts_ref[3], 1 - facts_ref[3])
             return (0, 0, up * (Z - 1), 0, 0)
 
-        block = pl.BlockSpec((1, 3, 1, Y, X), boundary)
         gradient = call(
             add_far,
             struct(*flow.shape),
-            [whole(x) for x in far0] + [block],
-            block,
-            [facts, *far0, gradient],
+            [whole(x) for x in (*far0, rim)] + [pl.BlockSpec(memory_space=pl.ANY)],
+            pl.BlockSpec((1, 3, 1, Y, X), boundary),
+            [facts, *far0, rim, gradient],
             "add_far",
             grid=(2,),
-            aliases={3: 0},
+            aliases={4: 0},
             prefetch=1,
         )
         return gradient[None], template_grad

time: 180 us -> 179 us (level)
  waiting for transfers between devices: 94 us -> 98.4 us
  local copies, waits for them, and re-layouts: 11.3 us -> 8.67 us
  starting transfers between devices: 28.4 us -> 26.5 us
    ppermute x14, waiting for transfers between devices: 92 us -> 96.6 us  [swap(): return lax.ppermute(x, 'slab', pairs[side])]
    slice x1 -> x0, local copies, waits for them, and re-layouts: 3.87 us -> none  [body(): flow[0]]
    ppermute x14, starting transfers between devices: 28.1 us -> 26.3 us  [swap(): return lax.ppermute(x, 'slab', pairs[side])]
    unnamed x23 -> x25, local copies, waits for them, and re-layouts: 3.51 us -> 4.79 us
  transfers between devices with their start and end apart: 17 -> 17, of which waited for: 11 -> 11; matrix products, arithmetic and copies ran while one was open for 5% -> 2% of each run, Pallas kernels for 22% -> 23%
where the time goes in v7:
time: 179 us; the launch traced here: 178 us
  waiting for transfers between devices  98.4 us (55%)
  Pallas kernels  42.1 us (24%)
  starting transfers between devices  26.5 us (15%)
  local copies, waits for them, and re-layouts  8.67 us (5%)
    ppermute x14, waiting for transfers between devices, swap(): return lax.ppermute(x, 'slab', pairs[side])  96.6 us
    pallas_call x8, Pallas kernels, call(): pl.pallas_call(kernel, out_shape=out_shape, grid_spec=pltpu.PrefetchScala...  42.1 us
    ppermute x14, starting transfers between devices, swap(): return lax.ppermute(x, 'slab', pairs[side])  26.3 us
    unnamed x25, local copies, waits for them, and re-layouts  4.79 us
  transfers between devices with their start and end apart: 17, of which 11 were waited for; matrix products, arithmetic and copies ran while one was open for 2% of the time, Pallas kernels for 23%

profile of v7, /device:TPU:2, one launch (start us, length us, event | category | flops | bytes accessed | tf_op | source)
XLA Modules:
  0.0 177.7 jit_solution(17078725649127437112)
XLA Ops:
  1.7 3.4 %collective-permute-start.2 = (f32[2,64,512]{2,1,0:T(8,128)S(1)}, f32[2,64,512]{2,1,0:T(8,128)S(1)}, u32[]{:S(2)}, u32[]{:S(2)}) collective-permute-start(f32[2,64,512]{2,1,0:T(8,128)S(1)} %get-tuple-element.74), channel_id=1, source_target_pairs={{1,2},{3,4},{5,6},{7,8},{9,10},{11,12},{13,14},{2,1},{4,3},{6,5},{... | collective-permute-start | bytes 786440 | tf_op jit(solution)/shard_map/ppermute | solution.py:105
  5.2 2.8 %dynamic-slice_bitcast_fusion = (f32[3,128,512]{2,1,0:T(8,128)}, f32[3,128,512]{2,1,0:T(8,128)}) fusion(f32[1,2,3,4,128,512]{5,4,3,2,1,0:T(8,128)} %param.5, s32[]{:T(128)S(6)} %select_n.29, s32[]{:T(128)S(6)} %select_n.28), kind=kLoop, calls=%fused_computation | loop fusion | bytes 3145736 | tf_op jit(solution)/shard_map/squeeze | solution.py:137
  8.0 4.8 %collective-permute-start.5 = (f32[3,128,512]{2,1,0:T(8,128)}, f32[3,128,512]{2,1,0:T(8,128)S(1)}, u32[]{:S(2)}, u32[]{:S(2)}) collective-permute-start(f32[3,128,512]{2,1,0:T(8,128)} %get-tuple-element.72), channel_id=1, source_target_pairs={{1,2},{3,4},{5,6},{7,8},{9,10},{11,12},{13,14},{2,1},{4,3},{6,5},{... | collective-permute-start | bytes 2359304 | tf_op jit(solution)/shard_map/ppermute | solution.py:105
  13.7 22.4 %collective-permute-done.1 = f32[2,64,512]{2,1,0:T(8,128)S(1)} collective-permute-done((f32[2,64,512]{2,1,0:T(8,128)S(1)}, f32[2,64,512]{2,1,0:T(8,128)S(1)}, u32[]{:S(2)}, u32[]{:S(2)}) %collective-permute-start.1) | collective-permute-done | bytes 262176 | tf_op jit(solution)/shard_map/ppermute | solution.py:105
  39.2 6.0 %forward.1 = (f32[8,128,512]{2,1,0:T(8,128)}, f32[4,128,512]{2,1,0:T(8,128)S(1)}, f32[2,128,512]{2,1,0:T(8,128)S(1)}, f32[3,128,512]{2,1,0:T(8,128)S(1)}, f32[3,128,512]{2,1,0:T(8,128)S(1)}) custom-call(s32[4]{0:T(128)S(1)} %pad_add_fusion.refs_0_.facts_ref, f32[4,64,512]{2,1,0:T(8,128)S(1)} %copy-done, f32[4,64,512]{2,1,0:T(8,128)S(1)} %collective-permute-done.refs_2_, ...), custom_call_target="tpu_custom_call" | custom-call | flops 1024 | bytes 1024 | tf_op jit(solution)/shard_map/forward/pallas_call | solution.py:66
  46.1 6.9 %collective-permute-done.4.halo0 = f32[3,128,512]{2,1,0:T(8,128)S(1)} collective-permute-done((f32[3,128,512]{2,1,0:T(8,128)}, f32[3,128,512]{2,1,0:T(8,128)S(1)}, u32[]{:S(2)}, u32[]{:S(2)}) %collective-permute-start.4) | collective-permute-done | bytes 786464 | tf_op jit(solution)/shard_map/ppermute | solution.py:105
  53.0 5.1 %middle.1 = (f32[3,128,512]{2,1,0:T(8,128)}, f32[3,128,512]{2,1,0:T(8,128)S(1)}, f32[128,512]{1,0:T(8,128)S(1)}, f32[128,512]{1,0:T(8,128)S(1)}, f32[2,128,512]{2,1,0:T(8,128)S(1)}, /*index=5*/f32[2,3,128,512]{3,2,1,0:T(8,128)}) custom-call(s32[4]{0:T(128)S(1)} %pad_add_fusion.refs_0_.facts_ref, f32[8,128,512]{2,1,0:T(8,128)} %get-tuple-element.39.tmpl, ...), custom_call_target="tpu_custom_call" | custom-call | flops 1024 | bytes 1024 | tf_op jit(solution)/shard_map/middle/pallas_call | solution.py:66
  58.7 3.3 %collective-permute-start.7 = (f32[128,512]{1,0:T(8,128)S(1)}, f32[128,512]{1,0:T(8,128)S(1)}, u32[]{:S(2)}, u32[]{:S(2)}) collective-permute-start(f32[128,512]{1,0:T(8,128)S(1)} %get-tuple-element.46), channel_id=1, source_target_pairs={{1,2},{3,4},{5,6},{7,8},{9,10},{11,12},{13,14},{2,1},{4,3},{6,5},{... | collective-permute-start | bytes 786440 | tf_op jit(solution)/shard_map/ppermute | solution.py:105
  62.1 3.3 %back.1 = (f32[4,128,512]{2,1,0:T(8,128)S(1)}, f32[128,512]{1,0:T(8,128)S(1)}, f32[128,512]{1,0:T(8,128)S(1)}) custom-call(s32[4]{0:T(128)S(1)} %pad_add_fusion.refs_0_.facts_ref, f32[2,128,512]{2,1,0:T(8,128)S(1)} %get-tuple-element.40.lam2_in, f32[2,128,512]{2,1,0:T(8,128)S(1)} %get-tuple-element.42.lam2_out, f32[2,3,4,128,512]{4,3,2,1,0:T(8,128)} %bitcast.14), custom_call_target="tpu_custom_call" | custom-call | flops 10000001024 | bytes 1024 | tf_op jit(solution)/shard_map/back/pallas_call | solution.py:66
  65.5 15.6 %collective-permute-done.6 = f32[128,512]{1,0:T(8,128)S(1)} collective-permute-done((f32[128,512]{1,0:T(8,128)S(1)}, f32[128,512]{1,0:T(8,128)S(1)}, u32[]{:S(2)}, u32[]{:S(2)}) %collective-permute-start.6) | collective-permute-done | bytes 262176 | tf_op jit(solution)/shard_map/ppermute | solution.py:105
  82.1 3.4 %collective-permute-start.12 = (f32[128,512]{1,0:T(8,128)S(1)}, f32[128,512]{1,0:T(8,128)}, u32[]{:S(2)}, u32[]{:S(2)}) collective-permute-start(f32[128,512]{1,0:T(8,128)S(1)} %multiply_subtract_fusion.edge1), channel_id=1, source_target_pairs={{1,2},{3,4},{5,6},{7,8},{9,10},{11,12},{13,14},{2,1},{4,3},{6,5},{... | collective-permute-start | bytes 786440 | tf_op jit(solution)/shard_map/ppermute | solution.py:105
  85.5 3.8 %sources.1 = (f32[4,128,512]{2,1,0:T(8,128)S(1)}, f32[3,128,512]{2,1,0:T(8,128)S(1)}, f32[3,128,512]{2,1,0:T(8,128)S(1)}, f32[3,128,512]{2,1,0:T(8,128)S(1)}, f32[3,128,512]{2,1,0:T(8,128)S(1)}) custom-call(s32[4]{0:T(128)S(1)} %pad_add_fusion.refs_0_.facts_ref, f32[8,128,512]{2,1,0:T(8,128)} %get-tuple-element.39.tmpl, ...), custom_call_target="tpu_custom_call" | custom-call | flops 1024 | bytes 1024 | tf_op jit(solution)/shard_map/sources/pallas_call | solution.py:66
  89.4 14.3 %collective-permute-done.10.near0 = f32[3,128,512]{2,1,0:T(8,128)} collective-permute-done((f32[3,128,512]{2,1,0:T(8,128)}, f32[3,128,512]{2,1,0:T(8,128)}, u32[]{:S(2)}, u32[]{:S(2)}) %collective-permute-start.10) | collective-permute-done | bytes 786464 | tf_op jit(solution)/shard_map/ppermute | solution.py:105
  103.7 5.5 %collective-permute-done.11.beyond0 = f32[128,512]{1,0:T(8,128)S(1)} collective-permute-done((f32[128,512]{1,0:T(8,128)S(1)}, f32[128,512]{1,0:T(8,128)S(1)}, u32[]{:S(2)}, u32[]{:S(2)}) %collective-permute-start.11) | collective-permute-done | bytes 262176 | tf_op jit(solution)/shard_map/ppermute | solution.py:105
  109.3 3.4 %collective-permute-start.14 = (f32[3,128,512]{2,1,0:T(8,128)S(1)}, f32[3,128,512]{2,1,0:T(8,128)S(1)}, u32[]{:S(2)}, u32[]{:S(2)}) collective-permute-start(f32[3,128,512]{2,1,0:T(8,128)S(1)} %copy-done.9), channel_id=1, source_target_pairs={{1,2},{3,4},{5,6},{7,8},{9,10},{11,12},{13,14},{2,1},{4,3},{6,5},{... | collective-permute-start | bytes 2359304 | tf_op jit(solution)/shard_map/ppermute | solution.py:105
  112.7 3.3 %collective-permute-start.15 = (f32[3,128,512]{2,1,0:T(8,128)S(1)}, f32[3,128,512]{2,1,0:T(8,128)S(1)}, u32[]{:S(2)}, u32[]{:S(2)}) collective-permute-start(f32[3,128,512]{2,1,0:T(8,128)S(1)} %copy-done.5), channel_id=1, source_target_pairs={{1,2},{3,4},{5,6},{7,8},{9,10},{11,12},{13,14},{2,1},{4,3},{6,5},{... | collective-permute-start | bytes 2359304 | tf_op jit(solution)/shard_map/ppermute | solution.py:105
  116.1 4.8 %last.1 = (f32[4,128,512]{2,1,0:T(8,128)S(1)}, f32[2,3,128,512]{3,2,1,0:T(8,128)S(1)}) custom-call(s32[4]{0:T(128)S(1)} %pad_add_fusion.refs_0_.facts_ref, f32[8,128,512]{2,1,0:T(8,128)} %get-tuple-element.39.tmpl, f32[4,128,512]{2,1,0:T(8,128)S(1)} %get-tuple-element.53.lam1, f32[128,512]{1,0:T(8,128)S(1)} %collective-permute-done.11.beyond0, ...), custom_call_target="tpu_custom_call" | custom-call | flops 20000002048 | bytes 1024 | tf_op jit(solution)/shard_map/last/pallas_call | solution.py:66
  122.2 3.6 %collective-permute-start.13 = (f32[3,128,512]{2,1,0:T(8,128)S(1)}, f32[3,128,512]{2,1,0:T(8,128)S(1)}, u32[]{:S(2)}, u32[]{:S(2)}) collective-permute-start(f32[3,128,512]{2,1,0:T(8,128)S(1)} %get-tuple-element.61.in1), channel_id=1, source_target_pairs={{1,2},{3,4},{5,6},{7,8},{9,10},{11,12},{13,14},{2,1},{4,3},{6,5},{... | collective-permute-start | bytes 2359304 | tf_op jit(solution)/shard_map/ppermute | solution.py:105
  125.8 8.6 %smooth_0.1 = (f32[2,3,4,128,512]{4,3,2,1,0:T(8,128)}, f32[2,3,128,512]{3,2,1,0:T(8,128)S(1)}) custom-call(s32[4]{0:T(128)S(1)} %pad_add_fusion.refs_0_.facts_ref, f32[3,128,512]{2,1,0:T(8,128)S(1)} %get-tuple-element.51.in0, f32[3,128,512]{2,1,0:T(8,128)S(1)} %get-tuple-element.61.in1, f32[3,128,512]{2,1,0:T(8,128)S(1)} %get-tuple-element.62.out0, ...), custom_call_target="tpu_custom_call" | custom-call | flops 10000001024 | bytes 1024 | tf_op jit(solution)/shard_map/smooth_0/pallas_call | solution.py:66
  135.3 7.7 %collective-permute-done.14.near1 = f32[3,128,512]{2,1,0:T(8,128)S(1)} collective-permute-done((f32[3,128,512]{2,1,0:T(8,128)S(1)}, f32[3,128,512]{2,1,0:T(8,128)S(1)}, u32[]{:S(2)}, u32[]{:S(2)}) %collective-permute-start.14) | collective-permute-done | bytes 786464 | tf_op jit(solution)/shard_map/ppermute | solution.py:105
  142.9 16.9 %collective-permute-done.15.far1 = f32[3,128,512]{2,1,0:T(8,128)S(1)} collective-permute-done((f32[3,128,512]{2,1,0:T(8,128)S(1)}, f32[3,128,512]{2,1,0:T(8,128)S(1)}, u32[]{:S(2)}, u32[]{:S(2)}) %collective-permute-start.15) | collective-permute-done | bytes 786464 | tf_op jit(solution)/shard_map/ppermute | solution.py:105
  160.7 8.6 %smooth_1.1._ = f32[2,3,4,128,512]{4,3,2,1,0:T(8,128)} custom-call(s32[4]{0:T(128)S(1)} %pad_add_fusion.refs_0_.facts_ref, f32[3,128,512]{2,1,0:T(8,128)S(1)} %copy-done.3, f32[3,128,512]{2,1,0:T(8,128)S(1)} %copy-done.5, f32[3,128,512]{2,1,0:T(8,128)} %get-tuple-element.56.out0, f32[3,128,512]{2,1,0:T(8,128)S(1)} %copy-done.9, ...), custom_call_target="tpu_custom_call", output_to_operand_aliasing={{}: (9, {})} | custom-call | flops 10000001024 | bytes 1024 | tf_op jit(solution)/shard_map/smooth_1/pallas_call | solution.py:66
  169.3 6.6 %collective-permute-done.9.far_0 = f32[3,128,512]{2,1,0:T(8,128)S(1)} collective-permute-done((f32[3,128,512]{2,1,0:T(8,128)S(1)}, f32[3,128,512]{2,1,0:T(8,128)S(1)}, u32[]{:S(2)}, u32[]{:S(2)}) %collective-permute-start.9) | collective-permute-done | bytes 786464 | tf_op jit(solution)/shard_map/ppermute | solution.py:105
  175.9 1.8 %add_far.1 = f32[2,3,4,128,512]{4,3,2,1,0:T(8,128)} custom-call(s32[4]{0:T(128)S(1)} %pad_add_fusion.refs_0_.facts_ref, f32[3,128,512]{2,1,0:T(8,128)S(1)} %collective-permute-done.9.far_0, f32[3,128,512]{2,1,0:T(8,128)S(1)} %collective-permute-done.13.far_1, f32[2,3,128,512]{3,2,1,0:T(8,128)S(1)} %get-tuple-element.65.rim, ...), custom_call_target="tpu_custom_call", output_to_operand_aliasing={{}: (4, {})} | custom-call | flops 1024 | bytes 1024 | tf_op jit(solution)/shard_map/add_far/pallas_call | solution.py:66
  (51 shorter events, 10.9 us)
Async XLA Ops:
  1.7 12.0 %collective-permute-start.2 = (f32[2,64,512]{2,1,0:T(8,128)S(1)}, f32[2,64,512]{2,1,0:T(8,128)S(1)}, u32[]{:S(2)}, u32[]{:S(2)}) collective-permute-start(f32[2,64,512]{2,1,0:T(8,128)S(1)} %get-tuple-element.74), channel_id=1, source_target_pairs={{1,2},{3,4},{5,6},{7,8},{9,10},{11,12},{13,14},{2,1},{4,3},{6,5},{... | collective-permute-start | bytes 786440 | tf_op jit(solution)/shard_map/ppermute | solution.py:105
  5.1 31.0 %collective-permute-start.1 = (f32[2,64,512]{2,1,0:T(8,128)S(1)}, f32[2,64,512]{2,1,0:T(8,128)S(1)}, u32[]{:S(2)}, u32[]{:S(2)}) collective-permute-start(f32[2,64,512]{2,1,0:T(8,128)S(1)} %get-tuple-element.75), channel_id=1, source_target_pairs={{0,1},{2,3},{4,5},{6,7},{8,9},{10,11},{12,13},{14,15},{1,0},{3,2},... | collective-permute-start | bytes 786440 | tf_op jit(solution)/shard_map/ppermute | solution.py:105
  8.0 38.2 %collective-permute-start.5 = (f32[3,128,512]{2,1,0:T(8,128)}, f32[3,128,512]{2,1,0:T(8,128)S(1)}, u32[]{:S(2)}, u32[]{:S(2)}) collective-permute-start(f32[3,128,512]{2,1,0:T(8,128)} %get-tuple-element.72), channel_id=1, source_target_pairs={{1,2},{3,4},{5,6},{7,8},{9,10},{11,12},{13,14},{2,1},{4,3},{6,5},{... | collective-permute-start | bytes 2359304 | tf_op jit(solution)/shard_map/ppermute | solution.py:105
  12.8 40.2 %collective-permute-start.4 = (f32[3,128,512]{2,1,0:T(8,128)}, f32[3,128,512]{2,1,0:T(8,128)S(1)}, u32[]{:S(2)}, u32[]{:S(2)}) collective-permute-start(f32[3,128,512]{2,1,0:T(8,128)} %get-tuple-element.73), channel_id=1, source_target_pairs={{0,1},{2,3},{4,5},{6,7},{8,9},{10,11},{12,13},{14,15},{1,0},{3,2},... | collective-permute-start | bytes 2359304 | tf_op jit(solution)/shard_map/ppermute | solution.py:105
  12.9 23.5 %collective-permute-start = (f32[4,64,512]{2,1,0:T(8,128)}, f32[4,64,512]{2,1,0:T(8,128)S(1)}, u32[]{:S(2)}, u32[]{:S(2)}) collective-permute-start(f32[4,64,512]{2,1,0:T(8,128)} %refs_1_.1), channel_id=1, source_target_pairs={{0,16},{16,0},{1,17},{17,1},{2,18},{18,2},{3,19},{19,3},{4,20},{20... | collective-permute-start | bytes 1572872 | tf_op jit(solution)/shard_map/ppermute | solution.py:108
  36.2 2.0 %collective-permute-start.3 = (f32[4,64,512]{2,1,0:T(8,128)S(1)}, f32[4,64,512]{2,1,0:T(8,128)S(1)}, u32[]{:S(2)}, u32[]{:S(2)}) collective-permute-start(f32[4,64,512]{2,1,0:T(8,128)S(1)} %constant_dynamic-update-slice_fusion.refs_3_), channel_id=1, source_target_pairs={{0,16},{16,0},{1,17},{17,1},{2,18},{18,2},{3,19},{19,3},{4,20},{20... | collective-permute-start | bytes 1572872 | tf_op jit(solution)/shard_map/ppermute | solution.py:108
  46.1 19.3 %copy-start.2 = (f32[3,128,512]{2,1,0:T(8,128)}, f32[3,128,512]{2,1,0:T(8,128)S(1)}, u32[]{:S(2)}) copy-start(f32[3,128,512]{2,1,0:T(8,128)S(1)} %get-tuple-element.47.in0) | copy-start | bytes 2359300
  46.1 35.0 %collective-permute-start.8 = (f32[3,128,512]{2,1,0:T(8,128)S(1)}, f32[3,128,512]{2,1,0:T(8,128)S(1)}, u32[]{:S(2)}, u32[]{:S(2)}) collective-permute-start(f32[3,128,512]{2,1,0:T(8,128)S(1)} %get-tuple-element.47.in0), channel_id=1, source_target_pairs={{0,1},{2,3},{4,5},{6,7},{8,9},{10,11},{12,13},{14,15},{1,0},{3,2},... | collective-permute-start | bytes 2359304 | tf_op jit(solution)/shard_map/ppermute | solution.py:105
  58.1 7.4 %copy-start.8 = (f32[3,128,512]{2,1,0:T(8,128)}, f32[3,128,512]{2,1,0:T(8,128)S(1)}, u32[]{:S(2)}) copy-start(f32[3,128,512]{2,1,0:T(8,128)S(1)} %get-tuple-element.67.out1) | copy-start | bytes 2359300
  58.1 23.0 %collective-permute-start.6 = (f32[128,512]{1,0:T(8,128)S(1)}, f32[128,512]{1,0:T(8,128)S(1)}, u32[]{:S(2)}, u32[]{:S(2)}) collective-permute-start(f32[128,512]{1,0:T(8,128)S(1)} %get-tuple-element.45), channel_id=1, source_target_pairs={{0,1},{2,3},{4,5},{6,7},{8,9},{10,11},{12,13},{14,15},{1,0},{3,2},... | collective-permute-start | bytes 786440 | tf_op jit(solution)/shard_map/ppermute | solution.py:105
  58.7 22.4 %collective-permute-start.7 = (f32[128,512]{1,0:T(8,128)S(1)}, f32[128,512]{1,0:T(8,128)S(1)}, u32[]{:S(2)}, u32[]{:S(2)}) collective-permute-start(f32[128,512]{1,0:T(8,128)S(1)} %get-tuple-element.46), channel_id=1, source_target_pairs={{1,2},{3,4},{5,6},{7,8},{9,10},{11,12},{13,14},{2,1},{4,3},{6,5},{... | collective-permute-start | bytes 786440 | tf_op jit(solution)/shard_map/ppermute | solution.py:105
  62.1 41.6 %collective-permute-start.10 = (f32[3,128,512]{2,1,0:T(8,128)}, f32[3,128,512]{2,1,0:T(8,128)}, u32[]{:S(2)}, u32[]{:S(2)}) collective-permute-start(f32[3,128,512]{2,1,0:T(8,128)} %get-tuple-element.56.out0), channel_id=1, source_target_pairs={{0,1},{2,3},{4,5},{6,7},{8,9},{10,11},{12,13},{14,15},{1,0},{3,2},... | collective-permute-start | bytes 2359304 | tf_op jit(solution)/shard_map/ppermute | solution.py:105
  65.5 50.6 %copy-start.1 = (f32[2,3,128,512]{3,2,1,0:T(8,128)S(1)}, f32[2,3,128,512]{3,2,1,0:T(8,128)}, u32[]{:S(2)}) copy-start(f32[2,3,128,512]{3,2,1,0:T(8,128)} %get-tuple-element.59.v0_far) | copy-start | bytes 4718596
  81.2 28.0 %collective-permute-start.11 = (f32[128,512]{1,0:T(8,128)S(1)}, f32[128,512]{1,0:T(8,128)S(1)}, u32[]{:S(2)}, u32[]{:S(2)}) collective-permute-start(f32[128,512]{1,0:T(8,128)S(1)} %multiply_add_fusion.edge0), channel_id=1, source_target_pairs={{0,1},{2,3},{4,5},{6,7},{8,9},{10,11},{12,13},{14,15},{1,0},{3,2},... | collective-permute-start | bytes 786440 | tf_op jit(solution)/shard_map/ppermute | solution.py:105
  82.1 27.3 %collective-permute-start.12 = (f32[128,512]{1,0:T(8,128)S(1)}, f32[128,512]{1,0:T(8,128)}, u32[]{:S(2)}, u32[]{:S(2)}) collective-permute-start(f32[128,512]{1,0:T(8,128)S(1)} %multiply_subtract_fusion.edge1), channel_id=1, source_target_pairs={{1,2},{3,4},{5,6},{7,8},{9,10},{11,12},{13,14},{2,1},{4,3},{6,5},{... | collective-permute-start | bytes 786440 | tf_op jit(solution)/shard_map/ppermute | solution.py:105
  85.5 23.9 %copy-start.9 = (f32[3,128,512]{2,1,0:T(8,128)S(1)}, f32[3,128,512]{2,1,0:T(8,128)}, u32[]{:S(2)}) copy-start(f32[3,128,512]{2,1,0:T(8,128)} %copy-done.8) | copy-start | bytes 2359300
  85.5 27.2 %copy-start.5 = (f32[3,128,512]{2,1,0:T(8,128)S(1)}, f32[3,128,512]{2,1,0:T(8,128)}, u32[]{:S(2)}) copy-start(f32[3,128,512]{2,1,0:T(8,128)} %copy-done.4) | copy-start | bytes 2359300
  89.3 86.6 %collective-permute-start.9 = (f32[3,128,512]{2,1,0:T(8,128)S(1)}, f32[3,128,512]{2,1,0:T(8,128)S(1)}, u32[]{:S(2)}, u32[]{:S(2)}) collective-permute-start(f32[3,128,512]{2,1,0:T(8,128)S(1)} %get-tuple-element.51.in0), channel_id=1, source_target_pairs={{0,1},{2,3},{4,5},{6,7},{8,9},{10,11},{12,13},{14,15},{1,0},{3,2},... | collective-permute-start | bytes 2359304 | tf_op jit(solution)/shard_map/ppermute | solution.py:105
  109.3 33.6 %collective-permute-start.14 = (f32[3,128,512]{2,1,0:T(8,128)S(1)}, f32[3,128,512]{2,1,0:T(8,128)S(1)}, u32[]{:S(2)}, u32[]{:S(2)}) collective-permute-start(f32[3,128,512]{2,1,0:T(8,128)S(1)} %copy-done.9), channel_id=1, source_target_pairs={{1,2},{3,4},{5,6},{7,8},{9,10},{11,12},{13,14},{2,1},{4,3},{6,5},{... | collective-permute-start | bytes 2359304 | tf_op jit(solution)/shard_map/ppermute | solution.py:105
  112.7 47.0 %collective-permute-start.15 = (f32[3,128,512]{2,1,0:T(8,128)S(1)}, f32[3,128,512]{2,1,0:T(8,128)S(1)}, u32[]{:S(2)}, u32[]{:S(2)}) collective-permute-start(f32[3,128,512]{2,1,0:T(8,128)S(1)} %copy-done.5), channel_id=1, source_target_pairs={{1,2},{3,4},{5,6},{7,8},{9,10},{11,12},{13,14},{2,1},{4,3},{6,5},{... | collective-permute-start | bytes 2359304 | tf_op jit(solution)/shard_map/ppermute | solution.py:105
  122.1 12.3 %collective-permute-start.16 = (f32[4,64,512]{2,1,0:T(8,128)S(1)}, f32[4,64,512]{2,1,0:T(8,128)S(1)}, u32[]{:S(2)}, u32[]{:S(2)}) collective-permute-start(f32[4,64,512]{2,1,0:T(8,128)S(1)} %constant_dynamic-slice_fusion), channel_id=1, source_target_pairs={{0,16},{16,0},{1,17},{17,1},{2,18},{18,2},{3,19},{19,3},{4,20},{20... | collective-permute-start | bytes 1572872 | tf_op jit(solution)/shard_map/ppermute | solution.py:108
  122.2 53.7 %collective-permute-start.13 = (f32[3,128,512]{2,1,0:T(8,128)S(1)}, f32[3,128,512]{2,1,0:T(8,128)S(1)}, u32[]{:S(2)}, u32[]{:S(2)}) collective-permute-start(f32[3,128,512]{2,1,0:T(8,128)S(1)} %get-tuple-element.61.in1), channel_id=1, source_target_pairs={{1,2},{3,4},{5,6},{7,8},{9,10},{11,12},{13,14},{2,1},{4,3},{6,5},{... | collective-permute-start | bytes 2359304 | tf_op jit(solution)/shard_map/ppermute | solution.py:105
  125.8 34.9 %copy-start.3 = (f32[3,128,512]{2,1,0:T(8,128)S(1)}, f32[3,128,512]{2,1,0:T(8,128)}, u32[]{:S(2)}) copy-start(f32[3,128,512]{2,1,0:T(8,128)} %copy-done.2) | copy-start | bytes 2359300
  125.8 34.9 %copy-start.7 = (f32[3,128,512]{2,1,0:T(8,128)S(1)}, f32[3,128,512]{2,1,0:T(8,128)}, u32[]{:S(2)}) copy-start(f32[3,128,512]{2,1,0:T(8,128)} %copy-done.6) | copy-start | bytes 2359300
  (5 other events, 4.9 us)

commit v8 on v7

--- a/solution.py
+++ b/solution.py
@@ -139,8 +139,8 @@
         ]
         flow0_far = [swap(flow0_edge[i], i) for i in SIDES]
         own_parts = [template] + [turn(template, k) for k in range(1, subj)]
-        tmpl_far[0], tmpl_far[1], _, _ = after(*tmpl_far, *flow0_edge)
-        edge = jnp.concatenate(tmpl_far, axis=0)
+        tmpl_far[1], tmpl_far[0], _, _ = after(*tmpl_far[::-1], *flow0_edge)
+        edge = jnp.concatenate(tmpl_far[::-1], axis=0)
         edge_parts = [edge] + [turn(edge, k) for k in range(1, subj)]
 
         def forward(*refs):
@@ -155,7 +155,7 @@
                 for i in SIDES:
                     up = up_at(facts_ref, i)
                     for j in range(2):
-                        tmpl[up * (Z + 2) + j, at, :] = edges[k][2 * i + j]
+                        tmpl[up * (Z + 2) + j, at, :] = edges[k][2 * (1 - i) + j]
             for z in range(Z):
                 v = [v0[0, d, z] for d in range(3)]
                 f = tmpl[z + 2]

time: 179 us -> 176 us (0.983)
  starting transfers between devices: 26.5 us -> 23.6 us
    ppermute x14, starting transfers between devices: 26.3 us -> 23.4 us  [swap(): return lax.ppermute(x, 'slab', pairs[side])]
  transfers between devices with their start and end apart: 17 -> 17, of which waited for: 11 -> 12; matrix products, arithmetic and copies ran while one was open for 2% -> 2% of each run, Pallas kernels for 23% -> 23%
where the time goes in v8:
time: 176 us
  waiting for transfers between devices  99.1 us (56%)
  Pallas kernels  42.1 us (24%)
  starting transfers between devices  23.6 us (13%)
  local copies, waits for them, and re-layouts  8.67 us (5%)
    ppermute x14, waiting for transfers between devices, swap(): return lax.ppermute(x, 'slab', pairs[side])  97.3 us
    pallas_call x8, Pallas kernels, call(): pl.pallas_call(kernel, out_shape=out_shape, grid_spec=pltpu.PrefetchScala...  42.1 us
    ppermute x14, starting transfers between devices, swap(): return lax.ppermute(x, 'slab', pairs[side])  23.4 us
    unnamed x25, local copies, waits for them, and re-layouts  4.79 us
  transfers between devices with their start and end apart: 17, of which 12 were waited for; matrix products, arithmetic and copies ran while one was open for 2% of the time, Pallas kernels for 23%

profile of v8, /device:TPU:2, one launch (start us, length us, event | category | flops | bytes accessed | tf_op | source)
XLA Modules:
  0.0 175.5 jit_solution(10537828618977593931)
XLA Ops:
  1.8 4.9 %collective-permute-start.1 = (f32[2,64,512]{2,1,0:T(8,128)S(1)}, f32[2,64,512]{2,1,0:T(8,128)S(1)}, u32[]{:S(2)}, u32[]{:S(2)}) collective-permute-start(f32[2,64,512]{2,1,0:T(8,128)S(1)} %get-tuple-element.75), channel_id=1, source_target_pairs={{1,2},{3,4},{5,6},{7,8},{9,10},{11,12},{13,14},{2,1},{4,3},{6,5},{... | collective-permute-start | bytes 786440 | tf_op jit(solution)/shard_map/ppermute | solution.py:105
  6.7 2.8 %dynamic-slice_bitcast_fusion = (f32[3,128,512]{2,1,0:T(8,128)}, f32[3,128,512]{2,1,0:T(8,128)}) fusion(f32[1,2,3,4,128,512]{5,4,3,2,1,0:T(8,128)} %param.5, s32[]{:T(128)S(6)} %select_n.29, s32[]{:T(128)S(6)} %select_n.28), kind=kLoop, calls=%fused_computation | loop fusion | bytes 3145736 | tf_op jit(solution)/shard_map/squeeze | solution.py:137
  9.5 1.9 %collective-permute-start.5 = (f32[3,128,512]{2,1,0:T(8,128)}, f32[3,128,512]{2,1,0:T(8,128)S(1)}, u32[]{:S(2)}, u32[]{:S(2)}) collective-permute-start(f32[3,128,512]{2,1,0:T(8,128)} %get-tuple-element.72), channel_id=1, source_target_pairs={{1,2},{3,4},{5,6},{7,8},{9,10},{11,12},{13,14},{2,1},{4,3},{6,5},{... | collective-permute-start | bytes 2359304 | tf_op jit(solution)/shard_map/ppermute | solution.py:105
  11.5 21.9 %collective-permute-done.2 = f32[2,64,512]{2,1,0:T(8,128)S(1)} collective-permute-done((f32[2,64,512]{2,1,0:T(8,128)S(1)}, f32[2,64,512]{2,1,0:T(8,128)S(1)}, u32[]{:S(2)}, u32[]{:S(2)}) %collective-permute-start.2) | collective-permute-done | bytes 262176 | tf_op jit(solution)/shard_map/ppermute | solution.py:105
  36.5 6.0 %forward.1 = (f32[8,128,512]{2,1,0:T(8,128)}, f32[4,128,512]{2,1,0:T(8,128)S(1)}, f32[2,128,512]{2,1,0:T(8,128)S(1)}, f32[3,128,512]{2,1,0:T(8,128)S(1)}, f32[3,128,512]{2,1,0:T(8,128)S(1)}) custom-call(s32[4]{0:T(128)S(1)} %pad_add_fusion.refs_0_.facts_ref, f32[4,64,512]{2,1,0:T(8,128)S(1)} %copy-done, f32[4,64,512]{2,1,0:T(8,128)S(1)} %collective-permute-done.refs_2_, ...), custom_call_target="tpu_custom_call" | custom-call | flops 1024 | bytes 1024 | tf_op jit(solution)/shard_map/forward/pallas_call | solution.py:66
  43.5 6.8 %collective-permute-done.4.halo0 = f32[3,128,512]{2,1,0:T(8,128)S(1)} collective-permute-done((f32[3,128,512]{2,1,0:T(8,128)}, f32[3,128,512]{2,1,0:T(8,128)S(1)}, u32[]{:S(2)}, u32[]{:S(2)}) %collective-permute-start.4) | collective-permute-done | bytes 786464 | tf_op jit(solution)/shard_map/ppermute | solution.py:105
  50.3 5.1 %middle.1 = (f32[3,128,512]{2,1,0:T(8,128)}, f32[3,128,512]{2,1,0:T(8,128)S(1)}, f32[128,512]{1,0:T(8,128)S(1)}, f32[128,512]{1,0:T(8,128)S(1)}, f32[2,128,512]{2,1,0:T(8,128)S(1)}, /*index=5*/f32[2,3,128,512]{3,2,1,0:T(8,128)}) custom-call(s32[4]{0:T(128)S(1)} %pad_add_fusion.refs_0_.facts_ref, f32[8,128,512]{2,1,0:T(8,128)} %get-tuple-element.39.tmpl, ...), custom_call_target="tpu_custom_call" | custom-call | flops 1024 | bytes 1024 | tf_op jit(solution)/shard_map/middle/pallas_call | solution.py:66
  55.4 4.9 %collective-permute-start.7 = (f32[128,512]{1,0:T(8,128)S(1)}, f32[128,512]{1,0:T(8,128)S(1)}, u32[]{:S(2)}, u32[]{:S(2)}) collective-permute-start(f32[128,512]{1,0:T(8,128)S(1)} %get-tuple-element.46), channel_id=1, source_target_pairs={{1,2},{3,4},{5,6},{7,8},{9,10},{11,12},{13,14},{2,1},{4,3},{6,5},{... | collective-permute-start | bytes 786440 | tf_op jit(solution)/shard_map/ppermute | solution.py:105
  60.4 3.3 %back.1 = (f32[4,128,512]{2,1,0:T(8,128)S(1)}, f32[128,512]{1,0:T(8,128)S(1)}, f32[128,512]{1,0:T(8,128)S(1)}) custom-call(s32[4]{0:T(128)S(1)} %pad_add_fusion.refs_0_.facts_ref, f32[2,128,512]{2,1,0:T(8,128)S(1)} %get-tuple-element.40.lam2_in, f32[2,128,512]{2,1,0:T(8,128)S(1)} %get-tuple-element.42.lam2_out, f32[2,3,4,128,512]{4,3,2,1,0:T(8,128)} %bitcast.14), custom_call_target="tpu_custom_call" | custom-call | flops 10000001024 | bytes 1024 | tf_op jit(solution)/shard_map/back/pallas_call | solution.py:66
  63.7 14.7 %collective-permute-done.6 = f32[128,512]{1,0:T(8,128)S(1)} collective-permute-done((f32[128,512]{1,0:T(8,128)S(1)}, f32[128,512]{1,0:T(8,128)S(1)}, u32[]{:S(2)}, u32[]{:S(2)}) %collective-permute-start.6) | collective-permute-done | bytes 262176 | tf_op jit(solution)/shard_map/ppermute | solution.py:105
  80.3 1.9 %collective-permute-start.12 = (f32[128,512]{1,0:T(8,128)S(1)}, f32[128,512]{1,0:T(8,128)}, u32[]{:S(2)}, u32[]{:S(2)}) collective-permute-start(f32[128,512]{1,0:T(8,128)S(1)} %multiply_subtract_fusion.edge1), channel_id=1, source_target_pairs={{1,2},{3,4},{5,6},{7,8},{9,10},{11,12},{13,14},{2,1},{4,3},{6,5},{... | collective-permute-start | bytes 786440 | tf_op jit(solution)/shard_map/ppermute | solution.py:105
  82.2 3.8 %sources.1 = (f32[4,128,512]{2,1,0:T(8,128)S(1)}, f32[3,128,512]{2,1,0:T(8,128)S(1)}, f32[3,128,512]{2,1,0:T(8,128)S(1)}, f32[3,128,512]{2,1,0:T(8,128)S(1)}, f32[3,128,512]{2,1,0:T(8,128)S(1)}) custom-call(s32[4]{0:T(128)S(1)} %pad_add_fusion.refs_0_.facts_ref, f32[8,128,512]{2,1,0:T(8,128)} %get-tuple-element.39.tmpl, ...), custom_call_target="tpu_custom_call" | custom-call | flops 1024 | bytes 1024 | tf_op jit(solution)/shard_map/sources/pallas_call | solution.py:66
  86.8 14.2 %collective-permute-done.10.near0 = f32[3,128,512]{2,1,0:T(8,128)} collective-permute-done((f32[3,128,512]{2,1,0:T(8,128)}, f32[3,128,512]{2,1,0:T(8,128)}, u32[]{:S(2)}, u32[]{:S(2)}) %collective-permute-start.10) | collective-permute-done | bytes 786464 | tf_op jit(solution)/shard_map/ppermute | solution.py:105
  101.0 5.5 %collective-permute-done.11.beyond0 = f32[128,512]{1,0:T(8,128)S(1)} collective-permute-done((f32[128,512]{1,0:T(8,128)S(1)}, f32[128,512]{1,0:T(8,128)S(1)}, u32[]{:S(2)}, u32[]{:S(2)}) %collective-permute-start.11) | collective-permute-done | bytes 262176 | tf_op jit(solution)/shard_map/ppermute | solution.py:105
  107.5 1.9 %collective-permute-start.14 = (f32[3,128,512]{2,1,0:T(8,128)S(1)}, f32[3,128,512]{2,1,0:T(8,128)S(1)}, u32[]{:S(2)}, u32[]{:S(2)}) collective-permute-start(f32[3,128,512]{2,1,0:T(8,128)S(1)} %copy-done.9), channel_id=1, source_target_pairs={{1,2},{3,4},{5,6},{7,8},{9,10},{11,12},{13,14},{2,1},{4,3},{6,5},{... | collective-permute-start | bytes 2359304 | tf_op jit(solution)/shard_map/ppermute | solution.py:105
  109.5 4.8 %collective-permute-start.15 = (f32[3,128,512]{2,1,0:T(8,128)S(1)}, f32[3,128,512]{2,1,0:T(8,128)S(1)}, u32[]{:S(2)}, u32[]{:S(2)}) collective-permute-start(f32[3,128,512]{2,1,0:T(8,128)S(1)} %copy-done.5), channel_id=1, source_target_pairs={{1,2},{3,4},{5,6},{7,8},{9,10},{11,12},{13,14},{2,1},{4,3},{6,5},{... | collective-permute-start | bytes 2359304 | tf_op jit(solution)/shard_map/ppermute | solution.py:105
  114.3 4.8 %last.1 = (f32[4,128,512]{2,1,0:T(8,128)S(1)}, f32[2,3,128,512]{3,2,1,0:T(8,128)S(1)}) custom-call(s32[4]{0:T(128)S(1)} %pad_add_fusion.refs_0_.facts_ref, f32[8,128,512]{2,1,0:T(8,128)} %get-tuple-element.39.tmpl, f32[4,128,512]{2,1,0:T(8,128)S(1)} %get-tuple-element.53.lam1, f32[128,512]{1,0:T(8,128)S(1)} %collective-permute-done.11.beyond0, ...), custom_call_target="tpu_custom_call" | custom-call | flops 20000002048 | bytes 1024 | tf_op jit(solution)/shard_map/last/pallas_call | solution.py:66
  120.4 2.1 %collective-permute-start.13 = (f32[3,128,512]{2,1,0:T(8,128)S(1)}, f32[3,128,512]{2,1,0:T(8,128)S(1)}, u32[]{:S(2)}, u32[]{:S(2)}) collective-permute-start(f32[3,128,512]{2,1,0:T(8,128)S(1)} %get-tuple-element.61.in1), channel_id=1, source_target_pairs={{1,2},{3,4},{5,6},{7,8},{9,10},{11,12},{13,14},{2,1},{4,3},{6,5},{... | collective-permute-start | bytes 2359304 | tf_op jit(solution)/shard_map/ppermute | solution.py:105
  122.5 8.6 %smooth_0.1 = (f32[2,3,4,128,512]{4,3,2,1,0:T(8,128)}, f32[2,3,128,512]{3,2,1,0:T(8,128)S(1)}) custom-call(s32[4]{0:T(128)S(1)} %pad_add_fusion.refs_0_.facts_ref, f32[3,128,512]{2,1,0:T(8,128)S(1)} %get-tuple-element.51.in0, f32[3,128,512]{2,1,0:T(8,128)S(1)} %get-tuple-element.61.in1, f32[3,128,512]{2,1,0:T(8,128)S(1)} %get-tuple-element.62.out0, ...), custom_call_target="tpu_custom_call" | custom-call | flops 10000001024 | bytes 1024 | tf_op jit(solution)/shard_map/smooth_0/pallas_call | solution.py:66
  132.0 9.1 %collective-permute-done.14.near1 = f32[3,128,512]{2,1,0:T(8,128)S(1)} collective-permute-done((f32[3,128,512]{2,1,0:T(8,128)S(1)}, f32[3,128,512]{2,1,0:T(8,128)S(1)}, u32[]{:S(2)}, u32[]{:S(2)}) %collective-permute-start.14) | collective-permute-done | bytes 786464 | tf_op jit(solution)/shard_map/ppermute | solution.py:105
  141.1 16.9 %collective-permute-done.15.far1 = f32[3,128,512]{2,1,0:T(8,128)S(1)} collective-permute-done((f32[3,128,512]{2,1,0:T(8,128)S(1)}, f32[3,128,512]{2,1,0:T(8,128)S(1)}, u32[]{:S(2)}, u32[]{:S(2)}) %collective-permute-start.15) | collective-permute-done | bytes 786464 | tf_op jit(solution)/shard_map/ppermute | solution.py:105
  158.9 8.6 %smooth_1.1._ = f32[2,3,4,128,512]{4,3,2,1,0:T(8,128)} custom-call(s32[4]{0:T(128)S(1)} %pad_add_fusion.refs_0_.facts_ref, f32[3,128,512]{2,1,0:T(8,128)S(1)} %copy-done.3, f32[3,128,512]{2,1,0:T(8,128)S(1)} %copy-done.5, f32[3,128,512]{2,1,0:T(8,128)} %get-tuple-element.56.out0, f32[3,128,512]{2,1,0:T(8,128)S(1)} %copy-done.9, ...), custom_call_target="tpu_custom_call", output_to_operand_aliasing={{}: (9, {})} | custom-call | flops 10000001024 | bytes 1024 | tf_op jit(solution)/shard_map/smooth_1/pallas_call | solution.py:66
  167.5 5.2 %collective-permute-done.9.far_0 = f32[3,128,512]{2,1,0:T(8,128)S(1)} collective-permute-done((f32[3,128,512]{2,1,0:T(8,128)S(1)}, f32[3,128,512]{2,1,0:T(8,128)S(1)}, u32[]{:S(2)}, u32[]{:S(2)}) %collective-permute-start.9) | collective-permute-done | bytes 786464 | tf_op jit(solution)/shard_map/ppermute | solution.py:105
  173.7 1.8 %add_far.1 = f32[2,3,4,128,512]{4,3,2,1,0:T(8,128)} custom-call(s32[4]{0:T(128)S(1)} %pad_add_fusion.refs_0_.facts_ref, f32[3,128,512]{2,1,0:T(8,128)S(1)} %collective-permute-done.9.far_0, f32[3,128,512]{2,1,0:T(8,128)S(1)} %collective-permute-done.13.far_1, f32[2,3,128,512]{3,2,1,0:T(8,128)S(1)} %get-tuple-element.65.rim, ...), custom_call_target="tpu_custom_call", output_to_operand_aliasing={{}: (4, {})} | custom-call | flops 1024 | bytes 1024 | tf_op jit(solution)/shard_map/add_far/pallas_call | solution.py:66
  (51 shorter events, 13.0 us)
Async XLA Ops:
  1.7 31.7 %collective-permute-start.2 = (f32[2,64,512]{2,1,0:T(8,128)S(1)}, f32[2,64,512]{2,1,0:T(8,128)S(1)}, u32[]{:S(2)}, u32[]{:S(2)}) collective-permute-start(f32[2,64,512]{2,1,0:T(8,128)S(1)} %get-tuple-element.74), channel_id=1, source_target_pairs={{0,1},{2,3},{4,5},{6,7},{8,9},{10,11},{12,13},{14,15},{1,0},{3,2},... | collective-permute-start | bytes 786440 | tf_op jit(solution)/shard_map/ppermute | solution.py:105
  1.8 31.7 %collective-permute-start.1 = (f32[2,64,512]{2,1,0:T(8,128)S(1)}, f32[2,64,512]{2,1,0:T(8,128)S(1)}, u32[]{:S(2)}, u32[]{:S(2)}) collective-permute-start(f32[2,64,512]{2,1,0:T(8,128)S(1)} %get-tuple-element.75), channel_id=1, source_target_pairs={{1,2},{3,4},{5,6},{7,8},{9,10},{11,12},{13,14},{2,1},{4,3},{6,5},{... | collective-permute-start | bytes 786440 | tf_op jit(solution)/shard_map/ppermute | solution.py:105
  9.5 34.0 %collective-permute-start.5 = (f32[3,128,512]{2,1,0:T(8,128)}, f32[3,128,512]{2,1,0:T(8,128)S(1)}, u32[]{:S(2)}, u32[]{:S(2)}) collective-permute-start(f32[3,128,512]{2,1,0:T(8,128)} %get-tuple-element.72), channel_id=1, source_target_pairs={{1,2},{3,4},{5,6},{7,8},{9,10},{11,12},{13,14},{2,1},{4,3},{6,5},{... | collective-permute-start | bytes 2359304 | tf_op jit(solution)/shard_map/ppermute | solution.py:105
  11.4 38.9 %collective-permute-start.4 = (f32[3,128,512]{2,1,0:T(8,128)}, f32[3,128,512]{2,1,0:T(8,128)S(1)}, u32[]{:S(2)}, u32[]{:S(2)}) collective-permute-start(f32[3,128,512]{2,1,0:T(8,128)} %get-tuple-element.73), channel_id=1, source_target_pairs={{0,1},{2,3},{4,5},{6,7},{8,9},{10,11},{12,13},{14,15},{1,0},{3,2},... | collective-permute-start | bytes 2359304 | tf_op jit(solution)/shard_map/ppermute | solution.py:105
  11.5 22.2 %collective-permute-start = (f32[4,64,512]{2,1,0:T(8,128)}, f32[4,64,512]{2,1,0:T(8,128)S(1)}, u32[]{:S(2)}, u32[]{:S(2)}) collective-permute-start(f32[4,64,512]{2,1,0:T(8,128)} %refs_1_.1), channel_id=1, source_target_pairs={{0,16},{16,0},{1,17},{17,1},{2,18},{18,2},{3,19},{19,3},{4,20},{20... | collective-permute-start | bytes 1572872 | tf_op jit(solution)/shard_map/ppermute | solution.py:108
  33.5 2.0 %collective-permute-start.3 = (f32[4,64,512]{2,1,0:T(8,128)S(1)}, f32[4,64,512]{2,1,0:T(8,128)S(1)}, u32[]{:S(2)}, u32[]{:S(2)}) collective-permute-start(f32[4,64,512]{2,1,0:T(8,128)S(1)} %constant_dynamic-update-slice_fusion.refs_3_), channel_id=1, source_target_pairs={{0,16},{16,0},{1,17},{17,1},{2,18},{18,2},{3,19},{19,3},{4,20},{20... | collective-permute-start | bytes 1572872 | tf_op jit(solution)/shard_map/ppermute | solution.py:108
  43.5 20.2 %copy-start.2 = (f32[3,128,512]{2,1,0:T(8,128)}, f32[3,128,512]{2,1,0:T(8,128)S(1)}, u32[]{:S(2)}) copy-start(f32[3,128,512]{2,1,0:T(8,128)S(1)} %get-tuple-element.47.in0) | copy-start | bytes 2359300
  43.5 35.9 %collective-permute-start.8 = (f32[3,128,512]{2,1,0:T(8,128)S(1)}, f32[3,128,512]{2,1,0:T(8,128)S(1)}, u32[]{:S(2)}, u32[]{:S(2)}) collective-permute-start(f32[3,128,512]{2,1,0:T(8,128)S(1)} %get-tuple-element.47.in0), channel_id=1, source_target_pairs={{0,1},{2,3},{4,5},{6,7},{8,9},{10,11},{12,13},{14,15},{1,0},{3,2},... | collective-permute-start | bytes 2359304 | tf_op jit(solution)/shard_map/ppermute | solution.py:105
  55.4 8.3 %copy-start.8 = (f32[3,128,512]{2,1,0:T(8,128)}, f32[3,128,512]{2,1,0:T(8,128)S(1)}, u32[]{:S(2)}) copy-start(f32[3,128,512]{2,1,0:T(8,128)S(1)} %get-tuple-element.67.out1) | copy-start | bytes 2359300
  55.4 23.0 %collective-permute-start.6 = (f32[128,512]{1,0:T(8,128)S(1)}, f32[128,512]{1,0:T(8,128)S(1)}, u32[]{:S(2)}, u32[]{:S(2)}) collective-permute-start(f32[128,512]{1,0:T(8,128)S(1)} %get-tuple-element.45), channel_id=1, source_target_pairs={{0,1},{2,3},{4,5},{6,7},{8,9},{10,11},{12,13},{14,15},{1,0},{3,2},... | collective-permute-start | bytes 786440 | tf_op jit(solution)/shard_map/ppermute | solution.py:105
  55.4 23.9 %collective-permute-start.7 = (f32[128,512]{1,0:T(8,128)S(1)}, f32[128,512]{1,0:T(8,128)S(1)}, u32[]{:S(2)}, u32[]{:S(2)}) collective-permute-start(f32[128,512]{1,0:T(8,128)S(1)} %get-tuple-element.46), channel_id=1, source_target_pairs={{1,2},{3,4},{5,6},{7,8},{9,10},{11,12},{13,14},{2,1},{4,3},{6,5},{... | collective-permute-start | bytes 786440 | tf_op jit(solution)/shard_map/ppermute | solution.py:105
  60.3 40.7 %collective-permute-start.10 = (f32[3,128,512]{2,1,0:T(8,128)}, f32[3,128,512]{2,1,0:T(8,128)}, u32[]{:S(2)}, u32[]{:S(2)}) collective-permute-start(f32[3,128,512]{2,1,0:T(8,128)} %get-tuple-element.56.out0), channel_id=1, source_target_pairs={{0,1},{2,3},{4,5},{6,7},{8,9},{10,11},{12,13},{14,15},{1,0},{3,2},... | collective-permute-start | bytes 2359304 | tf_op jit(solution)/shard_map/ppermute | solution.py:105
  63.7 50.6 %copy-start.1 = (f32[2,3,128,512]{3,2,1,0:T(8,128)S(1)}, f32[2,3,128,512]{3,2,1,0:T(8,128)}, u32[]{:S(2)}) copy-start(f32[2,3,128,512]{3,2,1,0:T(8,128)} %get-tuple-element.59.v0_far) | copy-start | bytes 4718596
  79.4 27.1 %collective-permute-start.11 = (f32[128,512]{1,0:T(8,128)S(1)}, f32[128,512]{1,0:T(8,128)S(1)}, u32[]{:S(2)}, u32[]{:S(2)}) collective-permute-start(f32[128,512]{1,0:T(8,128)S(1)} %multiply_add_fusion.edge0), channel_id=1, source_target_pairs={{0,1},{2,3},{4,5},{6,7},{8,9},{10,11},{12,13},{14,15},{1,0},{3,2},... | collective-permute-start | bytes 786440 | tf_op jit(solution)/shard_map/ppermute | solution.py:105
  80.3 27.3 %collective-permute-start.12 = (f32[128,512]{1,0:T(8,128)S(1)}, f32[128,512]{1,0:T(8,128)}, u32[]{:S(2)}, u32[]{:S(2)}) collective-permute-start(f32[128,512]{1,0:T(8,128)S(1)} %multiply_subtract_fusion.edge1), channel_id=1, source_target_pairs={{1,2},{3,4},{5,6},{7,8},{9,10},{11,12},{13,14},{2,1},{4,3},{6,5},{... | collective-permute-start | bytes 786440 | tf_op jit(solution)/shard_map/ppermute | solution.py:105
  82.2 25.3 %copy-start.9 = (f32[3,128,512]{2,1,0:T(8,128)S(1)}, f32[3,128,512]{2,1,0:T(8,128)}, u32[]{:S(2)}) copy-start(f32[3,128,512]{2,1,0:T(8,128)} %copy-done.8) | copy-start | bytes 2359300
  82.2 27.2 %copy-start.5 = (f32[3,128,512]{2,1,0:T(8,128)S(1)}, f32[3,128,512]{2,1,0:T(8,128)}, u32[]{:S(2)}) copy-start(f32[3,128,512]{2,1,0:T(8,128)} %copy-done.4) | copy-start | bytes 2359300
  86.1 86.7 %collective-permute-start.9 = (f32[3,128,512]{2,1,0:T(8,128)S(1)}, f32[3,128,512]{2,1,0:T(8,128)S(1)}, u32[]{:S(2)}, u32[]{:S(2)}) collective-permute-start(f32[3,128,512]{2,1,0:T(8,128)S(1)} %get-tuple-element.51.in0), channel_id=1, source_target_pairs={{0,1},{2,3},{4,5},{6,7},{8,9},{10,11},{12,13},{14,15},{1,0},{3,2},... | collective-permute-start | bytes 2359304 | tf_op jit(solution)/shard_map/ppermute | solution.py:105
  107.5 33.6 %collective-permute-start.14 = (f32[3,128,512]{2,1,0:T(8,128)S(1)}, f32[3,128,512]{2,1,0:T(8,128)S(1)}, u32[]{:S(2)}, u32[]{:S(2)}) collective-permute-start(f32[3,128,512]{2,1,0:T(8,128)S(1)} %copy-done.9), channel_id=1, source_target_pairs={{1,2},{3,4},{5,6},{7,8},{9,10},{11,12},{13,14},{2,1},{4,3},{6,5},{... | collective-permute-start | bytes 2359304 | tf_op jit(solution)/shard_map/ppermute | solution.py:105
  109.5 48.5 %collective-permute-start.15 = (f32[3,128,512]{2,1,0:T(8,128)S(1)}, f32[3,128,512]{2,1,0:T(8,128)S(1)}, u32[]{:S(2)}, u32[]{:S(2)}) collective-permute-start(f32[3,128,512]{2,1,0:T(8,128)S(1)} %copy-done.5), channel_id=1, source_target_pairs={{1,2},{3,4},{5,6},{7,8},{9,10},{11,12},{13,14},{2,1},{4,3},{6,5},{... | collective-permute-start | bytes 2359304 | tf_op jit(solution)/shard_map/ppermute | solution.py:105
  120.3 10.8 %collective-permute-start.16 = (f32[4,64,512]{2,1,0:T(8,128)S(1)}, f32[4,64,512]{2,1,0:T(8,128)S(1)}, u32[]{:S(2)}, u32[]{:S(2)}) collective-permute-start(f32[4,64,512]{2,1,0:T(8,128)S(1)} %constant_dynamic-slice_fusion), channel_id=1, source_target_pairs={{0,16},{16,0},{1,17},{17,1},{2,18},{18,2},{3,19},{19,3},{4,20},{20... | collective-permute-start | bytes 1572872 | tf_op jit(solution)/shard_map/ppermute | solution.py:108
  120.4 53.3 %collective-permute-start.13 = (f32[3,128,512]{2,1,0:T(8,128)S(1)}, f32[3,128,512]{2,1,0:T(8,128)S(1)}, u32[]{:S(2)}, u32[]{:S(2)}) collective-permute-start(f32[3,128,512]{2,1,0:T(8,128)S(1)} %get-tuple-element.61.in1), channel_id=1, source_target_pairs={{1,2},{3,4},{5,6},{7,8},{9,10},{11,12},{13,14},{2,1},{4,3},{6,5},{... | collective-permute-start | bytes 2359304 | tf_op jit(solution)/shard_map/ppermute | solution.py:105
  122.5 36.4 %copy-start.3 = (f32[3,128,512]{2,1,0:T(8,128)S(1)}, f32[3,128,512]{2,1,0:T(8,128)}, u32[]{:S(2)}) copy-start(f32[3,128,512]{2,1,0:T(8,128)} %copy-done.2) | copy-start | bytes 2359300
  122.5 36.4 %copy-start.7 = (f32[3,128,512]{2,1,0:T(8,128)S(1)}, f32[3,128,512]{2,1,0:T(8,128)}, u32[]{:S(2)}) copy-start(f32[3,128,512]{2,1,0:T(8,128)} %copy-done.6) | copy-start | bytes 2359300
  (5 other events, 4.9 us)

commit v9 on v8

--- a/solution.py
+++ b/solution.py
@@ -8,7 +8,7 @@
 MATCH = 5.0
 SEVENTH = 1.0 / 7.0
 MIB = 1 << 20
-FORWARD, MIDDLE, BACK, SOURCES, LAST, SMOOTH = 0, 0, 1000, 0, 2000, 1000
+FORWARD, MIDDLE, BACK, LAST, SMOOTH = 0, 0, 1000, 2000, 1000
 
 
 def col_prev(f):
@@ -185,8 +185,8 @@
         )
         far1 = [swap(inner1[0], 0), None]
 
-        def middle(facts_ref, tmpl, img1, halo0, halo1, v1, aim, src0, src1, flux0, flux1, lam2, v0_far):
-            for i, halo, src, flux in ((0, halo0, src0, flux0), (1, halo1, src1, flux1)):
+        def middle(facts_ref, tmpl, img1, halo0, halo1, v1, aim, src0, src1, lam2, v0_far):
+            for i, halo, src in ((0, halo0, src0), (1, halo1, src1)):
                 up = up_at(facts_ref, i)
                 at = 1 + up * (Z + 1)
                 v = [halo[d] for d in range(3)]
@@ -205,11 +205,10 @@
                 for d in range(3):
                     src[d] = (-MATCH * dt) * lam * diffs[d]
                 lam2[i] = lam
-                flux[...] = jnp.where(up == 1, jnp.minimum(v[0], 0.0), jnp.maximum(v[0], 0.0)) * lam
-
-        outs = [struct(3, Y, X)] * 2 + [struct(Y, X)] * 2 + [struct(2, Y, X), struct(2, 3, Y, X)]
+
+        outs = [struct(3, Y, X)] * 2 + [struct(2, Y, X), struct(2, 3, Y, X)]
         operands = [facts, tmpl, img1, *flow0_far, flow, target]
-        *outer1, flux_0, flux_1, lam2_out, v0_far = call(
+        *outer1, lam2_out, v0_far = call(
             middle,
             outs,
             [SMEM] + [whole(x) for x in operands[1:5]] + [flow_spec[1], whole(target)],
@@ -218,9 +217,7 @@
             "middle",
             weight=MIDDLE,
         )
-        flux_far = [swap(flux_0, 0), swap(flux_1, 1)]
-
-        def back(facts_ref, lam2_in, lam2_out, v1, lam1, part0, part1, lam2):
+        def back(facts_ref, lam2_in, lam2_out, v1, lam1, word0, word1, lam2):
             for i in SIDES:
                 up = up_at(facts_ref, i)
                 lam2[1 + up * (Z - 3)] = lam2_in[i]
@@ -230,12 +227,16 @@
                 above = jnp.maximum(v1[0, 0, z + 1], 0.0) * lam2[z + 1] if z < Z - 1 else None
                 below = jnp.minimum(v1[0, 0, z - 1], 0.0) * lam2[z - 1] if z > 0 else None
                 lam1[z] = retreat(lam2[z], v, above, below, dt)
-            for i, part in ((0, part0), (1, part1)):
-                part[...] = lam1[up_at(facts_ref, i) * (Z - 1)]
-
-        outs = [struct(Z, Y, X)] + [struct(Y, X)] * 2
+            for i, word in ((0, word0), (1, word1)):
+                up = up_at(facts_ref, i)
+                z = up * (Z - 1)
+                v = v1[0, 0, z]
+                word[0] = jnp.where(up == 1, jnp.minimum(v, 0.0), jnp.maximum(v, 0.0)) * lam2[z]
+                word[1] = lam1[z]
+
+        outs = [struct(Z, Y, X)] + [struct(2, Y, X)] * 2
         operands = [facts, lam2_in, lam2_out, flow]
-        lam1_part, part_0, part_1 = call(
+        lam1_part, *words = call(
             back,
             outs,
             [SMEM] + [whole(x) for x in operands[1:3]] + [flow_spec[1]],
@@ -245,41 +246,56 @@
             weight=BACK,
             scratch=[pltpu.VMEM((Z, Y, X), jnp.float32)],
         )
-
-        near1 = [swap(outer1[0], 0), None]
-
-        *flux_far, far1[0] = after(*flux_far, far1[0])
-        toward = (2 * even - 1).astype(jnp.float32) * dt
-        lam1_edge = [part_0 + toward * flux_far[0], part_1 - toward * flux_far[1]]
-        lam1_far = [swap(lam1_edge[i], i) for i in SIDES]
-
-        def sources(facts_ref, tmpl, part, edge0, edge1, v0, lam1, src0, src1, out0, out1):
-            for i, edge, inner, outer in ((0, edge0, src0, out0), (1, edge1, src1, out1)):
+        words_far = [swap(words[i], i) for i in SIDES]
+        near1 = [swap(after(outer1[0], *words)[0], 0), None]
+
+        held, far1[0], *words_far = after((inner1[1], outer1[1]), far1[0], *words_far)
+        far1[1], near1[1] = [swap(x, 1) for x in held]
+
+        def last(facts_ref, tmpl, part, own0, own1, far0, far1, v0_far, v0, lam0, src0, src1, out0, out1, near, lam):
+            for z in range(1, Z - 1):
+                lam[z + 1] = part[z]
+            for i, own, far in ((0, own0, far0), (1, own1, far1)):
+                up = up_at(facts_ref, i)
+                toward = dt * (2 * up - 1).astype(jnp.float32)
+                inside = jnp.where(up == 1, facts_ref[2], facts_ref[1]) > 0
+                lam[1 + up * (Z - 1)] = own[1] + toward * far[0]
+                lam[up * (Z + 1)] = jnp.where(inside, far[1] - toward * own[0], 0.0)
+
+            def flow_at(z, d):
+                return v0[0, d, z] if 0 <= z < Z else v0_far[0 if z < 0 else 1, d]
+
+            def source(z, v, src, *at):
+                diffs = upwind(tmpl[z + 1], tmpl[z + 2], tmpl[z + 3], v)
+                for d in range(3):
+                    src[(*at, d)] = (-MATCH * dt) * lam[z + 1] * diffs[d]
+
+            for i, inner, outer in ((0, src0, out0), (1, src1, out1)):
                 up = up_at(facts_ref, i)
                 for z, src in ((1 + up * (Z - 3), inner), (up * (Z - 1), outer)):
-                    lam = part[z] if src is inner else edge[...]
-                    lam1[z] = lam
-                    v = [v0[0, d, z] for d in range(3)]
-                    diffs = upwind(tmpl[z + 1], tmpl[z + 2], tmpl[z + 3], v)
-                    for d in range(3):
-                        src[d] = (-MATCH * dt) * lam * diffs[d]
-
-        outs = [struct(Z, Y, X)] + [struct(3, Y, X)] * 4
-        operands = [facts, tmpl, lam1_part, *lam1_edge, flow]
-        lam1, *inner_outer = call(
-            sources,
+                    source(z, [v0[0, d, z] for d in range(3)], src)
+            for j, z in enumerate((-1, Z)):
+                source(z, [flow_at(z, d) for d in range(3)], near, j)
+            for z in range(Z):
+                above = jnp.maximum(flow_at(z + 1, 0), 0.0) * lam[z + 2]
+                below = jnp.minimum(flow_at(z - 1, 0), 0.0) * lam[z]
+                v = [flow_at(z, d) for d in range(3)]
+                lam0[z] = retreat(lam[z + 1], v, above, below, dt)
+
+        outs = [struct(Z, Y, X)] + [struct(3, Y, X)] * 4 + [struct(2, 3, Y, X)]
+        operands = [facts, tmpl, lam1_part, *words, *words_far, v0_far, flow]
+        lam0, *inner_outer, near0 = call(
+            last,
             outs,
-            [SMEM] + [whole(x) for x in operands[1:5]] + [flow_spec[0]],
+            [SMEM] + [whole(x) for x in operands[1:8]] + [flow_spec[0]],
             [whole(x) for x in outs],
             operands,
-            "sources",
-            weight=SOURCES,
+            "last",
+            weight=LAST,
+            scratch=[pltpu.VMEM((Z + 2, Y, X), jnp.float32)],
         )
         inner0, outer0 = inner_outer[:2], inner_outer[2:]
-
-        far0 = [swap(inner0[0], 0), None]
-        held, near1[0], *lam1_far = after((inner1[1], outer1[1]), near1[0], *lam1_far)
-        far1[1], near1[1] = [swap(x, 1) for x in held]
+        far0 = [swap(inner0[i], i) for i in SIDES]
 
         def sweeps(facts_ref, s, v, out, u2):
             for z in range(-1, Z + 1):
@@ -315,42 +331,6 @@
         ]
         u2_scratch = pltpu.VMEM((Z + 2, Y, X), jnp.float32)
 
-        def last(facts_ref, tmpl, lam1, beyond0, beyond1, v0_far, v0, lam0, src, lam):
-            for z in range(Z):
-                lam[z + 1] = lam1[z]
-            for i, beyond in ((0, beyond0), (1, beyond1)):
-                lam[up_at(facts_ref, i) * (Z + 1)] = beyond[...]
-
-            def flow_at(z, d):
-                return v0[0, d, z] if 0 <= z < Z else v0_far[0 if z < 0 else 1, d]
-
-            for j, z in enumerate((-1, Z)):
-                v = [flow_at(z, d) for d in range(3)]
-                diffs = upwind(tmpl[z + 1], tmpl[z + 2], tmpl[z + 3], v)
-                for d in range(3):
-                    src[j, d] = (-MATCH * dt) * lam[z + 1] * diffs[d]
-            for z in range(Z):
-                above = jnp.maximum(flow_at(z + 1, 0), 0.0) * lam[z + 2]
-                below = jnp.minimum(flow_at(z - 1, 0), 0.0) * lam[z]
-                v = [flow_at(z, d) for d in range(3)]
-                lam0[z] = retreat(lam[z + 1], v, above, below, dt)
-
-        outs = [struct(Z, Y, X), struct(2, 3, Y, X)]
-        operands = [facts, tmpl, lam1, *lam1_far, v0_far, flow]
-        lam0, near0 = call(
-            last,
-            outs,
-            [SMEM] + [whole(x) for x in operands[1:6]] + [flow_spec[0]],
-            [whole(x) for x in outs],
-            operands,
-            "last",
-            weight=LAST,
-            scratch=[pltpu.VMEM((Z + 2, Y, X), jnp.float32)],
-        )
-
-        held, lam0 = after(inner0[1], lam0)
-        far0[1] = swap(held, 1)
-
         def share(k):
             start = lax.rem(group + k, subj) * rows
             return lax.dynamic_slice_in_dim(lam0, start, rows, axis=1)
@@ -405,28 +385,26 @@
             scratch=[u2_scratch, pltpu.VMEM((Z + 4, Y, X), jnp.float32)],
         )
 
-        def add_far(facts_ref, far_0, far_1, rim, _, out):
-            def add(i, far):
+        def add_far(facts_ref, far_0, far_1, rim, _, out, held, done):
+            copies = []
+            for i, far in ((0, far_0), (1, far_1)):
+                z = up_at(facts_ref, i) * (Z - 1)
                 for d in range(3):
-                    out[0, d, 0] = rim[i, d] + far[d] * SEVENTH**3
-
-            pl.when(pl.program_id(0) == 0)(lambda: add(0, far_0))
-            pl.when(pl.program_id(0) == 1)(lambda: add(1, far_1))
-
-        def boundary(i, facts_ref):
-            up = jnp.where(i == 0, facts_ref[3], 1 - facts_ref[3])
-            return (0, 0, up * (Z - 1), 0, 0)
+                    held[i, d] = rim[i, d] + far[d] * SEVENTH**3
+                    copies.append(pltpu.make_async_copy(held.at[i, d], out.at[0, d, z], done.at[i, d]))
+                    copies[-1].start()
+            for copy in copies:
+                copy.wait()
 
         gradient = call(
             add_far,
             struct(*flow.shape),
-            [whole(x) for x in (*far0, rim)] + [pl.BlockSpec(memory_space=pl.ANY)],
-            pl.BlockSpec((1, 3, 1, Y, X), boundary),
+            [SMEM] + [whole(x) for x in (*far0, rim)] + [pl.BlockSpec(memory_space=pl.ANY)],
+            pl.BlockSpec(memory_space=pl.ANY),
             [facts, *far0, rim, gradient],
             "add_far",
-            grid=(2,),
             aliases={4: 0},
-            prefetch=1,
+            scratch=[pltpu.VMEM((2, 3, Y, X), jnp.float32), pltpu.SemaphoreType.DMA((2, 3))],
         )
         return gradient[None], template_grad
 

time: 176 us -> 176 us (level)
  local copies, waits for them, and re-layouts: 8.67 us -> 12.4 us
  starting transfers between devices: 23.6 us -> 20.9 us
    ppermute x14 -> x12, starting transfers between devices: 23.4 us -> 20.7 us  [swap(): return lax.ppermute(x, 'slab', pairs[side])]
    unnamed x25 -> x27, local copies, waits for them, and re-layouts: 4.79 us -> 7.47 us
    ppermute x14 -> x12, waiting for transfers between devices: 97.3 us -> 96.5 us  [swap(): return lax.ppermute(x, 'slab', pairs[side])]
    pallas_call x8 -> x7, Pallas kernels: 42.1 us -> 42 us  [call(): pl.pallas_call(kernel, out_shape=out_shape, grid_spec=pltpu.PrefetchScala...]
  transfers between devices with their start and end apart: 17 -> 15, of which waited for: 12 -> 9; matrix products, arithmetic and copies ran while one was open for 2% -> 3% of each run, Pallas kernels for 23% -> 23%
where the time goes in v9:
time: 176 us
  waiting for transfers between devices  98.3 us (56%)
  Pallas kernels  42 us (24%)
  starting transfers between devices  20.9 us (12%)
  local copies, waits for them, and re-layouts  12.4 us (7%)
    ppermute x12, waiting for transfers between devices, swap(): return lax.ppermute(x, 'slab', pairs[side])  96.5 us
    pallas_call x7, Pallas kernels, call(): pl.pallas_call(kernel, out_shape=out_shape, grid_spec=pltpu.PrefetchScala...  42 us
    ppermute x12, starting transfers between devices, swap(): return lax.ppermute(x, 'slab', pairs[side])  20.7 us
    unnamed x27, local copies, waits for them, and re-layouts  7.47 us
  transfers between devices with their start and end apart: 15, of which 9 were waited for; matrix products, arithmetic and copies ran while one was open for 3% of the time, Pallas kernels for 23%

profile of v9, /device:TPU:2, one launch (start us, length us, event | category | flops | bytes accessed | tf_op | source)
XLA Modules:
  0.0 175.6 jit_solution(9009301237083169462)
XLA Ops:
  0.7 1.1 constant_dynamic-slice_fusion.1
  1.8 4.9 %collective-permute-start.1 = (f32[2,64,512]{2,1,0:T(8,128)S(1)}, f32[2,64,512]{2,1,0:T(8,128)S(1)}, u32[]{:S(2)}, u32[]{:S(2)}) collective-permute-start(f32[2,64,512]{2,1,0:T(8,128)S(1)} %get-tuple-element.61), channel_id=1, source_target_pairs={{1,2},{3,4},{5,6},{7,8},{9,10},{11,12},{13,14},{2,1},{4,3},{6,5},{... | collective-permute-start | bytes 786440 | tf_op jit(solution)/shard_map/ppermute | solution.py:105
  6.7 2.8 %dynamic-slice_bitcast_fusion = (f32[3,128,512]{2,1,0:T(8,128)}, f32[3,128,512]{2,1,0:T(8,128)}) fusion(f32[1,2,3,4,128,512]{5,4,3,2,1,0:T(8,128)} %param.5, s32[]{:T(128)S(6)} %select_n.29, s32[]{:T(128)S(6)} %select_n.28), kind=kLoop, calls=%fused_computation | loop fusion | bytes 3145736 | tf_op jit(solution)/shard_map/squeeze | solution.py:137
  9.5 1.9 %collective-permute-start.5 = (f32[3,128,512]{2,1,0:T(8,128)}, f32[3,128,512]{2,1,0:T(8,128)S(1)}, u32[]{:S(2)}, u32[]{:S(2)}) collective-permute-start(f32[3,128,512]{2,1,0:T(8,128)} %get-tuple-element.58), channel_id=1, source_target_pairs={{1,2},{3,4},{5,6},{7,8},{9,10},{11,12},{13,14},{2,1},{4,3},{6,5},{... | collective-permute-start | bytes 2359304 | tf_op jit(solution)/shard_map/ppermute | solution.py:105
  11.5 21.9 %collective-permute-done.2 = f32[2,64,512]{2,1,0:T(8,128)S(1)} collective-permute-done((f32[2,64,512]{2,1,0:T(8,128)S(1)}, f32[2,64,512]{2,1,0:T(8,128)S(1)}, u32[]{:S(2)}, u32[]{:S(2)}) %collective-permute-start.2) | collective-permute-done | bytes 262176 | tf_op jit(solution)/shard_map/ppermute | solution.py:105
  33.7 1.8 %collective-permute-done.3.refs_4_ = f32[4,64,512]{2,1,0:T(8,128)S(1)} collective-permute-done((f32[4,64,512]{2,1,0:T(8,128)S(1)}, f32[4,64,512]{2,1,0:T(8,128)S(1)}, u32[]{:S(2)}, u32[]{:S(2)}) %collective-permute-start.3) | collective-permute-done | bytes 524320 | tf_op jit(solution)/shard_map/ppermute | solution.py:108
  36.5 6.4 %forward.1 = (f32[8,128,512]{2,1,0:T(8,128)}, f32[4,128,512]{2,1,0:T(8,128)S(1)}, f32[2,128,512]{2,1,0:T(8,128)S(1)}, f32[3,128,512]{2,1,0:T(8,128)}, f32[3,128,512]{2,1,0:T(8,128)S(1)}) custom-call(s32[4]{0:T(128)S(1)} %pad_add_fusion.refs_0_.facts_ref, f32[4,64,512]{2,1,0:T(8,128)S(1)} %copy-done.1, f32[4,64,512]{2,1,0:T(8,128)S(1)} %collective-permute-done.refs_2_, ...), custom_call_target="tpu_custom_call" | custom-call | flops 1024 | bytes 1024 | tf_op jit(solution)/shard_map/forward/pallas_call | solution.py:66
  43.8 6.5 %collective-permute-done.4.halo0 = f32[3,128,512]{2,1,0:T(8,128)S(1)} collective-permute-done((f32[3,128,512]{2,1,0:T(8,128)}, f32[3,128,512]{2,1,0:T(8,128)S(1)}, u32[]{:S(2)}, u32[]{:S(2)}) %collective-permute-start.4) | collective-permute-done | bytes 786464 | tf_op jit(solution)/shard_map/ppermute | solution.py:105
  50.3 4.7 %middle.1 = (f32[3,128,512]{2,1,0:T(8,128)S(1)}, f32[3,128,512]{2,1,0:T(8,128)S(1)}, f32[2,128,512]{2,1,0:T(8,128)S(1)}, f32[2,3,128,512]{3,2,1,0:T(8,128)}) custom-call(s32[4]{0:T(128)S(1)} %pad_add_fusion.refs_0_.facts_ref, f32[8,128,512]{2,1,0:T(8,128)} %get-tuple-element.32.tmpl, f32[4,128,512]{2,1,0:T(8,128)S(1)} %get-tuple-element.34.img1, ...), custom_call_target="tpu_custom_call" | custom-call | flops 1024 | bytes 1024 | tf_op jit(solution)/shard_map/middle/pallas_call | solution.py:66
  56.8 3.5 %back.1 = (f32[4,128,512]{2,1,0:T(8,128)S(1)}, f32[2,128,512]{2,1,0:T(8,128)S(1)}, f32[2,128,512]{2,1,0:T(8,128)S(1)}) custom-call(s32[4]{0:T(128)S(1)} %pad_add_fusion.refs_0_.facts_ref, f32[2,128,512]{2,1,0:T(8,128)S(1)} %get-tuple-element.33.lam2_in, f32[2,128,512]{2,1,0:T(8,128)S(1)} %get-tuple-element.35.lam2_out, f32[2,3,4,128,512]{4,3,2,1,0:T(8,128)} %bitcast.16), custom_call_target="tpu_custom_call" | custom-call | flops 10000001024 | bytes 1024 | tf_op jit(solution)/shard_map/back/pallas_call | solution.py:66
  61.2 4.9 %collective-permute-start.8 = (f32[2,128,512]{2,1,0:T(8,128)S(1)}, f32[2,128,512]{2,1,0:T(8,128)}, u32[]{:S(2)}, u32[]{:S(2)}) collective-permute-start(f32[2,128,512]{2,1,0:T(8,128)S(1)} %get-tuple-element.38.own1), channel_id=1, source_target_pairs={{1,2},{3,4},{5,6},{7,8},{9,10},{11,12},{13,14},{2,1},{4,3},{6,5},{... | collective-permute-start | bytes 1572872 | tf_op jit(solution)/shard_map/ppermute | solution.py:105
  66.9 22.8 %collective-permute-done.7.far0 = f32[2,128,512]{2,1,0:T(8,128)} collective-permute-done((f32[2,128,512]{2,1,0:T(8,128)S(1)}, f32[2,128,512]{2,1,0:T(8,128)}, u32[]{:S(2)}, u32[]{:S(2)}) %collective-permute-start.7) | collective-permute-done | bytes 524320 | tf_op jit(solution)/shard_map/ppermute | solution.py:105
  90.7 1.0 copy-done.9
  91.7 8.6 %last.1 = (f32[4,128,512]{2,1,0:T(8,128)}, f32[3,128,512]{2,1,0:T(8,128)S(1)}, f32[3,128,512]{2,1,0:T(8,128)S(1)}, f32[3,128,512]{2,1,0:T(8,128)S(1)}, f32[3,128...) custom-call(s32[4]{0:T(128)S(1)} %pad_add_fusion.refs_0_.facts_ref, f32[8,128,512]{2,1,0:T(8,128)} %get-tuple-element.32.tmpl, ...), custom_call_target="tpu_custom_call" | custom-call | flops 20000002048 | bytes 1024 | tf_op jit(solution)/shard_map/last/pallas_call | solution.py:66
  100.3 1.1 constant_dynamic-slice_fusion
  101.6 1.9 %collective-permute-start.12 = (f32[3,128,512]{2,1,0:T(8,128)S(1)}, f32[3,128,512]{2,1,0:T(8,128)S(1)}, u32[]{:S(2)}, u32[]{:S(2)}) collective-permute-start(f32[3,128,512]{2,1,0:T(8,128)S(1)} %copy-done.7), channel_id=1, source_target_pairs={{1,2},{3,4},{5,6},{7,8},{9,10},{11,12},{13,14},{2,1},{4,3},{6,5},{... | collective-permute-start | bytes 2359304 | tf_op jit(solution)/shard_map/ppermute | solution.py:105
  103.5 5.0 %collective-permute-start.13 = (f32[3,128,512]{2,1,0:T(8,128)S(1)}, f32[3,128,512]{2,1,0:T(8,128)S(1)}, u32[]{:S(2)}, u32[]{:S(2)}) collective-permute-start(f32[3,128,512]{2,1,0:T(8,128)S(1)} %copy-done.3), channel_id=1, source_target_pairs={{1,2},{3,4},{5,6},{7,8},{9,10},{11,12},{13,14},{2,1},{4,3},{6,5},{... | collective-permute-start | bytes 2359304 | tf_op jit(solution)/shard_map/ppermute | solution.py:105
  108.5 8.6 %smooth_0.1 = (f32[2,3,4,128,512]{4,3,2,1,0:T(8,128)}, f32[2,3,128,512]{3,2,1,0:T(8,128)S(1)}) custom-call(s32[4]{0:T(128)S(1)} %pad_add_fusion.refs_0_.facts_ref, f32[3,128,512]{2,1,0:T(8,128)S(1)} %get-tuple-element.45.in0, f32[3,128,512]{2,1,0:T(8,128)S(1)} %get-tuple-element.46.in1, f32[3,128,512]{2,1,0:T(8,128)S(1)} %get-tuple-element.47.out0, ...), custom_call_target="tpu_custom_call" | custom-call | flops 10000001024 | bytes 1024 | tf_op jit(solution)/shard_map/smooth_0/pallas_call | solution.py:66
  117.1 1.9 %collective-permute-start.10 = (f32[3,128,512]{2,1,0:T(8,128)S(1)}, f32[3,128,512]{2,1,0:T(8,128)S(1)}, u32[]{:S(2)}, u32[]{:S(2)}) collective-permute-start(f32[3,128,512]{2,1,0:T(8,128)S(1)} %get-tuple-element.46.in1), channel_id=1, source_target_pairs={{1,2},{3,4},{5,6},{7,8},{9,10},{11,12},{13,14},{2,1},{4,3},{6,5},{... | collective-permute-start | bytes 2359304 | tf_op jit(solution)/shard_map/ppermute | solution.py:105
  119.9 21.2 %collective-permute-done.12.near1 = f32[3,128,512]{2,1,0:T(8,128)S(1)} collective-permute-done((f32[3,128,512]{2,1,0:T(8,128)S(1)}, f32[3,128,512]{2,1,0:T(8,128)S(1)}, u32[]{:S(2)}, u32[]{:S(2)}) %collective-permute-start.12) | collective-permute-done | bytes 786464 | tf_op jit(solution)/shard_map/ppermute | solution.py:105
  141.1 16.9 %collective-permute-done.13.far1 = f32[3,128,512]{2,1,0:T(8,128)S(1)} collective-permute-done((f32[3,128,512]{2,1,0:T(8,128)S(1)}, f32[3,128,512]{2,1,0:T(8,128)S(1)}, u32[]{:S(2)}, u32[]{:S(2)}) %collective-permute-start.13) | collective-permute-done | bytes 786464 | tf_op jit(solution)/shard_map/ppermute | solution.py:105
  158.9 8.5 %smooth_1.1._ = f32[2,3,4,128,512]{4,3,2,1,0:T(8,128)} custom-call(s32[4]{0:T(128)S(1)} %pad_add_fusion.refs_0_.facts_ref, f32[3,128,512]{2,1,0:T(8,128)} %get-tuple-element.41.in0, f32[3,128,512]{2,1,0:T(8,128)S(1)} %copy-done.3, f32[3,128,512]{2,1,0:T(8,128)S(1)} %copy-done.5, f32[3,128,512]{2,1,0:T(8,128)S(1)} %copy-done.7, ...), custom_call_target="tpu_custom_call", output_to_operand_aliasing={{}: (9, {})} | custom-call | flops 10000001024 | bytes 1024 | tf_op jit(solution)/shard_map/smooth_1/pallas_call | solution.py:66
  167.4 5.3 %collective-permute-done.9.far_0 = f32[3,128,512]{2,1,0:T(8,128)S(1)} collective-permute-done((f32[3,128,512]{2,1,0:T(8,128)S(1)}, f32[3,128,512]{2,1,0:T(8,128)S(1)}, u32[]{:S(2)}, u32[]{:S(2)}) %collective-permute-start.9) | collective-permute-done | bytes 786464 | tf_op jit(solution)/shard_map/ppermute | solution.py:105
  173.7 1.8 %add_far.1 = f32[2,3,4,128,512]{4,3,2,1,0:T(8,128)} custom-call(s32[4]{0:T(128)S(1)} %pad_add_fusion.refs_0_.facts_ref, f32[3,128,512]{2,1,0:T(8,128)S(1)} %collective-permute-done.9.far_0, f32[3,128,512]{2,1,0:T(8,128)S(1)} %collective-permute-done.10.far_1, f32[2,3,128,512]{3,2,1,0:T(8,128)S(1)} %get-tuple-element.50.rim, ...), custom_call_target="tpu_custom_call", output_to_operand_aliasing={{}: (4, {})} | custom-call | flops 1024 | bytes 1024 | tf_op jit(solution)/shard_map/add_far/pallas_call | solution.py:66
  (46 shorter events, 9.8 us)
Async XLA Ops:
  1.7 31.7 %collective-permute-start.2 = (f32[2,64,512]{2,1,0:T(8,128)S(1)}, f32[2,64,512]{2,1,0:T(8,128)S(1)}, u32[]{:S(2)}, u32[]{:S(2)}) collective-permute-start(f32[2,64,512]{2,1,0:T(8,128)S(1)} %get-tuple-element.60), channel_id=1, source_target_pairs={{0,1},{2,3},{4,5},{6,7},{8,9},{10,11},{12,13},{14,15},{1,0},{3,2},... | collective-permute-start | bytes 786440 | tf_op jit(solution)/shard_map/ppermute | solution.py:105
  1.8 31.7 %collective-permute-start.1 = (f32[2,64,512]{2,1,0:T(8,128)S(1)}, f32[2,64,512]{2,1,0:T(8,128)S(1)}, u32[]{:S(2)}, u32[]{:S(2)}) collective-permute-start(f32[2,64,512]{2,1,0:T(8,128)S(1)} %get-tuple-element.61), channel_id=1, source_target_pairs={{1,2},{3,4},{5,6},{7,8},{9,10},{11,12},{13,14},{2,1},{4,3},{6,5},{... | collective-permute-start | bytes 786440 | tf_op jit(solution)/shard_map/ppermute | solution.py:105
  9.5 34.4 %collective-permute-start.5 = (f32[3,128,512]{2,1,0:T(8,128)}, f32[3,128,512]{2,1,0:T(8,128)S(1)}, u32[]{:S(2)}, u32[]{:S(2)}) collective-permute-start(f32[3,128,512]{2,1,0:T(8,128)} %get-tuple-element.58), channel_id=1, source_target_pairs={{1,2},{3,4},{5,6},{7,8},{9,10},{11,12},{13,14},{2,1},{4,3},{6,5},{... | collective-permute-start | bytes 2359304 | tf_op jit(solution)/shard_map/ppermute | solution.py:105
  11.4 38.9 %collective-permute-start.4 = (f32[3,128,512]{2,1,0:T(8,128)}, f32[3,128,512]{2,1,0:T(8,128)S(1)}, u32[]{:S(2)}, u32[]{:S(2)}) collective-permute-start(f32[3,128,512]{2,1,0:T(8,128)} %get-tuple-element.59), channel_id=1, source_target_pairs={{0,1},{2,3},{4,5},{6,7},{8,9},{10,11},{12,13},{14,15},{1,0},{3,2},... | collective-permute-start | bytes 2359304 | tf_op jit(solution)/shard_map/ppermute | solution.py:105
  11.5 22.2 %collective-permute-start = (f32[4,64,512]{2,1,0:T(8,128)}, f32[4,64,512]{2,1,0:T(8,128)S(1)}, u32[]{:S(2)}, u32[]{:S(2)}) collective-permute-start(f32[4,64,512]{2,1,0:T(8,128)} %refs_1_.1), channel_id=1, source_target_pairs={{0,16},{16,0},{1,17},{17,1},{2,18},{18,2},{3,19},{19,3},{4,20},{20... | collective-permute-start | bytes 1572872 | tf_op jit(solution)/shard_map/ppermute | solution.py:108
  33.5 2.0 %collective-permute-start.3 = (f32[4,64,512]{2,1,0:T(8,128)S(1)}, f32[4,64,512]{2,1,0:T(8,128)S(1)}, u32[]{:S(2)}, u32[]{:S(2)}) collective-permute-start(f32[4,64,512]{2,1,0:T(8,128)S(1)} %constant_dynamic-update-slice_fusion.refs_3_), channel_id=1, source_target_pairs={{0,16},{16,0},{1,17},{17,1},{2,18},{18,2},{3,19},{19,3},{4,20},{20... | collective-permute-start | bytes 1572872 | tf_op jit(solution)/shard_map/ppermute | solution.py:108
  35.5 1.0 copy-start.1
  36.5 13.8 %copy-start = (f32[1,4,128,512]{3,2,1,0:T(8,128)S(1)}, f32[1,4,128,512]{3,2,1,0:T(8,128)}, u32[]{:S(2)}) copy-start(f32[1,4,128,512]{3,2,1,0:T(8,128)} %param.4) | copy-start | bytes 3145732
  42.9 0.9 copy-start.2
  43.8 46.9 %collective-permute-start.6 = (f32[3,128,512]{2,1,0:T(8,128)}, f32[3,128,512]{2,1,0:T(8,128)S(1)}, u32[]{:S(2)}, u32[]{:S(2)}) collective-permute-start(f32[3,128,512]{2,1,0:T(8,128)} %get-tuple-element.41.in0), channel_id=1, source_target_pairs={{0,1},{2,3},{4,5},{6,7},{8,9},{10,11},{12,13},{14,15},{1,0},{3,2},... | collective-permute-start | bytes 2359304 | tf_op jit(solution)/shard_map/ppermute | solution.py:105
  56.8 10.2 %copy-start.5 = (f32[3,128,512]{2,1,0:T(8,128)S(1)}, f32[3,128,512]{2,1,0:T(8,128)}, u32[]{:S(2)}) copy-start(f32[3,128,512]{2,1,0:T(8,128)} %copy-done.4) | copy-start | bytes 2359300
  60.3 1.0 copy-start.10
  61.2 28.5 %collective-permute-start.7 = (f32[2,128,512]{2,1,0:T(8,128)S(1)}, f32[2,128,512]{2,1,0:T(8,128)}, u32[]{:S(2)}, u32[]{:S(2)}) collective-permute-start(f32[2,128,512]{2,1,0:T(8,128)S(1)} %get-tuple-element.37.own0), channel_id=1, source_target_pairs={{0,1},{2,3},{4,5},{6,7},{8,9},{10,11},{12,13},{14,15},{1,0},{3,2},... | collective-permute-start | bytes 1572872 | tf_op jit(solution)/shard_map/ppermute | solution.py:105
  61.2 29.4 %collective-permute-start.8 = (f32[2,128,512]{2,1,0:T(8,128)S(1)}, f32[2,128,512]{2,1,0:T(8,128)}, u32[]{:S(2)}, u32[]{:S(2)}) collective-permute-start(f32[2,128,512]{2,1,0:T(8,128)S(1)} %get-tuple-element.38.own1), channel_id=1, source_target_pairs={{1,2},{3,4},{5,6},{7,8},{9,10},{11,12},{13,14},{2,1},{4,3},{6,5},{... | collective-permute-start | bytes 1572872 | tf_op jit(solution)/shard_map/ppermute | solution.py:105
  66.9 53.0 %collective-permute-start.11 = (f32[3,128,512]{2,1,0:T(8,128)S(1)}, f32[3,128,512]{2,1,0:T(8,128)S(1)}, u32[]{:S(2)}, u32[]{:S(2)}) collective-permute-start(f32[3,128,512]{2,1,0:T(8,128)S(1)} %copy-done.5), channel_id=1, source_target_pairs={{0,1},{2,3},{4,5},{6,7},{8,9},{10,11},{12,13},{14,15},{1,0},{3,2},... | collective-permute-start | bytes 2359304 | tf_op jit(solution)/shard_map/ppermute | solution.py:105
  90.7 1.0 copy-start.9
  91.7 9.8 %copy-start.7 = (f32[3,128,512]{2,1,0:T(8,128)S(1)}, f32[3,128,512]{2,1,0:T(8,128)}, u32[]{:S(2)}) copy-start(f32[3,128,512]{2,1,0:T(8,128)} %copy-done.6) | copy-start | bytes 2359300
  91.7 11.7 %copy-start.3 = (f32[3,128,512]{2,1,0:T(8,128)S(1)}, f32[3,128,512]{2,1,0:T(8,128)}, u32[]{:S(2)}) copy-start(f32[3,128,512]{2,1,0:T(8,128)} %copy-done.2) | copy-start | bytes 2359300
  101.4 15.7 %collective-permute-start.14 = (f32[4,64,512]{2,1,0:T(8,128)S(1)}, f32[4,64,512]{2,1,0:T(8,128)S(1)}, u32[]{:S(2)}, u32[]{:S(2)}) collective-permute-start(f32[4,64,512]{2,1,0:T(8,128)S(1)} %constant_dynamic-slice_fusion), channel_id=1, source_target_pairs={{0,16},{16,0},{1,17},{17,1},{2,18},{18,2},{3,19},{19,3},{4,20},{20... | collective-permute-start | bytes 1572872 | tf_op jit(solution)/shard_map/ppermute | solution.py:108
  101.5 71.3 %collective-permute-start.9 = (f32[3,128,512]{2,1,0:T(8,128)S(1)}, f32[3,128,512]{2,1,0:T(8,128)S(1)}, u32[]{:S(2)}, u32[]{:S(2)}) collective-permute-start(f32[3,128,512]{2,1,0:T(8,128)S(1)} %get-tuple-element.45.in0), channel_id=1, source_target_pairs={{0,1},{2,3},{4,5},{6,7},{8,9},{10,11},{12,13},{14,15},{1,0},{3,2},... | collective-permute-start | bytes 2359304 | tf_op jit(solution)/shard_map/ppermute | solution.py:105
  101.6 39.6 %collective-permute-start.12 = (f32[3,128,512]{2,1,0:T(8,128)S(1)}, f32[3,128,512]{2,1,0:T(8,128)S(1)}, u32[]{:S(2)}, u32[]{:S(2)}) collective-permute-start(f32[3,128,512]{2,1,0:T(8,128)S(1)} %copy-done.7), channel_id=1, source_target_pairs={{1,2},{3,4},{5,6},{7,8},{9,10},{11,12},{13,14},{2,1},{4,3},{6,5},{... | collective-permute-start | bytes 2359304 | tf_op jit(solution)/shard_map/ppermute | solution.py:105
  103.5 54.5 %collective-permute-start.13 = (f32[3,128,512]{2,1,0:T(8,128)S(1)}, f32[3,128,512]{2,1,0:T(8,128)S(1)}, u32[]{:S(2)}, u32[]{:S(2)}) collective-permute-start(f32[3,128,512]{2,1,0:T(8,128)S(1)} %copy-done.3), channel_id=1, source_target_pairs={{1,2},{3,4},{5,6},{7,8},{9,10},{11,12},{13,14},{2,1},{4,3},{6,5},{... | collective-permute-start | bytes 2359304 | tf_op jit(solution)/shard_map/ppermute | solution.py:105
  108.5 10.5 %copy-start.11 = (f32[4,128,512]{2,1,0:T(8,128)S(1)}, f32[4,128,512]{2,1,0:T(8,128)}, u32[]{:S(2)}) copy-start(f32[4,128,512]{2,1,0:T(8,128)} %get-tuple-element.57) | copy-start | bytes 3145732
  117.1 56.6 %collective-permute-start.10 = (f32[3,128,512]{2,1,0:T(8,128)S(1)}, f32[3,128,512]{2,1,0:T(8,128)S(1)}, u32[]{:S(2)}, u32[]{:S(2)}) collective-permute-start(f32[3,128,512]{2,1,0:T(8,128)S(1)} %get-tuple-element.46.in1), channel_id=1, source_target_pairs={{1,2},{3,4},{5,6},{7,8},{9,10},{11,12},{13,14},{2,1},{4,3},{6,5},{... | collective-permute-start | bytes 2359304 | tf_op jit(solution)/shard_map/ppermute | solution.py:105
  (4 other events, 3.5 us)

commit v10 on v9

--- a/solution.py
+++ b/solution.py
@@ -62,17 +62,14 @@
     return row_prev(f) + row_next(f) + col_prev(f) + col_next(f)
 
 
-def call(kernel, out_shape, in_specs, out_specs, operands, name, weight=0, grid=(1,), aliases=None, scratch=(), prefetch=0):
+def call(kernel, out_shape, in_specs, out_specs, operands, name, weight=0, grid=(), aliases=None, scratch=()):
     return pl.pallas_call(
         kernel,
         out_shape=out_shape,
-        grid_spec=pltpu.PrefetchScalarGridSpec(
-            num_scalar_prefetch=prefetch,
-            grid=grid,
-            in_specs=in_specs,
-            out_specs=out_specs,
-            scratch_shapes=list(scratch),
-        ),
+        grid=grid,
+        in_specs=in_specs,
+        out_specs=out_specs,
+        scratch_shapes=list(scratch),
         input_output_aliases=aliases or {},
         compiler_params=pltpu.CompilerParams(vmem_limit_bytes=48 * MIB),
         cost_estimate=pl.CostEstimate(
@@ -92,6 +89,7 @@
 
 
 SMEM = pl.BlockSpec(memory_space=pltpu.SMEM)
+VMEM = pl.BlockSpec(memory_space=pltpu.VMEM)
 SIDES = (0, 1)
 
 
@@ -181,6 +179,7 @@
             [whole(x) for x in outs],
             operands,
             "forward",
+            grid=(1,),
             weight=FORWARD,
         )
         far1 = [swap(inner1[0], 0), None]
@@ -215,6 +214,7 @@
             [whole(x) for x in outs],
             operands,
             "middle",
+            grid=(1,),
             weight=MIDDLE,
         )
         def back(facts_ref, lam2_in, lam2_out, v1, lam1, word0, word1, lam2):
@@ -243,6 +243,7 @@
             [whole(x) for x in outs],
             operands,
             "back",
+            grid=(1,),
             weight=BACK,
             scratch=[pltpu.VMEM((Z, Y, X), jnp.float32)],
         )
@@ -291,6 +292,7 @@
             [whole(x) for x in outs],
             operands,
             "last",
+            grid=(1,),
             weight=LAST,
             scratch=[pltpu.VMEM((Z + 2, Y, X), jnp.float32)],
         )
@@ -399,7 +401,7 @@
         gradient = call(
             add_far,
             struct(*flow.shape),
-            [SMEM] + [whole(x) for x in (*far0, rim)] + [pl.BlockSpec(memory_space=pl.ANY)],
+            [SMEM, VMEM, VMEM, VMEM, pl.BlockSpec(memory_space=pl.ANY)],
             pl.BlockSpec(memory_space=pl.ANY),
             [facts, *far0, rim, gradient],
             "add_far",

time: 176 us -> 176 us (level)
  no operation moved by 1% of the time
where the time goes in v10:
time: 176 us
  waiting for transfers between devices  98.3 us (56%)
  Pallas kernels  42 us (24%)
  starting transfers between devices  20.9 us (12%)
  local copies, waits for them, and re-layouts  12.4 us (7%)
    ppermute x12, waiting for transfers between devices, swap(): return lax.ppermute(x, 'slab', pairs[side])  96.5 us
    pallas_call x7, Pallas kernels, call(): pl.pallas_call(kernel, out_shape=out_shape, grid=grid, in_specs=in_specs,...  42 us
    ppermute x12, starting transfers between devices, swap(): return lax.ppermute(x, 'slab', pairs[side])  20.7 us
    unnamed x27, local copies, waits for them, and re-layouts  7.47 us
  transfers between devices with their start and end apart: 15, of which 9 were waited for; matrix products, arithmetic and copies ran while one was open for 3% of the time, Pallas kernels for 23%

profile of v10, /device:TPU:2, one launch (start us, length us, event | category | flops | bytes accessed | tf_op | source)
XLA Modules:
  0.0 175.6 jit_solution(9009301237083169462)
XLA Ops:
  0.7 1.1 constant_dynamic-slice_fusion.1
  1.8 4.9 %collective-permute-start.1 = (f32[2,64,512]{2,1,0:T(8,128)S(1)}, f32[2,64,512]{2,1,0:T(8,128)S(1)}, u32[]{:S(2)}, u32[]{:S(2)}) collective-permute-start(f32[2,64,512]{2,1,0:T(8,128)S(1)} %get-tuple-element.61), channel_id=1, source_target_pairs={{1,2},{3,4},{5,6},{7,8},{9,10},{11,12},{13,14},{2,1},{4,3},{6,5},{... | collective-permute-start | bytes 786440 | tf_op jit(solution)/shard_map/ppermute | solution.py:103
  6.7 2.8 %dynamic-slice_bitcast_fusion = (f32[3,128,512]{2,1,0:T(8,128)}, f32[3,128,512]{2,1,0:T(8,128)}) fusion(f32[1,2,3,4,128,512]{5,4,3,2,1,0:T(8,128)} %param.5, s32[]{:T(128)S(6)} %select_n.29, s32[]{:T(128)S(6)} %select_n.28), kind=kLoop, calls=%fused_computation | loop fusion | bytes 3145736 | tf_op jit(solution)/shard_map/squeeze | solution.py:135
  9.5 1.9 %collective-permute-start.5 = (f32[3,128,512]{2,1,0:T(8,128)}, f32[3,128,512]{2,1,0:T(8,128)S(1)}, u32[]{:S(2)}, u32[]{:S(2)}) collective-permute-start(f32[3,128,512]{2,1,0:T(8,128)} %get-tuple-element.58), channel_id=1, source_target_pairs={{1,2},{3,4},{5,6},{7,8},{9,10},{11,12},{13,14},{2,1},{4,3},{6,5},{... | collective-permute-start | bytes 2359304 | tf_op jit(solution)/shard_map/ppermute | solution.py:103
  11.5 21.9 %collective-permute-done.2 = f32[2,64,512]{2,1,0:T(8,128)S(1)} collective-permute-done((f32[2,64,512]{2,1,0:T(8,128)S(1)}, f32[2,64,512]{2,1,0:T(8,128)S(1)}, u32[]{:S(2)}, u32[]{:S(2)}) %collective-permute-start.2) | collective-permute-done | bytes 262176 | tf_op jit(solution)/shard_map/ppermute | solution.py:103
  33.7 1.8 %collective-permute-done.3.refs_4_ = f32[4,64,512]{2,1,0:T(8,128)S(1)} collective-permute-done((f32[4,64,512]{2,1,0:T(8,128)S(1)}, f32[4,64,512]{2,1,0:T(8,128)S(1)}, u32[]{:S(2)}, u32[]{:S(2)}) %collective-permute-start.3) | collective-permute-done | bytes 524320 | tf_op jit(solution)/shard_map/ppermute | solution.py:106
  36.5 6.4 %forward.1 = (f32[8,128,512]{2,1,0:T(8,128)}, f32[4,128,512]{2,1,0:T(8,128)S(1)}, f32[2,128,512]{2,1,0:T(8,128)S(1)}, f32[3,128,512]{2,1,0:T(8,128)}, f32[3,128,512]{2,1,0:T(8,128)S(1)}) custom-call(s32[4]{0:T(128)S(1)} %pad_add_fusion.refs_0_.facts_ref, f32[4,64,512]{2,1,0:T(8,128)S(1)} %copy-done.1, f32[4,64,512]{2,1,0:T(8,128)S(1)} %collective-permute-done.refs_2_, ...), custom_call_target="tpu_custom_call" | custom-call | flops 1024 | bytes 1024 | tf_op jit(solution)/shard_map/forward/pallas_call | solution.py:66
  43.8 6.5 %collective-permute-done.4.halo0 = f32[3,128,512]{2,1,0:T(8,128)S(1)} collective-permute-done((f32[3,128,512]{2,1,0:T(8,128)}, f32[3,128,512]{2,1,0:T(8,128)S(1)}, u32[]{:S(2)}, u32[]{:S(2)}) %collective-permute-start.4) | collective-permute-done | bytes 786464 | tf_op jit(solution)/shard_map/ppermute | solution.py:103
  50.3 4.7 %middle.1 = (f32[3,128,512]{2,1,0:T(8,128)S(1)}, f32[3,128,512]{2,1,0:T(8,128)S(1)}, f32[2,128,512]{2,1,0:T(8,128)S(1)}, f32[2,3,128,512]{3,2,1,0:T(8,128)}) custom-call(s32[4]{0:T(128)S(1)} %pad_add_fusion.refs_0_.facts_ref, f32[8,128,512]{2,1,0:T(8,128)} %get-tuple-element.32.tmpl, f32[4,128,512]{2,1,0:T(8,128)S(1)} %get-tuple-element.34.img1, ...), custom_call_target="tpu_custom_call" | custom-call | flops 1024 | bytes 1024 | tf_op jit(solution)/shard_map/middle/pallas_call | solution.py:66
  56.8 3.5 %back.1 = (f32[4,128,512]{2,1,0:T(8,128)S(1)}, f32[2,128,512]{2,1,0:T(8,128)S(1)}, f32[2,128,512]{2,1,0:T(8,128)S(1)}) custom-call(s32[4]{0:T(128)S(1)} %pad_add_fusion.refs_0_.facts_ref, f32[2,128,512]{2,1,0:T(8,128)S(1)} %get-tuple-element.33.lam2_in, f32[2,128,512]{2,1,0:T(8,128)S(1)} %get-tuple-element.35.lam2_out, f32[2,3,4,128,512]{4,3,2,1,0:T(8,128)} %bitcast.16), custom_call_target="tpu_custom_call" | custom-call | flops 10000001024 | bytes 1024 | tf_op jit(solution)/shard_map/back/pallas_call | solution.py:66
  61.2 4.9 %collective-permute-start.8 = (f32[2,128,512]{2,1,0:T(8,128)S(1)}, f32[2,128,512]{2,1,0:T(8,128)}, u32[]{:S(2)}, u32[]{:S(2)}) collective-permute-start(f32[2,128,512]{2,1,0:T(8,128)S(1)} %get-tuple-element.38.own1), channel_id=1, source_target_pairs={{1,2},{3,4},{5,6},{7,8},{9,10},{11,12},{13,14},{2,1},{4,3},{6,5},{... | collective-permute-start | bytes 1572872 | tf_op jit(solution)/shard_map/ppermute | solution.py:103
  66.9 22.8 %collective-permute-done.7.far0 = f32[2,128,512]{2,1,0:T(8,128)} collective-permute-done((f32[2,128,512]{2,1,0:T(8,128)S(1)}, f32[2,128,512]{2,1,0:T(8,128)}, u32[]{:S(2)}, u32[]{:S(2)}) %collective-permute-start.7) | collective-permute-done | bytes 524320 | tf_op jit(solution)/shard_map/ppermute | solution.py:103
  90.7 1.0 copy-done.9
  91.7 8.6 %last.1 = (f32[4,128,512]{2,1,0:T(8,128)}, f32[3,128,512]{2,1,0:T(8,128)S(1)}, f32[3,128,512]{2,1,0:T(8,128)S(1)}, f32[3,128,512]{2,1,0:T(8,128)S(1)}, f32[3,128...) custom-call(s32[4]{0:T(128)S(1)} %pad_add_fusion.refs_0_.facts_ref, f32[8,128,512]{2,1,0:T(8,128)} %get-tuple-element.32.tmpl, ...), custom_call_target="tpu_custom_call" | custom-call | flops 20000002048 | bytes 1024 | tf_op jit(solution)/shard_map/last/pallas_call | solution.py:66
  100.3 1.1 constant_dynamic-slice_fusion
  101.6 1.9 %collective-permute-start.12 = (f32[3,128,512]{2,1,0:T(8,128)S(1)}, f32[3,128,512]{2,1,0:T(8,128)S(1)}, u32[]{:S(2)}, u32[]{:S(2)}) collective-permute-start(f32[3,128,512]{2,1,0:T(8,128)S(1)} %copy-done.7), channel_id=1, source_target_pairs={{1,2},{3,4},{5,6},{7,8},{9,10},{11,12},{13,14},{2,1},{4,3},{6,5},{... | collective-permute-start | bytes 2359304 | tf_op jit(solution)/shard_map/ppermute | solution.py:103
  103.5 5.0 %collective-permute-start.13 = (f32[3,128,512]{2,1,0:T(8,128)S(1)}, f32[3,128,512]{2,1,0:T(8,128)S(1)}, u32[]{:S(2)}, u32[]{:S(2)}) collective-permute-start(f32[3,128,512]{2,1,0:T(8,128)S(1)} %copy-done.3), channel_id=1, source_target_pairs={{1,2},{3,4},{5,6},{7,8},{9,10},{11,12},{13,14},{2,1},{4,3},{6,5},{... | collective-permute-start | bytes 2359304 | tf_op jit(solution)/shard_map/ppermute | solution.py:103
  108.5 8.6 %smooth_0.1 = (f32[2,3,4,128,512]{4,3,2,1,0:T(8,128)}, f32[2,3,128,512]{3,2,1,0:T(8,128)S(1)}) custom-call(s32[4]{0:T(128)S(1)} %pad_add_fusion.refs_0_.facts_ref, f32[3,128,512]{2,1,0:T(8,128)S(1)} %get-tuple-element.45.in0, f32[3,128,512]{2,1,0:T(8,128)S(1)} %get-tuple-element.46.in1, f32[3,128,512]{2,1,0:T(8,128)S(1)} %get-tuple-element.47.out0, ...), custom_call_target="tpu_custom_call" | custom-call | flops 10000001024 | bytes 1024 | tf_op jit(solution)/shard_map/smooth_0/pallas_call | solution.py:66
  117.1 1.9 %collective-permute-start.10 = (f32[3,128,512]{2,1,0:T(8,128)S(1)}, f32[3,128,512]{2,1,0:T(8,128)S(1)}, u32[]{:S(2)}, u32[]{:S(2)}) collective-permute-start(f32[3,128,512]{2,1,0:T(8,128)S(1)} %get-tuple-element.46.in1), channel_id=1, source_target_pairs={{1,2},{3,4},{5,6},{7,8},{9,10},{11,12},{13,14},{2,1},{4,3},{6,5},{... | collective-permute-start | bytes 2359304 | tf_op jit(solution)/shard_map/ppermute | solution.py:103
  119.9 21.2 %collective-permute-done.12.near1 = f32[3,128,512]{2,1,0:T(8,128)S(1)} collective-permute-done((f32[3,128,512]{2,1,0:T(8,128)S(1)}, f32[3,128,512]{2,1,0:T(8,128)S(1)}, u32[]{:S(2)}, u32[]{:S(2)}) %collective-permute-start.12) | collective-permute-done | bytes 786464 | tf_op jit(solution)/shard_map/ppermute | solution.py:103
  141.1 16.9 %collective-permute-done.13.far1 = f32[3,128,512]{2,1,0:T(8,128)S(1)} collective-permute-done((f32[3,128,512]{2,1,0:T(8,128)S(1)}, f32[3,128,512]{2,1,0:T(8,128)S(1)}, u32[]{:S(2)}, u32[]{:S(2)}) %collective-permute-start.13) | collective-permute-done | bytes 786464 | tf_op jit(solution)/shard_map/ppermute | solution.py:103
  158.9 8.5 %smooth_1.1._ = f32[2,3,4,128,512]{4,3,2,1,0:T(8,128)} custom-call(s32[4]{0:T(128)S(1)} %pad_add_fusion.refs_0_.facts_ref, f32[3,128,512]{2,1,0:T(8,128)} %get-tuple-element.41.in0, f32[3,128,512]{2,1,0:T(8,128)S(1)} %copy-done.3, f32[3,128,512]{2,1,0:T(8,128)S(1)} %copy-done.5, f32[3,128,512]{2,1,0:T(8,128)S(1)} %copy-done.7, ...), custom_call_target="tpu_custom_call", output_to_operand_aliasing={{}: (9, {})} | custom-call | flops 10000001024 | bytes 1024 | tf_op jit(solution)/shard_map/smooth_1/pallas_call | solution.py:66
  167.4 5.3 %collective-permute-done.9.far_0 = f32[3,128,512]{2,1,0:T(8,128)S(1)} collective-permute-done((f32[3,128,512]{2,1,0:T(8,128)S(1)}, f32[3,128,512]{2,1,0:T(8,128)S(1)}, u32[]{:S(2)}, u32[]{:S(2)}) %collective-permute-start.9) | collective-permute-done | bytes 786464 | tf_op jit(solution)/shard_map/ppermute | solution.py:103
  173.7 1.8 %add_far.1 = f32[2,3,4,128,512]{4,3,2,1,0:T(8,128)} custom-call(s32[4]{0:T(128)S(1)} %pad_add_fusion.refs_0_.facts_ref, f32[3,128,512]{2,1,0:T(8,128)S(1)} %collective-permute-done.9.far_0, f32[3,128,512]{2,1,0:T(8,128)S(1)} %collective-permute-done.10.far_1, f32[2,3,128,512]{3,2,1,0:T(8,128)S(1)} %get-tuple-element.50.rim, ...), custom_call_target="tpu_custom_call", output_to_operand_aliasing={{}: (4, {})} | custom-call | flops 1024 | bytes 1024 | tf_op jit(solution)/shard_map/add_far/pallas_call | solution.py:66
  (46 shorter events, 9.8 us)
Async XLA Ops:
  1.7 31.7 %collective-permute-start.2 = (f32[2,64,512]{2,1,0:T(8,128)S(1)}, f32[2,64,512]{2,1,0:T(8,128)S(1)}, u32[]{:S(2)}, u32[]{:S(2)}) collective-permute-start(f32[2,64,512]{2,1,0:T(8,128)S(1)} %get-tuple-element.60), channel_id=1, source_target_pairs={{0,1},{2,3},{4,5},{6,7},{8,9},{10,11},{12,13},{14,15},{1,0},{3,2},... | collective-permute-start | bytes 786440 | tf_op jit(solution)/shard_map/ppermute | solution.py:103
  1.8 31.7 %collective-permute-start.1 = (f32[2,64,512]{2,1,0:T(8,128)S(1)}, f32[2,64,512]{2,1,0:T(8,128)S(1)}, u32[]{:S(2)}, u32[]{:S(2)}) collective-permute-start(f32[2,64,512]{2,1,0:T(8,128)S(1)} %get-tuple-element.61), channel_id=1, source_target_pairs={{1,2},{3,4},{5,6},{7,8},{9,10},{11,12},{13,14},{2,1},{4,3},{6,5},{... | collective-permute-start | bytes 786440 | tf_op jit(solution)/shard_map/ppermute | solution.py:103
  9.5 34.4 %collective-permute-start.5 = (f32[3,128,512]{2,1,0:T(8,128)}, f32[3,128,512]{2,1,0:T(8,128)S(1)}, u32[]{:S(2)}, u32[]{:S(2)}) collective-permute-start(f32[3,128,512]{2,1,0:T(8,128)} %get-tuple-element.58), channel_id=1, source_target_pairs={{1,2},{3,4},{5,6},{7,8},{9,10},{11,12},{13,14},{2,1},{4,3},{6,5},{... | collective-permute-start | bytes 2359304 | tf_op jit(solution)/shard_map/ppermute | solution.py:103
  11.4 38.9 %collective-permute-start.4 = (f32[3,128,512]{2,1,0:T(8,128)}, f32[3,128,512]{2,1,0:T(8,128)S(1)}, u32[]{:S(2)}, u32[]{:S(2)}) collective-permute-start(f32[3,128,512]{2,1,0:T(8,128)} %get-tuple-element.59), channel_id=1, source_target_pairs={{0,1},{2,3},{4,5},{6,7},{8,9},{10,11},{12,13},{14,15},{1,0},{3,2},... | collective-permute-start | bytes 2359304 | tf_op jit(solution)/shard_map/ppermute | solution.py:103
  11.5 22.2 %collective-permute-start = (f32[4,64,512]{2,1,0:T(8,128)}, f32[4,64,512]{2,1,0:T(8,128)S(1)}, u32[]{:S(2)}, u32[]{:S(2)}) collective-permute-start(f32[4,64,512]{2,1,0:T(8,128)} %refs_1_.1), channel_id=1, source_target_pairs={{0,16},{16,0},{1,17},{17,1},{2,18},{18,2},{3,19},{19,3},{4,20},{20... | collective-permute-start | bytes 1572872 | tf_op jit(solution)/shard_map/ppermute | solution.py:106
  33.5 2.0 %collective-permute-start.3 = (f32[4,64,512]{2,1,0:T(8,128)S(1)}, f32[4,64,512]{2,1,0:T(8,128)S(1)}, u32[]{:S(2)}, u32[]{:S(2)}) collective-permute-start(f32[4,64,512]{2,1,0:T(8,128)S(1)} %constant_dynamic-update-slice_fusion.refs_3_), channel_id=1, source_target_pairs={{0,16},{16,0},{1,17},{17,1},{2,18},{18,2},{3,19},{19,3},{4,20},{20... | collective-permute-start | bytes 1572872 | tf_op jit(solution)/shard_map/ppermute | solution.py:106
  35.5 1.0 copy-start.1
  36.5 13.8 %copy-start = (f32[1,4,128,512]{3,2,1,0:T(8,128)S(1)}, f32[1,4,128,512]{3,2,1,0:T(8,128)}, u32[]{:S(2)}) copy-start(f32[1,4,128,512]{3,2,1,0:T(8,128)} %param.4) | copy-start | bytes 3145732
  42.9 0.9 copy-start.2
  43.8 46.9 %collective-permute-start.6 = (f32[3,128,512]{2,1,0:T(8,128)}, f32[3,128,512]{2,1,0:T(8,128)S(1)}, u32[]{:S(2)}, u32[]{:S(2)}) collective-permute-start(f32[3,128,512]{2,1,0:T(8,128)} %get-tuple-element.41.in0), channel_id=1, source_target_pairs={{0,1},{2,3},{4,5},{6,7},{8,9},{10,11},{12,13},{14,15},{1,0},{3,2},... | collective-permute-start | bytes 2359304 | tf_op jit(solution)/shard_map/ppermute | solution.py:103
  56.8 10.2 %copy-start.5 = (f32[3,128,512]{2,1,0:T(8,128)S(1)}, f32[3,128,512]{2,1,0:T(8,128)}, u32[]{:S(2)}) copy-start(f32[3,128,512]{2,1,0:T(8,128)} %copy-done.4) | copy-start | bytes 2359300
  60.3 1.0 copy-start.10
  61.2 28.5 %collective-permute-start.7 = (f32[2,128,512]{2,1,0:T(8,128)S(1)}, f32[2,128,512]{2,1,0:T(8,128)}, u32[]{:S(2)}, u32[]{:S(2)}) collective-permute-start(f32[2,128,512]{2,1,0:T(8,128)S(1)} %get-tuple-element.37.own0), channel_id=1, source_target_pairs={{0,1},{2,3},{4,5},{6,7},{8,9},{10,11},{12,13},{14,15},{1,0},{3,2},... | collective-permute-start | bytes 1572872 | tf_op jit(solution)/shard_map/ppermute | solution.py:103
  61.2 29.4 %collective-permute-start.8 = (f32[2,128,512]{2,1,0:T(8,128)S(1)}, f32[2,128,512]{2,1,0:T(8,128)}, u32[]{:S(2)}, u32[]{:S(2)}) collective-permute-start(f32[2,128,512]{2,1,0:T(8,128)S(1)} %get-tuple-element.38.own1), channel_id=1, source_target_pairs={{1,2},{3,4},{5,6},{7,8},{9,10},{11,12},{13,14},{2,1},{4,3},{6,5},{... | collective-permute-start | bytes 1572872 | tf_op jit(solution)/shard_map/ppermute | solution.py:103
  66.9 53.0 %collective-permute-start.11 = (f32[3,128,512]{2,1,0:T(8,128)S(1)}, f32[3,128,512]{2,1,0:T(8,128)S(1)}, u32[]{:S(2)}, u32[]{:S(2)}) collective-permute-start(f32[3,128,512]{2,1,0:T(8,128)S(1)} %copy-done.5), channel_id=1, source_target_pairs={{0,1},{2,3},{4,5},{6,7},{8,9},{10,11},{12,13},{14,15},{1,0},{3,2},... | collective-permute-start | bytes 2359304 | tf_op jit(solution)/shard_map/ppermute | solution.py:103
  90.7 1.0 copy-start.9
  91.7 9.8 %copy-start.7 = (f32[3,128,512]{2,1,0:T(8,128)S(1)}, f32[3,128,512]{2,1,0:T(8,128)}, u32[]{:S(2)}) copy-start(f32[3,128,512]{2,1,0:T(8,128)} %copy-done.6) | copy-start | bytes 2359300
  91.7 11.7 %copy-start.3 = (f32[3,128,512]{2,1,0:T(8,128)S(1)}, f32[3,128,512]{2,1,0:T(8,128)}, u32[]{:S(2)}) copy-start(f32[3,128,512]{2,1,0:T(8,128)} %copy-done.2) | copy-start | bytes 2359300
  101.4 15.7 %collective-permute-start.14 = (f32[4,64,512]{2,1,0:T(8,128)S(1)}, f32[4,64,512]{2,1,0:T(8,128)S(1)}, u32[]{:S(2)}, u32[]{:S(2)}) collective-permute-start(f32[4,64,512]{2,1,0:T(8,128)S(1)} %constant_dynamic-slice_fusion), channel_id=1, source_target_pairs={{0,16},{16,0},{1,17},{17,1},{2,18},{18,2},{3,19},{19,3},{4,20},{20... | collective-permute-start | bytes 1572872 | tf_op jit(solution)/shard_map/ppermute | solution.py:106
  101.5 71.3 %collective-permute-start.9 = (f32[3,128,512]{2,1,0:T(8,128)S(1)}, f32[3,128,512]{2,1,0:T(8,128)S(1)}, u32[]{:S(2)}, u32[]{:S(2)}) collective-permute-start(f32[3,128,512]{2,1,0:T(8,128)S(1)} %get-tuple-element.45.in0), channel_id=1, source_target_pairs={{0,1},{2,3},{4,5},{6,7},{8,9},{10,11},{12,13},{14,15},{1,0},{3,2},... | collective-permute-start | bytes 2359304 | tf_op jit(solution)/shard_map/ppermute | solution.py:103
  101.6 39.6 %collective-permute-start.12 = (f32[3,128,512]{2,1,0:T(8,128)S(1)}, f32[3,128,512]{2,1,0:T(8,128)S(1)}, u32[]{:S(2)}, u32[]{:S(2)}) collective-permute-start(f32[3,128,512]{2,1,0:T(8,128)S(1)} %copy-done.7), channel_id=1, source_target_pairs={{1,2},{3,4},{5,6},{7,8},{9,10},{11,12},{13,14},{2,1},{4,3},{6,5},{... | collective-permute-start | bytes 2359304 | tf_op jit(solution)/shard_map/ppermute | solution.py:103
  103.5 54.5 %collective-permute-start.13 = (f32[3,128,512]{2,1,0:T(8,128)S(1)}, f32[3,128,512]{2,1,0:T(8,128)S(1)}, u32[]{:S(2)}, u32[]{:S(2)}) collective-permute-start(f32[3,128,512]{2,1,0:T(8,128)S(1)} %copy-done.3), channel_id=1, source_target_pairs={{1,2},{3,4},{5,6},{7,8},{9,10},{11,12},{13,14},{2,1},{4,3},{6,5},{... | collective-permute-start | bytes 2359304 | tf_op jit(solution)/shard_map/ppermute | solution.py:103
  108.5 10.5 %copy-start.11 = (f32[4,128,512]{2,1,0:T(8,128)S(1)}, f32[4,128,512]{2,1,0:T(8,128)}, u32[]{:S(2)}) copy-start(f32[4,128,512]{2,1,0:T(8,128)} %get-tuple-element.57) | copy-start | bytes 3145732
  117.1 56.6 %collective-permute-start.10 = (f32[3,128,512]{2,1,0:T(8,128)S(1)}, f32[3,128,512]{2,1,0:T(8,128)S(1)}, u32[]{:S(2)}, u32[]{:S(2)}) collective-permute-start(f32[3,128,512]{2,1,0:T(8,128)S(1)} %get-tuple-element.46.in1), channel_id=1, source_target_pairs={{1,2},{3,4},{5,6},{7,8},{9,10},{11,12},{13,14},{2,1},{4,3},{6,5},{... | collective-permute-start | bytes 2359304 | tf_op jit(solution)/shard_map/ppermute | solution.py:103
  (4 other events, 3.5 us)

commit v11 on v9

--- a/solution.py
+++ b/solution.py
@@ -8,7 +8,7 @@
 MATCH = 5.0
 SEVENTH = 1.0 / 7.0
 MIB = 1 << 20
-FORWARD, MIDDLE, BACK, LAST, SMOOTH = 0, 0, 1000, 2000, 1000
+FORWARD, MIDDLE, BACK, INSIDE, LAST, SMOOTH = 0, 0, 1000, 0, 2000, 1000
 
 
 def col_prev(f):
@@ -247,12 +247,33 @@
             scratch=[pltpu.VMEM((Z, Y, X), jnp.float32)],
         )
         words_far = [swap(words[i], i) for i in SIDES]
-        near1 = [swap(after(outer1[0], *words)[0], 0), None]
+        near1 = [swap(outer1[0], 0), None]
+
+        def inside(facts_ref, tmpl, lam1, v0, src0, src1):
+            for i, src in ((0, src0), (1, src1)):
+                z = 1 + up_at(facts_ref, i) * (Z - 3)
+                v = [v0[0, d, z] for d in range(3)]
+                diffs = upwind(tmpl[z + 1], tmpl[z + 2], tmpl[z + 3], v)
+                for d in range(3):
+                    src[d] = (-MATCH * dt) * lam1[z] * diffs[d]
+
+        outs = [struct(3, Y, X)] * 2
+        held = after(lam1_part, *words)[0]
+        inner0 = call(
+            inside,
+            outs,
+            [SMEM, whole(tmpl), whole(held), flow_spec[0]],
+            [whole(x) for x in outs],
+            [facts, tmpl, held, flow],
+            "inside",
+            weight=INSIDE,
+        )
+        far0 = [swap(inner0[0], 0), None]
 
         held, far1[0], *words_far = after((inner1[1], outer1[1]), far1[0], *words_far)
         far1[1], near1[1] = [swap(x, 1) for x in held]
 
-        def last(facts_ref, tmpl, part, own0, own1, far0, far1, v0_far, v0, lam0, src0, src1, out0, out1, near, lam):
+        def last(facts_ref, tmpl, part, own0, own1, far0, far1, v0_far, v0, lam0, out0, out1, near, lam):
             for z in range(1, Z - 1):
                 lam[z + 1] = part[z]
             for i, own, far in ((0, own0, far0), (1, own1, far1)):
@@ -270,10 +291,9 @@
                 for d in range(3):
                     src[(*at, d)] = (-MATCH * dt) * lam[z + 1] * diffs[d]
 
-            for i, inner, outer in ((0, src0, out0), (1, src1, out1)):
-                up = up_at(facts_ref, i)
-                for z, src in ((1 + up * (Z - 3), inner), (up * (Z - 1), outer)):
-                    source(z, [v0[0, d, z] for d in range(3)], src)
+            for i, outer in ((0, out0), (1, out1)):
+                z = up_at(facts_ref, i) * (Z - 1)
+                source(z, [v0[0, d, z] for d in range(3)], outer)
             for j, z in enumerate((-1, Z)):
                 source(z, [flow_at(z, d) for d in range(3)], near, j)
             for z in range(Z):
@@ -282,9 +302,9 @@
                 v = [flow_at(z, d) for d in range(3)]
                 lam0[z] = retreat(lam[z + 1], v, above, below, dt)
 
-        outs = [struct(Z, Y, X)] + [struct(3, Y, X)] * 4 + [struct(2, 3, Y, X)]
+        outs = [struct(Z, Y, X)] + [struct(3, Y, X)] * 2 + [struct(2, 3, Y, X)]
         operands = [facts, tmpl, lam1_part, *words, *words_far, v0_far, flow]
-        lam0, *inner_outer, near0 = call(
+        lam0, *outer0, near0 = call(
             last,
             outs,
             [SMEM] + [whole(x) for x in operands[1:8]] + [flow_spec[0]],
@@ -294,8 +314,8 @@
             weight=LAST,
             scratch=[pltpu.VMEM((Z + 2, Y, X), jnp.float32)],
         )
-        inner0, outer0 = inner_outer[:2], inner_outer[2:]
-        far0 = [swap(inner0[i], i) for i in SIDES]
+        held, lam0 = after(inner0[1], lam0)
+        far0[1] = swap(held, 1)
 
         def sweeps(facts_ref, s, v, out, u2):
             for z in range(-1, Z + 1):

time: 176 us -> 176 us (level)
  local copies, waits for them, and re-layouts: 12.4 us -> 6.8 us
  Pallas kernels: 42 us -> 44.9 us
  starting transfers between devices: 20.9 us -> 23 us
    unnamed x27 -> x21, local copies, waits for them, and re-layouts: 7.47 us -> 2.9 us
    pallas_call x7 -> x8, Pallas kernels: 42 us -> 44.9 us  [call(): pl.pallas_call(kernel, out_shape=out_shape, grid_spec=pltpu.PrefetchScala...]
    ppermute x12, starting transfers between devices: 20.7 us -> 22.8 us  [swap(): return lax.ppermute(x, 'slab', pairs[side])]
  transfers between devices with their start and end apart: 15 -> 15, of which waited for: 9 -> 9; matrix products, arithmetic and copies ran while one was open for 3% -> 2% of each run, Pallas kernels for 23% -> 25%
where the time goes in v11:
time: 176 us
  waiting for transfers between devices  99 us (56%)
  Pallas kernels  44.9 us (26%)
  starting transfers between devices  23 us (13%)
  local copies, waits for them, and re-layouts  6.8 us (4%)
    ppermute x12, waiting for transfers between devices, swap(): return lax.ppermute(x, 'slab', pairs[side])  97.2 us
    pallas_call x8, Pallas kernels, call(): pl.pallas_call(kernel, out_shape=out_shape, grid_spec=pltpu.PrefetchScala...  44.9 us
    ppermute x12, starting transfers between devices, swap(): return lax.ppermute(x, 'slab', pairs[side])  22.8 us
  transfers between devices with their start and end apart: 15, of which 9 were waited for; matrix products, arithmetic and copies ran while one was open for 2% of the time, Pallas kernels for 25%

profile of v11, /device:TPU:2, one launch (start us, length us, event | category | flops | bytes accessed | tf_op | source)
XLA Modules:
  0.0 175.6 jit_solution(13051767613042376864)
XLA Ops:
  0.7 1.1 constant_dynamic-slice_fusion.1
  1.8 4.9 %collective-permute-start.1 = (f32[2,64,512]{2,1,0:T(8,128)S(1)}, f32[2,64,512]{2,1,0:T(8,128)S(1)}, u32[]{:S(2)}, u32[]{:S(2)}) collective-permute-start(f32[2,64,512]{2,1,0:T(8,128)S(1)} %get-tuple-element.64), channel_id=1, source_target_pairs={{1,2},{3,4},{5,6},{7,8},{9,10},{11,12},{13,14},{2,1},{4,3},{6,5},{... | collective-permute-start | bytes 786440 | tf_op jit(solution)/shard_map/ppermute | solution.py:105
  6.7 2.8 %dynamic-slice_bitcast_fusion = (f32[3,128,512]{2,1,0:T(8,128)}, f32[3,128,512]{2,1,0:T(8,128)}) fusion(f32[1,2,3,4,128,512]{5,4,3,2,1,0:T(8,128)} %param.5, s32[]{:T(128)S(6)} %select_n.29, s32[]{:T(128)S(6)} %select_n.28), kind=kLoop, calls=%fused_computation | loop fusion | bytes 3145736 | tf_op jit(solution)/shard_map/squeeze | solution.py:137
  9.5 1.9 %collective-permute-start.5 = (f32[3,128,512]{2,1,0:T(8,128)}, f32[3,128,512]{2,1,0:T(8,128)S(1)}, u32[]{:S(2)}, u32[]{:S(2)}) collective-permute-start(f32[3,128,512]{2,1,0:T(8,128)} %get-tuple-element.61), channel_id=1, source_target_pairs={{1,2},{3,4},{5,6},{7,8},{9,10},{11,12},{13,14},{2,1},{4,3},{6,5},{... | collective-permute-start | bytes 2359304 | tf_op jit(solution)/shard_map/ppermute | solution.py:105
  11.6 21.9 %collective-permute-done.2 = f32[2,64,512]{2,1,0:T(8,128)S(1)} collective-permute-done((f32[2,64,512]{2,1,0:T(8,128)S(1)}, f32[2,64,512]{2,1,0:T(8,128)S(1)}, u32[]{:S(2)}, u32[]{:S(2)}) %collective-permute-start.2) | collective-permute-done | bytes 262176 | tf_op jit(solution)/shard_map/ppermute | solution.py:105
  33.7 1.8 %collective-permute-done.3.refs_4_ = f32[4,64,512]{2,1,0:T(8,128)S(1)} collective-permute-done((f32[4,64,512]{2,1,0:T(8,128)S(1)}, f32[4,64,512]{2,1,0:T(8,128)S(1)}, u32[]{:S(2)}, u32[]{:S(2)}) %collective-permute-start.3) | collective-permute-done | bytes 524320 | tf_op jit(solution)/shard_map/ppermute | solution.py:108
  35.5 1.0 copy-done.2
  36.5 6.3 %forward.1 = (f32[8,128,512]{2,1,0:T(8,128)}, f32[4,128,512]{2,1,0:T(8,128)S(1)}, f32[2,128,512]{2,1,0:T(8,128)S(1)}, f32[3,128,512]{2,1,0:T(8,128)}, f32[3,128,512]{2,1,0:T(8,128)S(1)}) custom-call(s32[4]{0:T(128)S(1)} %pad_add_fusion.refs_0_.facts_ref, f32[4,64,512]{2,1,0:T(8,128)S(1)} %copy-done.2, f32[4,64,512]{2,1,0:T(8,128)S(1)} %collective-permute-done.refs_2_, ...), custom_call_target="tpu_custom_call" | custom-call | flops 1024 | bytes 1024 | tf_op jit(solution)/shard_map/forward/pallas_call | solution.py:66
  43.8 6.5 %collective-permute-done.4.halo0 = f32[3,128,512]{2,1,0:T(8,128)S(1)} collective-permute-done((f32[3,128,512]{2,1,0:T(8,128)}, f32[3,128,512]{2,1,0:T(8,128)S(1)}, u32[]{:S(2)}, u32[]{:S(2)}) %collective-permute-start.4) | collective-permute-done | bytes 786464 | tf_op jit(solution)/shard_map/ppermute | solution.py:105
  50.3 4.7 %middle.1 = (f32[3,128,512]{2,1,0:T(8,128)S(1)}, f32[3,128,512]{2,1,0:T(8,128)S(1)}, f32[2,128,512]{2,1,0:T(8,128)S(1)}, f32[2,3,128,512]{3,2,1,0:T(8,128)}) custom-call(s32[4]{0:T(128)S(1)} %pad_add_fusion.refs_0_.facts_ref, f32[8,128,512]{2,1,0:T(8,128)} %get-tuple-element.34.tmpl, f32[4,128,512]{2,1,0:T(8,128)S(1)} %get-tuple-element.36.img1, ...), custom_call_target="tpu_custom_call" | custom-call | flops 1024 | bytes 1024 | tf_op jit(solution)/shard_map/middle/pallas_call | solution.py:66
  55.0 5.0 %back.1 = (f32[4,128,512]{2,1,0:T(8,128)S(1)}, f32[2,128,512]{2,1,0:T(8,128)}, f32[2,128,512]{2,1,0:T(8,128)}) custom-call(s32[4]{0:T(128)S(1)} %pad_add_fusion.refs_0_.facts_ref, f32[2,128,512]{2,1,0:T(8,128)S(1)} %get-tuple-element.35.lam2_in, f32[2,128,512]{2,1,0:T(8,128)S(1)} %get-tuple-element.37.lam2_out, f32[2,3,4,128,512]{4,3,2,1,0:T(8,128)} %bitcast.16), custom_call_target="tpu_custom_call" | custom-call | flops 10000001024 | bytes 1024 | tf_op jit(solution)/shard_map/back/pallas_call | solution.py:66
  59.9 4.9 %collective-permute-start.9 = (f32[2,128,512]{2,1,0:T(8,128)}, f32[2,128,512]{2,1,0:T(8,128)}, u32[]{:S(2)}, u32[]{:S(2)}) collective-permute-start(f32[2,128,512]{2,1,0:T(8,128)} %get-tuple-element.42.own1), channel_id=1, source_target_pairs={{1,2},{3,4},{5,6},{7,8},{9,10},{11,12},{13,14},{2,1},{4,3},{6,5},{... | collective-permute-start | bytes 1572872 | tf_op jit(solution)/shard_map/ppermute | solution.py:105
  64.9 2.5 %inside.1 = (f32[3,128,512]{2,1,0:T(8,128)S(1)}, f32[3,128,512]{2,1,0:T(8,128)S(1)}) custom-call(s32[4]{0:T(128)S(1)} %pad_add_fusion.refs_0_.facts_ref, f32[8,128,512]{2,1,0:T(8,128)S(1)} %copy-done, f32[4,128,512]{2,1,0:T(8,128)S(1)} %get-tuple-element.38.lam1.part, f32[2,3,4,128,512]{4,3,2,1,0:T(8,128)} %bitcast.17), custom_call_target="tpu_custom_call" | custom-call | flops 1024 | bytes 1024 | tf_op jit(solution)/shard_map/inside/pallas_call | solution.py:66
  67.5 2.1 %collective-permute-start.6 = (f32[3,128,512]{2,1,0:T(8,128)S(1)}, f32[3,128,512]{2,1,0:T(8,128)S(1)}, u32[]{:S(2)}, u32[]{:S(2)}) collective-permute-start(f32[3,128,512]{2,1,0:T(8,128)S(1)} %get-tuple-element.39.in0), channel_id=1, source_target_pairs={{0,1},{2,3},{4,5},{6,7},{8,9},{10,11},{12,13},{14,15},{1,0},{3,2},... | collective-permute-start | bytes 2359304 | tf_op jit(solution)/shard_map/ppermute | solution.py:105
  69.5 20.2 %collective-permute-done.8.far0 = f32[2,128,512]{2,1,0:T(8,128)} collective-permute-done((f32[2,128,512]{2,1,0:T(8,128)}, f32[2,128,512]{2,1,0:T(8,128)}, u32[]{:S(2)}, u32[]{:S(2)}) %collective-permute-start.8) | collective-permute-done | bytes 524320 | tf_op jit(solution)/shard_map/ppermute | solution.py:105
  90.7 7.5 %last.1 = (f32[4,128,512]{2,1,0:T(8,128)S(1)}, f32[3,128,512]{2,1,0:T(8,128)S(1)}, f32[3,128,512]{2,1,0:T(8,128)S(1)}, f32[2,3,128,512]{3,2,1,0:T(8,128)}) custom-call(s32[4]{0:T(128)S(1)} %pad_add_fusion.refs_0_.facts_ref, f32[8,128,512]{2,1,0:T(8,128)} %get-tuple-element.34.tmpl, f32[4,128,512]{2,1,0:T(8,128)S(1)} %get-tuple-element.38.lam1.part, ...), custom_call_target="tpu_custom_call" | custom-call | flops 20000002048 | bytes 1024 | tf_op jit(solution)/shard_map/last/pallas_call | solution.py:66
  98.3 1.9 %collective-permute-start.12 = (f32[3,128,512]{2,1,0:T(8,128)S(1)}, f32[3,128,512]{2,1,0:T(8,128)S(1)}, u32[]{:S(2)}, u32[]{:S(2)}) collective-permute-start(f32[3,128,512]{2,1,0:T(8,128)S(1)} %copy-done.8), channel_id=1, source_target_pairs={{1,2},{3,4},{5,6},{7,8},{9,10},{11,12},{13,14},{2,1},{4,3},{6,5},{... | collective-permute-start | bytes 2359304 | tf_op jit(solution)/shard_map/ppermute | solution.py:105
  100.2 5.0 %collective-permute-start.13 = (f32[3,128,512]{2,1,0:T(8,128)S(1)}, f32[3,128,512]{2,1,0:T(8,128)S(1)}, u32[]{:S(2)}, u32[]{:S(2)}) collective-permute-start(f32[3,128,512]{2,1,0:T(8,128)S(1)} %copy-done.4), channel_id=1, source_target_pairs={{1,2},{3,4},{5,6},{7,8},{9,10},{11,12},{13,14},{2,1},{4,3},{6,5},{... | collective-permute-start | bytes 2359304 | tf_op jit(solution)/shard_map/ppermute | solution.py:105
  105.3 8.6 %smooth_0.1 = (f32[2,3,4,128,512]{4,3,2,1,0:T(8,128)}, f32[2,3,128,512]{3,2,1,0:T(8,128)S(1)}) custom-call(s32[4]{0:T(128)S(1)} %pad_add_fusion.refs_0_.facts_ref, f32[3,128,512]{2,1,0:T(8,128)S(1)} %get-tuple-element.39.in0, f32[3,128,512]{2,1,0:T(8,128)S(1)} %get-tuple-element.50.in1, f32[3,128,512]{2,1,0:T(8,128)S(1)} %get-tuple-element.51.out0, ...), custom_call_target="tpu_custom_call" | custom-call | flops 10000001024 | bytes 1024 | tf_op jit(solution)/shard_map/smooth_0/pallas_call | solution.py:66
  113.8 1.9 %collective-permute-start.10 = (f32[3,128,512]{2,1,0:T(8,128)S(1)}, f32[3,128,512]{2,1,0:T(8,128)S(1)}, u32[]{:S(2)}, u32[]{:S(2)}) collective-permute-start(f32[3,128,512]{2,1,0:T(8,128)S(1)} %get-tuple-element.50.in1), channel_id=1, source_target_pairs={{1,2},{3,4},{5,6},{7,8},{9,10},{11,12},{13,14},{2,1},{4,3},{6,5},{... | collective-permute-start | bytes 2359304 | tf_op jit(solution)/shard_map/ppermute | solution.py:105
  116.6 40.4 %collective-permute-done.11.near0 = f32[3,128,512]{2,1,0:T(8,128)S(1)} collective-permute-done((f32[3,128,512]{2,1,0:T(8,128)}, f32[3,128,512]{2,1,0:T(8,128)S(1)}, u32[]{:S(2)}, u32[]{:S(2)}) %collective-permute-start.11) | collective-permute-done | bytes 786464 | tf_op jit(solution)/shard_map/ppermute | solution.py:105
  158.9 8.6 %smooth_1.1._ = f32[2,3,4,128,512]{4,3,2,1,0:T(8,128)} custom-call(s32[4]{0:T(128)S(1)} %pad_add_fusion.refs_0_.facts_ref, f32[3,128,512]{2,1,0:T(8,128)} %get-tuple-element.45.in0, f32[3,128,512]{2,1,0:T(8,128)S(1)} %copy-done.4, f32[3,128,512]{2,1,0:T(8,128)S(1)} %copy-done.6, f32[3,128,512]{2,1,0:T(8,128)S(1)} %copy-done.8, ...), custom_call_target="tpu_custom_call", output_to_operand_aliasing={{}: (9, {})} | custom-call | flops 10000001024 | bytes 1024 | tf_op jit(solution)/shard_map/smooth_1/pallas_call | solution.py:66
  167.5 5.2 %collective-permute-done.6.far_0 = f32[3,128,512]{2,1,0:T(8,128)S(1)} collective-permute-done((f32[3,128,512]{2,1,0:T(8,128)S(1)}, f32[3,128,512]{2,1,0:T(8,128)S(1)}, u32[]{:S(2)}, u32[]{:S(2)}) %collective-permute-start.6) | collective-permute-done | bytes 786464 | tf_op jit(solution)/shard_map/ppermute | solution.py:105
  173.7 1.8 %add_far.1 = f32[2,3,4,128,512]{4,3,2,1,0:T(8,128)} custom-call(s32[4]{0:T(128)S(1)} %pad_add_fusion.refs_0_.facts_ref, f32[3,128,512]{2,1,0:T(8,128)S(1)} %collective-permute-done.6.far_0, f32[3,128,512]{2,1,0:T(8,128)S(1)} %collective-permute-done.10.far_1, f32[2,3,128,512]{3,2,1,0:T(8,128)S(1)} %get-tuple-element.54.rim, ...), custom_call_target="tpu_custom_call", output_to_operand_aliasing={{}: (4, {})} | custom-call | flops 1024 | bytes 1024 | tf_op jit(solution)/shard_map/add_far/pallas_call | solution.py:66
  (41 shorter events, 6.2 us)
Async XLA Ops:
  1.7 31.7 %collective-permute-start.2 = (f32[2,64,512]{2,1,0:T(8,128)S(1)}, f32[2,64,512]{2,1,0:T(8,128)S(1)}, u32[]{:S(2)}, u32[]{:S(2)}) collective-permute-start(f32[2,64,512]{2,1,0:T(8,128)S(1)} %get-tuple-element.63), channel_id=1, source_target_pairs={{0,1},{2,3},{4,5},{6,7},{8,9},{10,11},{12,13},{14,15},{1,0},{3,2},... | collective-permute-start | bytes 786440 | tf_op jit(solution)/shard_map/ppermute | solution.py:105
  1.8 31.7 %collective-permute-start.1 = (f32[2,64,512]{2,1,0:T(8,128)S(1)}, f32[2,64,512]{2,1,0:T(8,128)S(1)}, u32[]{:S(2)}, u32[]{:S(2)}) collective-permute-start(f32[2,64,512]{2,1,0:T(8,128)S(1)} %get-tuple-element.64), channel_id=1, source_target_pairs={{1,2},{3,4},{5,6},{7,8},{9,10},{11,12},{13,14},{2,1},{4,3},{6,5},{... | collective-permute-start | bytes 786440 | tf_op jit(solution)/shard_map/ppermute | solution.py:105
  9.5 34.3 %collective-permute-start.5 = (f32[3,128,512]{2,1,0:T(8,128)}, f32[3,128,512]{2,1,0:T(8,128)S(1)}, u32[]{:S(2)}, u32[]{:S(2)}) collective-permute-start(f32[3,128,512]{2,1,0:T(8,128)} %get-tuple-element.61), channel_id=1, source_target_pairs={{1,2},{3,4},{5,6},{7,8},{9,10},{11,12},{13,14},{2,1},{4,3},{6,5},{... | collective-permute-start | bytes 2359304 | tf_op jit(solution)/shard_map/ppermute | solution.py:105
  11.4 38.9 %collective-permute-start.4 = (f32[3,128,512]{2,1,0:T(8,128)}, f32[3,128,512]{2,1,0:T(8,128)S(1)}, u32[]{:S(2)}, u32[]{:S(2)}) collective-permute-start(f32[3,128,512]{2,1,0:T(8,128)} %get-tuple-element.62), channel_id=1, source_target_pairs={{0,1},{2,3},{4,5},{6,7},{8,9},{10,11},{12,13},{14,15},{1,0},{3,2},... | collective-permute-start | bytes 2359304 | tf_op jit(solution)/shard_map/ppermute | solution.py:105
  11.5 22.2 %collective-permute-start = (f32[4,64,512]{2,1,0:T(8,128)}, f32[4,64,512]{2,1,0:T(8,128)S(1)}, u32[]{:S(2)}, u32[]{:S(2)}) collective-permute-start(f32[4,64,512]{2,1,0:T(8,128)} %refs_1_.1), channel_id=1, source_target_pairs={{0,16},{16,0},{1,17},{17,1},{2,18},{18,2},{3,19},{19,3},{4,20},{20... | collective-permute-start | bytes 1572872 | tf_op jit(solution)/shard_map/ppermute | solution.py:108
  33.5 2.0 %collective-permute-start.3 = (f32[4,64,512]{2,1,0:T(8,128)S(1)}, f32[4,64,512]{2,1,0:T(8,128)S(1)}, u32[]{:S(2)}, u32[]{:S(2)}) collective-permute-start(f32[4,64,512]{2,1,0:T(8,128)S(1)} %constant_dynamic-update-slice_fusion.refs_3_), channel_id=1, source_target_pairs={{0,16},{16,0},{1,17},{17,1},{2,18},{18,2},{3,19},{19,3},{4,20},{20... | collective-permute-start | bytes 1572872 | tf_op jit(solution)/shard_map/ppermute | solution.py:108
  35.5 1.0 copy-start.2
  36.5 13.8 %copy-start.1 = (f32[1,4,128,512]{3,2,1,0:T(8,128)S(1)}, f32[1,4,128,512]{3,2,1,0:T(8,128)}, u32[]{:S(2)}) copy-start(f32[1,4,128,512]{3,2,1,0:T(8,128)} %param.4) | copy-start | bytes 3145732
  43.8 46.9 %collective-permute-start.7 = (f32[3,128,512]{2,1,0:T(8,128)}, f32[3,128,512]{2,1,0:T(8,128)}, u32[]{:S(2)}, u32[]{:S(2)}) collective-permute-start(f32[3,128,512]{2,1,0:T(8,128)} %get-tuple-element.45.in0), channel_id=1, source_target_pairs={{0,1},{2,3},{4,5},{6,7},{8,9},{10,11},{12,13},{14,15},{1,0},{3,2},... | collective-permute-start | bytes 2359304 | tf_op jit(solution)/shard_map/ppermute | solution.py:105
  55.0 5.0 %copy-start.5 = (f32[3,128,512]{2,1,0:T(8,128)}, f32[3,128,512]{2,1,0:T(8,128)S(1)}, u32[]{:S(2)}) copy-start(f32[3,128,512]{2,1,0:T(8,128)S(1)} %get-tuple-element.55.out0) | copy-start | bytes 2359300
  55.0 5.0 %copy-start.7 = (f32[3,128,512]{2,1,0:T(8,128)}, f32[3,128,512]{2,1,0:T(8,128)S(1)}, u32[]{:S(2)}) copy-start(f32[3,128,512]{2,1,0:T(8,128)S(1)} %get-tuple-element.56.out1) | copy-start | bytes 2359300
  55.0 9.9 %copy-start = (f32[8,128,512]{2,1,0:T(8,128)S(1)}, f32[8,128,512]{2,1,0:T(8,128)}, u32[]{:S(2)}) copy-start(f32[8,128,512]{2,1,0:T(8,128)} %get-tuple-element.34.tmpl) | copy-start | bytes 6291460
  59.9 29.8 %collective-permute-start.8 = (f32[2,128,512]{2,1,0:T(8,128)}, f32[2,128,512]{2,1,0:T(8,128)}, u32[]{:S(2)}, u32[]{:S(2)}) collective-permute-start(f32[2,128,512]{2,1,0:T(8,128)} %get-tuple-element.41.own0), channel_id=1, source_target_pairs={{0,1},{2,3},{4,5},{6,7},{8,9},{10,11},{12,13},{14,15},{1,0},{3,2},... | collective-permute-start | bytes 1572872 | tf_op jit(solution)/shard_map/ppermute | solution.py:105
  59.9 30.7 %collective-permute-start.9 = (f32[2,128,512]{2,1,0:T(8,128)}, f32[2,128,512]{2,1,0:T(8,128)}, u32[]{:S(2)}, u32[]{:S(2)}) collective-permute-start(f32[2,128,512]{2,1,0:T(8,128)} %get-tuple-element.42.own1), channel_id=1, source_target_pairs={{1,2},{3,4},{5,6},{7,8},{9,10},{11,12},{13,14},{2,1},{4,3},{6,5},{... | collective-permute-start | bytes 1572872 | tf_op jit(solution)/shard_map/ppermute | solution.py:105
  64.8 92.2 %collective-permute-start.11 = (f32[3,128,512]{2,1,0:T(8,128)}, f32[3,128,512]{2,1,0:T(8,128)S(1)}, u32[]{:S(2)}, u32[]{:S(2)}) collective-permute-start(f32[3,128,512]{2,1,0:T(8,128)} %copy-done.5), channel_id=1, source_target_pairs={{0,1},{2,3},{4,5},{6,7},{8,9},{10,11},{12,13},{14,15},{1,0},{3,2},... | collective-permute-start | bytes 2359304 | tf_op jit(solution)/shard_map/ppermute | solution.py:105
  67.5 105.3 %collective-permute-start.6 = (f32[3,128,512]{2,1,0:T(8,128)S(1)}, f32[3,128,512]{2,1,0:T(8,128)S(1)}, u32[]{:S(2)}, u32[]{:S(2)}) collective-permute-start(f32[3,128,512]{2,1,0:T(8,128)S(1)} %get-tuple-element.39.in0), channel_id=1, source_target_pairs={{0,1},{2,3},{4,5},{6,7},{8,9},{10,11},{12,13},{14,15},{1,0},{3,2},... | collective-permute-start | bytes 2359304 | tf_op jit(solution)/shard_map/ppermute | solution.py:105
  90.7 7.6 %copy-start.8 = (f32[3,128,512]{2,1,0:T(8,128)S(1)}, f32[3,128,512]{2,1,0:T(8,128)}, u32[]{:S(2)}) copy-start(f32[3,128,512]{2,1,0:T(8,128)} %copy-done.7) | copy-start | bytes 2359300
  90.7 9.5 %copy-start.4 = (f32[3,128,512]{2,1,0:T(8,128)S(1)}, f32[3,128,512]{2,1,0:T(8,128)}, u32[]{:S(2)}) copy-start(f32[3,128,512]{2,1,0:T(8,128)} %copy-done.3) | copy-start | bytes 2359300
  98.2 15.6 %collective-permute-start.14 = (f32[4,64,512]{2,1,0:T(8,128)S(1)}, f32[4,64,512]{2,1,0:T(8,128)S(1)}, u32[]{:S(2)}, u32[]{:S(2)}) collective-permute-start(f32[4,64,512]{2,1,0:T(8,128)S(1)} %constant_dynamic-slice_fusion), channel_id=1, source_target_pairs={{0,16},{16,0},{1,17},{17,1},{2,18},{18,2},{3,19},{19,3},{4,20},{20... | collective-permute-start | bytes 1572872 | tf_op jit(solution)/shard_map/ppermute | solution.py:108
  98.3 58.7 %collective-permute-start.12 = (f32[3,128,512]{2,1,0:T(8,128)S(1)}, f32[3,128,512]{2,1,0:T(8,128)S(1)}, u32[]{:S(2)}, u32[]{:S(2)}) collective-permute-start(f32[3,128,512]{2,1,0:T(8,128)S(1)} %copy-done.8), channel_id=1, source_target_pairs={{1,2},{3,4},{5,6},{7,8},{9,10},{11,12},{13,14},{2,1},{4,3},{6,5},{... | collective-permute-start | bytes 2359304 | tf_op jit(solution)/shard_map/ppermute | solution.py:105
  100.2 57.8 %collective-permute-start.13 = (f32[3,128,512]{2,1,0:T(8,128)S(1)}, f32[3,128,512]{2,1,0:T(8,128)S(1)}, u32[]{:S(2)}, u32[]{:S(2)}) collective-permute-start(f32[3,128,512]{2,1,0:T(8,128)S(1)} %copy-done.4), channel_id=1, source_target_pairs={{1,2},{3,4},{5,6},{7,8},{9,10},{11,12},{13,14},{2,1},{4,3},{6,5},{... | collective-permute-start | bytes 2359304 | tf_op jit(solution)/shard_map/ppermute | solution.py:105
  105.3 53.7 %copy-start.6 = (f32[3,128,512]{2,1,0:T(8,128)S(1)}, f32[3,128,512]{2,1,0:T(8,128)}, u32[]{:S(2)}) copy-start(f32[3,128,512]{2,1,0:T(8,128)} %copy-done.5) | copy-start | bytes 2359300
  113.8 59.9 %collective-permute-start.10 = (f32[3,128,512]{2,1,0:T(8,128)S(1)}, f32[3,128,512]{2,1,0:T(8,128)S(1)}, u32[]{:S(2)}, u32[]{:S(2)}) collective-permute-start(f32[3,128,512]{2,1,0:T(8,128)S(1)} %get-tuple-element.50.in1), channel_id=1, source_target_pairs={{1,2},{3,4},{5,6},{7,8},{9,10},{11,12},{13,14},{2,1},{4,3},{6,5},{... | collective-permute-start | bytes 2359304 | tf_op jit(solution)/shard_map/ppermute | solution.py:105
  158.0 0.9 copy-start.9
  (1 other events, 0.9 us)

commit v12 on v9

--- a/solution.py
+++ b/solution.py
@@ -74,7 +74,7 @@
             scratch_shapes=list(scratch),
         ),
         input_output_aliases=aliases or {},
-        compiler_params=pltpu.CompilerParams(vmem_limit_bytes=48 * MIB),
+        compiler_params=pltpu.CompilerParams(vmem_limit_bytes=24 * MIB),
         cost_estimate=pl.CostEstimate(
             flops=1024 + weight * 10000000, bytes_accessed=1024, transcendentals=0
         ),

time: 176 us -> 176 us (level)
  Pallas kernels: 42 us -> 29.7 us
  local copies, waits for them, and re-layouts: 12.4 us -> 22.1 us
    pallas_call x7, Pallas kernels: 42 us -> 29.7 us  [call(): pl.pallas_call(kernel, out_shape=out_shape, grid_spec=pltpu.PrefetchScala...]
    unnamed x27 -> x43, local copies, waits for them, and re-layouts: 7.47 us -> 18.2 us
    ppermute x12, waiting for transfers between devices: 96.5 us -> 98.7 us  [swap(): return lax.ppermute(x, 'slab', pairs[side])]
  transfers between devices with their start and end apart: 15 -> 15, of which waited for: 9 -> 9; matrix products, arithmetic and copies ran while one was open for 3% -> 2% of each run, Pallas kernels for 23% -> 16%
where the time goes in v12:
time: 176 us
  waiting for transfers between devices  99.7 us (57%)
  Pallas kernels  29.7 us (17%)
  local copies, waits for them, and re-layouts  22.1 us (13%)
  starting transfers between devices  22.1 us (13%)
    ppermute x12, waiting for transfers between devices, swap(): return lax.ppermute(x, 'slab', pairs[side])  98.7 us
    pallas_call x7, Pallas kernels, call(): pl.pallas_call(kernel, out_shape=out_shape, grid_spec=pltpu.PrefetchScala...  29.7 us
    ppermute x12, starting transfers between devices, swap(): return lax.ppermute(x, 'slab', pairs[side])  21.9 us
    unnamed x43, local copies, waits for them, and re-layouts  18.2 us
  transfers between devices with their start and end apart: 15, of which 9 were waited for; matrix products, arithmetic and copies ran while one was open for 2% of the time, Pallas kernels for 16%

profile of v12, /device:TPU:2, one launch (start us, length us, event | category | flops | bytes accessed | tf_op | source)
XLA Modules:
  0.0 175.6 jit_solution(15699564948352858237)
XLA Ops:
  1.8 4.9 %collective-permute-start.1 = (f32[2,64,512]{2,1,0:T(8,128)S(1)}, f32[2,64,512]{2,1,0:T(8,128)S(1)}, u32[]{:S(2)}, u32[]{:S(2)}) collective-permute-start(f32[2,64,512]{2,1,0:T(8,128)S(1)} %get-tuple-element.61), channel_id=1, source_target_pairs={{1,2},{3,4},{5,6},{7,8},{9,10},{11,12},{13,14},{2,1},{4,3},{6,5},{... | collective-permute-start | bytes 786440 | tf_op jit(solution)/shard_map/ppermute | solution.py:105
  6.7 2.8 %dynamic-slice_bitcast_fusion = (f32[3,128,512]{2,1,0:T(8,128)}, f32[3,128,512]{2,1,0:T(8,128)}) fusion(f32[1,2,3,4,128,512]{5,4,3,2,1,0:T(8,128)} %param.5, s32[]{:T(128)S(6)} %select_n.29, s32[]{:T(128)S(6)} %select_n.28), kind=kLoop, calls=%fused_computation | loop fusion | bytes 3145736 | tf_op jit(solution)/shard_map/squeeze | solution.py:137
  9.5 1.9 %collective-permute-start.5 = (f32[3,128,512]{2,1,0:T(8,128)}, f32[3,128,512]{2,1,0:T(8,128)S(1)}, u32[]{:S(2)}, u32[]{:S(2)}) collective-permute-start(f32[3,128,512]{2,1,0:T(8,128)} %get-tuple-element.58), channel_id=1, source_target_pairs={{1,2},{3,4},{5,6},{7,8},{9,10},{11,12},{13,14},{2,1},{4,3},{6,5},{... | collective-permute-start | bytes 2359304 | tf_op jit(solution)/shard_map/ppermute | solution.py:105
  11.5 21.9 %collective-permute-done.2 = f32[2,64,512]{2,1,0:T(8,128)S(1)} collective-permute-done((f32[2,64,512]{2,1,0:T(8,128)S(1)}, f32[2,64,512]{2,1,0:T(8,128)S(1)}, u32[]{:S(2)}, u32[]{:S(2)}) %collective-permute-start.2) | collective-permute-done | bytes 262176 | tf_op jit(solution)/shard_map/ppermute | solution.py:105
  36.3 2.8 %copy-done = f32[1,2,3,4,128,512]{5,4,3,2,1,0:T(8,128)S(1)} copy-done((f32[1,2,3,4,128,512]{5,4,3,2,1,0:T(8,128)S(1)}, f32[1,2,3,4,128,512]{5,4,3,2,1,0:T(8,128)}, u32[]{:S(2)}) %copy-start) | copy-done | bytes 6291480
  39.1 1.2 copy-done.2
  43.4 3.0 %forward.1 = (f32[8,128,512]{2,1,0:T(8,128)S(1)}, f32[4,128,512]{2,1,0:T(8,128)S(1)}, f32[2,128,512]{2,1,0:T(8,128)S(1)}, f32[3,128,512]{2,1,0:T(8,128)}, f32[3,128,512]{2,1,0:T(8,128)S(1)}) custom-call(s32[4]{0:T(128)S(1)} %pad_add_fusion.refs_0_.facts_ref, f32[4,64,512]{2,1,0:T(8,128)S(1)} %copy-done.4, f32[4,64,512]{2,1,0:T(8,128)S(1)} %copy-done.6, ...), custom_call_target="tpu_custom_call" | custom-call | flops 1024 | bytes 1024 | tf_op jit(solution)/shard_map/forward/pallas_call | solution.py:66
  46.5 2.8 %collective-permute-done.4.halo0 = f32[3,128,512]{2,1,0:T(8,128)} collective-permute-done((f32[3,128,512]{2,1,0:T(8,128)}, f32[3,128,512]{2,1,0:T(8,128)}, u32[]{:S(2)}, u32[]{:S(2)}) %collective-permute-start.4) | collective-permute-done | bytes 786464 | tf_op jit(solution)/shard_map/ppermute | solution.py:105
  49.3 2.4 %middle.1 = (f32[3,128,512]{2,1,0:T(8,128)S(1)}, f32[3,128,512]{2,1,0:T(8,128)S(1)}, f32[2,128,512]{2,1,0:T(8,128)S(1)}, f32[2,3,128,512]{3,2,1,0:T(8,128)S(1)}) custom-call(s32[4]{0:T(128)S(1)} %pad_add_fusion.refs_0_.facts_ref, f32[8,128,512]{2,1,0:T(8,128)S(1)} %get-tuple-element.32.tmpl, f32[4,128,512]{2,1,0:T(8,128)S(1)} %get-tuple-element.34.img1, ...), custom_call_target="tpu_custom_call" | custom-call | flops 1024 | bytes 1024 | tf_op jit(solution)/shard_map/middle/pallas_call | solution.py:66
  52.9 2.1 %back.1 = (f32[4,128,512]{2,1,0:T(8,128)S(1)}, f32[2,128,512]{2,1,0:T(8,128)S(1)}, f32[2,128,512]{2,1,0:T(8,128)S(1)}) custom-call(s32[4]{0:T(128)S(1)} %pad_add_fusion.refs_0_.facts_ref, f32[2,128,512]{2,1,0:T(8,128)S(1)} %get-tuple-element.33.lam2_in, f32[2,128,512]{2,1,0:T(8,128)S(1)} %get-tuple-element.35.lam2_out, f32[2,3,4,128,512]{4,3,2,1,0:T(8,128)S(1)} %bitcast.14), custom_call_target="tpu_custom_call" | custom-call | flops 10000001024 | bytes 1024 | tf_op jit(solution)/shard_map/back/pallas_call | solution.py:66
  56.2 5.7 %collective-permute-start.8 = (f32[2,128,512]{2,1,0:T(8,128)S(1)}, f32[2,128,512]{2,1,0:T(8,128)}, u32[]{:S(2)}, u32[]{:S(2)}) collective-permute-start(f32[2,128,512]{2,1,0:T(8,128)S(1)} %get-tuple-element.38.own1), channel_id=1, source_target_pairs={{1,2},{3,4},{5,6},{7,8},{9,10},{11,12},{13,14},{2,1},{4,3},{6,5},{... | collective-permute-start | bytes 1572872 | tf_op jit(solution)/shard_map/ppermute | solution.py:105
  62.8 26.9 %collective-permute-done.7.far0 = f32[2,128,512]{2,1,0:T(8,128)} collective-permute-done((f32[2,128,512]{2,1,0:T(8,128)S(1)}, f32[2,128,512]{2,1,0:T(8,128)}, u32[]{:S(2)}, u32[]{:S(2)}) %collective-permute-start.7) | collective-permute-done | bytes 524320 | tf_op jit(solution)/shard_map/ppermute | solution.py:105
  90.7 2.8 %copy-done.1 = f32[1,2,3,4,128,512]{5,4,3,2,1,0:T(8,128)S(1)} copy-done((f32[1,2,3,4,128,512]{5,4,3,2,1,0:T(8,128)S(1)}, f32[1,2,3,4,128,512]{5,4,3,2,1,0:T(8,128)}, u32[]{:S(2)}) %copy-start.1) | copy-done | bytes 6291480
  93.5 1.4 copy-done.10
  97.2 4.6 %last.1 = (f32[4,128,512]{2,1,0:T(8,128)S(1)}, f32[3,128,512]{2,1,0:T(8,128)S(1)}, f32[3,128,512]{2,1,0:T(8,128)S(1)}, f32[3,128,512]{2,1,0:T(8,128)S(1)}, f32[3...) custom-call(s32[4]{0:T(128)S(1)} %pad_add_fusion.refs_0_.facts_ref, f32[8,128,512]{2,1,0:T(8,128)S(1)} %get-tuple-element.32.tmpl, ...), custom_call_target="tpu_custom_call" | custom-call | flops 20000002048 | bytes 1024 | tf_op jit(solution)/shard_map/last/pallas_call | solution.py:66
  102.0 1.9 %collective-permute-start.12 = (f32[3,128,512]{2,1,0:T(8,128)S(1)}, f32[3,128,512]{2,1,0:T(8,128)S(1)}, u32[]{:S(2)}, u32[]{:S(2)}) collective-permute-start(f32[3,128,512]{2,1,0:T(8,128)S(1)} %copy-done.16), channel_id=1, source_target_pairs={{1,2},{3,4},{5,6},{7,8},{9,10},{11,12},{13,14},{2,1},{4,3},{6,5},{... | collective-permute-start | bytes 2359304 | tf_op jit(solution)/shard_map/ppermute | solution.py:105
  103.9 5.0 %collective-permute-start.13 = (f32[3,128,512]{2,1,0:T(8,128)S(1)}, f32[3,128,512]{2,1,0:T(8,128)S(1)}, u32[]{:S(2)}, u32[]{:S(2)}) collective-permute-start(f32[3,128,512]{2,1,0:T(8,128)S(1)} %copy-done.12), channel_id=1, source_target_pairs={{1,2},{3,4},{5,6},{7,8},{9,10},{11,12},{13,14},{2,1},{4,3},{6,5},{... | collective-permute-start | bytes 2359304 | tf_op jit(solution)/shard_map/ppermute | solution.py:105
  108.9 7.7 %smooth_0.1 = (f32[2,3,4,128,512]{4,3,2,1,0:T(8,128)}, f32[2,3,128,512]{3,2,1,0:T(8,128)S(1)}) custom-call(s32[4]{0:T(128)S(1)} %pad_add_fusion.refs_0_.facts_ref, f32[3,128,512]{2,1,0:T(8,128)S(1)} %get-tuple-element.45.in0, f32[3,128,512]{2,1,0:T(8,128)S(1)} %get-tuple-element.46.in1, f32[3,128,512]{2,1,0:T(8,128)S(1)} %get-tuple-element.47.out0, ...), custom_call_target="tpu_custom_call" | custom-call | flops 10000001024 | bytes 1024 | tf_op jit(solution)/shard_map/smooth_0/pallas_call | solution.py:66
  116.6 1.9 %collective-permute-start.10 = (f32[3,128,512]{2,1,0:T(8,128)S(1)}, f32[3,128,512]{2,1,0:T(8,128)S(1)}, u32[]{:S(2)}, u32[]{:S(2)}) collective-permute-start(f32[3,128,512]{2,1,0:T(8,128)S(1)} %get-tuple-element.46.in1), channel_id=1, source_target_pairs={{1,2},{3,4},{5,6},{7,8},{9,10},{11,12},{13,14},{2,1},{4,3},{6,5},{... | collective-permute-start | bytes 2359304 | tf_op jit(solution)/shard_map/ppermute | solution.py:105
  119.5 21.7 %collective-permute-done.12.near1 = f32[3,128,512]{2,1,0:T(8,128)S(1)} collective-permute-done((f32[3,128,512]{2,1,0:T(8,128)S(1)}, f32[3,128,512]{2,1,0:T(8,128)S(1)}, u32[]{:S(2)}, u32[]{:S(2)}) %collective-permute-start.12) | collective-permute-done | bytes 786464 | tf_op jit(solution)/shard_map/ppermute | solution.py:105
  141.1 16.9 %collective-permute-done.13.far1 = f32[3,128,512]{2,1,0:T(8,128)S(1)} collective-permute-done((f32[3,128,512]{2,1,0:T(8,128)S(1)}, f32[3,128,512]{2,1,0:T(8,128)S(1)}, u32[]{:S(2)}, u32[]{:S(2)}) %collective-permute-start.13) | collective-permute-done | bytes 786464 | tf_op jit(solution)/shard_map/ppermute | solution.py:105
  158.0 8.2 %smooth_1.1._ = f32[2,3,4,128,512]{4,3,2,1,0:T(8,128)} custom-call(s32[4]{0:T(128)S(1)} %pad_add_fusion.refs_0_.facts_ref, f32[3,128,512]{2,1,0:T(8,128)} %get-tuple-element.41.in0, f32[3,128,512]{2,1,0:T(8,128)S(1)} %copy-done.12, f32[3,128,512]{2,1,0:T(8,128)S(1)} %copy-done.14, f32[3,128,512]{2,1,0:T(8,128)S(1)} %copy-done.16, ...), custom_call_target="tpu_custom_call", output_to_operand_aliasing={{}: (9, {})} | custom-call | flops 10000001024 | bytes 1024 | tf_op jit(solution)/shard_map/smooth_1/pallas_call | solution.py:66
  166.2 6.8 %collective-permute-done.9.far_0 = f32[3,128,512]{2,1,0:T(8,128)S(1)} collective-permute-done((f32[3,128,512]{2,1,0:T(8,128)S(1)}, f32[3,128,512]{2,1,0:T(8,128)S(1)}, u32[]{:S(2)}, u32[]{:S(2)}) %collective-permute-start.9) | collective-permute-done | bytes 786464 | tf_op jit(solution)/shard_map/ppermute | solution.py:105
  173.7 1.8 %add_far.1 = f32[2,3,4,128,512]{4,3,2,1,0:T(8,128)} custom-call(s32[4]{0:T(128)S(1)} %pad_add_fusion.refs_0_.facts_ref, f32[3,128,512]{2,1,0:T(8,128)S(1)} %collective-permute-done.9.far_0, f32[3,128,512]{2,1,0:T(8,128)S(1)} %collective-permute-done.10.far_1, f32[2,3,128,512]{3,2,1,0:T(8,128)S(1)} %get-tuple-element.50.rim, ...), custom_call_target="tpu_custom_call", output_to_operand_aliasing={{}: (4, {})} | custom-call | flops 1024 | bytes 1024 | tf_op jit(solution)/shard_map/add_far/pallas_call | solution.py:66
  (62 shorter events, 15.6 us)
Async XLA Ops:
  1.7 31.7 %collective-permute-start.2 = (f32[2,64,512]{2,1,0:T(8,128)S(1)}, f32[2,64,512]{2,1,0:T(8,128)S(1)}, u32[]{:S(2)}, u32[]{:S(2)}) collective-permute-start(f32[2,64,512]{2,1,0:T(8,128)S(1)} %get-tuple-element.60), channel_id=1, source_target_pairs={{0,1},{2,3},{4,5},{6,7},{8,9},{10,11},{12,13},{14,15},{1,0},{3,2},... | collective-permute-start | bytes 786440 | tf_op jit(solution)/shard_map/ppermute | solution.py:105
  1.8 31.7 %collective-permute-start.1 = (f32[2,64,512]{2,1,0:T(8,128)S(1)}, f32[2,64,512]{2,1,0:T(8,128)S(1)}, u32[]{:S(2)}, u32[]{:S(2)}) collective-permute-start(f32[2,64,512]{2,1,0:T(8,128)S(1)} %get-tuple-element.61), channel_id=1, source_target_pairs={{1,2},{3,4},{5,6},{7,8},{9,10},{11,12},{13,14},{2,1},{4,3},{6,5},{... | collective-permute-start | bytes 786440 | tf_op jit(solution)/shard_map/ppermute | solution.py:105
  9.5 37.0 %collective-permute-start.5 = (f32[3,128,512]{2,1,0:T(8,128)}, f32[3,128,512]{2,1,0:T(8,128)S(1)}, u32[]{:S(2)}, u32[]{:S(2)}) collective-permute-start(f32[3,128,512]{2,1,0:T(8,128)} %get-tuple-element.58), channel_id=1, source_target_pairs={{1,2},{3,4},{5,6},{7,8},{9,10},{11,12},{13,14},{2,1},{4,3},{6,5},{... | collective-permute-start | bytes 2359304 | tf_op jit(solution)/shard_map/ppermute | solution.py:105
  11.4 37.9 %collective-permute-start.4 = (f32[3,128,512]{2,1,0:T(8,128)}, f32[3,128,512]{2,1,0:T(8,128)}, u32[]{:S(2)}, u32[]{:S(2)}) collective-permute-start(f32[3,128,512]{2,1,0:T(8,128)} %get-tuple-element.59), channel_id=1, source_target_pairs={{0,1},{2,3},{4,5},{6,7},{8,9},{10,11},{12,13},{14,15},{1,0},{3,2},... | collective-permute-start | bytes 2359304 | tf_op jit(solution)/shard_map/ppermute | solution.py:105
  11.4 22.2 %collective-permute-start = (f32[4,64,512]{2,1,0:T(8,128)}, f32[4,64,512]{2,1,0:T(8,128)S(1)}, u32[]{:S(2)}, u32[]{:S(2)}) collective-permute-start(f32[4,64,512]{2,1,0:T(8,128)} %refs_1_.1), channel_id=1, source_target_pairs={{0,16},{16,0},{1,17},{17,1},{2,18},{18,2},{3,19},{19,3},{4,20},{20... | collective-permute-start | bytes 1572872 | tf_op jit(solution)/shard_map/ppermute | solution.py:108
  33.5 2.0 %collective-permute-start.3 = (f32[4,64,512]{2,1,0:T(8,128)S(1)}, f32[4,64,512]{2,1,0:T(8,128)S(1)}, u32[]{:S(2)}, u32[]{:S(2)}) collective-permute-start(f32[4,64,512]{2,1,0:T(8,128)S(1)} %constant_dynamic-update-slice_fusion.refs_3_), channel_id=1, source_target_pairs={{0,16},{16,0},{1,17},{17,1},{2,18},{18,2},{3,19},{19,3},{4,20},{20... | collective-permute-start | bytes 1572872 | tf_op jit(solution)/shard_map/ppermute | solution.py:108
  36.3 2.8 %copy-start = (f32[1,2,3,4,128,512]{5,4,3,2,1,0:T(8,128)S(1)}, f32[1,2,3,4,128,512]{5,4,3,2,1,0:T(8,128)}, u32[]{:S(2)}) copy-start(f32[1,2,3,4,128,512]{5,4,3,2,1,0:T(8,128)} %param.5) | copy-start | bytes 18874372
  43.4 5.8 %copy-start.3 = (f32[1,4,128,512]{3,2,1,0:T(8,128)S(1)}, f32[1,4,128,512]{3,2,1,0:T(8,128)}, u32[]{:S(2)}) copy-start(f32[1,4,128,512]{3,2,1,0:T(8,128)} %param.4) | copy-start | bytes 3145732
  46.5 8.5 %copy-start.11 = (f32[3,128,512]{2,1,0:T(8,128)}, f32[3,128,512]{2,1,0:T(8,128)S(1)}, u32[]{:S(2)}) copy-start(f32[3,128,512]{2,1,0:T(8,128)S(1)} %get-tuple-element.55.in1) | copy-start | bytes 2359300
  46.5 44.2 %collective-permute-start.6 = (f32[3,128,512]{2,1,0:T(8,128)}, f32[3,128,512]{2,1,0:T(8,128)}, u32[]{:S(2)}, u32[]{:S(2)}) collective-permute-start(f32[3,128,512]{2,1,0:T(8,128)} %get-tuple-element.41.in0), channel_id=1, source_target_pairs={{0,1},{2,3},{4,5},{6,7},{8,9},{10,11},{12,13},{14,15},{1,0},{3,2},... | collective-permute-start | bytes 2359304 | tf_op jit(solution)/shard_map/ppermute | solution.py:105
  52.8 2.1 %copy-start.13 = (f32[3,128,512]{2,1,0:T(8,128)}, f32[3,128,512]{2,1,0:T(8,128)S(1)}, u32[]{:S(2)}) copy-start(f32[3,128,512]{2,1,0:T(8,128)S(1)} %get-tuple-element.52.out0) | copy-start | bytes 2359300
  52.8 2.1 %copy-start.15 = (f32[3,128,512]{2,1,0:T(8,128)}, f32[3,128,512]{2,1,0:T(8,128)S(1)}, u32[]{:S(2)}) copy-start(f32[3,128,512]{2,1,0:T(8,128)S(1)} %get-tuple-element.53.out1) | copy-start | bytes 2359300
  55.9 33.7 %collective-permute-start.7 = (f32[2,128,512]{2,1,0:T(8,128)S(1)}, f32[2,128,512]{2,1,0:T(8,128)}, u32[]{:S(2)}, u32[]{:S(2)}) collective-permute-start(f32[2,128,512]{2,1,0:T(8,128)S(1)} %get-tuple-element.37.own0), channel_id=1, source_target_pairs={{0,1},{2,3},{4,5},{6,7},{8,9},{10,11},{12,13},{14,15},{1,0},{3,2},... | collective-permute-start | bytes 1572872 | tf_op jit(solution)/shard_map/ppermute | solution.py:105
  56.2 34.5 %collective-permute-start.8 = (f32[2,128,512]{2,1,0:T(8,128)S(1)}, f32[2,128,512]{2,1,0:T(8,128)}, u32[]{:S(2)}, u32[]{:S(2)}) collective-permute-start(f32[2,128,512]{2,1,0:T(8,128)S(1)} %get-tuple-element.38.own1), channel_id=1, source_target_pairs={{1,2},{3,4},{5,6},{7,8},{9,10},{11,12},{13,14},{2,1},{4,3},{6,5},{... | collective-permute-start | bytes 1572872 | tf_op jit(solution)/shard_map/ppermute | solution.py:105
  62.8 56.7 %collective-permute-start.11 = (f32[3,128,512]{2,1,0:T(8,128)}, f32[3,128,512]{2,1,0:T(8,128)S(1)}, u32[]{:S(2)}, u32[]{:S(2)}) collective-permute-start(f32[3,128,512]{2,1,0:T(8,128)} %copy-done.13), channel_id=1, source_target_pairs={{0,1},{2,3},{4,5},{6,7},{8,9},{10,11},{12,13},{14,15},{1,0},{3,2},... | collective-permute-start | bytes 2359304 | tf_op jit(solution)/shard_map/ppermute | solution.py:105
  90.7 2.8 %copy-start.1 = (f32[1,2,3,4,128,512]{5,4,3,2,1,0:T(8,128)S(1)}, f32[1,2,3,4,128,512]{5,4,3,2,1,0:T(8,128)}, u32[]{:S(2)}) copy-start(f32[1,2,3,4,128,512]{5,4,3,2,1,0:T(8,128)} %param.5) | copy-start | bytes 18874372
  97.2 4.8 %copy-start.16 = (f32[3,128,512]{2,1,0:T(8,128)S(1)}, f32[3,128,512]{2,1,0:T(8,128)}, u32[]{:S(2)}) copy-start(f32[3,128,512]{2,1,0:T(8,128)} %copy-done.15) | copy-start | bytes 2359300
  97.2 6.8 %copy-start.12 = (f32[3,128,512]{2,1,0:T(8,128)S(1)}, f32[3,128,512]{2,1,0:T(8,128)}, u32[]{:S(2)}) copy-start(f32[3,128,512]{2,1,0:T(8,128)} %copy-done.11) | copy-start | bytes 2359300
  101.8 14.8 %collective-permute-start.14 = (f32[4,64,512]{2,1,0:T(8,128)S(1)}, f32[4,64,512]{2,1,0:T(8,128)S(1)}, u32[]{:S(2)}, u32[]{:S(2)}) collective-permute-start(f32[4,64,512]{2,1,0:T(8,128)S(1)} %constant_dynamic-slice_fusion), channel_id=1, source_target_pairs={{0,16},{16,0},{1,17},{17,1},{2,18},{18,2},{3,19},{19,3},{4,20},{20... | collective-permute-start | bytes 1572872 | tf_op jit(solution)/shard_map/ppermute | solution.py:108
  101.9 71.1 %collective-permute-start.9 = (f32[3,128,512]{2,1,0:T(8,128)S(1)}, f32[3,128,512]{2,1,0:T(8,128)S(1)}, u32[]{:S(2)}, u32[]{:S(2)}) collective-permute-start(f32[3,128,512]{2,1,0:T(8,128)S(1)} %get-tuple-element.45.in0), channel_id=1, source_target_pairs={{0,1},{2,3},{4,5},{6,7},{8,9},{10,11},{12,13},{14,15},{1,0},{3,2},... | collective-permute-start | bytes 2359304 | tf_op jit(solution)/shard_map/ppermute | solution.py:105
  102.0 39.2 %collective-permute-start.12 = (f32[3,128,512]{2,1,0:T(8,128)S(1)}, f32[3,128,512]{2,1,0:T(8,128)S(1)}, u32[]{:S(2)}, u32[]{:S(2)}) collective-permute-start(f32[3,128,512]{2,1,0:T(8,128)S(1)} %copy-done.16), channel_id=1, source_target_pairs={{1,2},{3,4},{5,6},{7,8},{9,10},{11,12},{13,14},{2,1},{4,3},{6,5},{... | collective-permute-start | bytes 2359304 | tf_op jit(solution)/shard_map/ppermute | solution.py:105
  103.9 54.1 %collective-permute-start.13 = (f32[3,128,512]{2,1,0:T(8,128)S(1)}, f32[3,128,512]{2,1,0:T(8,128)S(1)}, u32[]{:S(2)}, u32[]{:S(2)}) collective-permute-start(f32[3,128,512]{2,1,0:T(8,128)S(1)} %copy-done.12), channel_id=1, source_target_pairs={{1,2},{3,4},{5,6},{7,8},{9,10},{11,12},{13,14},{2,1},{4,3},{6,5},{... | collective-permute-start | bytes 2359304 | tf_op jit(solution)/shard_map/ppermute | solution.py:105
  108.9 49.1 %copy-start.14 = (f32[3,128,512]{2,1,0:T(8,128)S(1)}, f32[3,128,512]{2,1,0:T(8,128)}, u32[]{:S(2)}) copy-start(f32[3,128,512]{2,1,0:T(8,128)} %copy-done.13) | copy-start | bytes 2359300
  116.6 57.1 %collective-permute-start.10 = (f32[3,128,512]{2,1,0:T(8,128)S(1)}, f32[3,128,512]{2,1,0:T(8,128)S(1)}, u32[]{:S(2)}, u32[]{:S(2)}) collective-permute-start(f32[3,128,512]{2,1,0:T(8,128)S(1)} %get-tuple-element.46.in1), channel_id=1, source_target_pairs={{1,2},{3,4},{5,6},{7,8},{9,10},{11,12},{13,14},{2,1},{4,3},{6,5},{... | collective-permute-start | bytes 2359304 | tf_op jit(solution)/shard_map/ppermute | solution.py:105
  (12 other events, 12.6 us)

commit v13 on v10

--- a/solution.py
+++ b/solution.py
@@ -62,7 +62,7 @@
     return row_prev(f) + row_next(f) + col_prev(f) + col_next(f)
 
 
-def call(kernel, out_shape, in_specs, out_specs, operands, name, weight=0, grid=(), aliases=None, scratch=()):
+def call(kernel, out_shape, in_specs, out_specs, operands, name, weight=0, grid=(1,), aliases=None, scratch=()):
     return pl.pallas_call(
         kernel,
         out_shape=out_shape,
@@ -90,6 +90,7 @@
 
 SMEM = pl.BlockSpec(memory_space=pltpu.SMEM)
 VMEM = pl.BlockSpec(memory_space=pltpu.VMEM)
+ANY = pl.BlockSpec(memory_space=pl.ANY)
 SIDES = (0, 1)
 
 
@@ -126,6 +127,10 @@
 
         def up_at(facts_ref, i):
             return facts_ref[3] if i == 0 else 1 - facts_ref[3]
+
+        def up_here(i):
+            odd = lax.rem(lax.axis_index("slab"), 2)
+            return 1 - odd if i == 0 else odd
 
         tmpl_far = [
             swap(lax.dynamic_slice_in_dim(template, up * (Z - 2), 2, 0), i)
@@ -179,7 +184,6 @@
             [whole(x) for x in outs],
             operands,
             "forward",
-            grid=(1,),
             weight=FORWARD,
         )
         far1 = [swap(inner1[0], 0), None]
@@ -214,7 +218,6 @@
             [whole(x) for x in outs],
             operands,
             "middle",
-            grid=(1,),
             weight=MIDDLE,
         )
         def back(facts_ref, lam2_in, lam2_out, v1, lam1, word0, word1, lam2):
@@ -243,7 +246,6 @@
             [whole(x) for x in outs],
             operands,
             "back",
-            grid=(1,),
             weight=BACK,
             scratch=[pltpu.VMEM((Z, Y, X), jnp.float32)],
         )
@@ -292,7 +294,6 @@
             [whole(x) for x in outs],
             operands,
             "last",
-            grid=(1,),
             weight=LAST,
             scratch=[pltpu.VMEM((Z + 2, Y, X), jnp.float32)],
         )
@@ -387,10 +388,10 @@
             scratch=[u2_scratch, pltpu.VMEM((Z + 4, Y, X), jnp.float32)],
         )
 
-        def add_far(facts_ref, far_0, far_1, rim, _, out, held, done):
+        def add_far(far_0, far_1, rim, _, out, held, done):
             copies = []
             for i, far in ((0, far_0), (1, far_1)):
-                z = up_at(facts_ref, i) * (Z - 1)
+                z = up_here(i) * (Z - 1)
                 for d in range(3):
                     held[i, d] = rim[i, d] + far[d] * SEVENTH**3
                     copies.append(pltpu.make_async_copy(held.at[i, d], out.at[0, d, z], done.at[i, d]))
@@ -401,11 +402,12 @@
         gradient = call(
             add_far,
             struct(*flow.shape),
-            [SMEM, VMEM, VMEM, VMEM, pl.BlockSpec(memory_space=pl.ANY)],
-            pl.BlockSpec(memory_space=pl.ANY),
-            [facts, *far0, rim, gradient],
+            [VMEM, VMEM, VMEM, ANY],
+            ANY,
+            [*far0, rim, gradient],
             "add_far",
-            aliases={4: 0},
+            grid=(),
+            aliases={3: 0},
             scratch=[pltpu.VMEM((2, 3, Y, X), jnp.float32), pltpu.SemaphoreType.DMA((2, 3))],
         )
         return gradient[None], template_grad

time: 176 us -> 176 us (level)
  no operation moved by 1% of the time
where the time goes in v13:
time: 176 us; the launch traced here: 175 us
  waiting for transfers between devices  98.5 us (56%)
  Pallas kernels  41.2 us (23%)
  starting transfers between devices  20.9 us (12%)
  local copies, waits for them, and re-layouts  12.4 us (7%)
    ppermute x12, waiting for transfers between devices, swap(): return lax.ppermute(x, 'slab', pairs[side])  96.7 us
    pallas_call x7, Pallas kernels, call(): pl.pallas_call(kernel, out_shape=out_shape, grid=grid, in_specs=in_specs,...  41.2 us
    ppermute x12, starting transfers between devices, swap(): return lax.ppermute(x, 'slab', pairs[side])  20.7 us
    unnamed x27, local copies, waits for them, and re-layouts  7.47 us
  transfers between devices with their start and end apart: 15, of which 9 were waited for; matrix products, arithmetic and copies ran while one was open for 3% of the time, Pallas kernels for 23%

profile of v13, /device:TPU:2, one launch (start us, length us, event | category | flops | bytes accessed | tf_op | source)
XLA Modules:
  0.0 175.1 jit_solution(15053084109573339945)
XLA Ops:
  0.7 1.1 constant_dynamic-slice_fusion.1
  1.8 4.9 %collective-permute-start.1 = (f32[2,64,512]{2,1,0:T(8,128)S(1)}, f32[2,64,512]{2,1,0:T(8,128)S(1)}, u32[]{:S(2)}, u32[]{:S(2)}) collective-permute-start(f32[2,64,512]{2,1,0:T(8,128)S(1)} %get-tuple-element.61), channel_id=1, source_target_pairs={{1,2},{3,4},{5,6},{7,8},{9,10},{11,12},{13,14},{2,1},{4,3},{6,5},{... | collective-permute-start | bytes 786440 | tf_op jit(solution)/shard_map/ppermute | solution.py:104
  6.7 2.8 %dynamic-slice_bitcast_fusion = (f32[3,128,512]{2,1,0:T(8,128)}, f32[3,128,512]{2,1,0:T(8,128)}) fusion(f32[1,2,3,4,128,512]{5,4,3,2,1,0:T(8,128)} %param.5, s32[]{:T(128)S(6)} %select_n.29, s32[]{:T(128)S(6)} %select_n.28), kind=kLoop, calls=%fused_computation | loop fusion | bytes 3145736 | tf_op jit(solution)/shard_map/squeeze | solution.py:140
  9.5 1.9 %collective-permute-start.5 = (f32[3,128,512]{2,1,0:T(8,128)}, f32[3,128,512]{2,1,0:T(8,128)S(1)}, u32[]{:S(2)}, u32[]{:S(2)}) collective-permute-start(f32[3,128,512]{2,1,0:T(8,128)} %get-tuple-element.58), channel_id=1, source_target_pairs={{1,2},{3,4},{5,6},{7,8},{9,10},{11,12},{13,14},{2,1},{4,3},{6,5},{... | collective-permute-start | bytes 2359304 | tf_op jit(solution)/shard_map/ppermute | solution.py:104
  11.5 21.9 %collective-permute-done.2 = f32[2,64,512]{2,1,0:T(8,128)S(1)} collective-permute-done((f32[2,64,512]{2,1,0:T(8,128)S(1)}, f32[2,64,512]{2,1,0:T(8,128)S(1)}, u32[]{:S(2)}, u32[]{:S(2)}) %collective-permute-start.2) | collective-permute-done | bytes 262176 | tf_op jit(solution)/shard_map/ppermute | solution.py:104
  33.7 1.8 %collective-permute-done.3.refs_4_ = f32[4,64,512]{2,1,0:T(8,128)S(1)} collective-permute-done((f32[4,64,512]{2,1,0:T(8,128)S(1)}, f32[4,64,512]{2,1,0:T(8,128)S(1)}, u32[]{:S(2)}, u32[]{:S(2)}) %collective-permute-start.3) | collective-permute-done | bytes 524320 | tf_op jit(solution)/shard_map/ppermute | solution.py:107
  36.5 6.3 %forward.1 = (f32[8,128,512]{2,1,0:T(8,128)}, f32[4,128,512]{2,1,0:T(8,128)S(1)}, f32[2,128,512]{2,1,0:T(8,128)S(1)}, f32[3,128,512]{2,1,0:T(8,128)}, f32[3,128,512]{2,1,0:T(8,128)S(1)}) custom-call(s32[4]{0:T(128)S(1)} %pad_add_fusion.refs_0_.facts_ref, f32[4,64,512]{2,1,0:T(8,128)S(1)} %copy-done.1, f32[4,64,512]{2,1,0:T(8,128)S(1)} %collective-permute-done.refs_2_, ...), custom_call_target="tpu_custom_call" | custom-call | flops 1024 | bytes 1024 | tf_op jit(solution)/shard_map/forward/pallas_call | solution.py:66
  43.8 6.5 %collective-permute-done.4.halo0 = f32[3,128,512]{2,1,0:T(8,128)S(1)} collective-permute-done((f32[3,128,512]{2,1,0:T(8,128)}, f32[3,128,512]{2,1,0:T(8,128)S(1)}, u32[]{:S(2)}, u32[]{:S(2)}) %collective-permute-start.4) | collective-permute-done | bytes 786464 | tf_op jit(solution)/shard_map/ppermute | solution.py:104
  50.3 4.6 %middle.1 = (f32[3,128,512]{2,1,0:T(8,128)S(1)}, f32[3,128,512]{2,1,0:T(8,128)S(1)}, f32[2,128,512]{2,1,0:T(8,128)S(1)}, f32[2,3,128,512]{3,2,1,0:T(8,128)}) custom-call(s32[4]{0:T(128)S(1)} %pad_add_fusion.refs_0_.facts_ref, f32[8,128,512]{2,1,0:T(8,128)} %get-tuple-element.32.tmpl, f32[4,128,512]{2,1,0:T(8,128)S(1)} %get-tuple-element.34.img1, ...), custom_call_target="tpu_custom_call" | custom-call | flops 1024 | bytes 1024 | tf_op jit(solution)/shard_map/middle/pallas_call | solution.py:66
  56.7 3.5 %back.1 = (f32[4,128,512]{2,1,0:T(8,128)S(1)}, f32[2,128,512]{2,1,0:T(8,128)S(1)}, f32[2,128,512]{2,1,0:T(8,128)S(1)}) custom-call(s32[4]{0:T(128)S(1)} %pad_add_fusion.refs_0_.facts_ref, f32[2,128,512]{2,1,0:T(8,128)S(1)} %get-tuple-element.33.lam2_in, f32[2,128,512]{2,1,0:T(8,128)S(1)} %get-tuple-element.35.lam2_out, f32[2,3,4,128,512]{4,3,2,1,0:T(8,128)} %bitcast.16), custom_call_target="tpu_custom_call" | custom-call | flops 10000001024 | bytes 1024 | tf_op jit(solution)/shard_map/back/pallas_call | solution.py:66
  61.2 4.9 %collective-permute-start.8 = (f32[2,128,512]{2,1,0:T(8,128)S(1)}, f32[2,128,512]{2,1,0:T(8,128)}, u32[]{:S(2)}, u32[]{:S(2)}) collective-permute-start(f32[2,128,512]{2,1,0:T(8,128)S(1)} %get-tuple-element.38.own1), channel_id=1, source_target_pairs={{1,2},{3,4},{5,6},{7,8},{9,10},{11,12},{13,14},{2,1},{4,3},{6,5},{... | collective-permute-start | bytes 1572872 | tf_op jit(solution)/shard_map/ppermute | solution.py:104
  66.9 22.8 %collective-permute-done.7.far0 = f32[2,128,512]{2,1,0:T(8,128)} collective-permute-done((f32[2,128,512]{2,1,0:T(8,128)S(1)}, f32[2,128,512]{2,1,0:T(8,128)}, u32[]{:S(2)}, u32[]{:S(2)}) %collective-permute-start.7) | collective-permute-done | bytes 524320 | tf_op jit(solution)/shard_map/ppermute | solution.py:104
  90.7 1.0 copy-done.9
  91.7 8.4 %last.1 = (f32[4,128,512]{2,1,0:T(8,128)}, f32[3,128,512]{2,1,0:T(8,128)S(1)}, f32[3,128,512]{2,1,0:T(8,128)S(1)}, f32[3,128,512]{2,1,0:T(8,128)S(1)}, f32[3,128...) custom-call(s32[4]{0:T(128)S(1)} %pad_add_fusion.refs_0_.facts_ref, f32[8,128,512]{2,1,0:T(8,128)} %get-tuple-element.32.tmpl, ...), custom_call_target="tpu_custom_call" | custom-call | flops 20000002048 | bytes 1024 | tf_op jit(solution)/shard_map/last/pallas_call | solution.py:66
  100.2 1.1 constant_dynamic-slice_fusion
  101.4 1.9 %collective-permute-start.12 = (f32[3,128,512]{2,1,0:T(8,128)S(1)}, f32[3,128,512]{2,1,0:T(8,128)S(1)}, u32[]{:S(2)}, u32[]{:S(2)}) collective-permute-start(f32[3,128,512]{2,1,0:T(8,128)S(1)} %copy-done.7), channel_id=1, source_target_pairs={{1,2},{3,4},{5,6},{7,8},{9,10},{11,12},{13,14},{2,1},{4,3},{6,5},{... | collective-permute-start | bytes 2359304 | tf_op jit(solution)/shard_map/ppermute | solution.py:104
  103.4 5.0 %collective-permute-start.13 = (f32[3,128,512]{2,1,0:T(8,128)S(1)}, f32[3,128,512]{2,1,0:T(8,128)S(1)}, u32[]{:S(2)}, u32[]{:S(2)}) collective-permute-start(f32[3,128,512]{2,1,0:T(8,128)S(1)} %copy-done.3), channel_id=1, source_target_pairs={{1,2},{3,4},{5,6},{7,8},{9,10},{11,12},{13,14},{2,1},{4,3},{6,5},{... | collective-permute-start | bytes 2359304 | tf_op jit(solution)/shard_map/ppermute | solution.py:104
  108.4 8.6 %smooth_0.1 = (f32[2,3,4,128,512]{4,3,2,1,0:T(8,128)}, f32[2,3,128,512]{3,2,1,0:T(8,128)S(1)}) custom-call(s32[4]{0:T(128)S(1)} %pad_add_fusion.refs_0_.facts_ref, f32[3,128,512]{2,1,0:T(8,128)S(1)} %get-tuple-element.45.in0, f32[3,128,512]{2,1,0:T(8,128)S(1)} %get-tuple-element.46.in1, f32[3,128,512]{2,1,0:T(8,128)S(1)} %get-tuple-element.47.out0, ...), custom_call_target="tpu_custom_call" | custom-call | flops 10000001024 | bytes 1024 | tf_op jit(solution)/shard_map/smooth_0/pallas_call | solution.py:66
  117.0 1.9 %collective-permute-start.10 = (f32[3,128,512]{2,1,0:T(8,128)S(1)}, f32[3,128,512]{2,1,0:T(8,128)S(1)}, u32[]{:S(2)}, u32[]{:S(2)}) collective-permute-start(f32[3,128,512]{2,1,0:T(8,128)S(1)} %get-tuple-element.46.in1), channel_id=1, source_target_pairs={{1,2},{3,4},{5,6},{7,8},{9,10},{11,12},{13,14},{2,1},{4,3},{6,5},{... | collective-permute-start | bytes 2359304 | tf_op jit(solution)/shard_map/ppermute | solution.py:104
  119.8 21.4 %collective-permute-done.12.near1 = f32[3,128,512]{2,1,0:T(8,128)S(1)} collective-permute-done((f32[3,128,512]{2,1,0:T(8,128)S(1)}, f32[3,128,512]{2,1,0:T(8,128)S(1)}, u32[]{:S(2)}, u32[]{:S(2)}) %collective-permute-start.12) | collective-permute-done | bytes 786464 | tf_op jit(solution)/shard_map/ppermute | solution.py:104
  141.1 16.9 %collective-permute-done.13.far1 = f32[3,128,512]{2,1,0:T(8,128)S(1)} collective-permute-done((f32[3,128,512]{2,1,0:T(8,128)S(1)}, f32[3,128,512]{2,1,0:T(8,128)S(1)}, u32[]{:S(2)}, u32[]{:S(2)}) %collective-permute-start.13) | collective-permute-done | bytes 786464 | tf_op jit(solution)/shard_map/ppermute | solution.py:104
  158.9 8.5 %smooth_1.1._ = f32[2,3,4,128,512]{4,3,2,1,0:T(8,128)} custom-call(s32[4]{0:T(128)S(1)} %pad_add_fusion.refs_0_.facts_ref, f32[3,128,512]{2,1,0:T(8,128)} %get-tuple-element.41.in0, f32[3,128,512]{2,1,0:T(8,128)S(1)} %copy-done.3, f32[3,128,512]{2,1,0:T(8,128)S(1)} %copy-done.5, f32[3,128,512]{2,1,0:T(8,128)S(1)} %copy-done.7, ...), custom_call_target="tpu_custom_call", output_to_operand_aliasing={{}: (9, {})} | custom-call | flops 10000001024 | bytes 1024 | tf_op jit(solution)/shard_map/smooth_1/pallas_call | solution.py:66
  167.4 5.3 %collective-permute-done.9.far_0 = f32[3,128,512]{2,1,0:T(8,128)S(1)} collective-permute-done((f32[3,128,512]{2,1,0:T(8,128)S(1)}, f32[3,128,512]{2,1,0:T(8,128)S(1)}, u32[]{:S(2)}, u32[]{:S(2)}) %collective-permute-start.9) | collective-permute-done | bytes 786464 | tf_op jit(solution)/shard_map/ppermute | solution.py:104
  173.7 1.2 add_far.1
  (46 shorter events, 9.8 us)
Async XLA Ops:
  1.7 31.7 %collective-permute-start.2 = (f32[2,64,512]{2,1,0:T(8,128)S(1)}, f32[2,64,512]{2,1,0:T(8,128)S(1)}, u32[]{:S(2)}, u32[]{:S(2)}) collective-permute-start(f32[2,64,512]{2,1,0:T(8,128)S(1)} %get-tuple-element.60), channel_id=1, source_target_pairs={{0,1},{2,3},{4,5},{6,7},{8,9},{10,11},{12,13},{14,15},{1,0},{3,2},... | collective-permute-start | bytes 786440 | tf_op jit(solution)/shard_map/ppermute | solution.py:104
  1.8 31.7 %collective-permute-start.1 = (f32[2,64,512]{2,1,0:T(8,128)S(1)}, f32[2,64,512]{2,1,0:T(8,128)S(1)}, u32[]{:S(2)}, u32[]{:S(2)}) collective-permute-start(f32[2,64,512]{2,1,0:T(8,128)S(1)} %get-tuple-element.61), channel_id=1, source_target_pairs={{1,2},{3,4},{5,6},{7,8},{9,10},{11,12},{13,14},{2,1},{4,3},{6,5},{... | collective-permute-start | bytes 786440 | tf_op jit(solution)/shard_map/ppermute | solution.py:104
  9.5 34.3 %collective-permute-start.5 = (f32[3,128,512]{2,1,0:T(8,128)}, f32[3,128,512]{2,1,0:T(8,128)S(1)}, u32[]{:S(2)}, u32[]{:S(2)}) collective-permute-start(f32[3,128,512]{2,1,0:T(8,128)} %get-tuple-element.58), channel_id=1, source_target_pairs={{1,2},{3,4},{5,6},{7,8},{9,10},{11,12},{13,14},{2,1},{4,3},{6,5},{... | collective-permute-start | bytes 2359304 | tf_op jit(solution)/shard_map/ppermute | solution.py:104
  11.4 38.9 %collective-permute-start.4 = (f32[3,128,512]{2,1,0:T(8,128)}, f32[3,128,512]{2,1,0:T(8,128)S(1)}, u32[]{:S(2)}, u32[]{:S(2)}) collective-permute-start(f32[3,128,512]{2,1,0:T(8,128)} %get-tuple-element.59), channel_id=1, source_target_pairs={{0,1},{2,3},{4,5},{6,7},{8,9},{10,11},{12,13},{14,15},{1,0},{3,2},... | collective-permute-start | bytes 2359304 | tf_op jit(solution)/shard_map/ppermute | solution.py:104
  11.5 22.2 %collective-permute-start = (f32[4,64,512]{2,1,0:T(8,128)}, f32[4,64,512]{2,1,0:T(8,128)S(1)}, u32[]{:S(2)}, u32[]{:S(2)}) collective-permute-start(f32[4,64,512]{2,1,0:T(8,128)} %refs_1_.1), channel_id=1, source_target_pairs={{0,16},{16,0},{1,17},{17,1},{2,18},{18,2},{3,19},{19,3},{4,20},{20... | collective-permute-start | bytes 1572872 | tf_op jit(solution)/shard_map/ppermute | solution.py:107
  33.5 2.0 %collective-permute-start.3 = (f32[4,64,512]{2,1,0:T(8,128)S(1)}, f32[4,64,512]{2,1,0:T(8,128)S(1)}, u32[]{:S(2)}, u32[]{:S(2)}) collective-permute-start(f32[4,64,512]{2,1,0:T(8,128)S(1)} %constant_dynamic-update-slice_fusion.refs_3_), channel_id=1, source_target_pairs={{0,16},{16,0},{1,17},{17,1},{2,18},{18,2},{3,19},{19,3},{4,20},{20... | collective-permute-start | bytes 1572872 | tf_op jit(solution)/shard_map/ppermute | solution.py:107
  35.5 1.0 copy-start.1
  36.5 13.8 %copy-start = (f32[1,4,128,512]{3,2,1,0:T(8,128)S(1)}, f32[1,4,128,512]{3,2,1,0:T(8,128)}, u32[]{:S(2)}) copy-start(f32[1,4,128,512]{3,2,1,0:T(8,128)} %param.4) | copy-start | bytes 3145732
  42.9 0.9 copy-start.2
  43.8 46.9 %collective-permute-start.6 = (f32[3,128,512]{2,1,0:T(8,128)}, f32[3,128,512]{2,1,0:T(8,128)S(1)}, u32[]{:S(2)}, u32[]{:S(2)}) collective-permute-start(f32[3,128,512]{2,1,0:T(8,128)} %get-tuple-element.41.in0), channel_id=1, source_target_pairs={{0,1},{2,3},{4,5},{6,7},{8,9},{10,11},{12,13},{14,15},{1,0},{3,2},... | collective-permute-start | bytes 2359304 | tf_op jit(solution)/shard_map/ppermute | solution.py:104
  56.7 10.2 %copy-start.5 = (f32[3,128,512]{2,1,0:T(8,128)S(1)}, f32[3,128,512]{2,1,0:T(8,128)}, u32[]{:S(2)}) copy-start(f32[3,128,512]{2,1,0:T(8,128)} %copy-done.4) | copy-start | bytes 2359300
  60.2 1.0 copy-start.10
  61.2 28.5 %collective-permute-start.7 = (f32[2,128,512]{2,1,0:T(8,128)S(1)}, f32[2,128,512]{2,1,0:T(8,128)}, u32[]{:S(2)}, u32[]{:S(2)}) collective-permute-start(f32[2,128,512]{2,1,0:T(8,128)S(1)} %get-tuple-element.37.own0), channel_id=1, source_target_pairs={{0,1},{2,3},{4,5},{6,7},{8,9},{10,11},{12,13},{14,15},{1,0},{3,2},... | collective-permute-start | bytes 1572872 | tf_op jit(solution)/shard_map/ppermute | solution.py:104
  61.2 29.5 %collective-permute-start.8 = (f32[2,128,512]{2,1,0:T(8,128)S(1)}, f32[2,128,512]{2,1,0:T(8,128)}, u32[]{:S(2)}, u32[]{:S(2)}) collective-permute-start(f32[2,128,512]{2,1,0:T(8,128)S(1)} %get-tuple-element.38.own1), channel_id=1, source_target_pairs={{1,2},{3,4},{5,6},{7,8},{9,10},{11,12},{13,14},{2,1},{4,3},{6,5},{... | collective-permute-start | bytes 1572872 | tf_op jit(solution)/shard_map/ppermute | solution.py:104
  66.9 52.9 %collective-permute-start.11 = (f32[3,128,512]{2,1,0:T(8,128)S(1)}, f32[3,128,512]{2,1,0:T(8,128)S(1)}, u32[]{:S(2)}, u32[]{:S(2)}) collective-permute-start(f32[3,128,512]{2,1,0:T(8,128)S(1)} %copy-done.5), channel_id=1, source_target_pairs={{0,1},{2,3},{4,5},{6,7},{8,9},{10,11},{12,13},{14,15},{1,0},{3,2},... | collective-permute-start | bytes 2359304 | tf_op jit(solution)/shard_map/ppermute | solution.py:104
  90.7 1.0 copy-start.9
  91.7 9.7 %copy-start.7 = (f32[3,128,512]{2,1,0:T(8,128)S(1)}, f32[3,128,512]{2,1,0:T(8,128)}, u32[]{:S(2)}) copy-start(f32[3,128,512]{2,1,0:T(8,128)} %copy-done.6) | copy-start | bytes 2359300
  91.7 11.6 %copy-start.3 = (f32[3,128,512]{2,1,0:T(8,128)S(1)}, f32[3,128,512]{2,1,0:T(8,128)}, u32[]{:S(2)}) copy-start(f32[3,128,512]{2,1,0:T(8,128)} %copy-done.2) | copy-start | bytes 2359300
  101.3 15.7 %collective-permute-start.14 = (f32[4,64,512]{2,1,0:T(8,128)S(1)}, f32[4,64,512]{2,1,0:T(8,128)S(1)}, u32[]{:S(2)}, u32[]{:S(2)}) collective-permute-start(f32[4,64,512]{2,1,0:T(8,128)S(1)} %constant_dynamic-slice_fusion), channel_id=1, source_target_pairs={{0,16},{16,0},{1,17},{17,1},{2,18},{18,2},{3,19},{19,3},{4,20},{20... | collective-permute-start | bytes 1572872 | tf_op jit(solution)/shard_map/ppermute | solution.py:107
  101.3 71.4 %collective-permute-start.9 = (f32[3,128,512]{2,1,0:T(8,128)S(1)}, f32[3,128,512]{2,1,0:T(8,128)S(1)}, u32[]{:S(2)}, u32[]{:S(2)}) collective-permute-start(f32[3,128,512]{2,1,0:T(8,128)S(1)} %get-tuple-element.45.in0), channel_id=1, source_target_pairs={{0,1},{2,3},{4,5},{6,7},{8,9},{10,11},{12,13},{14,15},{1,0},{3,2},... | collective-permute-start | bytes 2359304 | tf_op jit(solution)/shard_map/ppermute | solution.py:104
  101.4 39.7 %collective-permute-start.12 = (f32[3,128,512]{2,1,0:T(8,128)S(1)}, f32[3,128,512]{2,1,0:T(8,128)S(1)}, u32[]{:S(2)}, u32[]{:S(2)}) collective-permute-start(f32[3,128,512]{2,1,0:T(8,128)S(1)} %copy-done.7), channel_id=1, source_target_pairs={{1,2},{3,4},{5,6},{7,8},{9,10},{11,12},{13,14},{2,1},{4,3},{6,5},{... | collective-permute-start | bytes 2359304 | tf_op jit(solution)/shard_map/ppermute | solution.py:104
  103.4 54.6 %collective-permute-start.13 = (f32[3,128,512]{2,1,0:T(8,128)S(1)}, f32[3,128,512]{2,1,0:T(8,128)S(1)}, u32[]{:S(2)}, u32[]{:S(2)}) collective-permute-start(f32[3,128,512]{2,1,0:T(8,128)S(1)} %copy-done.3), channel_id=1, source_target_pairs={{1,2},{3,4},{5,6},{7,8},{9,10},{11,12},{13,14},{2,1},{4,3},{6,5},{... | collective-permute-start | bytes 2359304 | tf_op jit(solution)/shard_map/ppermute | solution.py:104
  108.4 10.5 %copy-start.11 = (f32[4,128,512]{2,1,0:T(8,128)S(1)}, f32[4,128,512]{2,1,0:T(8,128)}, u32[]{:S(2)}) copy-start(f32[4,128,512]{2,1,0:T(8,128)} %get-tuple-element.57) | copy-start | bytes 3145732
  117.0 56.7 %collective-permute-start.10 = (f32[3,128,512]{2,1,0:T(8,128)S(1)}, f32[3,128,512]{2,1,0:T(8,128)S(1)}, u32[]{:S(2)}, u32[]{:S(2)}) collective-permute-start(f32[3,128,512]{2,1,0:T(8,128)S(1)} %get-tuple-element.46.in1), channel_id=1, source_target_pairs={{1,2},{3,4},{5,6},{7,8},{9,10},{11,12},{13,14},{2,1},{4,3},{6,5},{... | collective-permute-start | bytes 2359304 | tf_op jit(solution)/shard_map/ppermute | solution.py:104
  (4 other events, 3.5 us)

commit v14 on v13

--- a/solution.py
+++ b/solution.py
@@ -71,7 +71,7 @@
         out_specs=out_specs,
         scratch_shapes=list(scratch),
         input_output_aliases=aliases or {},
-        compiler_params=pltpu.CompilerParams(vmem_limit_bytes=48 * MIB),
+        compiler_params=pltpu.CompilerParams(vmem_limit_bytes=24 * MIB),
         cost_estimate=pl.CostEstimate(
             flops=1024 + weight * 10000000, bytes_accessed=1024, transcendentals=0
         ),

time: 176 us -> 176 us (level)
  Pallas kernels: 41.2 us -> 29.2 us
  local copies, waits for them, and re-layouts: 12.4 us -> 22.1 us
    pallas_call x7, Pallas kernels: 41.2 us -> 29.2 us  [call(): pl.pallas_call(kernel, out_shape=out_shape, grid=grid, in_specs=in_specs,...]
    unnamed x27 -> x43, local copies, waits for them, and re-layouts: 7.47 us -> 18.2 us
    ppermute x12, waiting for transfers between devices: 96.7 us -> 98.7 us  [swap(): return lax.ppermute(x, 'slab', pairs[side])]
  transfers between devices with their start and end apart: 15 -> 15, of which waited for: 9 -> 9; matrix products, arithmetic and copies ran while one was open for 3% -> 2% of each run, Pallas kernels for 23% -> 16%
where the time goes in v14:
time: 176 us; the launch traced here: 175 us
  waiting for transfers between devices  99.7 us (57%)
  Pallas kernels  29.2 us (17%)
  local copies, waits for them, and re-layouts  22.1 us (13%)
  starting transfers between devices  22.1 us (13%)
    ppermute x12, waiting for transfers between devices, swap(): return lax.ppermute(x, 'slab', pairs[side])  98.7 us
    pallas_call x7, Pallas kernels, call(): pl.pallas_call(kernel, out_shape=out_shape, grid=grid, in_specs=in_specs,...  29.2 us
    ppermute x12, starting transfers between devices, swap(): return lax.ppermute(x, 'slab', pairs[side])  21.9 us
    unnamed x43, local copies, waits for them, and re-layouts  18.2 us
  transfers between devices with their start and end apart: 15, of which 9 were waited for; matrix products, arithmetic and copies ran while one was open for 2% of the time, Pallas kernels for 16%

profile of v14, /device:TPU:2, one launch (start us, length us, event | category | flops | bytes accessed | tf_op | source)
XLA Modules:
  0.0 175.1 jit_solution(2695651981155377381)
XLA Ops:
  1.8 4.9 %collective-permute-start.1 = (f32[2,64,512]{2,1,0:T(8,128)S(1)}, f32[2,64,512]{2,1,0:T(8,128)S(1)}, u32[]{:S(2)}, u32[]{:S(2)}) collective-permute-start(f32[2,64,512]{2,1,0:T(8,128)S(1)} %get-tuple-element.61), channel_id=1, source_target_pairs={{1,2},{3,4},{5,6},{7,8},{9,10},{11,12},{13,14},{2,1},{4,3},{6,5},{... | collective-permute-start | bytes 786440 | tf_op jit(solution)/shard_map/ppermute | solution.py:104
  6.7 2.8 %dynamic-slice_bitcast_fusion = (f32[3,128,512]{2,1,0:T(8,128)}, f32[3,128,512]{2,1,0:T(8,128)}) fusion(f32[1,2,3,4,128,512]{5,4,3,2,1,0:T(8,128)} %param.5, s32[]{:T(128)S(6)} %select_n.29, s32[]{:T(128)S(6)} %select_n.28), kind=kLoop, calls=%fused_computation | loop fusion | bytes 3145736 | tf_op jit(solution)/shard_map/squeeze | solution.py:140
  9.5 1.9 %collective-permute-start.5 = (f32[3,128,512]{2,1,0:T(8,128)}, f32[3,128,512]{2,1,0:T(8,128)S(1)}, u32[]{:S(2)}, u32[]{:S(2)}) collective-permute-start(f32[3,128,512]{2,1,0:T(8,128)} %get-tuple-element.58), channel_id=1, source_target_pairs={{1,2},{3,4},{5,6},{7,8},{9,10},{11,12},{13,14},{2,1},{4,3},{6,5},{... | collective-permute-start | bytes 2359304 | tf_op jit(solution)/shard_map/ppermute | solution.py:104
  11.5 21.9 %collective-permute-done.2 = f32[2,64,512]{2,1,0:T(8,128)S(1)} collective-permute-done((f32[2,64,512]{2,1,0:T(8,128)S(1)}, f32[2,64,512]{2,1,0:T(8,128)S(1)}, u32[]{:S(2)}, u32[]{:S(2)}) %collective-permute-start.2) | collective-permute-done | bytes 262176 | tf_op jit(solution)/shard_map/ppermute | solution.py:104
  36.3 2.8 %copy-done = f32[1,2,3,4,128,512]{5,4,3,2,1,0:T(8,128)S(1)} copy-done((f32[1,2,3,4,128,512]{5,4,3,2,1,0:T(8,128)S(1)}, f32[1,2,3,4,128,512]{5,4,3,2,1,0:T(8,128)}, u32[]{:S(2)}) %copy-start) | copy-done | bytes 6291480
  39.1 1.2 copy-done.2
  43.4 3.0 %forward.1 = (f32[8,128,512]{2,1,0:T(8,128)S(1)}, f32[4,128,512]{2,1,0:T(8,128)S(1)}, f32[2,128,512]{2,1,0:T(8,128)S(1)}, f32[3,128,512]{2,1,0:T(8,128)}, f32[3,128,512]{2,1,0:T(8,128)S(1)}) custom-call(s32[4]{0:T(128)S(1)} %pad_add_fusion.refs_0_.facts_ref, f32[4,64,512]{2,1,0:T(8,128)S(1)} %copy-done.4, f32[4,64,512]{2,1,0:T(8,128)S(1)} %copy-done.6, ...), custom_call_target="tpu_custom_call" | custom-call | flops 1024 | bytes 1024 | tf_op jit(solution)/shard_map/forward/pallas_call | solution.py:66
  46.5 2.8 %collective-permute-done.4.halo0 = f32[3,128,512]{2,1,0:T(8,128)} collective-permute-done((f32[3,128,512]{2,1,0:T(8,128)}, f32[3,128,512]{2,1,0:T(8,128)}, u32[]{:S(2)}, u32[]{:S(2)}) %collective-permute-start.4) | collective-permute-done | bytes 786464 | tf_op jit(solution)/shard_map/ppermute | solution.py:104
  49.3 2.4 %middle.1 = (f32[3,128,512]{2,1,0:T(8,128)S(1)}, f32[3,128,512]{2,1,0:T(8,128)S(1)}, f32[2,128,512]{2,1,0:T(8,128)S(1)}, f32[2,3,128,512]{3,2,1,0:T(8,128)S(1)}) custom-call(s32[4]{0:T(128)S(1)} %pad_add_fusion.refs_0_.facts_ref, f32[8,128,512]{2,1,0:T(8,128)S(1)} %get-tuple-element.32.tmpl, f32[4,128,512]{2,1,0:T(8,128)S(1)} %get-tuple-element.34.img1, ...), custom_call_target="tpu_custom_call" | custom-call | flops 1024 | bytes 1024 | tf_op jit(solution)/shard_map/middle/pallas_call | solution.py:66
  52.9 2.1 %back.1 = (f32[4,128,512]{2,1,0:T(8,128)S(1)}, f32[2,128,512]{2,1,0:T(8,128)S(1)}, f32[2,128,512]{2,1,0:T(8,128)S(1)}) custom-call(s32[4]{0:T(128)S(1)} %pad_add_fusion.refs_0_.facts_ref, f32[2,128,512]{2,1,0:T(8,128)S(1)} %get-tuple-element.33.lam2_in, f32[2,128,512]{2,1,0:T(8,128)S(1)} %get-tuple-element.35.lam2_out, f32[2,3,4,128,512]{4,3,2,1,0:T(8,128)S(1)} %bitcast.14), custom_call_target="tpu_custom_call" | custom-call | flops 10000001024 | bytes 1024 | tf_op jit(solution)/shard_map/back/pallas_call | solution.py:66
  56.2 5.7 %collective-permute-start.8 = (f32[2,128,512]{2,1,0:T(8,128)S(1)}, f32[2,128,512]{2,1,0:T(8,128)}, u32[]{:S(2)}, u32[]{:S(2)}) collective-permute-start(f32[2,128,512]{2,1,0:T(8,128)S(1)} %get-tuple-element.38.own1), channel_id=1, source_target_pairs={{1,2},{3,4},{5,6},{7,8},{9,10},{11,12},{13,14},{2,1},{4,3},{6,5},{... | collective-permute-start | bytes 1572872 | tf_op jit(solution)/shard_map/ppermute | solution.py:104
  62.8 26.9 %collective-permute-done.7.far0 = f32[2,128,512]{2,1,0:T(8,128)} collective-permute-done((f32[2,128,512]{2,1,0:T(8,128)S(1)}, f32[2,128,512]{2,1,0:T(8,128)}, u32[]{:S(2)}, u32[]{:S(2)}) %collective-permute-start.7) | collective-permute-done | bytes 524320 | tf_op jit(solution)/shard_map/ppermute | solution.py:104
  90.7 2.8 %copy-done.1 = f32[1,2,3,4,128,512]{5,4,3,2,1,0:T(8,128)S(1)} copy-done((f32[1,2,3,4,128,512]{5,4,3,2,1,0:T(8,128)S(1)}, f32[1,2,3,4,128,512]{5,4,3,2,1,0:T(8,128)}, u32[]{:S(2)}) %copy-start.1) | copy-done | bytes 6291480
  93.5 1.4 copy-done.10
  95.9 1.2 copy-done.20
  97.2 4.6 %last.1 = (f32[4,128,512]{2,1,0:T(8,128)S(1)}, f32[3,128,512]{2,1,0:T(8,128)S(1)}, f32[3,128,512]{2,1,0:T(8,128)S(1)}, f32[3,128,512]{2,1,0:T(8,128)S(1)}, f32[3...) custom-call(s32[4]{0:T(128)S(1)} %pad_add_fusion.refs_0_.facts_ref, f32[8,128,512]{2,1,0:T(8,128)S(1)} %get-tuple-element.32.tmpl, ...), custom_call_target="tpu_custom_call" | custom-call | flops 20000002048 | bytes 1024 | tf_op jit(solution)/shard_map/last/pallas_call | solution.py:66
  102.0 1.9 %collective-permute-start.12 = (f32[3,128,512]{2,1,0:T(8,128)S(1)}, f32[3,128,512]{2,1,0:T(8,128)S(1)}, u32[]{:S(2)}, u32[]{:S(2)}) collective-permute-start(f32[3,128,512]{2,1,0:T(8,128)S(1)} %copy-done.16), channel_id=1, source_target_pairs={{1,2},{3,4},{5,6},{7,8},{9,10},{11,12},{13,14},{2,1},{4,3},{6,5},{... | collective-permute-start | bytes 2359304 | tf_op jit(solution)/shard_map/ppermute | solution.py:104
  103.9 5.0 %collective-permute-start.13 = (f32[3,128,512]{2,1,0:T(8,128)S(1)}, f32[3,128,512]{2,1,0:T(8,128)S(1)}, u32[]{:S(2)}, u32[]{:S(2)}) collective-permute-start(f32[3,128,512]{2,1,0:T(8,128)S(1)} %copy-done.12), channel_id=1, source_target_pairs={{1,2},{3,4},{5,6},{7,8},{9,10},{11,12},{13,14},{2,1},{4,3},{6,5},{... | collective-permute-start | bytes 2359304 | tf_op jit(solution)/shard_map/ppermute | solution.py:104
  108.9 7.7 %smooth_0.1 = (f32[2,3,4,128,512]{4,3,2,1,0:T(8,128)}, f32[2,3,128,512]{3,2,1,0:T(8,128)S(1)}) custom-call(s32[4]{0:T(128)S(1)} %pad_add_fusion.refs_0_.facts_ref, f32[3,128,512]{2,1,0:T(8,128)S(1)} %get-tuple-element.45.in0, f32[3,128,512]{2,1,0:T(8,128)S(1)} %get-tuple-element.46.in1, f32[3,128,512]{2,1,0:T(8,128)S(1)} %get-tuple-element.47.out0, ...), custom_call_target="tpu_custom_call" | custom-call | flops 10000001024 | bytes 1024 | tf_op jit(solution)/shard_map/smooth_0/pallas_call | solution.py:66
  116.6 1.9 %collective-permute-start.10 = (f32[3,128,512]{2,1,0:T(8,128)S(1)}, f32[3,128,512]{2,1,0:T(8,128)S(1)}, u32[]{:S(2)}, u32[]{:S(2)}) collective-permute-start(f32[3,128,512]{2,1,0:T(8,128)S(1)} %get-tuple-element.46.in1), channel_id=1, source_target_pairs={{1,2},{3,4},{5,6},{7,8},{9,10},{11,12},{13,14},{2,1},{4,3},{6,5},{... | collective-permute-start | bytes 2359304 | tf_op jit(solution)/shard_map/ppermute | solution.py:104
  119.5 21.7 %collective-permute-done.12.near1 = f32[3,128,512]{2,1,0:T(8,128)S(1)} collective-permute-done((f32[3,128,512]{2,1,0:T(8,128)S(1)}, f32[3,128,512]{2,1,0:T(8,128)S(1)}, u32[]{:S(2)}, u32[]{:S(2)}) %collective-permute-start.12) | collective-permute-done | bytes 786464 | tf_op jit(solution)/shard_map/ppermute | solution.py:104
  141.1 16.9 %collective-permute-done.13.far1 = f32[3,128,512]{2,1,0:T(8,128)S(1)} collective-permute-done((f32[3,128,512]{2,1,0:T(8,128)S(1)}, f32[3,128,512]{2,1,0:T(8,128)S(1)}, u32[]{:S(2)}, u32[]{:S(2)}) %collective-permute-start.13) | collective-permute-done | bytes 786464 | tf_op jit(solution)/shard_map/ppermute | solution.py:104
  158.0 8.2 %smooth_1.1._ = f32[2,3,4,128,512]{4,3,2,1,0:T(8,128)} custom-call(s32[4]{0:T(128)S(1)} %pad_add_fusion.refs_0_.facts_ref, f32[3,128,512]{2,1,0:T(8,128)} %get-tuple-element.41.in0, f32[3,128,512]{2,1,0:T(8,128)S(1)} %copy-done.12, f32[3,128,512]{2,1,0:T(8,128)S(1)} %copy-done.14, f32[3,128,512]{2,1,0:T(8,128)S(1)} %copy-done.16, ...), custom_call_target="tpu_custom_call", output_to_operand_aliasing={{}: (9, {})} | custom-call | flops 10000001024 | bytes 1024 | tf_op jit(solution)/shard_map/smooth_1/pallas_call | solution.py:66
  166.2 6.8 %collective-permute-done.9.far_0 = f32[3,128,512]{2,1,0:T(8,128)S(1)} collective-permute-done((f32[3,128,512]{2,1,0:T(8,128)S(1)}, f32[3,128,512]{2,1,0:T(8,128)S(1)}, u32[]{:S(2)}, u32[]{:S(2)}) %collective-permute-start.9) | collective-permute-done | bytes 786464 | tf_op jit(solution)/shard_map/ppermute | solution.py:104
  (62 shorter events, 15.6 us)
Async XLA Ops:
  1.7 31.7 %collective-permute-start.2 = (f32[2,64,512]{2,1,0:T(8,128)S(1)}, f32[2,64,512]{2,1,0:T(8,128)S(1)}, u32[]{:S(2)}, u32[]{:S(2)}) collective-permute-start(f32[2,64,512]{2,1,0:T(8,128)S(1)} %get-tuple-element.60), channel_id=1, source_target_pairs={{0,1},{2,3},{4,5},{6,7},{8,9},{10,11},{12,13},{14,15},{1,0},{3,2},... | collective-permute-start | bytes 786440 | tf_op jit(solution)/shard_map/ppermute | solution.py:104
  1.8 31.7 %collective-permute-start.1 = (f32[2,64,512]{2,1,0:T(8,128)S(1)}, f32[2,64,512]{2,1,0:T(8,128)S(1)}, u32[]{:S(2)}, u32[]{:S(2)}) collective-permute-start(f32[2,64,512]{2,1,0:T(8,128)S(1)} %get-tuple-element.61), channel_id=1, source_target_pairs={{1,2},{3,4},{5,6},{7,8},{9,10},{11,12},{13,14},{2,1},{4,3},{6,5},{... | collective-permute-start | bytes 786440 | tf_op jit(solution)/shard_map/ppermute | solution.py:104
  9.5 37.0 %collective-permute-start.5 = (f32[3,128,512]{2,1,0:T(8,128)}, f32[3,128,512]{2,1,0:T(8,128)S(1)}, u32[]{:S(2)}, u32[]{:S(2)}) collective-permute-start(f32[3,128,512]{2,1,0:T(8,128)} %get-tuple-element.58), channel_id=1, source_target_pairs={{1,2},{3,4},{5,6},{7,8},{9,10},{11,12},{13,14},{2,1},{4,3},{6,5},{... | collective-permute-start | bytes 2359304 | tf_op jit(solution)/shard_map/ppermute | solution.py:104
  11.4 37.9 %collective-permute-start.4 = (f32[3,128,512]{2,1,0:T(8,128)}, f32[3,128,512]{2,1,0:T(8,128)}, u32[]{:S(2)}, u32[]{:S(2)}) collective-permute-start(f32[3,128,512]{2,1,0:T(8,128)} %get-tuple-element.59), channel_id=1, source_target_pairs={{0,1},{2,3},{4,5},{6,7},{8,9},{10,11},{12,13},{14,15},{1,0},{3,2},... | collective-permute-start | bytes 2359304 | tf_op jit(solution)/shard_map/ppermute | solution.py:104
  11.4 22.2 %collective-permute-start = (f32[4,64,512]{2,1,0:T(8,128)}, f32[4,64,512]{2,1,0:T(8,128)S(1)}, u32[]{:S(2)}, u32[]{:S(2)}) collective-permute-start(f32[4,64,512]{2,1,0:T(8,128)} %refs_1_.1), channel_id=1, source_target_pairs={{0,16},{16,0},{1,17},{17,1},{2,18},{18,2},{3,19},{19,3},{4,20},{20... | collective-permute-start | bytes 1572872 | tf_op jit(solution)/shard_map/ppermute | solution.py:107
  33.5 2.0 %collective-permute-start.3 = (f32[4,64,512]{2,1,0:T(8,128)S(1)}, f32[4,64,512]{2,1,0:T(8,128)S(1)}, u32[]{:S(2)}, u32[]{:S(2)}) collective-permute-start(f32[4,64,512]{2,1,0:T(8,128)S(1)} %constant_dynamic-update-slice_fusion.refs_3_), channel_id=1, source_target_pairs={{0,16},{16,0},{1,17},{17,1},{2,18},{18,2},{3,19},{19,3},{4,20},{20... | collective-permute-start | bytes 1572872 | tf_op jit(solution)/shard_map/ppermute | solution.py:107
  36.3 2.8 %copy-start = (f32[1,2,3,4,128,512]{5,4,3,2,1,0:T(8,128)S(1)}, f32[1,2,3,4,128,512]{5,4,3,2,1,0:T(8,128)}, u32[]{:S(2)}) copy-start(f32[1,2,3,4,128,512]{5,4,3,2,1,0:T(8,128)} %param.5) | copy-start | bytes 18874372
  43.4 5.8 %copy-start.3 = (f32[1,4,128,512]{3,2,1,0:T(8,128)S(1)}, f32[1,4,128,512]{3,2,1,0:T(8,128)}, u32[]{:S(2)}) copy-start(f32[1,4,128,512]{3,2,1,0:T(8,128)} %param.4) | copy-start | bytes 3145732
  46.5 8.5 %copy-start.11 = (f32[3,128,512]{2,1,0:T(8,128)}, f32[3,128,512]{2,1,0:T(8,128)S(1)}, u32[]{:S(2)}) copy-start(f32[3,128,512]{2,1,0:T(8,128)S(1)} %get-tuple-element.55.in1) | copy-start | bytes 2359300
  46.5 44.2 %collective-permute-start.6 = (f32[3,128,512]{2,1,0:T(8,128)}, f32[3,128,512]{2,1,0:T(8,128)}, u32[]{:S(2)}, u32[]{:S(2)}) collective-permute-start(f32[3,128,512]{2,1,0:T(8,128)} %get-tuple-element.41.in0), channel_id=1, source_target_pairs={{0,1},{2,3},{4,5},{6,7},{8,9},{10,11},{12,13},{14,15},{1,0},{3,2},... | collective-permute-start | bytes 2359304 | tf_op jit(solution)/shard_map/ppermute | solution.py:104
  52.8 2.1 %copy-start.13 = (f32[3,128,512]{2,1,0:T(8,128)}, f32[3,128,512]{2,1,0:T(8,128)S(1)}, u32[]{:S(2)}) copy-start(f32[3,128,512]{2,1,0:T(8,128)S(1)} %get-tuple-element.52.out0) | copy-start | bytes 2359300
  52.8 2.1 %copy-start.15 = (f32[3,128,512]{2,1,0:T(8,128)}, f32[3,128,512]{2,1,0:T(8,128)S(1)}, u32[]{:S(2)}) copy-start(f32[3,128,512]{2,1,0:T(8,128)S(1)} %get-tuple-element.53.out1) | copy-start | bytes 2359300
  55.9 33.7 %collective-permute-start.7 = (f32[2,128,512]{2,1,0:T(8,128)S(1)}, f32[2,128,512]{2,1,0:T(8,128)}, u32[]{:S(2)}, u32[]{:S(2)}) collective-permute-start(f32[2,128,512]{2,1,0:T(8,128)S(1)} %get-tuple-element.37.own0), channel_id=1, source_target_pairs={{0,1},{2,3},{4,5},{6,7},{8,9},{10,11},{12,13},{14,15},{1,0},{3,2},... | collective-permute-start | bytes 1572872 | tf_op jit(solution)/shard_map/ppermute | solution.py:104
  56.2 34.5 %collective-permute-start.8 = (f32[2,128,512]{2,1,0:T(8,128)S(1)}, f32[2,128,512]{2,1,0:T(8,128)}, u32[]{:S(2)}, u32[]{:S(2)}) collective-permute-start(f32[2,128,512]{2,1,0:T(8,128)S(1)} %get-tuple-element.38.own1), channel_id=1, source_target_pairs={{1,2},{3,4},{5,6},{7,8},{9,10},{11,12},{13,14},{2,1},{4,3},{6,5},{... | collective-permute-start | bytes 1572872 | tf_op jit(solution)/shard_map/ppermute | solution.py:104
  62.8 56.7 %collective-permute-start.11 = (f32[3,128,512]{2,1,0:T(8,128)}, f32[3,128,512]{2,1,0:T(8,128)S(1)}, u32[]{:S(2)}, u32[]{:S(2)}) collective-permute-start(f32[3,128,512]{2,1,0:T(8,128)} %copy-done.13), channel_id=1, source_target_pairs={{0,1},{2,3},{4,5},{6,7},{8,9},{10,11},{12,13},{14,15},{1,0},{3,2},... | collective-permute-start | bytes 2359304 | tf_op jit(solution)/shard_map/ppermute | solution.py:104
  90.7 2.8 %copy-start.1 = (f32[1,2,3,4,128,512]{5,4,3,2,1,0:T(8,128)S(1)}, f32[1,2,3,4,128,512]{5,4,3,2,1,0:T(8,128)}, u32[]{:S(2)}) copy-start(f32[1,2,3,4,128,512]{5,4,3,2,1,0:T(8,128)} %param.5) | copy-start | bytes 18874372
  97.2 4.8 %copy-start.16 = (f32[3,128,512]{2,1,0:T(8,128)S(1)}, f32[3,128,512]{2,1,0:T(8,128)}, u32[]{:S(2)}) copy-start(f32[3,128,512]{2,1,0:T(8,128)} %copy-done.15) | copy-start | bytes 2359300
  97.2 6.8 %copy-start.12 = (f32[3,128,512]{2,1,0:T(8,128)S(1)}, f32[3,128,512]{2,1,0:T(8,128)}, u32[]{:S(2)}) copy-start(f32[3,128,512]{2,1,0:T(8,128)} %copy-done.11) | copy-start | bytes 2359300
  101.8 14.8 %collective-permute-start.14 = (f32[4,64,512]{2,1,0:T(8,128)S(1)}, f32[4,64,512]{2,1,0:T(8,128)S(1)}, u32[]{:S(2)}, u32[]{:S(2)}) collective-permute-start(f32[4,64,512]{2,1,0:T(8,128)S(1)} %constant_dynamic-slice_fusion), channel_id=1, source_target_pairs={{0,16},{16,0},{1,17},{17,1},{2,18},{18,2},{3,19},{19,3},{4,20},{20... | collective-permute-start | bytes 1572872 | tf_op jit(solution)/shard_map/ppermute | solution.py:107
  101.9 71.1 %collective-permute-start.9 = (f32[3,128,512]{2,1,0:T(8,128)S(1)}, f32[3,128,512]{2,1,0:T(8,128)S(1)}, u32[]{:S(2)}, u32[]{:S(2)}) collective-permute-start(f32[3,128,512]{2,1,0:T(8,128)S(1)} %get-tuple-element.45.in0), channel_id=1, source_target_pairs={{0,1},{2,3},{4,5},{6,7},{8,9},{10,11},{12,13},{14,15},{1,0},{3,2},... | collective-permute-start | bytes 2359304 | tf_op jit(solution)/shard_map/ppermute | solution.py:104
  102.0 39.2 %collective-permute-start.12 = (f32[3,128,512]{2,1,0:T(8,128)S(1)}, f32[3,128,512]{2,1,0:T(8,128)S(1)}, u32[]{:S(2)}, u32[]{:S(2)}) collective-permute-start(f32[3,128,512]{2,1,0:T(8,128)S(1)} %copy-done.16), channel_id=1, source_target_pairs={{1,2},{3,4},{5,6},{7,8},{9,10},{11,12},{13,14},{2,1},{4,3},{6,5},{... | collective-permute-start | bytes 2359304 | tf_op jit(solution)/shard_map/ppermute | solution.py:104
  103.9 54.1 %collective-permute-start.13 = (f32[3,128,512]{2,1,0:T(8,128)S(1)}, f32[3,128,512]{2,1,0:T(8,128)S(1)}, u32[]{:S(2)}, u32[]{:S(2)}) collective-permute-start(f32[3,128,512]{2,1,0:T(8,128)S(1)} %copy-done.12), channel_id=1, source_target_pairs={{1,2},{3,4},{5,6},{7,8},{9,10},{11,12},{13,14},{2,1},{4,3},{6,5},{... | collective-permute-start | bytes 2359304 | tf_op jit(solution)/shard_map/ppermute | solution.py:104
  108.9 49.1 %copy-start.14 = (f32[3,128,512]{2,1,0:T(8,128)S(1)}, f32[3,128,512]{2,1,0:T(8,128)}, u32[]{:S(2)}) copy-start(f32[3,128,512]{2,1,0:T(8,128)} %copy-done.13) | copy-start | bytes 2359300
  116.6 57.1 %collective-permute-start.10 = (f32[3,128,512]{2,1,0:T(8,128)S(1)}, f32[3,128,512]{2,1,0:T(8,128)S(1)}, u32[]{:S(2)}, u32[]{:S(2)}) collective-permute-start(f32[3,128,512]{2,1,0:T(8,128)S(1)} %get-tuple-element.46.in1), channel_id=1, source_target_pairs={{1,2},{3,4},{5,6},{7,8},{9,10},{11,12},{13,14},{2,1},{4,3},{6,5},{... | collective-permute-start | bytes 2359304 | tf_op jit(solution)/shard_map/ppermute | solution.py:104
  (12 other events, 12.6 us)
